TPU v7x, 32 devices: a whole 2x2x4 slice. The times are simulated.
32 devices in a mesh: img: 8 (over y, x, core), patch: 4 (over z).
Axes of the slice: x: 2, y: 2, z: 4, core: 2. Of those that a mesh axis runs over, the one named last changes fastest.
Arguments:
- tokens: bfloat16 [4, 8, 324, 512], P(None, 'img', 'patch')
- cotangent: bfloat16 [4, 8, 324, 512], P(None, 'img', 'patch'), may hold values from -6 to 6
- patch_count: int32 [4, 8], P(None, 'img'), may hold values from 100 to 324, as said below
- crop_index: int32 [4, 8, 324], P(None, 'img'), may hold values from 0 to 323, as said below
- in_weight: float32 [512, 3072], P('patch'), may hold values from -0.25 to 0.25
- in_moment: float32 [512, 3072], P('patch'), may hold values from -320 to 320
- in_average: float32 [512, 3072], P('patch'), may hold values from -0.25 to 0.25
- out_weight: float32 [1536, 512], P('patch'), may hold values from -0.3125 to 0.3125
- out_moment: float32 [1536, 512], P('patch'), may hold values from -256 to 256
- out_average: float32 [1536, 512], P('patch'), may hold values from -0.3125 to 0.3125
- spatial_weight: float32 [324, 324], P('patch'), may hold values from -0.3125 to 0.3125
- spatial_moment: float32 [324, 324], P('patch'), may hold values from -640 to 640
- spatial_average: float32 [324, 324], P('patch'), may hold values from -0.3125 to 0.3125
- vectors: float32 [8004], replicated
- vector_moment: float32 [8004], replicated, may hold values from -512 to 512
- vector_average: float32 [8004], replicated
Outputs:
- out_tokens: bfloat16 [4, 8, 324, 512], P(None, 'img', 'patch')
- in_grad: float32 [4, 8, 324, 512], P(None, 'img', 'patch')
- in_weight_new: float32 [512, 3072], P('patch')
- in_moment_new: float32 [512, 3072], P('patch')
- in_average_new: float32 [512, 3072], P('patch')
- out_weight_new: float32 [1536, 512], P('patch')
- out_moment_new: float32 [1536, 512], P('patch')
- out_average_new: float32 [1536, 512], P('patch')
- spatial_weight_new: float32 [324, 324], P('patch')
- spatial_moment_new: float32 [324, 324], P('patch')
- spatial_average_new: float32 [324, 324], P('patch')
- vectors_new: float32 [8004], replicated
- vector_moment_new: float32 [8004], replicated
- vector_average_new: float32 [8004], replicated
Inputs may be any that keep to these rules, and one draw needn't show every extreme that they name: `patch_count`: each image has 100, 196 or 324 patches, a square grid of side 10, 14 or 18; every micro-batch holds an image of 324 patches. `crop_index`: for an image of n patches, entries 0 to n - 1 are the cells of a square window of the 18 x 18 grid, row by row, as row * 18 + column; later entries are unused.
All inputs are finite; a program needn't handle non-finite values.
Results may differ from a plain program's by a relative error of at most 0.008.
Values may be sent and summed in bfloat16 or wider, within the bound.
No kernel may reach another device: no remote copies, remote signals or barrier semaphores. Data moves between devices by JAX's collectives and lax.ppermute only.
A program may use at most 192 MiB of HBM per device.

v0:
```python
import math

import jax
import jax.numpy as jnp
from jax import lax
from jax.sharding import PartitionSpec as P

EPS = 1e-05
MOMENTUM = 0.9
AVG_DECAY = 0.8


def layer_norm(values, gain_vec, shift_vec):
    row_mean = jnp.mean(values, axis=-1, keepdims=True)
    centered = values - row_mean
    variance = jnp.mean(centered * centered, axis=-1, keepdims=True)
    return centered * lax.rsqrt(variance + EPS) * gain_vec + shift_vec


def exact_gelu(values):
    return jax.nn.gelu(values, approximate=False)


def split_vectors(vectors, model_width, hidden_width, gate_width, cell_count):
    bounds = [
        model_width,
        model_width,
        hidden_width,
        gate_width,
        gate_width,
        cell_count,
        model_width,
    ]
    pieces = []
    offset = 0
    for length in bounds:
        pieces.append(vectors[offset : offset + length])
        offset = offset + length
    return pieces


def step_rates(images, model_width, gate_width, cell_count):
    live_rows = 207.0 * images
    rate_in = 1.0 / (math.sqrt(model_width) * 1.4 * math.sqrt(live_rows))
    rate_out = 1.0 / (math.sqrt(gate_width / 4.0) * 1.2 * math.sqrt(live_rows))
    rate_mix = 1.0 / (math.sqrt(cell_count) * 1.5 * math.sqrt(gate_width * images / 2.0))
    rate_vec = 0.1 / (2.0 * math.sqrt(live_rows))
    return (rate_in, rate_out, rate_mix, rate_vec)


def nesterov(weight, grads, moment, average, rate):
    moment_new = MOMENTUM * moment + grads
    weight_new = weight - rate * (grads + MOMENTUM * moment_new)
    average_new = AVG_DECAY * average + (1.0 - AVG_DECAY) * weight_new
    return (weight_new, moment_new, average_new)


def shards(
    tokens,
    cotangent,
    patch_count,
    crop_index,
    in_weight,
    in_moment,
    in_average,
    out_weight,
    out_moment,
    out_average,
    spatial_weight,
    spatial_moment,
    spatial_average,
    vectors,
    vector_moment,
    vector_average,
):
    group_size = lax.axis_size("patch")
    shard_idx = lax.axis_index("patch")
    in_low, out_low, mix_low = (
        lax.all_gather(in_weight.astype(jnp.bfloat16), "patch", axis=0, tiled=True),
        lax.all_gather(out_weight.astype(jnp.bfloat16), "patch", axis=0, tiled=True),
        lax.all_gather(spatial_weight.astype(jnp.bfloat16), "patch", axis=0, tiled=True),
    )
    micro_count, slot_count, row_count, model_width = tokens.shape
    hidden_width = in_low.shape[1]
    gate_width = hidden_width // 2
    cell_count = mix_low.shape[0]
    flat_rows = slot_count * row_count
    gain_one, shift_one, bias_in, gain_two, shift_two, bias_mix, bias_out = split_vectors(
        vectors, model_width, hidden_width, gate_width, cell_count
    )
    within = jnp.arange(row_count, dtype=jnp.int32)
    every_slot = jnp.arange(cell_count, dtype=jnp.int32)
    slot_block = every_slot // row_count
    slot_within = every_slot % row_count
    grad_in = jnp.zeros((model_width, hidden_width), jnp.float32)
    grad_out = jnp.zeros((gate_width, model_width), jnp.float32)
    grad_mix = jnp.zeros((cell_count, cell_count), jnp.float32)
    grad_pieces = [
        jnp.zeros((length,), jnp.float32)
        for length in [
            model_width,
            model_width,
            hidden_width,
            gate_width,
            gate_width,
            cell_count,
            model_width,
        ]
    ]
    outs_tok = []
    outs_grad = []
    for micro_idx in range(micro_count):
        tok_rows = tokens[micro_idx].reshape(flat_rows, model_width).astype(jnp.float32)
        cot_rows = cotangent[micro_idx].reshape(flat_rows, model_width)
        per_shard = patch_count[micro_idx] // group_size
        crop_rows = crop_index[micro_idx]
        live_rows = within[None, :] < per_shard[:, None]
        row_order = jnp.clip(shard_idx * per_shard[:, None] + within[None, :], 0, cell_count - 1)
        row_place = jnp.where(live_rows, jnp.take_along_axis(crop_rows, row_order, axis=1), 0)
        col_live = slot_within[None, :] < per_shard[:, None]
        col_order = jnp.clip(
            slot_block[None, :] * per_shard[:, None] + slot_within[None, :], 0, cell_count - 1
        )
        col_place = jnp.where(col_live, jnp.take_along_axis(crop_rows, col_order, axis=1), 0)
        live_flat = live_rows.reshape(flat_rows)[:, None]
        normed, norm_back = jax.vjp(layer_norm, tok_rows, gain_one, shift_one)
        normed_low = normed.astype(jnp.bfloat16)
        pre_act = jnp.dot(normed_low, in_low, preferred_element_type=jnp.float32) + bias_in
        activated, gelu_back = jax.vjp(exact_gelu, pre_act)
        left_half = activated[:, :gate_width]
        right_normed, right_back = jax.vjp(
            layer_norm, activated[:, gate_width:], gain_two, shift_two
        )
        right_low = right_normed.astype(jnp.bfloat16).reshape(slot_count, row_count, gate_width)
        gathered = lax.all_gather(right_low, "patch", axis=1, tiled=True)
        mixing = mix_low[row_place[:, :, None], col_place[:, None, :]] * col_live[
            :, None, :
        ].astype(jnp.bfloat16)
        spatial = (
            jnp.einsum("gst,gtc->gsc", mixing, gathered, preferred_element_type=jnp.float32)
            + bias_mix[row_place][:, :, None]
        )
        spatial = spatial.reshape(flat_rows, gate_width)
        gated_low = (left_half * spatial).astype(jnp.bfloat16)
        branch = jnp.dot(gated_low, out_low, preferred_element_type=jnp.float32) + bias_out
        outs_tok.append(
            jnp.where(live_flat, tok_rows + branch, 0.0)
            .astype(jnp.bfloat16)
            .reshape(slot_count, row_count, model_width)
        )
        cot_low = jnp.where(live_flat, cot_rows, jnp.zeros_like(cot_rows))
        cot_full = cot_low.astype(jnp.float32)
        grad_out = grad_out + jnp.einsum(
            "nc,nd->cd", gated_low, cot_low, preferred_element_type=jnp.float32
        )
        gated_grad = jnp.einsum("nd,cd->nc", cot_low, out_low, preferred_element_type=jnp.float32)
        left_grad = gated_grad * spatial
        spatial_grad = (
            (gated_grad * left_half).astype(jnp.bfloat16).reshape(slot_count, row_count, gate_width)
        )
        pair_grads = jnp.einsum(
            "gsc,gtc->gst", spatial_grad, gathered, preferred_element_type=jnp.float32
        ) * col_live[:, None, :].astype(jnp.float32)
        grad_mix = grad_mix.at[row_place[:, :, None], col_place[:, None, :]].add(pair_grads)
        mix_bias_grad = (
            jnp.zeros((cell_count,), jnp.float32)
            .at[row_place]
            .add(jnp.sum(spatial_grad.astype(jnp.float32), axis=2))
        )
        partial_value = jnp.einsum(
            "gst,gsc->gtc", mixing, spatial_grad, preferred_element_type=jnp.float32
        )
        right_grad = lax.psum_scatter(partial_value, "patch", scatter_dimension=1, tiled=True)
        right_in_grad, gain_two_grad, shift_two_grad = right_back(
            right_grad.reshape(flat_rows, gate_width)
        )
        (pre_grad,) = gelu_back(jnp.concatenate([left_grad, right_in_grad], axis=1))
        pre_low = pre_grad.astype(jnp.bfloat16)
        grad_in = grad_in + jnp.einsum(
            "nd,nf->df", normed_low, pre_low, preferred_element_type=jnp.float32
        )
        normed_grad = jnp.einsum("nf,df->nd", pre_low, in_low, preferred_element_type=jnp.float32)
        token_grad, gain_one_grad, shift_one_grad = norm_back(normed_grad)
        outs_grad.append(
            jnp.where(live_flat, cot_full + token_grad, 0.0).reshape(
                slot_count, row_count, model_width
            )
        )
        new_terms = [
            gain_one_grad,
            shift_one_grad,
            jnp.sum(pre_low.astype(jnp.float32), axis=0),
            gain_two_grad,
            shift_two_grad,
            mix_bias_grad,
            jnp.sum(cot_full, axis=0),
        ]
        grad_pieces = [old_term + new_term for old_term, new_term in zip(grad_pieces, new_terms)]
    grad_vec = jnp.concatenate(grad_pieces)
    in_rows = in_weight.shape[0]
    out_rows = out_weight.shape[0]
    mix_rows = spatial_weight.shape[0]
    in_sum, out_sum, mix_sum, vec_sum = lax.psum(
        (grad_in, grad_out, grad_mix, grad_vec), ("img", "patch")
    )
    in_share = lax.dynamic_slice_in_dim(in_sum, shard_idx * in_rows, in_rows, 0)
    out_share = lax.dynamic_slice_in_dim(out_sum, shard_idx * out_rows, out_rows, 0)
    mix_share = lax.dynamic_slice_in_dim(mix_sum, shard_idx * mix_rows, mix_rows, 0)
    images = micro_count * slot_count * lax.axis_size("img")
    rate_in, rate_out, rate_mix, rate_vec = step_rates(images, model_width, gate_width, cell_count)
    in_new = nesterov(in_weight, in_share, in_moment, in_average, rate_in)
    out_new = nesterov(out_weight, out_share, out_moment, out_average, rate_out)
    mix_new = nesterov(spatial_weight, mix_share, spatial_moment, spatial_average, rate_mix)
    vec_new = nesterov(vectors, vec_sum, vector_moment, vector_average, rate_vec)
    return (
        jnp.stack(outs_tok),
        jnp.stack(outs_grad),
        in_new[0],
        in_new[1],
        in_new[2],
        out_new[0],
        out_new[1],
        out_new[2],
        mix_new[0],
        mix_new[1],
        mix_new[2],
        vec_new[0],
        vec_new[1],
        vec_new[2],
    )


def solution(mesh):
    return jax.shard_map(
        shards,
        mesh=mesh,
        in_specs=(
            P(None, "img", "patch", None),
            P(None, "img", "patch", None),
            P(None, "img"),
            P(None, "img", None),
            P("patch", None),
            P("patch", None),
            P("patch", None),
            P("patch", None),
            P("patch", None),
            P("patch", None),
            P("patch", None),
            P("patch", None),
            P("patch", None),
            P(),
            P(),
            P(),
        ),
        out_specs=(
            P(None, "img", "patch", None),
            P(None, "img", "patch", None),
            P("patch", None),
            P("patch", None),
            P("patch", None),
            P("patch", None),
            P("patch", None),
            P("patch", None),
            P("patch", None),
            P("patch", None),
            P("patch", None),
            P(),
            P(),
            P(),
        ),
        check_vma=False,
    )
```

profile of v0, /device:TPU:0, one launch (start us, length us, event | category | flops | bytes accessed | tf_op | source)
XLA Modules:
  0.0 2770.6 jit_solution(6014967229902178396)
XLA Ops:
  7.2 2.5 convert_element_type.212
  25.6 2.8 gather_fusion.13
  29.7 2.8 gather_fusion.15
  33.8 2.8 gather_fusion.9
  37.9 2.8 gather_fusion.11
  42.6 18.6 all-gather.4
  63.1 315.5 %gather_fusion = bf16[26244]{0:T(1024)(128)(2,1)S(1)} fusion(bf16[324,324]{1,0:T(8,128)(2,1)S(1)} %reshape.1537, s32[26244]{0:T(1024)S(1)} %reshape.1375), kind=kCustom, calls=%fused_computation.8 | custom fusion | bytes 314928 | tf_op jit(solution)/shard_map/gather | solution.py:136
  379.6 315.5 %gather_fusion.4 = bf16[26244]{0:T(1024)(128)(2,1)S(1)} fusion(bf16[324,324]{1,0:T(8,128)(2,1)S(1)} %reshape.1537, s32[26244]{0:T(1024)S(1)} %reshape.1407), kind=kCustom, calls=%fused_computation.12 | custom fusion | bytes 314928 | tf_op jit(solution)/shard_map/gather | solution.py:136
  695.5 315.5 %gather_fusion.2 = bf16[26244]{0:T(1024)(128)(2,1)S(1)} fusion(bf16[324,324]{1,0:T(8,128)(2,1)S(1)} %reshape.1537, s32[26244]{0:T(1024)S(1)} %reshape.1391), kind=kCustom, calls=%fused_computation.10 | custom fusion | bytes 314928 | tf_op jit(solution)/shard_map/gather | solution.py:136
  1011.8 315.8 %gather_fusion.6 = bf16[26244]{0:T(1024)(128)(2,1)S(1)} fusion(bf16[324,324]{1,0:T(8,128)(2,1)S(1)} %reshape.1537, s32[26244]{0:T(1024)S(1)} %reshape.1423), kind=kCustom, calls=%fused_computation.14 | custom fusion | bytes 314928 | tf_op jit(solution)/shard_map/gather | solution.py:136
  1333.4 6.0 multiply_multiply_fusion.20
  1339.5 3.7 convert_reduce_fusion.4
  1344.3 3.3 copy.61
  1347.6 4.4 multiply_multiply_fusion.21
  1355.4 3.3 copy.59
  1358.7 3.9 multiply_multiply_fusion.22
  1366.0 3.3 copy.57
  1369.4 3.9 multiply_multiply_fusion.23
  1376.8 3.4 copy.55
  1421.7 2.4 scatter_custom_fusion
  1427.2 233.4 %all-reduce.11.cloned.1.call-done = (f32[1,324,1536]{2,0,1:T(1,128)}, f32[1,324,1536]{2,0,1:T(1,128)}, f32[1,324,1536]{2,0,1:T(1,128)}, f32[1,324,1536]{2,0,1:T(1,128)}) async-done(((f32[1,324,1536]{2,0,1:T(1,128)}, f32[1,324,1536]{2,0,1:T(1,128)}, f32[1,324,1536]{2,0,1:T(1,128)}, f32[1,324,1536]{2,0,1:T(1,128)}), (f32[1,324,1536]{2,0,1:T(1,128)}, f32[1,324,1536]{2,0,1:T(1,128)}, f32[1,324,1536]{2,0,1:T(1,128)}, ...) | async-done | bytes 7962640
  1660.7 2.3 fusion.242
  1663.0 2.3 fusion.241
  1665.3 2.3 fusion.239
  1671.1 2.4 fusion.43
  1677.3 22.0 all-gather.8
  1703.1 22.9 all-gather.5
  1725.9 2.5 reshape.1539
  1730.9 23.4 all-gather.6
  1754.3 2.5 reshape.1541
  1756.9 2.4 convolution_multiply_fusion.2
  1760.3 21.7 all-gather.7
  1782.1 2.5 reshape.1543
  1784.6 2.3 convolution_multiply_fusion.1
  1788.0 2.7 fusion.251
  1790.7 2.3 fusion.262
  1801.9 182.2 %scatter_custom_fusion.2 = f32[104976]{0:T(1024)S(1)} fusion(s32[26244]{0:T(1024)} %reshape.1455, f32[26244]{0:T(1024)} %reshape.1457, f32[]{:T(128)} %constant.194.clone.1), kind=kCustom, calls=%fused_computation.274 | custom fusion | flops 26244 | bytes 420416
  1984.1 182.5 %scatter_fusion = f32[104976]{0:T(1024)S(1)} fusion(f32[104976]{0:T(1024)S(1)} %scatter_custom_fusion.2, s32[26244]{0:T(1024)S(1)} %copy-done.91, f32[26244]{0:T(1024)S(1)} %reshape.1465), kind=kCustom, calls=%fused_computation.19 | custom fusion | flops 26244 | bytes 419904
  2166.6 182.5 %scatter_fusion.1 = f32[104976]{0:T(1024)S(1)} fusion(f32[104976]{0:T(1024)S(1)} %scatter_fusion, s32[26244]{0:T(1024)S(1)} %copy-done.92, f32[26244]{0:T(1024)S(1)} %reshape.1473), kind=kCustom, calls=%fused_computation.20 | custom fusion | flops 26244 | bytes 419904
  2349.2 182.8 %scatter_fusion.2 = f32[104976]{0:T(1024)S(1)} fusion(f32[104976]{0:T(1024)S(1)} %scatter_fusion.1, s32[26244]{0:T(1024)S(1)} %copy-done.90, f32[26244]{0:T(1024)S(1)} %copy-done.93), kind=kCustom, calls=%fused_computation.21 | custom fusion | flops 26244 | bytes 419904
  2533.3 2.5 convolution_add_fusion.6
  2536.9 2.3 convolution_add_fusion.4
  2552.4 3.9 add_add_fusion
  2558.2 2.3 fusion.231
  2569.2 41.1 %psum.31 = f32[8004]{0:T(1024)S(1)} all-reduce(f32[8004]{0:T(1024)S(1)} %concatenate.51), channel_id=1, replica_groups=mesh['img'=8,'patch'=4] {'img','patch'}, use_global_device_ids=true, to_apply=%region_73.76 | all-reduce | flops 8004 | bytes 64032 | tf_op jit(solution)/shard_map/psum | solution.py:203
  2611.7 142.6 %all-reduce.9.cloned.1.call-done = (f32[512,3072]{1,0:T(8,128)}, f32[1536,512]{1,0:T(8,128)}, f32[324,324]{1,0:T(8,128)}) async-done(((f32[512,3072]{1,0:T(8,128)}, f32[1536,512]{1,0:T(8,128)}, f32[324,324]{1,0:T(8,128)}), (f32[512,3072]{1,0:T(8,128)}, f32[1536,512]{1,0:T(8,128)}, f32[324,324]{1,0:T(8,128)})) %all-reduce.9.cloned.1.call-update) | async-done | bytes 9857104 | tf_op jit(solution)/shard_map/psum | solution.py:203
  2754.4 4.8 multiply_add_fusion
  2761.0 2.8 multiply_add_fusion.2
  (626 shorter events, 128.7 us)
Async XLA Ops:
  7.2 1326.2 %all-gather.12.cloned.1.call-start = ((), (), s32[]{:S(2)}) async-start(), calls=%async_computation | async-start | bytes 3932160 | tf_op jit(solution)/shard_map/all_gather | solution.py:79
  9.7 14.6 copy-start.149
  9.7 1329.8 %all-gather.14.cloned.1.call-start = ((), (), s32[]{:S(2)}) async-start(), calls=%async_computation.1 | async-start | bytes 1966080 | tf_op jit(solution)/shard_map/all_gather | solution.py:80
  10.6 1650.1 %all-reduce.11.cloned.1.call-start = ((), (), s32[]{:S(2)}) async-start(), calls=%async_computation.3 | async-start | bytes 15925248
  21.7 1310.2 %copy-start.165 = (pred[81]{0:T(512)(128)(4,1)}, pred[81]{0:T(512)(128)(4,1)S(1)}, u32[]{:S(2)}) copy-start(pred[81]{0:T(512)(128)(4,1)S(1)} %iota_compare_fusion.3) | copy-start | bytes 247
  22.3 1309.6 %copy-start.171 = (pred[81]{0:T(512)(128)(4,1)}, pred[81]{0:T(512)(128)(4,1)S(1)}, u32[]{:S(2)}) copy-start(pred[81]{0:T(512)(128)(4,1)S(1)} %iota_compare_fusion.2) | copy-start | bytes 247
  22.9 1309.7 %copy-start.168 = (pred[81]{0:T(512)(128)(4,1)}, pred[81]{0:T(512)(128)(4,1)S(1)}, u32[]{:S(2)}) copy-start(pred[81]{0:T(512)(128)(4,1)S(1)} %iota_compare_fusion) | copy-start | bytes 247
  23.4 1309.2 %copy-start.174 = (pred[81]{0:T(512)(128)(4,1)}, pred[81]{0:T(512)(128)(4,1)S(1)}, u32[]{:S(2)}) copy-start(pred[81]{0:T(512)(128)(4,1)S(1)} %iota_compare_fusion.1) | copy-start | bytes 247
  29.7 31.6 %copy-start.164 = (s32[81]{0:T(128)}, s32[81]{0:T(128)S(1)}, u32[]{:S(2)}) copy-start(s32[81]{0:T(128)S(1)} %gather_fusion.14) | copy-start | bytes 976
  41.2 20.6 copy-start.161
  41.8 20.0 copy-start.163
  42.5 19.3 copy-start.179
  42.5 1316.1 %copy-start.131 = (f32[3072]{0:T(1024)}, f32[3072]{0:T(1024)S(1)}, u32[]{:S(2)}) copy-start(f32[3072]{0:T(1024)S(1)} %slice.97) | copy-start | bytes 36868
  42.5 19.3 copy-start.193
  378.6 316.5 %copy-start.86 = (bf16[26244]{0:T(1024)(128)(2,1)}, bf16[26244]{0:T(1024)(128)(2,1)S(1)}, u32[]{:S(2)}) copy-start(bf16[26244]{0:T(1024)(128)(2,1)S(1)} %gather_fusion) | copy-start | bytes 157468
  695.1 315.9 %copy-start.87 = (bf16[26244]{0:T(1024)(128)(2,1)}, bf16[26244]{0:T(1024)(128)(2,1)S(1)}, u32[]{:S(2)}) copy-start(bf16[26244]{0:T(1024)(128)(2,1)S(1)} %gather_fusion.4) | copy-start | bytes 157468
  1011.8 316.6 %copy-start.65 = (bf16[4,1,81,512]{3,0,2,1:T(4,128)(2,1)S(1)}, bf16[4,1,81,512]{3,0,2,1:T(4,128)(2,1)}, u32[]{:S(2)}) copy-start(bf16[4,1,81,512]{3,0,2,1:T(4,128)(2,1)} %param.20) | copy-start | bytes 995332
  1329.0 469.9 %copy-start.16 = (bf16[1,1,81,512]{3,2,1,0:T(8,128)(2,1)}, bf16[1,1,81,512]{3,2,1,0:T(8,128)(2,1)S(1)}, u32[]{:S(2)}) copy-start(bf16[1,1,81,512]{3,2,1,0:T(8,128)(2,1)S(1)} %get-tuple-element.247) | copy-start | bytes 248836
  1329.0 470.9 %copy-start.20 = (bf16[1,1,81,512]{3,2,1,0:T(8,128)(2,1)}, bf16[1,1,81,512]{3,2,1,0:T(8,128)(2,1)S(1)}, u32[]{:S(2)}) copy-start(bf16[1,1,81,512]{3,2,1,0:T(8,128)(2,1)S(1)} %get-tuple-element.162) | copy-start | bytes 248836
  1329.0 29.6 %copy-start.126 = (f32[81]{0:T(128)}, f32[81]{0:T(128)S(1)}, u32[]{:S(2)}) copy-start(f32[81]{0:T(128)S(1)} %broadcast_multiply_fusion.6) | copy-start | bytes 976
  1330.0 28.7 %copy-start.139 = (f32[81]{0:T(128)}, f32[81]{0:T(128)S(1)}, u32[]{:S(2)}) copy-start(f32[81]{0:T(128)S(1)} %fusion.204) | copy-start | bytes 976
  1330.1 469.2 %copy-start.29 = (bf16[1,1,81,512]{3,2,1,0:T(8,128)(2,1)}, bf16[1,1,81,512]{3,2,1,0:T(8,128)(2,1)S(1)}, u32[]{:S(2)}) copy-start(bf16[1,1,81,512]{3,2,1,0:T(8,128)(2,1)S(1)} %get-tuple-element.170) | copy-start | bytes 248836
  1330.1 470.3 %copy-start.18 = (bf16[1,1,81,512]{3,2,1,0:T(8,128)(2,1)}, bf16[1,1,81,512]{3,2,1,0:T(8,128)(2,1)S(1)}, u32[]{:S(2)}) copy-start(bf16[1,1,81,512]{3,2,1,0:T(8,128)(2,1)S(1)} %get-tuple-element.245) | copy-start | bytes 248836
  1330.1 17.5 copy-start.123
  1330.5 17.2 copy-start.136
  1331.4 38.0 %copy-start.82 = (f32[512]{0:T(512)}, f32[512]{0:T(512)S(1)}, u32[]{:S(2)}) copy-start(f32[512]{0:T(512)S(1)} %get-tuple-element.201) | copy-start | bytes 6148
  1331.4 38.0 %copy-start.96 = (f32[512]{0:T(512)}, f32[512]{0:T(512)S(1)}, u32[]{:S(2)}) copy-start(f32[512]{0:T(512)S(1)} %get-tuple-element.200) | copy-start | bytes 6148
  1332.6 30.2 %copy-start.62 = (bf16[81,512]{1,0:T(8,128)(2,1)}, bf16[81,512]{1,0:T(8,128)(2,1)S(1)}, u32[]{:S(2)}) copy-start(bf16[81,512]{1,0:T(8,128)(2,1)S(1)} %get-tuple-element.101) | copy-start | bytes 248836
  1332.6 458.1 %copy-start.54 = (bf16[81,512]{1,0:T(8,128)(2,1)}, bf16[81,512]{1,0:T(8,128)(2,1)S(1)}, u32[]{:S(2)}) copy-start(bf16[81,512]{1,0:T(8,128)(2,1)S(1)} %get-tuple-element.251) | copy-start | bytes 248836
  1333.3 18.9 copy-start.59
  1373.3 301.2 %copy-start.5 = (f32[81,3072]{1,0:T(8,128)}, f32[81,3072]{1,0:T(8,128)S(1)}, u32[]{:S(2)}) copy-start(f32[81,3072]{1,0:T(8,128)S(1)} %get-tuple-element.155) | copy-start | bytes 2985988
  1380.1 8.1 copy-start.162
  1380.2 1374.2 %all-reduce.9.cloned.1.call-start = ((), (), s32[]{:S(2)}) async-start(), calls=%async_computation.2 | async-start | bytes 19881984 | tf_op jit(solution)/shard_map/psum | solution.py:203
  1396.7 7.2 copy-start.180
  1403.9 14.5 copy-start.141
  1403.9 14.5 copy-start.142
  1403.9 14.5 copy-start.143
  1660.7 9.1 copy-start.13
  1663.0 6.8 copy-start.10
  1800.9 183.2 %copy-start.91 = (s32[26244]{0:T(1024)S(1)}, s32[26244]{0:T(1024)}, u32[]{:S(2)}) copy-start(s32[26244]{0:T(1024)} %reshape.1463) | copy-start | bytes 314932
  1984.1 182.5 %copy-start.92 = (s32[26244]{0:T(1024)S(1)}, s32[26244]{0:T(1024)}, u32[]{:S(2)}) copy-start(s32[26244]{0:T(1024)} %reshape.1471) | copy-start | bytes 314932
  2166.6 182.5 %copy-start.90 = (s32[26244]{0:T(1024)S(1)}, s32[26244]{0:T(1024)}, u32[]{:S(2)}) copy-start(s32[26244]{0:T(1024)} %reshape.1479) | copy-start | bytes 314932
  2166.6 182.5 %copy-start.93 = (f32[26244]{0:T(1024)S(1)}, f32[26244]{0:T(1024)}, u32[]{:S(2)}) copy-start(f32[26244]{0:T(1024)} %reshape.1481) | copy-start | bytes 314932
  2349.2 184.2 %copy-start.63 = (bf16[81,512]{1,0:T(8,128)(2,1)S(1)}, bf16[81,512]{1,0:T(8,128)(2,1)}, u32[]{:S(2)}) copy-start(bf16[81,512]{1,0:T(8,128)(2,1)} %copy-done.62) | copy-start | bytes 248836
  2564.0 46.3 %copy-start.104 = (f32[8004]{0:T(1024)S(1)}, f32[8004]{0:T(1024)}, u32[]{:S(2)}) copy-start(f32[8004]{0:T(1024)} %param.33) | copy-start | bytes 96052
  2566.6 187.7 %copy-start.53 = (f32[128,3072]{1,0:T(8,128)S(1)}, f32[128,3072]{1,0:T(8,128)}, u32[]{:S(2)}) copy-start(f32[128,3072]{1,0:T(8,128)} %param.26) | copy-start | bytes 4718596
  2566.7 187.7 %copy-start.15 = (f32[128,3072]{1,0:T(8,128)S(1)}, f32[128,3072]{1,0:T(8,128)}, u32[]{:S(2)}) copy-start(f32[128,3072]{1,0:T(8,128)} %param.24) | copy-start | bytes 4718596
  2754.4 6.6 copy-start.84
  (158 other events, 322.0 us)
Sparse Core Ops, SparseCore 0:
  10.2 70.3 all-gather.11
  82.7 35.8 all-gather.13
  1380.3 280.3 all-reduce.10
  2556.4 197.8 all-reduce.8
where the time goes:
time: 2780 us; the launch traced here: 2770 us
  local copies, waits for them, and re-layouts  1350 us (49%)
  other arithmetic  800 us (29%)
  waiting for transfers between devices  376 us (14%)
  blocking collectives  150 us (5%)
  matrix products  70.3 us (3%)
    gather x12, local copies, waits for them, and re-layouts, shards(): mix_low[row_place[:, :, None], col_place[:, None, :]]  1270 us
    unnamed x14, other arithmetic  741 us
    unnamed x5, waiting for transfers between devices  234 us
    psum x1, waiting for transfers between devices, shards(): lax.psum((grad_in, grad_out, grad_mix, grad_vec), ('img', 'patch'))  143 us
    all_gather x4, blocking collectives, shards(): gathered = lax.all_gather(right_low, 'patch', axis=1, tiled=True)  90 us
  transfers between devices with their start and end apart: 4, of which 2 were waited for; matrix products, arithmetic and copies ran while one was open for 49% of the time, Pallas kernels for 0%

commit v1 on v0

v1 whole, which is shorter than its diff:
```python
import math

import jax
import jax.numpy as jnp
from jax import lax
from jax.sharding import PartitionSpec as P

EPS = 1e-05
MOMENTUM = 0.9
AVG_DECAY = 0.8
BF = jnp.bfloat16
F32 = jnp.float32


def step_rates(images, model_width, gate_width, cell_count):
    live_rows = 207.0 * images
    rate_in = 1.0 / (math.sqrt(model_width) * 1.4 * math.sqrt(live_rows))
    rate_out = 1.0 / (math.sqrt(gate_width / 4.0) * 1.2 * math.sqrt(live_rows))
    rate_mix = 1.0 / (math.sqrt(cell_count) * 1.5 * math.sqrt(gate_width * images / 2.0))
    rate_vec = 0.1 / (2.0 * math.sqrt(live_rows))
    return (rate_in, rate_out, rate_mix, rate_vec)


def nesterov(weight, grads, moment, average, rate):
    moment_new = MOMENTUM * moment + grads
    weight_new = weight - rate * (grads + MOMENTUM * moment_new)
    average_new = AVG_DECAY * average + (1.0 - AVG_DECAY) * weight_new
    return (weight_new, moment_new, average_new)


def xor_pairs(n, mask):
    return [(k, k ^ mask) for k in range(n)]


def turn(arr, r):
    n = lax.axis_size("patch")
    if r % n == 0:
        return arr
    return lax.ppermute(arr, "patch", [(s, (s + r) % n) for s in range(n)])


def swap(arr, mask):
    return lax.ppermute(arr, "img", xor_pairs(lax.axis_size("img"), mask))


def own_bit(mask):
    return (lax.axis_index("img") & mask) != 0


def join(arr, mask, axis):
    other = swap(arr, mask)
    bit = own_bit(mask)
    return jnp.concatenate([jnp.where(bit, other, arr), jnp.where(bit, arr, other)], axis)


def halve(arr, mask, axis):
    half = arr.shape[axis] // 2
    low = lax.slice_in_dim(arr, 0, half, axis=axis)
    high = lax.slice_in_dim(arr, half, 2 * half, axis=axis)
    bit = own_bit(mask)
    keep = jnp.where(bit, high, low).astype(F32)
    got = swap(jnp.where(bit, low, high).astype(BF), mask)
    return keep + got.astype(F32)


CORE, XBIT, YBIT = 1, 2, 4


def gather_shards(shard):
    rows, cols = shard.shape
    unit = rows // 8
    u = lax.axis_index("img") % 8
    piece = lax.dynamic_slice_in_dim(shard, u * unit, unit, 0)
    got = jnp.stack([turn(piece, r) for r in (1, 2, 3)]).reshape(3, 1, 1, 1, unit, cols)
    half = cols // 2
    left, right = got[..., :half], got[..., half:]
    left = join(left, XBIT, 2)
    right = join(right, YBIT, 1)
    left = join(left, YBIT, 1)
    right = join(right, XBIT, 2)
    both = jnp.concatenate([left, right], axis=-1)
    both = join(both, CORE, 3)
    return jnp.concatenate([shard[None], both.reshape(3, rows, cols)])


def to_absolute(rel):
    p = lax.axis_index("patch")
    flipped = rel[::-1]
    twice = jnp.concatenate([flipped, flipped])
    return lax.dynamic_slice_in_dim(twice, (3 - p) % 4, 4, 0)


def reduce_shards(grad):
    n, rows, cols = grad.shape
    unit = rows // 8
    p = lax.axis_index("patch")
    g = grad.reshape(n, 2, 2, 2, unit, cols)
    g = halve(g, CORE, 3).astype(BF)
    half = cols // 2
    left, right = g[..., :half], g[..., half:]
    left = halve(left, XBIT, 2).astype(BF)
    right = halve(right, YBIT, 1).astype(BF)
    left = halve(left, YBIT, 1)
    right = halve(right, XBIT, 2)
    g = jnp.concatenate([left, right], axis=-1)
    mask = 8
    while mask < lax.axis_size("img"):
        g = g + swap(g, mask)
        mask = mask * 2
    mine = lax.dynamic_slice_in_dim(g, p, 1, 0)
    for r in (1, 2, 3):
        away = lax.dynamic_slice_in_dim(g, (p + r) % 4, 1, 0).astype(BF)
        mine = mine + turn(away, r).astype(F32)
    mine = mine.astype(BF)
    left, right = mine[..., :half], mine[..., half:]
    left = join(left, YBIT, 1)
    right = join(right, XBIT, 2)
    left = join(left, XBIT, 2)
    right = join(right, YBIT, 1)
    whole = join(jnp.concatenate([left, right], axis=-1), CORE, 3)
    return whole.reshape(rows, cols).astype(F32)


def all_sum(arr):
    mask = 1
    while mask < lax.axis_size("img"):
        arr = arr + swap(arr, mask)
        mask = mask * 2
    for mask in (1, 2):
        arr = arr + lax.ppermute(arr, "patch", xor_pairs(4, mask))
    return arr


def dot(a, b, ca, cb):
    return lax.dot_general(a, b, (((ca,), (cb,)), ((), ())), preferred_element_type=F32)


def shards(
    tokens,
    cotangent,
    patch_count,
    crop_index,
    in_weight,
    in_moment,
    in_average,
    out_weight,
    out_moment,
    out_average,
    spatial_weight,
    spatial_moment,
    spatial_average,
    vectors,
    vector_moment,
    vector_average,
):
    p = lax.axis_index("patch")
    nz = lax.axis_size("patch")
    micro_count, slot_count, row_count, width = tokens.shape
    assert micro_count == nz == 4 and slot_count == 1
    hidden = in_weight.shape[1]
    gate = hidden // 2
    cells = spatial_weight.shape[1]
    grid = math.isqrt(cells)

    in_low = to_absolute(gather_shards(in_weight.astype(BF))).reshape(width, hidden)
    mix_rows = spatial_weight.shape[0]
    mix_pad = 128
    mixed = jnp.pad(spatial_weight.astype(BF), ((0, mix_pad - mix_rows), (0, width - cells)))
    out_rows = out_weight.shape[0]
    second = jnp.concatenate(
        [out_weight.astype(BF).reshape(8, out_rows // 8, width), mixed.reshape(8, mix_pad // 8, width)], axis=1
    ).reshape(out_rows + mix_pad, width)
    second = to_absolute(gather_shards(second)).reshape(4, 8, (out_rows + mix_pad) // 8, width)
    out_low = second[:, :, : out_rows // 8].reshape(gate, width)
    mix_low = second[:, :, out_rows // 8 :].reshape(4, mix_pad, width)[:, :mix_rows, :cells].reshape(cells, cells)

    def collect(arr):
        return jnp.concatenate(
            [turn(lax.dynamic_index_in_dim(arr, (p + r) % 4, 0, keepdims=False)[0], r) for r in range(4)]
        )

    count = lax.dynamic_index_in_dim(patch_count, p, 0, keepdims=False)[0]
    first = lax.dynamic_index_in_dim(crop_index, p, 0, keepdims=False)[0, 0]
    quarter = count // 4
    side = jnp.round(jnp.sqrt(count.astype(F32))).astype(jnp.int32)
    place = jnp.arange(cells, dtype=jnp.int32)
    drow = place // grid - first // grid
    dcol = place % grid - first % grid
    inside = (drow >= 0) & (drow < side) & (dcol >= 0) & (dcol < side)
    order = drow * side + dcol
    block = (
        (order >= quarter).astype(jnp.int32)
        + (order >= 2 * quarter).astype(jnp.int32)
        + (order >= 3 * quarter).astype(jnp.int32)
    )
    slot = ((p - block) % 4) * row_count + order - block * quarter
    slot = jnp.where(inside, slot, -1)
    onehot = (slot[:, None] == jnp.arange(cells, dtype=jnp.int32)[None, :]).astype(BF)
    live = inside[:, None]

    tok_low = dot(onehot, collect(tokens), 1, 0).astype(BF)
    cot_low = dot(onehot, collect(cotangent), 1, 0).astype(BF)

    bounds = [width, width, hidden, gate, gate, cells, width]
    pieces = []
    offset = 0
    for length in bounds:
        pieces.append(vectors[offset : offset + length])
        offset += length
    gain_one, shift_one, bias_in, gain_two, shift_two, bias_mix, bias_out = pieces

    x = tok_low.astype(F32)
    mean1 = jnp.mean(x, -1, keepdims=True)
    cen1 = x - mean1
    rstd1 = lax.rsqrt(jnp.mean(cen1 * cen1, -1, keepdims=True) + EPS)
    xhat = cen1 * rstd1
    xn = (xhat * gain_one + shift_one).astype(BF)
    pre = dot(xn, in_low, 1, 0) + bias_in
    phi = 0.5 * (1.0 + lax.erf(pre * math.sqrt(0.5)))
    slope = phi + pre * jnp.exp(-0.5 * pre * pre) * (1.0 / math.sqrt(2.0 * math.pi))
    act = pre * phi
    u = act[:, :gate]
    v = act[:, gate:]
    mean2 = jnp.mean(v, -1, keepdims=True)
    cen2 = v - mean2
    rstd2 = lax.rsqrt(jnp.mean(cen2 * cen2, -1, keepdims=True) + EPS)
    vhat = cen2 * rstd2
    vn = jnp.where(live, vhat * gain_two + shift_two, 0.0).astype(BF)
    spatial = dot(mix_low, vn, 1, 0) + bias_mix[:, None]
    gated = (u * spatial).astype(BF)
    branch = dot(gated, out_low, 1, 0) + bias_out
    out_pos = jnp.where(live, x + branch, 0.0).astype(BF)

    grad_out = dot(gated, cot_low, 0, 0)
    gated_grad = dot(cot_low, out_low, 1, 1)
    spatial_grad = (gated_grad * u).astype(BF)
    u_grad = gated_grad * spatial
    grad_mix = dot(spatial_grad, vn, 1, 1)
    vn_grad = jnp.where(live, dot(mix_low, spatial_grad, 0, 0), 0.0)
    h = vn_grad * gain_two
    v_grad = rstd2 * (h - jnp.mean(h, -1, keepdims=True) - vhat * jnp.mean(h * vhat, -1, keepdims=True))
    pre_grad = (jnp.concatenate([u_grad, v_grad], axis=1) * slope).astype(BF)
    grad_in = dot(xn, pre_grad, 0, 0)
    xn_grad = dot(pre_grad, in_low, 1, 1)
    h1 = xn_grad * gain_one
    x_grad = rstd1 * (h1 - jnp.mean(h1, -1, keepdims=True) - xhat * jnp.mean(h1 * xhat, -1, keepdims=True))
    in_pos = jnp.where(live, cot_low.astype(F32) + x_grad, 0.0).astype(BF)

    grad_vec = jnp.concatenate(
        [
            jnp.sum(xn_grad * xhat, 0),
            jnp.sum(xn_grad, 0),
            jnp.sum(pre_grad.astype(F32), 0),
            jnp.sum(vn_grad * vhat, 0),
            jnp.sum(vn_grad, 0),
            jnp.sum(spatial_grad.astype(F32), 1),
            jnp.sum(cot_low.astype(F32), 0),
        ]
    )

    def spread(pos, kind):
        slots = dot(onehot, pos, 0, 0).astype(BF).reshape(4, row_count, width)
        back = jnp.stack([turn(slots[r], -r) for r in range(4)])
        twice = jnp.concatenate([back, back])
        return lax.dynamic_slice_in_dim(twice, (4 - p) % 4, 4, 0).astype(kind).reshape(tokens.shape)

    out_tokens = spread(out_pos, BF)
    in_grad = spread(in_pos, F32)

    mix_part = jnp.pad(
        grad_mix.reshape(4, mix_rows, cells), ((0, 0), (0, mix_pad - mix_rows), (0, width - cells))
    )
    packed = jnp.concatenate(
        [grad_out.astype(BF).reshape(4, 8, out_rows // 8, width), mix_part.astype(BF).reshape(4, 8, mix_pad // 8, width)],
        axis=2,
    ).reshape(4, out_rows + mix_pad, width)
    second_sum = reduce_shards(packed).reshape(8, (out_rows + mix_pad) // 8, width)
    out_share = second_sum[:, : out_rows // 8].reshape(out_rows, width)
    mix_share = second_sum[:, out_rows // 8 :].reshape(mix_pad, width)[:mix_rows, :cells]
    in_share = reduce_shards(grad_in.astype(BF).reshape(4, width // 4, hidden))
    vec_sum = all_sum(grad_vec)

    images = micro_count * slot_count * lax.axis_size("img")
    rate_in, rate_out, rate_mix, rate_vec = step_rates(images, width, gate, cells)
    in_new = nesterov(in_weight, in_share, in_moment, in_average, rate_in)
    out_new = nesterov(out_weight, out_share, out_moment, out_average, rate_out)
    mix_new = nesterov(spatial_weight, mix_share, spatial_moment, spatial_average, rate_mix)
    vec_new = nesterov(vectors, vec_sum, vector_moment, vector_average, rate_vec)
    return (out_tokens, in_grad, *in_new, *out_new, *mix_new, *vec_new)


def solution(mesh):
    rows = P("patch", None)
    act = P(None, "img", "patch", None)
    return jax.shard_map(
        shards,
        mesh=mesh,
        in_specs=(act, act, P(None, "img"), P(None, "img", None), *([rows] * 9), P(), P(), P()),
        out_specs=(act, act, *([rows] * 9), P(), P(), P()),
        check_vma=False,
    )
```

time: 2780 us -> 222 us (0.08)
  local copies, waits for them, and re-layouts: 1350 us -> 29.1 us
  other arithmetic: 800 us -> 32 us
  waiting for transfers between devices: 376 us -> 61 us
  blocking collectives: 150 us -> 0 us
  starting transfers between devices: 0.34 us -> 73.4 us
  matrix products: 70.3 us -> 19 us
    gather x24 -> x0, local copies, waits for them, and re-layouts: 1290 us -> none  [the longest x12 1270 us: shards(): mix_low[row_place[:, :, None], col_place[:, None, :]]]
    unnamed x14 -> x0, other arithmetic: 741 us -> none
    unnamed x5 -> x0, waiting for transfers between devices: 234 us -> none
    psum x1 -> x0, waiting for transfers between devices: 143 us -> none  [shards(): lax.psum((grad_in, grad_out, grad_mix, grad_vec), ('img', 'patch'))]
    all_gather x5 -> x0, blocking collectives: 109 us -> none  [the longest x4 90 us: shards(): gathered = lax.all_gather(right_low, 'patch', axis=1, tiled=True)]
    ppermute x0 -> x59, starting transfers between devices: none -> 73.4 us  [the longest x24 39.8 us: turn(): return lax.ppermute(arr, 'patch', [(s, (s + r) % n) for s in range(n)])]
    ppermute x0 -> x59, waiting for transfers between devices: none -> 61 us  [the longest x33 52 us: swap(): return lax.ppermute(arr, 'img', xor_pairs(lax.axis_size('img'), mask))]
    dot_general x36 -> x12, matrix products: 70.3 us -> 19 us  [dot(): lax.dot_general(a, b, (((ca,), (cb,)), ((), ())), preferred_element_type=...]
  transfers between devices with their start and end apart: 4 -> 59, of which waited for: 2 -> 28; matrix products, arithmetic and copies ran while one was open for 49% -> 17% of each run, Pallas kernels for 0% -> 0%
where the time goes in v1:
time: 222 us
  starting transfers between devices  73.4 us (33%)
  waiting for transfers between devices  61 us (27%)
  other arithmetic  32 us (14%)
  local copies, waits for them, and re-layouts  29.1 us (13%)
  matrix products  19 us (9%)
  between operations  7.21 us (3%)
    ppermute x33, waiting for transfers between devices, swap(): return lax.ppermute(arr, 'img', xor_pairs(lax.axis_size('img'), mask))  52 us
    ppermute x24, starting transfers between devices, turn(): return lax.ppermute(arr, 'patch', [(s, (s + r) % n) for s in range(n)])  39.8 us
    ppermute x33, starting transfers between devices, swap(): return lax.ppermute(arr, 'img', xor_pairs(lax.axis_size('img'), mask))  31.2 us
    dot_general x12, matrix products, dot(): lax.dot_general(a, b, (((ca,), (cb,)), ((), ())), preferred_element_type=...  19 us
    unnamed x93, local copies, waits for them, and re-layouts  8.79 us
    ppermute x24, waiting for transfers between devices, turn(): return lax.ppermute(arr, 'patch', [(s, (s + r) % n) for s in range(n)])  6.95 us
    rev x2, local copies, waits for them, and re-layouts, to_absolute(): flipped = rel[::-1]  6.86 us
    add x4, other arithmetic, nesterov(): average_new = AVG_DECAY * average + (1.0 - AVG_DECAY) * weight_new  5.93 us
  transfers between devices with their start and end apart: 59, of which 28 were waited for; matrix products, arithmetic and copies ran while one was open for 17% of the time, Pallas kernels for 0%

profile of v1, /device:TPU:0, one launch (start us, length us, event | category | flops | bytes accessed | tf_op | source)
XLA Modules:
  0.0 221.7 jit_solution(14031269822966803100)
XLA Ops:
  3.6 5.0 %collective-permute-start.13 = (bf16[64,512]{1,0:T(8,128)(2,1)}, bf16[64,512]{1,0:T(8,128)(2,1)}, u32[]{:S(2)}, u32[]{:S(2)}) collective-permute-start(bf16[64,512]{1,0:T(8,128)(2,1)} %constant_dynamic-slice_fusion.5), channel_id=1, source_target_pairs={{0,3},{1,0},{2,1},{3,2},{4,7},{5,4},{6,5},{7,6},{8,11},{9,8},{10,9... | collective-permute-start | bytes 196616 | tf_op jit(solution)/shard_map/ppermute | solution.py:39
  10.5 2.8 %collective-permute-start.5 = (bf16[16,3072]{1,0:T(8,128)(2,1)}, bf16[16,3072]{1,0:T(8,128)(2,1)S(1)}, u32[]{:S(2)}, u32[]{:S(2)}) collective-permute-start(bf16[16,3072]{1,0:T(8,128)(2,1)} %constant_dynamic-slice_fusion.6), channel_id=1, source_target_pairs={{0,3},{1,0},{2,1},{3,2},{4,7},{5,4},{6,5},{7,6},{8,11},{9,8},{10,9... | collective-permute-start | bytes 294920 | tf_op jit(solution)/shard_map/ppermute | solution.py:39
  25.3 1.7 constant_dynamic-slice_fusion.3
  28.5 1.9 collective-permute-start.1
  30.4 3.8 %collective-permute-start.2 = (bf16[81,512]{1,0:T(8,128)(2,1)S(1)}, bf16[81,512]{1,0:T(8,128)(2,1)S(1)}, u32[]{:S(2)}, u32[]{:S(2)}) collective-permute-start(bf16[81,512]{1,0:T(8,128)(2,1)S(1)} %bitcast.151), channel_id=1, source_target_pairs={{0,3},{1,0},{2,1},{3,2},{4,7},{5,4},{6,5},{7,6},{8,11},{9,8},{10,9... | collective-permute-start | bytes 248840 | tf_op jit(solution)/shard_map/ppermute | solution.py:39
  35.2 1.9 collective-permute-done.1
  37.1 3.8 %collective-permute-start.24 = (bf16[81,512]{1,0:T(8,128)(2,1)}, bf16[81,512]{1,0:T(8,128)(2,1)S(1)}, u32[]{:S(2)}, u32[]{:S(2)}) collective-permute-start(bf16[81,512]{1,0:T(8,128)(2,1)} %bitcast.116), channel_id=1, source_target_pairs={{0,3},{1,0},{2,1},{3,2},{4,7},{5,4},{6,5},{7,6},{8,11},{9,8},{10,9... | collective-permute-start | bytes 248840 | tf_op jit(solution)/shard_map/ppermute | solution.py:39
  45.9 2.4 %collective-permute-done.14 = bf16[3,1,1,1,64,256]{5,4,3,2,1,0:T(8,128)(2,1)S(1)} collective-permute-done((bf16[3,1,1,1,64,256]{5,4,3,2,1,0:T(8,128)(2,1)S(1)}, bf16[3,1,1,1,64,256]{5,4,3,2,1,0:T(8,128)(2,1)S(1)}, u32[]{:S(2)}, u32[]{:S(2)}) %collective-permute-start.14) | collective-permute-done | bytes 98336 | tf_op jit(solution)/shard_map/ppermute | solution.py:43
  51.4 3.1 %collective-permute-done.6 = bf16[3,1,1,1,16,1536]{5,4,0,3,2,1:T(8,128)(2,1)S(1)} collective-permute-done((bf16[3,1,1,1,16,1536]{5,4,0,3,2,1:T(8,128)(2,1)S(1)}, bf16[3,1,1,1,16,1536]{5,4,0,3,2,1:T(8,128)(2,1)S(1)}, u32[]{:S(2)}, u32[]{:S(2)}) %collective-permute-start.6) | collective-permute-done | bytes 147488 | tf_op jit(solution)/shard_map/ppermute | solution.py:43
  57.7 4.3 %collective-permute-done.17 = bf16[3,2,1,1,64,256]{5,4,3,2,1,0:T(8,128)(2,1)S(1)} collective-permute-done((bf16[3,2,1,1,64,256]{5,4,3,2,1,0:T(8,128)(2,1)S(1)}, bf16[3,2,1,1,64,256]{5,4,3,2,1,0:T(8,128)(2,1)S(1)}, u32[]{:S(2)}, u32[]{:S(2)}) %collective-permute-start.17) | collective-permute-done | bytes 196640 | tf_op jit(solution)/shard_map/ppermute | solution.py:43
  63.6 1.6 collective-permute-start.7
  65.3 3.5 %collective-permute-done.9 = bf16[3,2,1,1,16,1536]{5,4,0,3,2,1:T(8,128)(2,1)S(1)} collective-permute-done((bf16[3,2,1,1,16,1536]{5,4,0,3,2,1:T(8,128)(2,1)S(1)}, bf16[3,2,1,1,16,1536]{5,4,0,3,2,1:T(8,128)(2,1)S(1)}, u32[]{:S(2)}, u32[]{:S(2)}) %collective-permute-start.9) | collective-permute-done | bytes 294944 | tf_op jit(solution)/shard_map/ppermute | solution.py:43
  74.8 3.1 %rev.7 = bf16[4,512,512]{2,1,0:T(8,128)(2,1)} reverse(bf16[4,512,512]{2,1,0:T(8,128)(2,1)} %pad_maximum_fusion.2), dimensions={0} | reverse | bytes 4194304 | tf_op jit(solution)/shard_map/rev | solution.py:88
  77.9 2.3 %fusion.7 = bf16[4,512,512]{2,1,0:T(8,128)(2,1)S(1)} fusion(s32[]{:T(128)S(6)} %select_n.550, bf16[4,512,512]{2,1,0:T(8,128)(2,1)} %rev.7), kind=kLoop, calls=%fused_computation.22 | loop fusion | flops 1048576 | bytes 4194308 | tf_op jit(solution)/shard_map/concatenate | solution.py:89
  81.2 1.8 reshape.241
  82.9 2.1 broadcast_select_fusion.2
  86.4 1.9 pad_maximum_fusion
  88.3 3.8 %rev.6 = bf16[4,128,3072]{2,1,0:T(8,128)(2,1)} reverse(bf16[4,128,3072]{2,1,0:T(8,128)(2,1)} %pad_maximum_fusion), dimensions={0} | reverse | bytes 6291456 | tf_op jit(solution)/shard_map/rev | solution.py:88
  92.1 3.1 %fusion.6 = bf16[4,128,3072]{2,1,0:T(8,128)(2,1)S(1)} fusion(s32[]{:T(128)S(6)} %select_n.550, bf16[4,128,3072]{2,1,0:T(8,128)(2,1)} %rev.6), kind=kLoop, calls=%fused_computation.15 | loop fusion | flops 1572864 | bytes 6291460 | tf_op jit(solution)/shard_map/concatenate | solution.py:89
  95.2 1.6 fusion.87
  101.6 2.7 %subtract_multiply_fusion = (f32[324,1536]{1,0:T(8,128)S(1)}, bf16[324,1536]{1,0:T(8,128)(2,1)}, f32[324,1536]{1,0:T(8,128)S(1)}) fusion(f32[324,1536]{1,0:T(8,128)S(1)} %get-tuple-element.156, f32[324]{0:T(512)S(1)} %broadcast_multiply_fusion, f32[324]{0:T(512)S(1)} %broadcast_multiply_fusion.1, f32[1536]{0:T(1024)S(1)} %copy-done.28, ...), kind=kOutput, calls=%fused_computation.29 | convolution fusion | flops 330946560 | bytes 15344128 | tf_op jit(solution)/shard_map/dot_general | solution.py:135
  104.3 2.3 %convert_reduce_fusion = (f32[3072]{0:T(1024)S(1)}, bf16[324,3072]{1,0:T(8,128)(2,1)S(1)}) fusion(f32[324,3072]{1,0:T(8,128)S(1)} %get-tuple-element.154, f32[324,1536]{1,0:T(8,128)S(1)} %get-tuple-element.66, f32[324,1536]{1,0:T(8,128)S(1)} %get-tuple-element.71), kind=kLoop, calls=%fused_computation.13 | loop fusion | flops 12936192 | bytes 9965568 | tf_op jit(solution)/shard_map/reduce_sum | solution.py:253
  108.1 3.7 %convolution_convert_fusion = bf16[512,3072]{1,0:T(8,128)(2,1)} fusion(bf16[324,3072]{1,0:T(8,128)(2,1)S(1)} %get-tuple-element.56, f32[324,512]{1,0:T(8,128)S(1)} %copy-done.5, f32[512]{0:T(512)S(1)} %get-tuple-element.147, f32[512]{0:T(512)S(1)} %get-tuple-element.148, f32[324]{0:T(512)S(1)} %add_rsqrt_fusion.1, f32[324]{0:T(512)S(1)} %broadcast_multiply_fusion.5), kind=kOutput, calls=%fused_computation.3 | convolution fusion | flops 1021618176 | bytes 5806624 | tf_op jit(solution)/shard_map/dot_general | solution.py:135
  113.9 2.4 %convolution_convert_fusion.4 = bf16[324,512]{1,0:T(8,128)(2,1)S(1)} fusion(f32[324,512]{1,0:T(8,128)} %copy-done.4, bf16[324,1536]{1,0:T(8,128)(2,1)} %get-tuple-element.67, bf16[1536,512]{1,0:T(8,128)(2,1)S(1)} %bitcast.132, f32[512]{0:T(512)S(1)} %copy-done.32, pred[324]{0:T(512)(128)(4,1)S(1)} %compare_and_fusion, s32[324]{0:T(512)} %copy-done.33), kind=kOutput, calls=%fused_computation.60 | convolution fusion | flops 618037760 | bytes 3567188 | tf_op jit(solution)/shard_map/dot_general | solution.py:135
  118.7 3.8 %collective-permute-start.25 = (bf16[81,512]{1,0:T(8,128)(2,1)}, bf16[81,512]{1,0:T(8,128)(2,1)S(1)}, u32[]{:S(2)}, u32[]{:S(2)}) collective-permute-start(bf16[81,512]{1,0:T(8,128)(2,1)} %get-tuple-element.98), channel_id=1, source_target_pairs={{0,3},{1,0},{2,1},{3,2},{4,7},{5,4},{6,5},{7,6},{8,11},{9,8},{10,9... | collective-permute-start | bytes 248840 | tf_op jit(solution)/shard_map/ppermute | solution.py:39
  123.1 2.2 broadcast_select_fusion
  127.3 3.1 %collective-permute-done.55 = f32[8004]{0:T(1024)S(1)} collective-permute-done((f32[8004]{0:T(1024)S(1)}, f32[8004]{0:T(1024)S(1)}, u32[]{:S(2)}, u32[]{:S(2)}) %collective-permute-start.55) | collective-permute-done | bytes 32048 | tf_op jit(solution)/shard_map/ppermute | solution.py:43
  131.9 3.0 %collective-permute-start.19 = (bf16[81,512]{1,0:T(8,128)(2,1)S(1)}, bf16[81,512]{1,0:T(8,128)(2,1)S(1)}, u32[]{:S(2)}, u32[]{:S(2)}) collective-permute-start(bf16[81,512]{1,0:T(8,128)(2,1)S(1)} %get-tuple-element.101), channel_id=1, source_target_pairs={{0,3},{1,0},{2,1},{3,2},{4,7},{5,4},{6,5},{7,6},{8,11},{9,8},{10,9... | collective-permute-start | bytes 248840 | tf_op jit(solution)/shard_map/ppermute | solution.py:39
  142.8 1.6 collective-permute-start.44
  144.4 2.4 %collective-permute-done.42 = bf16[4,2,1,1,64,256]{5,4,3,2,1,0:T(8,128)(2,1)S(1)} collective-permute-done((bf16[4,2,1,1,64,256]{5,4,3,2,1,0:T(8,128)(2,1)S(1)}, bf16[4,2,1,1,64,256]{5,4,3,2,1,0:T(8,128)(2,1)S(1)}, u32[]{:S(2)}, u32[]{:S(2)}) %collective-permute-start.42) | collective-permute-done | bytes 262176 | tf_op jit(solution)/shard_map/ppermute | solution.py:43
  148.3 2.0 collective-permute-done.44
  152.1 3.4 %collective-permute-done.45 = bf16[4,1,1,1,64,256]{5,4,3,2,1,0:T(8,128)(2,1)S(1)} collective-permute-done((bf16[4,1,1,1,64,256]{5,4,3,2,1,0:T(8,128)(2,1)S(1)}, bf16[4,1,1,1,64,256]{5,4,3,2,1,0:T(8,128)(2,1)S(1)}, u32[]{:S(2)}, u32[]{:S(2)}) %collective-permute-start.45) | collective-permute-done | bytes 131104 | tf_op jit(solution)/shard_map/ppermute | solution.py:43
  156.1 2.3 %collective-permute-start.47 = (bf16[1,1,1,1,64,512]{5,4,3,2,1,0:T(8,128)(2,1)S(1)}, bf16[1,1,1,1,64,512]{5,4,3,2,1,0:T(8,128)(2,1)S(1)}, u32[]{:S(2)}, u32[]{:S(2)}) collective-permute-start(bf16[1,1,1,1,64,512]{5,4,3,2,1,0:T(8,128)(2,1)S(1)} %get-tuple-element.86), channel_id=1, source_target_pairs={{0,2},{1,3},{2,0},{3,1},{4,6},{5,7},{6,4},{7,5},{8,10},{9,11},{10,... | collective-permute-start | bytes 196616 | tf_op jit(solution)/shard_map/ppermute | solution.py:39
  158.4 2.3 %collective-permute-start.48 = (bf16[1,1,1,1,64,512]{5,4,3,2,1,0:T(8,128)(2,1)S(1)}, bf16[1,1,1,1,64,512]{5,4,3,2,1,0:T(8,128)(2,1)S(1)}, u32[]{:S(2)}, u32[]{:S(2)}) collective-permute-start(bf16[1,1,1,1,64,512]{5,4,3,2,1,0:T(8,128)(2,1)S(1)} %get-tuple-element.87), channel_id=1, source_target_pairs={{0,3},{1,0},{2,1},{3,2},{4,7},{5,4},{6,5},{7,6},{8,11},{9,8},{10,9... | collective-permute-start | bytes 196616 | tf_op jit(solution)/shard_map/ppermute | solution.py:39
  166.0 2.1 collective-permute-done.58
  176.7 3.2 %collective-permute-done.29 = bf16[4,2,1,1,16,1536]{5,4,3,2,1,0:T(8,128)(2,1)S(1)} collective-permute-done((bf16[4,2,1,1,16,1536]{5,4,3,2,1,0:T(8,128)(2,1)S(1)}, bf16[4,2,1,1,16,1536]{5,4,3,2,1,0:T(8,128)(2,1)S(1)}, u32[]{:S(2)}, u32[]{:S(2)}) %collective-permute-start.29) | collective-permute-done | bytes 393248 | tf_op jit(solution)/shard_map/ppermute | solution.py:43
  181.3 5.8 %collective-permute-done.31 = bf16[4,1,2,1,16,1536]{5,4,3,2,1,0:T(8,128)(2,1)S(1)} collective-permute-done((bf16[4,1,2,1,16,1536]{5,4,3,2,1,0:T(8,128)(2,1)S(1)}, bf16[4,1,2,1,16,1536]{5,4,3,2,1,0:T(8,128)(2,1)S(1)}, u32[]{:S(2)}, u32[]{:S(2)}) %collective-permute-start.31) | collective-permute-done | bytes 393248 | tf_op jit(solution)/shard_map/ppermute | solution.py:43
  187.9 3.0 %collective-permute-done.30 = bf16[4,1,1,1,16,1536]{5,4,3,2,1,0:T(8,128)(2,1)S(1)} collective-permute-done((bf16[4,1,1,1,16,1536]{5,4,3,2,1,0:T(8,128)(2,1)S(1)}, bf16[4,1,1,1,16,1536]{5,4,3,2,1,0:T(8,128)(2,1)S(1)}, u32[]{:S(2)}, u32[]{:S(2)}) %collective-permute-start.30) | collective-permute-done | bytes 196640 | tf_op jit(solution)/shard_map/ppermute | solution.py:43
  191.0 2.5 %collective-permute-done.32 = bf16[4,1,1,1,16,1536]{5,4,3,2,1,0:T(8,128)(2,1)S(1)} collective-permute-done((bf16[4,1,1,1,16,1536]{5,4,3,2,1,0:T(8,128)(2,1)S(1)}, bf16[4,1,1,1,16,1536]{5,4,3,2,1,0:T(8,128)(2,1)S(1)}, u32[]{:S(2)}, u32[]{:S(2)}) %collective-permute-start.32) | collective-permute-done | bytes 196640 | tf_op jit(solution)/shard_map/ppermute | solution.py:43
  194.3 2.7 %collective-permute-start.34 = (bf16[1,1,1,1,16,3072]{5,4,3,2,1,0:T(8,128)(2,1)S(1)}, bf16[1,1,1,1,16,3072]{5,4,3,2,1,0:T(8,128)(2,1)S(1)}, u32[]{:S(2)}, u32[]{:S(2)}) collective-permute-start(bf16[1,1,1,1,16,3072]{5,4,3,2,1,0:T(8,128)(2,1)S(1)} %get-tuple-element.77), channel_id=1, source_target_pairs={{0,2},{1,3},{2,0},{3,1},{4,6},{5,7},{6,4},{7,5},{8,10},{9,11},{10,... | collective-permute-start | bytes 294920 | tf_op jit(solution)/shard_map/ppermute | solution.py:39
  197.0 1.8 collective-permute-start.35
  198.8 1.9 collective-permute-done.33
  200.7 2.3 %collective-permute-done.34 = bf16[1,1,1,1,16,3072]{5,4,3,2,1,0:T(8,128)(2,1)S(1)} collective-permute-done((bf16[1,1,1,1,16,3072]{5,4,3,2,1,0:T(8,128)(2,1)S(1)}, bf16[1,1,1,1,16,3072]{5,4,3,2,1,0:T(8,128)(2,1)S(1)}, u32[]{:S(2)}, u32[]{:S(2)}) %collective-permute-start.34) | collective-permute-done | bytes 98336 | tf_op jit(solution)/shard_map/ppermute | solution.py:39
  205.5 1.7 collective-permute-done.36
  207.2 1.9 collective-permute-done.38
  210.4 3.5 %collective-permute-done.39 = bf16[1,1,2,1,16,1536]{5,4,3,2,1,0:T(8,128)(2,1)S(1)} collective-permute-done((bf16[1,1,2,1,16,1536]{5,4,3,2,1,0:T(8,128)(2,1)S(1)}, bf16[1,1,2,1,16,1536]{5,4,3,2,1,0:T(8,128)(2,1)S(1)}, u32[]{:S(2)}, u32[]{:S(2)}) %collective-permute-start.39) | collective-permute-done | bytes 98336 | tf_op jit(solution)/shard_map/ppermute | solution.py:43
  215.3 1.7 multiply_add_fusion.1
  218.9 2.8 %multiply_add_fusion = (f32[128,3072]{1,0:T(8,128)}, f32[128,3072]{1,0:T(8,128)}, f32[128,3072]{1,0:T(8,128)}) fusion(f32[128,3072]{1,0:T(8,128)S(1)} %copy-done.11, f32[128,3072]{1,0:T(8,128)S(1)} %copy-done.2, bf16[1,2,2,2,16,3072]{5,4,3,2,1,0:T(8,128)(2,1)S(1)} %pad_maximum_fusion.5, f32[128,3072]{1,0:T(8,128)S(1)} %copy-done.12), kind=kLoop, calls=%fused_computation.44 | loop fusion | flops 3932160 | bytes 10223616 | tf_op jit(solution)/shard_map/add | solution.py:27
  (300 shorter events, 85.0 us)
Async XLA Ops:
  3.6 24.9 %collective-permute-start.13 = (bf16[64,512]{1,0:T(8,128)(2,1)}, bf16[64,512]{1,0:T(8,128)(2,1)}, u32[]{:S(2)}, u32[]{:S(2)}) collective-permute-start(bf16[64,512]{1,0:T(8,128)(2,1)} %constant_dynamic-slice_fusion.5), channel_id=1, source_target_pairs={{0,3},{1,0},{2,1},{3,2},{4,7},{5,4},{6,5},{7,6},{8,11},{9,8},{10,9... | collective-permute-start | bytes 196616 | tf_op jit(solution)/shard_map/ppermute | solution.py:39
  8.7 21.7 %collective-permute-start.12 = (bf16[64,512]{1,0:T(8,128)(2,1)}, bf16[64,512]{1,0:T(8,128)(2,1)}, u32[]{:S(2)}, u32[]{:S(2)}) collective-permute-start(bf16[64,512]{1,0:T(8,128)(2,1)} %constant_dynamic-slice_fusion.5), channel_id=1, source_target_pairs={{0,2},{1,3},{2,0},{3,1},{4,6},{5,7},{6,4},{7,5},{8,10},{9,11},{10,... | collective-permute-start | bytes 196616 | tf_op jit(solution)/shard_map/ppermute | solution.py:39
  8.7 21.7 %collective-permute-start.11 = (bf16[64,512]{1,0:T(8,128)(2,1)}, bf16[64,512]{1,0:T(8,128)(2,1)}, u32[]{:S(2)}, u32[]{:S(2)}) collective-permute-start(bf16[64,512]{1,0:T(8,128)(2,1)} %constant_dynamic-slice_fusion.5), channel_id=1, source_target_pairs={{0,1},{1,2},{2,3},{3,0},{4,5},{5,6},{6,7},{7,4},{8,9},{9,10},{10,1... | collective-permute-start | bytes 196616 | tf_op jit(solution)/shard_map/ppermute | solution.py:39
  10.5 31.2 %collective-permute-start.5 = (bf16[16,3072]{1,0:T(8,128)(2,1)}, bf16[16,3072]{1,0:T(8,128)(2,1)S(1)}, u32[]{:S(2)}, u32[]{:S(2)}) collective-permute-start(bf16[16,3072]{1,0:T(8,128)(2,1)} %constant_dynamic-slice_fusion.6), channel_id=1, source_target_pairs={{0,3},{1,0},{2,1},{3,2},{4,7},{5,4},{6,5},{7,6},{8,11},{9,8},{10,9... | collective-permute-start | bytes 294920 | tf_op jit(solution)/shard_map/ppermute | solution.py:39
  13.3 29.6 %collective-permute-start.4 = (bf16[16,3072]{1,0:T(8,128)(2,1)}, bf16[16,3072]{1,0:T(8,128)(2,1)S(1)}, u32[]{:S(2)}, u32[]{:S(2)}) collective-permute-start(bf16[16,3072]{1,0:T(8,128)(2,1)} %constant_dynamic-slice_fusion.6), channel_id=1, source_target_pairs={{0,2},{1,3},{2,0},{3,1},{4,6},{5,7},{6,4},{7,5},{8,10},{9,11},{10,... | collective-permute-start | bytes 294920 | tf_op jit(solution)/shard_map/ppermute | solution.py:39
  28.5 8.6 %collective-permute-start.1 = (bf16[81,512]{1,0:T(8,128)(2,1)S(1)}, bf16[81,512]{1,0:T(8,128)(2,1)S(1)}, u32[]{:S(2)}, u32[]{:S(2)}) collective-permute-start(bf16[81,512]{1,0:T(8,128)(2,1)S(1)} %bitcast.153), channel_id=1, source_target_pairs={{0,2},{1,3},{2,0},{3,1},{4,6},{5,7},{6,4},{7,5},{8,10},{9,11},{10,... | collective-permute-start | bytes 248840 | tf_op jit(solution)/shard_map/ppermute | solution.py:39
  30.4 6.7 %collective-permute-start = (bf16[81,512]{1,0:T(8,128)(2,1)S(1)}, bf16[81,512]{1,0:T(8,128)(2,1)S(1)}, u32[]{:S(2)}, u32[]{:S(2)}) collective-permute-start(bf16[81,512]{1,0:T(8,128)(2,1)S(1)} %bitcast.152), channel_id=1, source_target_pairs={{0,1},{1,2},{2,3},{3,0},{4,5},{5,6},{6,7},{7,4},{8,9},{9,10},{10,1... | collective-permute-start | bytes 248840 | tf_op jit(solution)/shard_map/ppermute | solution.py:39
  30.4 10.5 %collective-permute-start.2 = (bf16[81,512]{1,0:T(8,128)(2,1)S(1)}, bf16[81,512]{1,0:T(8,128)(2,1)S(1)}, u32[]{:S(2)}, u32[]{:S(2)}) collective-permute-start(bf16[81,512]{1,0:T(8,128)(2,1)S(1)} %bitcast.151), channel_id=1, source_target_pairs={{0,3},{1,0},{2,1},{3,2},{4,7},{5,4},{6,5},{7,6},{8,11},{9,8},{10,9... | collective-permute-start | bytes 248840 | tf_op jit(solution)/shard_map/ppermute | solution.py:39
  37.1 7.2 %collective-permute-start.3 = (bf16[16,3072]{1,0:T(8,128)(2,1)}, bf16[16,3072]{1,0:T(8,128)(2,1)S(1)}, u32[]{:S(2)}, u32[]{:S(2)}) collective-permute-start(bf16[16,3072]{1,0:T(8,128)(2,1)} %constant_dynamic-slice_fusion.6), channel_id=1, source_target_pairs={{0,1},{1,2},{2,3},{3,0},{4,5},{5,6},{6,7},{7,4},{8,9},{9,10},{10,1... | collective-permute-start | bytes 294920 | tf_op jit(solution)/shard_map/ppermute | solution.py:39
  37.1 34.5 %collective-permute-start.24 = (bf16[81,512]{1,0:T(8,128)(2,1)}, bf16[81,512]{1,0:T(8,128)(2,1)S(1)}, u32[]{:S(2)}, u32[]{:S(2)}) collective-permute-start(bf16[81,512]{1,0:T(8,128)(2,1)} %bitcast.116), channel_id=1, source_target_pairs={{0,3},{1,0},{2,1},{3,2},{4,7},{5,4},{6,5},{7,6},{8,11},{9,8},{10,9... | collective-permute-start | bytes 248840 | tf_op jit(solution)/shard_map/ppermute | solution.py:39
  41.0 30.7 %collective-permute-start.22 = (bf16[81,512]{1,0:T(8,128)(2,1)}, bf16[81,512]{1,0:T(8,128)(2,1)S(1)}, u32[]{:S(2)}, u32[]{:S(2)}) collective-permute-start(bf16[81,512]{1,0:T(8,128)(2,1)} %bitcast.118), channel_id=1, source_target_pairs={{0,1},{1,2},{2,3},{3,0},{4,5},{5,6},{6,7},{7,4},{8,9},{9,10},{10,1... | collective-permute-start | bytes 248840 | tf_op jit(solution)/shard_map/ppermute | solution.py:39
  41.7 29.9 %collective-permute-start.23 = (bf16[81,512]{1,0:T(8,128)(2,1)S(1)}, bf16[81,512]{1,0:T(8,128)(2,1)S(1)}, u32[]{:S(2)}, u32[]{:S(2)}) collective-permute-start(bf16[81,512]{1,0:T(8,128)(2,1)S(1)} %bitcast.149), channel_id=1, source_target_pairs={{0,2},{1,3},{2,0},{3,1},{4,6},{5,7},{6,4},{7,5},{8,10},{9,11},{10,... | collective-permute-start | bytes 248840 | tf_op jit(solution)/shard_map/ppermute | solution.py:39
  42.8 5.5 %collective-permute-start.14 = (bf16[3,1,1,1,64,256]{5,4,3,2,1,0:T(8,128)(2,1)S(1)}, bf16[3,1,1,1,64,256]{5,4,3,2,1,0:T(8,128)(2,1)S(1)}, u32[]{:S(2)}, u32[]{:S(2)}) collective-permute-start(bf16[3,1,1,1,64,256]{5,4,3,2,1,0:T(8,128)(2,1)S(1)} %get-tuple-element.124), channel_id=1, source_target_pairs={{0,8},{4,12},{8,0},{12,4},{16,24},{20,28},{24,16},{28,20},{1,9},{5... | collective-permute-start | bytes 294920 | tf_op jit(solution)/shard_map/ppermute | solution.py:43
  44.3 5.5 %collective-permute-start.16 = (bf16[3,1,1,1,64,256]{5,4,3,2,1,0:T(8,128)(2,1)S(1)}, bf16[3,1,1,1,64,256]{5,4,3,2,1,0:T(8,128)(2,1)S(1)}, u32[]{:S(2)}, u32[]{:S(2)}) collective-permute-start(bf16[3,1,1,1,64,256]{5,4,3,2,1,0:T(8,128)(2,1)S(1)} %get-tuple-element.125), channel_id=1, source_target_pairs={{0,16},{4,20},{8,24},{12,28},{16,0},{20,4},{24,8},{28,12},{1,17},{... | collective-permute-start | bytes 294920 | tf_op jit(solution)/shard_map/ppermute | solution.py:43
  48.3 6.2 %collective-permute-start.6 = (bf16[3,1,1,1,16,1536]{5,4,0,3,2,1:T(8,128)(2,1)S(1)}, bf16[3,1,1,1,16,1536]{5,4,0,3,2,1:T(8,128)(2,1)S(1)}, u32[]{:S(2)}, u32[]{:S(2)}) collective-permute-start(bf16[3,1,1,1,16,1536]{5,4,0,3,2,1:T(8,128)(2,1)S(1)} %get-tuple-element.112), channel_id=1, source_target_pairs={{0,8},{4,12},{8,0},{12,4},{16,24},{20,28},{24,16},{28,20},{1,9},{5... | collective-permute-start | bytes 442376 | tf_op jit(solution)/shard_map/ppermute | solution.py:43
  49.8 6.2 %collective-permute-start.8 = (bf16[3,1,1,1,16,1536]{5,4,0,3,2,1:T(8,128)(2,1)S(1)}, bf16[3,1,1,1,16,1536]{5,4,0,3,2,1:T(8,128)(2,1)S(1)}, u32[]{:S(2)}, u32[]{:S(2)}) collective-permute-start(bf16[3,1,1,1,16,1536]{5,4,0,3,2,1:T(8,128)(2,1)S(1)} %get-tuple-element.113), channel_id=1, source_target_pairs={{0,16},{4,20},{8,24},{12,28},{16,0},{20,4},{24,8},{28,12},{1,17},{... | collective-permute-start | bytes 442376 | tf_op jit(solution)/shard_map/ppermute | solution.py:43
  54.5 7.5 %collective-permute-start.17 = (bf16[3,2,1,1,64,256]{5,4,3,2,1,0:T(8,128)(2,1)S(1)}, bf16[3,2,1,1,64,256]{5,4,3,2,1,0:T(8,128)(2,1)S(1)}, u32[]{:S(2)}, u32[]{:S(2)}) collective-permute-start(bf16[3,2,1,1,64,256]{5,4,3,2,1,0:T(8,128)(2,1)S(1)} %pad_maximum_fusion.11), channel_id=1, source_target_pairs={{0,8},{4,12},{8,0},{12,4},{16,24},{20,28},{24,16},{28,20},{1,9},{5... | collective-permute-start | bytes 589832 | tf_op jit(solution)/shard_map/ppermute | solution.py:43
  56.0 7.5 %collective-permute-start.15 = (bf16[3,1,2,1,64,256]{5,4,3,2,1,0:T(8,128)(2,1)S(1)}, bf16[3,1,2,1,64,256]{5,4,3,2,1,0:T(8,128)(2,1)S(1)}, u32[]{:S(2)}, u32[]{:S(2)}) collective-permute-start(bf16[3,1,2,1,64,256]{5,4,3,2,1,0:T(8,128)(2,1)S(1)} %pad_maximum_fusion.10), channel_id=1, source_target_pairs={{0,16},{4,20},{8,24},{12,28},{16,0},{20,4},{24,8},{28,12},{1,17},{... | collective-permute-start | bytes 589832 | tf_op jit(solution)/shard_map/ppermute | solution.py:43
  62.0 6.7 %collective-permute-start.9 = (bf16[3,2,1,1,16,1536]{5,4,0,3,2,1:T(8,128)(2,1)S(1)}, bf16[3,2,1,1,16,1536]{5,4,0,3,2,1:T(8,128)(2,1)S(1)}, u32[]{:S(2)}, u32[]{:S(2)}) collective-permute-start(bf16[3,2,1,1,16,1536]{5,4,0,3,2,1:T(8,128)(2,1)S(1)} %pad_maximum_fusion.9), channel_id=1, source_target_pairs={{0,8},{4,12},{8,0},{12,4},{16,24},{20,28},{24,16},{28,20},{1,9},{5... | collective-permute-start | bytes 884744 | tf_op jit(solution)/shard_map/ppermute | solution.py:43
  63.6 6.8 %collective-permute-start.7 = (bf16[3,1,2,1,16,1536]{5,4,0,3,2,1:T(8,128)(2,1)S(1)}, bf16[3,1,2,1,16,1536]{5,4,0,3,2,1:T(8,128)(2,1)S(1)}, u32[]{:S(2)}, u32[]{:S(2)}) collective-permute-start(bf16[3,1,2,1,16,1536]{5,4,0,3,2,1:T(8,128)(2,1)S(1)} %pad_maximum_fusion.8), channel_id=1, source_target_pairs={{0,16},{4,20},{8,24},{12,28},{16,0},{20,4},{24,8},{28,12},{1,17},{... | collective-permute-start | bytes 884744 | tf_op jit(solution)/shard_map/ppermute | solution.py:43
  71.6 11.3 %collective-permute-start.10 = (bf16[3,2,2,1,16,3072]{5,4,0,3,2,1:T(8,128)(2,1)}, bf16[3,2,2,1,16,3072]{5,4,0,3,2,1:T(8,128)(2,1)}, u32[]{:S(2)}, u32[]{:S(2)}) collective-permute-start(bf16[3,2,2,1,16,3072]{5,4,0,3,2,1:T(8,128)(2,1)} %maximum_maximum_fusion), channel_id=1, source_target_pairs={{0,4},{4,0},{8,12},{12,8},{16,20},{20,16},{24,28},{28,24},{1,5},{5... | collective-permute-start | bytes 3538952 | tf_op jit(solution)/shard_map/ppermute | solution.py:43
  118.2 8.2 %collective-permute-start.54 = (f32[8004]{0:T(1024)S(1)}, f32[8004]{0:T(1024)S(1)}, u32[]{:S(2)}, u32[]{:S(2)}) collective-permute-start(f32[8004]{0:T(1024)S(1)} %concatenate.160), channel_id=1, source_target_pairs={{0,4},{4,0},{8,12},{12,8},{16,20},{20,16},{24,28},{28,24},{1,5},{5... | collective-permute-start | bytes 96056 | tf_op jit(solution)/shard_map/ppermute | solution.py:43
  118.7 16.3 %collective-permute-start.27 = (bf16[81,512]{1,0:T(8,128)(2,1)}, bf16[81,512]{1,0:T(8,128)(2,1)S(1)}, u32[]{:S(2)}, u32[]{:S(2)}) collective-permute-start(bf16[81,512]{1,0:T(8,128)(2,1)} %get-tuple-element.96), channel_id=1, source_target_pairs={{0,1},{1,2},{2,3},{3,0},{4,5},{5,6},{6,7},{7,4},{8,9},{9,10},{10,1... | collective-permute-start | bytes 248840 | tf_op jit(solution)/shard_map/ppermute | solution.py:39
  118.7 16.1 %collective-permute-start.26 = (bf16[81,512]{1,0:T(8,128)(2,1)}, bf16[81,512]{1,0:T(8,128)(2,1)S(1)}, u32[]{:S(2)}, u32[]{:S(2)}) collective-permute-start(bf16[81,512]{1,0:T(8,128)(2,1)} %get-tuple-element.97), channel_id=1, source_target_pairs={{0,2},{1,3},{2,0},{3,1},{4,6},{5,7},{6,4},{7,5},{8,10},{9,11},{10,... | collective-permute-start | bytes 248840 | tf_op jit(solution)/shard_map/ppermute | solution.py:39
  118.7 13.2 %collective-permute-start.25 = (bf16[81,512]{1,0:T(8,128)(2,1)}, bf16[81,512]{1,0:T(8,128)(2,1)S(1)}, u32[]{:S(2)}, u32[]{:S(2)}) collective-permute-start(bf16[81,512]{1,0:T(8,128)(2,1)} %get-tuple-element.98), channel_id=1, source_target_pairs={{0,3},{1,0},{2,1},{3,2},{4,7},{5,4},{6,5},{7,6},{8,11},{9,8},{10,9... | collective-permute-start | bytes 248840 | tf_op jit(solution)/shard_map/ppermute | solution.py:39
  122.5 16.3 %collective-permute-start.21 = (bf16[81,512]{1,0:T(8,128)(2,1)S(1)}, bf16[81,512]{1,0:T(8,128)(2,1)S(1)}, u32[]{:S(2)}, u32[]{:S(2)}) collective-permute-start(bf16[81,512]{1,0:T(8,128)(2,1)S(1)} %get-tuple-element.99), channel_id=1, source_target_pairs={{0,1},{1,2},{2,3},{3,0},{4,5},{5,6},{6,7},{7,4},{8,9},{9,10},{10,1... | collective-permute-start | bytes 248840 | tf_op jit(solution)/shard_map/ppermute | solution.py:39
  130.4 8.4 %collective-permute-start.20 = (bf16[81,512]{1,0:T(8,128)(2,1)S(1)}, bf16[81,512]{1,0:T(8,128)(2,1)S(1)}, u32[]{:S(2)}, u32[]{:S(2)}) collective-permute-start(bf16[81,512]{1,0:T(8,128)(2,1)S(1)} %get-tuple-element.100), channel_id=1, source_target_pairs={{0,2},{1,3},{2,0},{3,1},{4,6},{5,7},{6,4},{7,5},{8,10},{9,11},{10,... | collective-permute-start | bytes 248840 | tf_op jit(solution)/shard_map/ppermute | solution.py:39
  131.9 5.4 %collective-permute-start.19 = (bf16[81,512]{1,0:T(8,128)(2,1)S(1)}, bf16[81,512]{1,0:T(8,128)(2,1)S(1)}, u32[]{:S(2)}, u32[]{:S(2)}) collective-permute-start(bf16[81,512]{1,0:T(8,128)(2,1)S(1)} %get-tuple-element.101), channel_id=1, source_target_pairs={{0,3},{1,0},{2,1},{3,2},{4,7},{5,4},{6,5},{7,6},{8,11},{9,8},{10,9... | collective-permute-start | bytes 248840 | tf_op jit(solution)/shard_map/ppermute | solution.py:39
  135.0 36.3 %collective-permute-start.28 = (bf16[4,2,2,1,16,3072]{5,4,3,2,1,0:T(8,128)(2,1)S(1)}, bf16[4,2,2,1,16,3072]{5,4,3,2,1,0:T(8,128)(2,1)S(1)}, u32[]{:S(2)}, u32[]{:S(2)}) collective-permute-start(bf16[4,2,2,1,16,3072]{5,4,3,2,1,0:T(8,128)(2,1)S(1)} %broadcast_select_fusion), channel_id=1, source_target_pairs={{0,4},{4,0},{8,12},{12,8},{16,20},{20,16},{24,28},{28,24},{1,5},{5... | collective-permute-start | bytes 4718600 | tf_op jit(solution)/shard_map/ppermute | solution.py:43
  139.5 7.3 %collective-permute-start.42 = (bf16[4,2,1,1,64,256]{5,4,3,2,1,0:T(8,128)(2,1)S(1)}, bf16[4,2,1,1,64,256]{5,4,3,2,1,0:T(8,128)(2,1)S(1)}, u32[]{:S(2)}, u32[]{:S(2)}) collective-permute-start(bf16[4,2,1,1,64,256]{5,4,3,2,1,0:T(8,128)(2,1)S(1)} %broadcast_select_fusion.15), channel_id=1, source_target_pairs={{0,8},{4,12},{8,0},{12,4},{16,24},{20,28},{24,16},{28,20},{1,9},{5... | collective-permute-start | bytes 786440 | tf_op jit(solution)/shard_map/ppermute | solution.py:43
  141.2 22.1 %collective-permute-start.57 = (f32[8004]{0:T(1024)S(1)}, f32[8004]{0:T(1024)S(1)}, u32[]{:S(2)}, u32[]{:S(2)}) collective-permute-start(f32[8004]{0:T(1024)S(1)} %add.404), channel_id=1, source_target_pairs={{0,1},{1,0},{2,3},{3,2},{4,5},{5,4},{6,7},{7,6},{8,9},{9,8},{10,11... | collective-permute-start | bytes 96056 | tf_op jit(solution)/shard_map/ppermute | solution.py:130
  142.8 7.5 %collective-permute-start.44 = (bf16[4,1,2,1,64,256]{5,4,3,2,1,0:T(8,128)(2,1)S(1)}, bf16[4,1,2,1,64,256]{5,4,3,2,1,0:T(8,128)(2,1)S(1)}, u32[]{:S(2)}, u32[]{:S(2)}) collective-permute-start(bf16[4,1,2,1,64,256]{5,4,3,2,1,0:T(8,128)(2,1)S(1)} %broadcast_select_fusion.14), channel_id=1, source_target_pairs={{0,16},{4,20},{8,24},{12,28},{16,0},{20,4},{24,8},{28,12},{1,17},{... | collective-permute-start | bytes 786440 | tf_op jit(solution)/shard_map/ppermute | solution.py:43
  146.9 5.1 %collective-permute-start.43 = (bf16[4,1,1,1,64,256]{5,4,3,2,1,0:T(8,128)(2,1)S(1)}, bf16[4,1,1,1,64,256]{5,4,3,2,1,0:T(8,128)(2,1)S(1)}, u32[]{:S(2)}, u32[]{:S(2)}) collective-permute-start(bf16[4,1,1,1,64,256]{5,4,3,2,1,0:T(8,128)(2,1)S(1)} %broadcast_select_fusion.29), channel_id=1, source_target_pairs={{0,16},{4,20},{8,24},{12,28},{16,0},{20,4},{24,8},{28,12},{1,17},{... | collective-permute-start | bytes 393224 | tf_op jit(solution)/shard_map/ppermute | solution.py:43
  150.4 5.0 %collective-permute-start.45 = (bf16[4,1,1,1,64,256]{5,4,3,2,1,0:T(8,128)(2,1)S(1)}, bf16[4,1,1,1,64,256]{5,4,3,2,1,0:T(8,128)(2,1)S(1)}, u32[]{:S(2)}, u32[]{:S(2)}) collective-permute-start(bf16[4,1,1,1,64,256]{5,4,3,2,1,0:T(8,128)(2,1)S(1)} %broadcast_select_fusion.28), channel_id=1, source_target_pairs={{0,8},{4,12},{8,0},{12,4},{16,24},{20,28},{24,16},{28,20},{1,9},{5... | collective-permute-start | bytes 393224 | tf_op jit(solution)/shard_map/ppermute | solution.py:43
  155.6 8.4 %collective-permute-start.46 = (bf16[1,1,1,1,64,512]{5,4,3,2,1,0:T(8,128)(2,1)S(1)}, bf16[1,1,1,1,64,512]{5,4,3,2,1,0:T(8,128)(2,1)S(1)}, u32[]{:S(2)}, u32[]{:S(2)}) collective-permute-start(bf16[1,1,1,1,64,512]{5,4,3,2,1,0:T(8,128)(2,1)S(1)} %get-tuple-element.85), channel_id=1, source_target_pairs={{0,1},{1,2},{2,3},{3,0},{4,5},{5,6},{6,7},{7,4},{8,9},{9,10},{10,1... | collective-permute-start | bytes 196616 | tf_op jit(solution)/shard_map/ppermute | solution.py:39
  156.1 7.9 %collective-permute-start.47 = (bf16[1,1,1,1,64,512]{5,4,3,2,1,0:T(8,128)(2,1)S(1)}, bf16[1,1,1,1,64,512]{5,4,3,2,1,0:T(8,128)(2,1)S(1)}, u32[]{:S(2)}, u32[]{:S(2)}) collective-permute-start(bf16[1,1,1,1,64,512]{5,4,3,2,1,0:T(8,128)(2,1)S(1)} %get-tuple-element.86), channel_id=1, source_target_pairs={{0,2},{1,3},{2,0},{3,1},{4,6},{5,7},{6,4},{7,5},{8,10},{9,11},{10,... | collective-permute-start | bytes 196616 | tf_op jit(solution)/shard_map/ppermute | solution.py:39
  158.4 5.6 %collective-permute-start.48 = (bf16[1,1,1,1,64,512]{5,4,3,2,1,0:T(8,128)(2,1)S(1)}, bf16[1,1,1,1,64,512]{5,4,3,2,1,0:T(8,128)(2,1)S(1)}, u32[]{:S(2)}, u32[]{:S(2)}) collective-permute-start(bf16[1,1,1,1,64,512]{5,4,3,2,1,0:T(8,128)(2,1)S(1)} %get-tuple-element.87), channel_id=1, source_target_pairs={{0,3},{1,0},{2,1},{3,2},{4,7},{5,4},{6,5},{7,6},{8,11},{9,8},{10,9... | collective-permute-start | bytes 196616 | tf_op jit(solution)/shard_map/ppermute | solution.py:39
  163.2 4.9 %collective-permute-start.58 = (f32[8004]{0:T(1024)S(1)}, f32[8004]{0:T(1024)S(1)}, u32[]{:S(2)}, u32[]{:S(2)}) collective-permute-start(f32[8004]{0:T(1024)S(1)} %add.405), channel_id=1, source_target_pairs={{0,2},{1,3},{2,0},{3,1},{4,6},{5,7},{6,4},{7,5},{8,10},{9,11},{10,... | collective-permute-start | bytes 96056 | tf_op jit(solution)/shard_map/ppermute | solution.py:130
  164.1 4.7 %collective-permute-start.49 = (bf16[1,1,1,1,64,256]{5,4,3,2,1,0:T(8,128)(2,1)S(1)}, bf16[1,1,1,1,64,256]{5,4,3,2,1,0:T(8,128)(2,1)S(1)}, u32[]{:S(2)}, u32[]{:S(2)}) collective-permute-start(bf16[1,1,1,1,64,256]{5,4,3,2,1,0:T(8,128)(2,1)S(1)} %get-tuple-element.144), channel_id=1, source_target_pairs={{0,16},{4,20},{8,24},{12,28},{16,0},{20,4},{24,8},{28,12},{1,17},{... | collective-permute-start | bytes 98312 | tf_op jit(solution)/shard_map/ppermute | solution.py:43
  172.1 7.8 %collective-permute-start.29 = (bf16[4,2,1,1,16,1536]{5,4,3,2,1,0:T(8,128)(2,1)S(1)}, bf16[4,2,1,1,16,1536]{5,4,3,2,1,0:T(8,128)(2,1)S(1)}, u32[]{:S(2)}, u32[]{:S(2)}) collective-permute-start(bf16[4,2,1,1,16,1536]{5,4,3,2,1,0:T(8,128)(2,1)S(1)} %broadcast_select_fusion.7), channel_id=1, source_target_pairs={{0,8},{4,12},{8,0},{12,4},{16,24},{20,28},{24,16},{28,20},{1,9},{5... | collective-permute-start | bytes 1179656 | tf_op jit(solution)/shard_map/ppermute | solution.py:43
  175.1 12.0 %collective-permute-start.31 = (bf16[4,1,2,1,16,1536]{5,4,3,2,1,0:T(8,128)(2,1)S(1)}, bf16[4,1,2,1,16,1536]{5,4,3,2,1,0:T(8,128)(2,1)S(1)}, u32[]{:S(2)}, u32[]{:S(2)}) collective-permute-start(bf16[4,1,2,1,16,1536]{5,4,3,2,1,0:T(8,128)(2,1)S(1)} %broadcast_select_fusion.6), channel_id=1, source_target_pairs={{0,16},{4,20},{8,24},{12,28},{16,0},{20,4},{24,8},{28,12},{1,17},{... | collective-permute-start | bytes 1179656 | tf_op jit(solution)/shard_map/ppermute | solution.py:43
  180.1 10.8 %collective-permute-start.30 = (bf16[4,1,1,1,16,1536]{5,4,3,2,1,0:T(8,128)(2,1)S(1)}, bf16[4,1,1,1,16,1536]{5,4,3,2,1,0:T(8,128)(2,1)S(1)}, u32[]{:S(2)}, u32[]{:S(2)}) collective-permute-start(bf16[4,1,1,1,16,1536]{5,4,3,2,1,0:T(8,128)(2,1)S(1)} %broadcast_select_fusion.19), channel_id=1, source_target_pairs={{0,16},{4,20},{8,24},{12,28},{16,0},{20,4},{24,8},{28,12},{1,17},{... | collective-permute-start | bytes 589832 | tf_op jit(solution)/shard_map/ppermute | solution.py:43
  187.3 6.2 %collective-permute-start.32 = (bf16[4,1,1,1,16,1536]{5,4,3,2,1,0:T(8,128)(2,1)S(1)}, bf16[4,1,1,1,16,1536]{5,4,3,2,1,0:T(8,128)(2,1)S(1)}, u32[]{:S(2)}, u32[]{:S(2)}) collective-permute-start(bf16[4,1,1,1,16,1536]{5,4,3,2,1,0:T(8,128)(2,1)S(1)} %broadcast_select_fusion.18), channel_id=1, source_target_pairs={{0,8},{4,12},{8,0},{12,4},{16,24},{20,28},{24,16},{28,20},{1,9},{5... | collective-permute-start | bytes 589832 | tf_op jit(solution)/shard_map/ppermute | solution.py:43
  193.6 7.1 %collective-permute-start.33 = (bf16[1,1,1,1,16,3072]{5,4,3,2,1,0:T(8,128)(2,1)S(1)}, bf16[1,1,1,1,16,3072]{5,4,3,2,1,0:T(8,128)(2,1)S(1)}, u32[]{:S(2)}, u32[]{:S(2)}) collective-permute-start(bf16[1,1,1,1,16,3072]{5,4,3,2,1,0:T(8,128)(2,1)S(1)} %get-tuple-element.76), channel_id=1, source_target_pairs={{0,1},{1,2},{2,3},{3,0},{4,5},{5,6},{6,7},{7,4},{8,9},{9,10},{10,1... | collective-permute-start | bytes 294920 | tf_op jit(solution)/shard_map/ppermute | solution.py:39
  194.3 8.7 %collective-permute-start.34 = (bf16[1,1,1,1,16,3072]{5,4,3,2,1,0:T(8,128)(2,1)S(1)}, bf16[1,1,1,1,16,3072]{5,4,3,2,1,0:T(8,128)(2,1)S(1)}, u32[]{:S(2)}, u32[]{:S(2)}) collective-permute-start(bf16[1,1,1,1,16,3072]{5,4,3,2,1,0:T(8,128)(2,1)S(1)} %get-tuple-element.77), channel_id=1, source_target_pairs={{0,2},{1,3},{2,0},{3,1},{4,6},{5,7},{6,4},{7,5},{8,10},{9,11},{10,... | collective-permute-start | bytes 294920 | tf_op jit(solution)/shard_map/ppermute | solution.py:39
  197.0 6.0 %collective-permute-start.35 = (bf16[1,1,1,1,16,3072]{5,4,3,2,1,0:T(8,128)(2,1)S(1)}, bf16[1,1,1,1,16,3072]{5,4,3,2,1,0:T(8,128)(2,1)S(1)}, u32[]{:S(2)}, u32[]{:S(2)}) collective-permute-start(bf16[1,1,1,1,16,3072]{5,4,3,2,1,0:T(8,128)(2,1)S(1)} %get-tuple-element.78), channel_id=1, source_target_pairs={{0,3},{1,0},{2,1},{3,2},{4,7},{5,4},{6,5},{7,6},{8,11},{9,8},{10,9... | collective-permute-start | bytes 294920 | tf_op jit(solution)/shard_map/ppermute | solution.py:39
  209.2 4.7 %collective-permute-start.39 = (bf16[1,1,2,1,16,1536]{5,4,3,2,1,0:T(8,128)(2,1)S(1)}, bf16[1,1,2,1,16,1536]{5,4,3,2,1,0:T(8,128)(2,1)S(1)}, u32[]{:S(2)}, u32[]{:S(2)}) collective-permute-start(bf16[1,1,2,1,16,1536]{5,4,3,2,1,0:T(8,128)(2,1)S(1)} %pad_maximum_fusion.13), channel_id=1, source_target_pairs={{0,16},{4,20},{8,24},{12,28},{16,0},{20,4},{24,8},{28,12},{1,17},{... | collective-permute-start | bytes 294920 | tf_op jit(solution)/shard_map/ppermute | solution.py:43
  209.6 4.7 %collective-permute-start.37 = (bf16[1,2,1,1,16,1536]{5,4,3,2,1,0:T(8,128)(2,1)S(1)}, bf16[1,2,1,1,16,1536]{5,4,3,2,1,0:T(8,128)(2,1)S(1)}, u32[]{:S(2)}, u32[]{:S(2)}) collective-permute-start(bf16[1,2,1,1,16,1536]{5,4,3,2,1,0:T(8,128)(2,1)S(1)} %pad_maximum_fusion.12), channel_id=1, source_target_pairs={{0,8},{4,12},{8,0},{12,4},{16,24},{20,28},{24,16},{28,20},{1,9},{5... | collective-permute-start | bytes 294920 | tf_op jit(solution)/shard_map/ppermute | solution.py:43
  (48 other events, 314.4 us)

commit v2 on v1

v2 whole, which is shorter than its diff:
```python
import functools
import math

import jax
import jax.numpy as jnp
from jax import lax
from jax.experimental import pallas as pl
from jax.experimental.pallas import tpu as pltpu
from jax.sharding import PartitionSpec as P

EPS = 1e-05
MOMENTUM = 0.9
AVG_DECAY = 0.8
BF = jnp.bfloat16
F32 = jnp.float32
I32 = jnp.int32
CORE, XBIT, YBIT = 1, 2, 4
LANE = 512
STEP = 16


def step_rates(images, model_width, gate_width, cell_count):
    live_rows = 207.0 * images
    rate_in = 1.0 / (math.sqrt(model_width) * 1.4 * math.sqrt(live_rows))
    rate_out = 1.0 / (math.sqrt(gate_width / 4.0) * 1.2 * math.sqrt(live_rows))
    rate_mix = 1.0 / (math.sqrt(cell_count) * 1.5 * math.sqrt(gate_width * images / 2.0))
    rate_vec = 0.1 / (2.0 * math.sqrt(live_rows))
    return (rate_in, rate_out, rate_mix, rate_vec)


def nesterov(weight, grads, moment, average, rate):
    moment_new = MOMENTUM * moment + grads
    weight_new = weight - rate * (grads + MOMENTUM * moment_new)
    average_new = AVG_DECAY * average + (1.0 - AVG_DECAY) * weight_new
    return (weight_new, moment_new, average_new)


def turn(arr, r):
    n = lax.axis_size("patch")
    return lax.ppermute(arr, "patch", [(s, (s + r) % n) for s in range(n)])


def swap(arr, mask):
    n = lax.axis_size("img")
    return lax.ppermute(arr, "img", [(k, k ^ mask) for k in range(n)])


def dot(a, b, ca=1, cb=0):
    return lax.dot_general(a, b, (((ca,), (cb,)), ((), ())), preferred_element_type=F32)


def aligned(v, by):
    return pl.multiple_of(v, by)


def rows_of(i):
    return pl.ds(aligned(i * STEP, STEP), STEP)


def each_tile(n):
    steps = n // STEP
    return pl.loop(0, steps, unroll=7 if steps % 7 == 0 else 1)


def gelu_parts(pre):
    phi = 0.5 * (1.0 + lax.erf(pre * math.sqrt(0.5)))
    slope = phi + pre * (jnp.exp(-0.5 * pre * pre) * (1.0 / math.sqrt(2.0 * math.pi)))
    return pre * phi, slope


def mean_rows(v):
    return jnp.sum(v, axis=-1, keepdims=True) * (1.0 / v.shape[-1])


def onehot(slot, lanes, base):
    lane = lax.broadcasted_iota(I32, (slot.shape[0], lanes), 1) + base
    return jnp.where(slot == lane, 1.0, 0.0).astype(BF)


def prep_kernel(scal, tok, cot, weight, mix, m1, m2, m3, tok_own, c1, c2, c3, cot_own, wo_own, mx_own):
    own, unit = scal[0], scal[1]
    rows = weight.shape[0] // 8
    wo_own[...] = weight[...].astype(BF)
    mx_own[...] = jnp.zeros_like(mx_own)
    mx_own[0 : mix.shape[0], 0 : mix.shape[1]] = mix[...].astype(BF)
    piece = weight[pl.ds(aligned(unit * rows, STEP), rows), :].astype(BF)
    strip = mx_own[pl.ds(aligned(unit * STEP, STEP), STEP), :]
    for r, (msg, out) in enumerate(((m1, c1), (m2, c2), (m3, c3)), 1):
        to = lax.rem(own + r, 4)
        msg[0:rows, :] = piece
        msg[rows : rows + STEP, :] = strip
        msg[rows + STEP :, :] = tok[to]
        out[...] = cot[to]
    tok_own[...] = tok[own]
    cot_own[...] = cot[own]


def place_kernel(slot_ref, b0, b1, b2, b3, pos_ref):
    slot = slot_ref[...]
    lanes = b0.shape[0]
    total = None
    for r, blk in enumerate((b0, b1, b2, b3)):
        part = dot(onehot(slot, lanes, r * lanes), blk[blk.shape[0] - lanes :, :])
        total = part if total is None else total + part
    pos_ref[...] = total.astype(BF)


ORDER = [(c, y, x, r) for c in (0, 1) for y in (0, 1) for x in (0, 1) for r in range(4)]


def norm_kernel(scal, slot_ref, b0, b1, b2, b3, gain, shift, pos_ref, xn_ref, xt_ref, turned):
    place_kernel(slot_ref, b0, b1, b2, b3, pos_ref)
    own, unit = scal[0], scal[1]

    @each_tile(pos_ref.shape[0])
    def _(i):
        x = pos_ref[rows_of(i), :].astype(F32)
        cen = x - mean_rows(x)
        rstd = lax.rsqrt(mean_rows(cen * cen) + EPS)
        xn_ref[rows_of(i), :] = (cen * rstd * gain[...] + shift[...]).astype(BF)

    turned[...] = xn_ref[...].T
    for k, (c, y, x, r) in enumerate(ORDER):
        who = lax.rem(own + r, 4)
        e = c + 2 * x + 4 * y
        src = who * 128 + (unit ^ e) * STEP
        xt_ref[k * STEP : (k + 1) * STEP, :] = turned[pl.ds(aligned(src, STEP), STEP), :]


class Copies:
    def __init__(self, sems):
        self.sems, self.all = sems, []

    def bring(self, src, dst):
        copy = pltpu.make_async_copy(src, dst, self.sems.at[len(self.all)])
        copy.start()
        self.all.append(copy)

    def wait(self):
        for copy in self.all:
            copy.wait()


def gate_kernel(scal, slot_ref, xn_ref, b_in, g_two, s_two, wi_own, *rest):
    wi, rest = rest[:8], rest[8:]
    win, u_ref, slope_u, vhat_ref, rstd_ref, slope_v, vn_ref, pre, sems = rest
    own, unit = scal[0], scal[1]
    n, gate = vhat_ref.shape
    tiles = gate // LANE
    copies = Copies(sems)
    copies.bring(wi_own, win.at[pl.ds(aligned(own * 128, 128), 128), :])
    for e in range(8):
        for r in (1, 2, 3):
            who = lax.rem(own + (4 - r), 4)
            at = who * 128 + (unit ^ e) * STEP
            copies.bring(wi[e].at[r - 1], win.at[pl.ds(aligned(at, STEP), STEP), :])
    copies.wait()

    xn = xn_ref[...]
    for k in range(tiles):
        cols = slice(k * LANE, (k + 1) * LANE)
        wide = slice(gate + k * LANE, gate + (k + 1) * LANE)
        pre[:, cols] = dot(xn, win[:, wide]) + b_in[:, wide]

    @each_tile(n)
    def _(i):
        rows = rows_of(i)
        v, slope = gelu_parts(pre[rows, :])
        slope_v[rows, :] = slope
        cen = v - mean_rows(v)
        rstd = lax.rsqrt(mean_rows(cen * cen) + EPS)
        vhat = cen * rstd
        vhat_ref[rows, :] = vhat
        rstd_ref[rows, :] = rstd
        vn = jnp.where(slot_ref[rows, :] >= 0, vhat * g_two[...] + s_two[...], 0.0)
        vn_ref[rows, :] = vn.astype(BF)

    for k in range(tiles):
        cols = slice(k * LANE, (k + 1) * LANE)
        pre[:, cols] = dot(xn, win[:, cols]) + b_in[:, cols]

    @each_tile(n)
    def _(i):
        rows = rows_of(i)
        u, slope = gelu_parts(pre[rows, :])
        u_ref[rows, :] = u
        slope_u[rows, :] = slope


def spatial_kernel(scal, slot_ref, pos_ref, xt_ref, cot_ref, u_ref, slope_u, vn_ref, b_mix, b_out, wo_own, mx_own, *rest):
    wo, rest = rest[:8], rest[8:]
    out_ref, mix_ref, pre_u, sg_ref, keep, send, *rest = rest
    wout, mixp, spat, gated, gtmp, sems = rest
    own, unit = scal[0], scal[1]
    n, gate = u_ref.shape
    tiles = gate // LANE
    out_unit = wout.shape[0] // 32
    copies = Copies(sems)
    copies.bring(wo_own, wout.at[pl.ds(aligned(own * 8 * out_unit, STEP), 8 * out_unit), :])
    copies.bring(mx_own, mixp.at[pl.ds(aligned(own * 128, 128), 128), :])
    for e in range(8):
        for r in (1, 2, 3):
            who = lax.rem(own + (4 - r), 4)
            at = (who * 8 + (unit ^ e)) * out_unit
            copies.bring(wo[e].at[r - 1, pl.ds(0, out_unit)], wout.at[pl.ds(aligned(at, STEP), out_unit), :])
            at = who * 128 + (unit ^ e) * STEP
            copies.bring(wo[e].at[r - 1, pl.ds(out_unit, STEP)], mixp.at[pl.ds(aligned(at, STEP), STEP), :])
    copies.wait()
    per = 81
    cell = lax.broadcasted_iota(I32, (n, mixp.shape[0]), 0)
    lane = lax.broadcasted_iota(I32, (n, mixp.shape[0]), 1)
    part = jnp.where(cell >= per, 1, 0) + jnp.where(cell >= 2 * per, 1, 0) + jnp.where(cell >= 3 * per, 1, 0)
    pick = jnp.where(lane == cell + part * (128 - per), 1.0, 0.0).astype(BF)
    mix_ref[...] = dot(pick, mixp[:, :n]).astype(BF)
    mix = mix_ref[...]
    for k in range(tiles):
        cols = slice(k * LANE, (k + 1) * LANE)
        sp = dot(mix, vn_ref[:, cols]) + b_mix[...]
        spat[:, cols] = sp
        gated[:, cols] = (u_ref[:, cols] * sp).astype(BF)

    cot = cot_ref[...]
    for k in range(tiles):
        cols = slice(k * LANE, (k + 1) * LANE)
        gg = dot(cot, wout[cols, :], 1, 1)
        sg_ref[:, cols] = (gg * u_ref[:, cols]).astype(BF)
        pre_u[:, cols] = (gg * spat[:, cols] * slope_u[:, cols]).astype(BF)

    low = out_unit + STEP
    for k in range(tiles):
        rows = slice(k * LANE, (k + 1) * LANE)
        gtmp[rows, :] = dot(gated[:, rows], cot, 0, 0).astype(BF)
    height = keep.shape[1] // 4
    for c, dst in ((0, keep), (1, send)):
        for e in range(4):
            for r in range(4):
                at = (lax.rem(own + r, 4) * 8 + (unit ^ (c + 2 * e))) * out_unit
                dst[e, r * height : r * height + out_unit, :] = gtmp[pl.ds(aligned(at, STEP), out_unit), :]
    gmix = dot(sg_ref[...], vn_ref[...], 1, 1).astype(BF)
    big = lax.broadcasted_iota(I32, (512, n), 0)
    lane = lax.broadcasted_iota(I32, (512, n), 1)
    within = ((big >> 6) ^ unit) * STEP + (big & 15)
    a = (((big >> 4) + own) & 3) * per + within
    pick = jnp.where((lane == a) & (within < per), 1.0, 0.0).astype(BF)
    padded = dot(pick, gmix).astype(BF)
    for c, dst in ((0, keep), (1, send)):
        for e in range(4):
            for r in range(4):
                at = (c + 2 * e) * 64 + r * STEP
                to = r * height + out_unit
                dst[e, to : to + STEP, :] = jnp.zeros((STEP, LANE), BF)
                dst[e, to : to + STEP, 0:n] = padded[at : at + STEP, :]
    for k in range(tiles):
        cols = slice(k * LANE, (k + 1) * LANE)
        part = dot(xt_ref[...], pre_u[:, cols]).astype(BF)
        for j, (c, y, x, r) in enumerate(ORDER):
            to = r * height + low + k * STEP
            (send if c else keep)[x + 2 * y, to : to + STEP, :] = part[j * STEP : (j + 1) * STEP, :]
    branch = dot(gated[...], wout[...]) + b_out[...]
    live = slot_ref[...] >= 0
    out_ref[...] = jnp.where(live, pos_ref[...].astype(F32) + branch, 0.0).astype(BF)


def back_kernel(slot_ref, xt_ref, mix_ref, sg_ref, vhat_ref, rstd_ref, slope_v, g_two, pre_v, keep, send, rows_ref, vng, gain, shift):
    n, gate = vhat_ref.shape
    tiles = gate // LANE
    mix = mix_ref[...]
    for k in range(tiles):
        cols = slice(k * LANE, (k + 1) * LANE)
        vng[:, cols] = dot(mix, sg_ref[:, cols], 0, 0)
    gain[...] = jnp.zeros_like(gain)
    shift[...] = jnp.zeros_like(shift)

    @each_tile(n)
    def _(i):
        rows = rows_of(i)
        vg = jnp.where(slot_ref[rows, :] >= 0, vng[rows, :], 0.0)
        vhat = vhat_ref[rows, :]
        gain[...] += jnp.sum((vg * vhat).reshape(2, 8, gate), 0)
        shift[...] += jnp.sum(vg.reshape(2, 8, gate), 0)
        h = vg * g_two[...]
        v_grad = rstd_ref[rows, :] * (h - mean_rows(h) - vhat * mean_rows(h * vhat))
        pre_v[rows, :] = (v_grad * slope_v[rows, :]).astype(BF)

    height = keep.shape[1] // 4
    for k in range(tiles):
        cols = slice(k * LANE, (k + 1) * LANE)
        part = dot(xt_ref[...], pre_v[:, cols]).astype(BF)
        for j, (c, y, x, r) in enumerate(ORDER):
            to = r * height + k * STEP
            (send if c else keep)[x + 2 * y, to : to + STEP, :] = part[j * STEP : (j + 1) * STEP, :]
        rows_ref[k : k + 1, :] = jnp.sum(gain[:, cols], 0, keepdims=True)
        rows_ref[tiles + k : tiles + k + 1, :] = jnp.sum(shift[:, cols], 0, keepdims=True)


def token_kernel(slot_ref, slot_row, pos_ref, cot_ref, win, pre_u, pre_v, sg_ref, out_ref, g_one, rows_ref, *rest):
    _, o0, o1, o2, o3, vec, xg, in_ref, gain, shift = rest
    n, gate = pre_u.shape
    xg[...] = dot(pre_u[...], win[:, :gate], 1, 1) + dot(pre_v[...], win[:, gate:], 1, 1)
    gain[...] = jnp.zeros_like(gain)
    shift[...] = jnp.zeros_like(shift)
    width = xg.shape[1]

    @each_tile(n)
    def _(i):
        rows = rows_of(i)
        x = pos_ref[rows, :].astype(F32)
        cen = x - mean_rows(x)
        rstd = lax.rsqrt(mean_rows(cen * cen) + EPS)
        xhat = cen * rstd
        g = xg[rows, :]
        gain[...] += jnp.sum((g * xhat).reshape(2, 8, width), 0)
        shift[...] += jnp.sum(g.reshape(2, 8, width), 0)
        h = g * g_one[...]
        x_grad = rstd * (h - mean_rows(h) - xhat * mean_rows(h * xhat))
        total = cot_ref[rows, :].astype(F32) + x_grad
        in_ref[rows, :] = jnp.where(slot_ref[rows, :] >= 0, total, 0.0).astype(BF)

    count = o0.shape[1]
    for r, dst in enumerate((o0, o1, o2, o3)):
        spot = lax.broadcasted_iota(I32, (count, n), 0) + r * count
        pick = jnp.where(slot_row[...] == spot, 1.0, 0.0).astype(BF)
        dst[0] = dot(pick, out_ref[...]).astype(BF)
        dst[1] = dot(pick, in_ref[...]).astype(BF)

    ones = jnp.ones((8, n), BF)
    tiles = gate // LANE
    vec[0:1, :] = jnp.sum(gain[...], 0, keepdims=True)
    vec[1:2, :] = jnp.sum(shift[...], 0, keepdims=True)
    for k in range(tiles):
        cols = slice(k * LANE, (k + 1) * LANE)
        vec[2 + k : 3 + k, :] = dot(ones, pre_u[:, cols])[0:1]
        vec[2 + tiles + k : 3 + tiles + k, :] = dot(ones, pre_v[:, cols])[0:1]
    at = 2 + 2 * tiles
    vec[at : at + 2 * tiles, :] = rows_ref[...]
    at += 2 * tiles
    vec[at : at + 1, :] = dot(ones, cot_ref[...])[0:1]
    vec[at + 1 : at + 2, :] = jnp.zeros((1, LANE), F32)
    vec[at + 1 : at + 2, 0:n] = dot(jnp.ones((8, gate), BF), sg_ref[...], 1, 1)[0:1]


def split_low(v):
    high = v.astype(BF)
    return high, (v - high.astype(F32)).astype(BF)


def put_vec(ref, at, v):
    high, low = split_low(v)
    ref[at : at + STEP, :] = high
    ref[at + STEP : at + 2 * STEP, :] = low


def get_vec(ref, at):
    return ref[at : at + STEP, :].astype(F32) + ref[at + STEP : at + 2 * STEP, :].astype(F32)


def core_kernel(keep, got, own, s1, s2, s3):
    for e, dst in enumerate((own, s1, s2, s3)):
        dst[...] = (keep[e].astype(F32) + got[e].astype(F32)).astype(dst.dtype)


def core_vec_kernel(keep, got, vec, vec_got, own, s1, s2, s3, vec_own):
    rows = own.shape[0]
    total = vec[...] + vec_got[...]
    put_vec(vec_own, 0, total)
    for e, dst in enumerate((own, s1, s2, s3)):
        dst[0:rows, :] = (keep[e].astype(F32) + got[e].astype(F32)).astype(dst.dtype)
        if e:
            put_vec(dst, rows, total)


def plane_kernel(own, g1, g2, g3, z0, z1, z2, z3):
    rows = z0.shape[0]
    for r, dst in enumerate((z0, z1, z2, z3)):
        at = slice(r * rows, (r + 1) * rows)
        total = (own[at, :] + g1[at, :].astype(F32)) + (g2[at, :].astype(F32) + g3[at, :].astype(F32))
        dst[...] = total.astype(dst.dtype)


def plane_vec_kernel(own, vec_own, g1, g2, g3, z0, z1, z2, z3, vec_out):
    rows, at = z0.shape[0], own.shape[0]
    vec = (get_vec(vec_own, 0) + get_vec(g1, at)) + (get_vec(g2, at) + get_vec(g3, at))
    put_vec(vec_out, 0, vec)
    for r, dst in enumerate((z0, z1, z2, z3)):
        at = slice(r * rows, (r + 1) * rows)
        total = (own[at, :] + g1[at, :].astype(F32)) + (g2[at, :].astype(F32) + g3[at, :].astype(F32))
        dst[0:rows, :] = total.astype(dst.dtype)
        if r:
            put_vec(dst, rows, vec)


def patch_kernel(own, g1, g2, g3, out):
    rows = own.shape[0]
    total = own[...]
    for g in (g1, g2, g3):
        total = total + g[0:rows, :].astype(F32)
    out[...] = total.astype(out.dtype)


def patch_vec_kernel(scal, own, vec_own, g1, g2, g3, out, vec_out, held):
    patch_kernel(own, g1, g2, g3, out)
    rows = own.shape[0]
    me = scal[0]
    held[me] = get_vec(vec_own, 0)
    for r, g in enumerate((g1, g2, g3), 1):
        held[lax.rem(me + (4 - r), 4)] = get_vec(g, rows)
    vec_out[...] = (held[0] + held[1]) + (held[2] + held[3])


def home_kernel(scal, h0, h1, h2, h3, out_ref, grad_ref):
    own = scal[0]
    for r, h in enumerate((h0, h1, h2, h3)):
        m = lax.rem(own + r, 4)
        out_ref[m] = h[0]
        grad_ref[m] = h[1].astype(F32)


VM = pl.BlockSpec(memory_space=pltpu.VMEM)
SM = pl.BlockSpec(memory_space=pltpu.SMEM)
ANY = pl.BlockSpec(memory_space=pl.ANY)


def call(body, ins, outs, scratch=(), specs=None, flops=100_000_000, limit=16, name=None):
    moved = sum(math.prod(a.shape) * a.dtype.itemsize for a in ins)
    return pl.pallas_call(
        body,
        out_shape=[jax.ShapeDtypeStruct(s, d) for s, d in outs],
        in_specs=specs or [VM] * len(ins),
        out_specs=[VM] * len(outs),
        scratch_shapes=list(scratch),
        compiler_params=pltpu.CompilerParams(vmem_limit_bytes=limit * 2**20),
        cost_estimate=pl.CostEstimate(flops=flops, bytes_accessed=moved, transcendentals=0),
        name=name,
    )(*ins)


def rest_of_img(total):
    mask = 8
    while mask < lax.axis_size("img"):
        total = total + swap(total, mask)
        mask *= 2
    return total


def img_gather(arr):
    size = lax.axis_size("img")
    groups = [[g * 8 + k for k in range(8)] for g in range(size // 8)]
    return lax.all_gather(arr, "img", axis_index_groups=groups)


def shards(
    tokens,
    cotangent,
    patch_count,
    crop_index,
    in_weight,
    in_moment,
    in_average,
    out_weight,
    out_moment,
    out_average,
    spatial_weight,
    spatial_moment,
    spatial_average,
    vectors,
    vector_moment,
    vector_average,
):
    p = lax.axis_index("patch")
    unit = lax.axis_index("img") % 8
    micro_count, slot_count, row_count, width = tokens.shape
    hidden = in_weight.shape[1]
    gate = hidden // 2
    mix_rows, cells = spatial_weight.shape
    assert micro_count == lax.axis_size("patch") == 4 and slot_count == 1
    assert width == LANE and in_weight.shape[0] == 128 and row_count == mix_rows == 81
    grid = math.isqrt(cells)
    n = -(-cells // STEP) * STEP
    in_unit = in_weight.shape[0] // 8
    out_unit = out_weight.shape[0] // 8
    low = out_unit + STEP
    side_rows = in_unit * gate // LANE
    scal = jnp.stack([p, unit]).astype(I32)

    def over_plane(base):
        chips = [base] + [swap(base, m) for m in (2, 4, 6)]
        found = []
        for arr in chips:
            found += [arr, swap(arr, CORE)]
        return found

    wi_piece = lax.dynamic_slice_in_dim(in_weight, unit * in_unit, in_unit, 0).astype(BF)
    wi = over_plane(jnp.stack([turn(wi_piece, r) for r in (1, 2, 3)]))
    wi_own = in_weight.astype(BF)

    blk = ((row_count, width), BF)
    msg = ((low + row_count, width), BF)
    m1, m2, m3, tok_own, c1, c2, c3, cot_own, wo_own, mx_own = call(
        prep_kernel,
        [scal, tokens.reshape(4, row_count, width), cotangent.reshape(4, row_count, width), out_weight, spatial_weight],
        [msg, msg, msg, blk, blk, blk, blk, blk, (out_weight.shape, BF), ((128, LANE), BF)],
        specs=[SM] + [VM] * 4,
        name="prep",
    )
    got = [turn(m, r) for r, m in enumerate((m1, m2, m3), 1)]
    cot = [cot_own] + [turn(c, r) for r, c in enumerate((c1, c2, c3), 1)]
    wo = over_plane(jnp.stack([g[:low] for g in got]))

    count = lax.dynamic_index_in_dim(patch_count, p, 0, keepdims=False)[0]
    start = lax.dynamic_index_in_dim(crop_index, p, 0, keepdims=False)[0, 0]
    quarter = count // 4
    side = jnp.round(jnp.sqrt(count.astype(F32))).astype(I32)
    place = jnp.arange(n, dtype=I32)
    drow = place // grid - start // grid
    dcol = place % grid - start % grid
    inside = (drow >= 0) & (drow < side) & (dcol >= 0) & (dcol < side) & (place < cells)
    order = drow * side + dcol
    block = (order >= quarter).astype(I32) + (order >= 2 * quarter).astype(I32) + (order >= 3 * quarter).astype(I32)
    slot = jnp.where(inside, ((p - block) % 4) * row_count + order - block * quarter, -1)
    slot_col, slot_row = slot[:, None], slot[None, :]

    bounds = [width, width, hidden, gate, gate, cells, width]
    pieces = []
    offset = 0
    for length in bounds:
        pieces.append(vectors[None, offset : offset + length])
        offset += length
    g_one, s_one, b_in, g_two, s_two, b_mix, b_out = pieces
    b_mix = jnp.pad(b_mix[0], (0, n - cells))[:, None]

    pos, xn, xt = call(
        norm_kernel,
        [scal, slot_col, tok_own, *got, g_one, s_one],
        [((n, width), BF), ((n, width), BF), ((width, n), BF)],
        [pltpu.VMEM((width, n), BF)],
        specs=[SM] + [VM] * 7,
        name="norm_in",
    )
    (cot_pos,) = call(place_kernel, [slot_col, *cot], [((n, width), BF)], name="place_cot")
    sized = lambda kind: ((n, gate), kind)
    win, u, slope_u, vhat, rstd, slope_v, vn = call(
        gate_kernel,
        [scal, slot_col, xn, b_in, g_two, s_two, wi_own, *wi],
        [((width, hidden), BF), sized(F32), sized(F32), sized(F32), ((n, 1), F32), sized(F32), sized(BF)],
        [pltpu.VMEM((n, gate), F32), pltpu.SemaphoreType.DMA((25,))],
        specs=[SM] + [VM] * 5 + [ANY] * 9,
        flops=2_000_000_000,
        limit=24,
        name="gate",
    )
    packed = ((4, 4 * (low + side_rows), LANE), BF)
    out_pos, mix, pre_u, sg, keep_a, send_a = call(
        spatial_kernel,
        [scal, slot_col, pos, xt, cot_pos, u, slope_u, vn, b_mix, b_out, wo_own, mx_own, *wo],
        [((n, width), BF), ((n, n), BF), sized(BF), sized(BF), packed, packed],
        [
            pltpu.VMEM((gate, width), BF),
            pltpu.VMEM((512, LANE), BF),
            pltpu.VMEM((n, gate), F32),
            pltpu.VMEM((n, gate), BF),
            pltpu.VMEM((gate, width), BF),
            pltpu.SemaphoreType.DMA((50,)),
        ],
        specs=[SM] + [VM] * 9 + [ANY] * 10,
        flops=4_000_000_000,
        limit=24,
        name="spatial",
    )
    core_a = swap(send_a, CORE)
    half = ((4, 4 * side_rows, LANE), BF)
    pre_v, keep_b, send_b, rows_b = call(
        back_kernel,
        [slot_col, xt, mix, sg, vhat, rstd, slope_v, g_two],
        [sized(BF), half, half, ((6, LANE), F32)],
        [pltpu.VMEM((n, gate), F32), pltpu.VMEM((8, gate), F32), pltpu.VMEM((8, gate), F32)],
        flops=2_000_000_000,
        limit=20,
        name="back",
    )
    core_b = swap(send_b, CORE)
    rows_a, rows_b4 = 4 * (low + side_rows), 4 * side_rows
    own_a, *send_a = call(
        core_kernel, [keep_a, core_a], [((rows_a, LANE), F32)] + [((rows_a, LANE), BF)] * 3, limit=12, name="core_a"
    )
    plane_a = [swap(s, m) for s, m in zip(send_a, (2, 4, 6))]
    pair = ((2, row_count, width), BF)
    h0, h1, h2, h3, vec = call(
        token_kernel,
        [slot_col, slot_row, pos, cot_pos, win, pre_u, pre_v, sg, out_pos, g_one, rows_b, send_a[2]],
        [pair, pair, pair, pair, ((STEP, LANE), F32)],
        [
            pltpu.VMEM((n, width), F32),
            pltpu.VMEM((n, width), BF),
            pltpu.VMEM((8, width), F32),
            pltpu.VMEM((8, width), F32),
        ],
        specs=[VM] * 11 + [ANY],
        flops=2_000_000_000,
        limit=20,
        name="token_grad",
    )
    vec_got = swap(vec, CORE)
    own_b, *send_b, vec_own = call(
        core_vec_kernel,
        [keep_b, core_b, vec, vec_got],
        [((rows_b4, LANE), F32)] + [((rows_b4 + 2 * STEP, LANE), BF)] * 3 + [((2 * STEP, LANE), BF)],
        name="core_b",
    )
    plane_b = [swap(s, m) for s, m in zip(send_b, (2, 4, 6))]
    home = [h0] + [turn(h, -r) for r, h in enumerate((h1, h2, h3), 1)]
    out_tokens, in_grad = call(
        home_kernel,
        [scal, *home],
        [((4, row_count, width), BF), ((4, row_count, width), F32)],
        specs=[SM] + [VM] * 4,
        name="home",
    )
    z_rows = low + side_rows
    own_a, *patch_a = call(
        plane_kernel, [own_a, *plane_a], [((z_rows, LANE), F32)] + [((z_rows, LANE), BF)] * 3, name="plane_a"
    )
    got_a = [turn(z, r) for r, z in enumerate(patch_a, 1)]
    own_b, *patch_b, vec_own = call(
        plane_vec_kernel,
        [own_b, vec_own, *plane_b],
        [((side_rows, LANE), F32)] + [((side_rows + 2 * STEP, LANE), BF)] * 3 + [((2 * STEP, LANE), BF)],
        name="plane_b",
    )
    got_b = [turn(z, r) for r, z in enumerate(patch_b, 1)]
    kind = BF if lax.axis_size("img") == 8 else F32
    (first,) = call(patch_kernel, [own_a, *got_a], [((z_rows, LANE), kind)], name="patch_a")
    second, vec_sum = call(
        patch_vec_kernel,
        [scal, own_b, vec_own, *got_b],
        [((side_rows, LANE), kind), ((STEP, LANE), F32)],
        [pltpu.VMEM((4, STEP, LANE), F32)],
        specs=[SM] + [VM] * 5,
        name="patch_b",
    )
    first = img_gather(rest_of_img(first).astype(BF))
    second = img_gather(rest_of_img(second).astype(BF))
    vec_sum = rest_of_img(vec_sum).reshape(STEP * LANE)

    def unpack(arr):
        arr = arr.reshape(8, gate // LANE, in_unit, LANE).transpose(0, 2, 1, 3)
        return arr.reshape(8 * in_unit, gate)

    out_share = first[:, :out_unit].reshape(8 * out_unit, width).astype(F32)
    mix_share = first[:, out_unit:low].reshape(128, LANE)[:mix_rows, :cells].astype(F32)
    in_share = jnp.concatenate([unpack(first[:, low:]), unpack(second)], axis=1).astype(F32)
    head_len = 2 * width + hidden + 2 * gate
    vec_sum = jnp.concatenate(
        [vec_sum[:head_len], vec_sum[head_len + width : head_len + width + cells], vec_sum[head_len : head_len + width]]
    )

    images = micro_count * slot_count * lax.axis_size("img")
    rate_in, rate_out, rate_mix, rate_vec = step_rates(images, width, gate, cells)
    in_new = nesterov(in_weight, in_share, in_moment, in_average, rate_in)
    out_new = nesterov(out_weight, out_share, out_moment, out_average, rate_out)
    mix_new = nesterov(spatial_weight, mix_share, spatial_moment, spatial_average, rate_mix)
    vec_new = nesterov(vectors, vec_sum, vector_moment, vector_average, rate_vec)
    return (out_tokens.reshape(tokens.shape), in_grad.reshape(tokens.shape), *in_new, *out_new, *mix_new, *vec_new)


def solution(mesh):
    rows = P("patch", None)
    act = P(None, "img", "patch", None)
    return jax.shard_map(
        shards,
        mesh=mesh,
        in_specs=(act, act, P(None, "img"), P(None, "img", None), *([rows] * 9), P(), P(), P()),
        out_specs=(act, act, *([rows] * 9), P(), P(), P()),
        check_vma=False,
    )
```

time: 222 us -> 171 us (0.77)
  Pallas kernels: 0 us -> 30.4 us
  starting transfers between devices: 73.4 us -> 43.8 us
  other arithmetic: 32 us -> 7.76 us
  local copies, waits for them, and re-layouts: 29.1 us -> 8.99 us
  blocking collectives: 0 us -> 19.3 us
  matrix products: 19 us -> 0 us
  waiting for transfers between devices: 61 us -> 53.8 us
    ppermute x35 -> x23, waiting for transfers between devices: 54.1 us -> 18.3 us  [swap(): return lax.ppermute(arr, 'img', [(k, k ^ mask) for k in range(n)])]
    pallas_call x0 -> x14, Pallas kernels: none -> 30.4 us  [call(): pl.pallas_call(body, out_shape=[jax.ShapeDtypeStruct(s, d) for s, d in ou...]
    ppermute x24 -> x18, waiting for transfers between devices: 6.95 us -> 35.5 us  [turn(): return lax.ppermute(arr, 'patch', [(s, (s + r) % n) for s in range(n)])]
    all_gather x0 -> x2, blocking collectives: none -> 19.3 us  [img_gather(): return lax.all_gather(arr, 'img', axis_index_groups=groups)]
    dot_general x12 -> x0, matrix products: 19 us -> none  [dot(): lax.dot_general(a, b, (((ca,), (cb,)), ((), ())), preferred_element_type=...]
    ppermute x24 -> x18, starting transfers between devices: 39.8 us -> 24.9 us  [turn(): return lax.ppermute(arr, 'patch', [(s, (s + r) % n) for s in range(n)])]
    ppermute x35 -> x23, starting transfers between devices: 33.6 us -> 19 us  [swap(): return lax.ppermute(arr, 'img', [(k, k ^ mask) for k in range(n)])]
    concatenate x21 -> x0, other arithmetic: 10.8 us -> none  [the longest x2 5.41 us: to_absolute(): twice = jnp.concatenate([flipped, flipped])]
  transfers between devices with their start and end apart: 59 -> 41, of which waited for: 28 -> 13; matrix products, arithmetic and copies ran while one was open for 17% -> 5% of each run, Pallas kernels for 0% -> 12%
where the time goes in v2:
time: 171 us
  waiting for transfers between devices  53.8 us (31%)
  starting transfers between devices  43.8 us (26%)
  Pallas kernels  30.4 us (18%)
  blocking collectives  19.3 us (11%)
  local copies, waits for them, and re-layouts  8.99 us (5%)
  other arithmetic  7.76 us (5%)
  between operations  6.42 us (4%)
    ppermute x18, waiting for transfers between devices, turn(): return lax.ppermute(arr, 'patch', [(s, (s + r) % n) for s in range(n)])  35.5 us
    pallas_call x14, Pallas kernels, call(): pl.pallas_call(body, out_shape=[jax.ShapeDtypeStruct(s, d) for s, d in ou...  30.4 us
    ppermute x18, starting transfers between devices, turn(): return lax.ppermute(arr, 'patch', [(s, (s + r) % n) for s in range(n)])  24.9 us
    all_gather x2, blocking collectives, img_gather(): return lax.all_gather(arr, 'img', axis_index_groups=groups)  19.3 us
    ppermute x23, starting transfers between devices, swap(): return lax.ppermute(arr, 'img', [(k, k ^ mask) for k in range(n)])  19 us
    ppermute x23, waiting for transfers between devices, swap(): return lax.ppermute(arr, 'img', [(k, k ^ mask) for k in range(n)])  18.3 us
    add x4, other arithmetic, nesterov(): average_new = AVG_DECAY * average + (1.0 - AVG_DECAY) * weight_new  5.81 us
    unnamed x37, local copies, waits for them, and re-layouts  4.62 us
  transfers between devices with their start and end apart: 41, of which 13 were waited for; matrix products, arithmetic and copies ran while one was open for 5% of the time, Pallas kernels for 12%

profile of v2, /device:TPU:0, one launch (start us, length us, event | category | flops | bytes accessed | tf_op | source)
XLA Modules:
  0.0 170.5 jit_solution(16606514849871845704)
XLA Ops:
  0.7 1.0 dynamic-slice_convert_fusion
  1.7 5.1 %collective-permute-start.8 = (bf16[16,3072]{1,0:T(8,128)(2,1)S(1)}, bf16[16,3072]{1,0:T(8,128)(2,1)S(1)}, u32[]{:S(2)}, u32[]{:S(2)}) collective-permute-start(bf16[16,3072]{1,0:T(8,128)(2,1)S(1)} %dynamic-slice_convert_fusion), channel_id=1, source_target_pairs={{0,3},{1,0},{2,1},{3,2},{4,7},{5,4},{6,5},{7,6},{8,11},{9,8},{10,9... | collective-permute-start | bytes 294920 | tf_op jit(solution)/shard_map/ppermute | solution.py:40
  6.8 1.0 collective-permute-start.6
  7.8 1.2 copy_bitcast_fusion
  9.8 2.5 %collective-permute-start.3 = (bf16[81,512]{1,0:T(8,128)(2,1)S(1)}, bf16[81,512]{1,0:T(8,128)(2,1)S(1)}, u32[]{:S(2)}, u32[]{:S(2)}) collective-permute-start(bf16[81,512]{1,0:T(8,128)(2,1)S(1)} %get-tuple-element.77), channel_id=1, source_target_pairs={{0,1},{1,2},{2,3},{3,0},{4,5},{5,6},{6,7},{7,4},{8,9},{9,10},{10,1... | collective-permute-start | bytes 248840 | tf_op jit(solution)/shard_map/ppermute | solution.py:40
  12.3 0.9 collective-permute-start.4
  13.3 1.5 collective-permute-start.5
  14.8 5.2 %collective-permute-done.7 = bf16[16,3072]{1,0:T(8,128)(2,1)S(1)} collective-permute-done((bf16[16,3072]{1,0:T(8,128)(2,1)S(1)}, bf16[16,3072]{1,0:T(8,128)(2,1)S(1)}, u32[]{:S(2)}, u32[]{:S(2)}) %collective-permute-start.7) | collective-permute-done | bytes 98336 | tf_op jit(solution)/shard_map/ppermute | solution.py:40
  20.0 2.6 %collective-permute-start.1 = (bf16[145,512]{1,0:T(8,128)(2,1)S(1)}, bf16[145,512]{1,0:T(8,128)(2,1)S(1)}, u32[]{:S(2)}, u32[]{:S(2)}) collective-permute-start(bf16[145,512]{1,0:T(8,128)(2,1)S(1)} %get-tuple-element.73), channel_id=1, source_target_pairs={{0,2},{1,3},{2,0},{3,1},{4,6},{5,7},{6,4},{7,5},{8,10},{9,11},{10,... | collective-permute-start | bytes 445448 | tf_op jit(solution)/shard_map/ppermute | solution.py:40
  22.6 5.8 %collective-permute-done.b1 = bf16[145,512]{1,0:T(8,128)(2,1)S(1)} collective-permute-done((bf16[145,512]{1,0:T(8,128)(2,1)S(1)}, bf16[145,512]{1,0:T(8,128)(2,1)S(1)}, u32[]{:S(2)}, u32[]{:S(2)}) %collective-permute-start) | collective-permute-done | bytes 148512 | tf_op jit(solution)/shard_map/ppermute | solution.py:40
  28.5 4.9 %collective-permute-done.1.b2 = bf16[145,512]{1,0:T(8,128)(2,1)S(1)} collective-permute-done((bf16[145,512]{1,0:T(8,128)(2,1)S(1)}, bf16[145,512]{1,0:T(8,128)(2,1)S(1)}, u32[]{:S(2)}, u32[]{:S(2)}) %collective-permute-start.1) | collective-permute-done | bytes 148512 | tf_op jit(solution)/shard_map/ppermute | solution.py:40
  33.4 2.4 %collective-permute-start.14 = (bf16[3,16,3072]{2,1,0:T(8,128)(2,1)S(1)}, bf16[3,16,3072]{2,1,0:T(8,128)(2,1)S(1)}, u32[]{:S(2)}, u32[]{:S(2)}) collective-permute-start(bf16[3,16,3072]{2,1,0:T(8,128)(2,1)S(1)} %pad_maximum_fusion.1.rest_0_), channel_id=1, source_target_pairs={{0,24},{4,28},{8,16},{12,20},{16,8},{20,12},{24,0},{28,4},{1,25},{... | collective-permute-start | bytes 884744 | tf_op jit(solution)/shard_map/ppermute | solution.py:45
  35.9 1.9 %collective-permute-done.2.b3 = bf16[145,512]{1,0:T(8,128)(2,1)S(1)} collective-permute-done((bf16[145,512]{1,0:T(8,128)(2,1)S(1)}, bf16[145,512]{1,0:T(8,128)(2,1)S(1)}, u32[]{:S(2)}, u32[]{:S(2)}) %collective-permute-start.2) | collective-permute-done | bytes 148512 | tf_op jit(solution)/shard_map/ppermute | solution.py:40
  37.8 1.5 collective-permute-start.12
  39.3 1.6 collective-permute-start.10
  45.2 1.6 collective-permute-start.19
  49.3 4.0 %collective-permute-done.21.rest_6_ = bf16[3,64,512]{2,1,0:T(8,128)(2,1)S(1)} collective-permute-done((bf16[3,64,512]{2,1,0:T(8,128)(2,1)S(1)}, bf16[3,64,512]{2,1,0:T(8,128)(2,1)S(1)}, u32[]{:S(2)}, u32[]{:S(2)}) %collective-permute-start.21) | collective-permute-done | bytes 196640 | tf_op jit(solution)/shard_map/ppermute | solution.py:45
  54.7 1.5 convert_element_type.91.wi_own
  56.3 1.1 collective-permute-done.19.rest_4_
  57.4 1.5 collective-permute-start.17
  59.5 4.6 %collective-permute-done.17.rest_2_ = bf16[3,64,512]{2,1,0:T(8,128)(2,1)S(1)} collective-permute-done((bf16[3,64,512]{2,1,0:T(8,128)(2,1)S(1)}, bf16[3,64,512]{2,1,0:T(8,128)(2,1)S(1)}, u32[]{:S(2)}, u32[]{:S(2)}) %collective-permute-start.17) | collective-permute-done | bytes 196640 | tf_op jit(solution)/shard_map/ppermute | solution.py:45
  65.2 2.1 %norm_in.1 = (bf16[336,512]{1,0:T(8,128)(2,1)S(1)}, bf16[336,512]{1,0:T(8,128)(2,1)S(1)}, bf16[512,336]{1,0:T(8,128)(2,1)S(1)}) custom-call(s32[2]{0:T(128)S(1)} %pad_add_fusion.scal, s32[336,1]{1,0:T(8,128)S(1)} %fusion.15.slot_ref, bf16[81,512]{1,0:T(8,128)(2,1)S(1)} %get-tuple-element.71.b0, bf16[145,512]{1,0:T(8,128)(2,1)S(1)} %collective-permute-done.b1, ...), custom_call_target="tpu_custom_call" | custom-call | flops 100000000 | bytes 533832 | tf_op jit(solution)/shard_map/norm_in/pallas_call | solution.py:425
  67.3 7.3 %gate.1 = (bf16[512,3072]{1,0:T(8,128)(2,1)S(1)}, f32[336,1536]{1,0:T(8,128)S(1)}, f32[336,1536]{1,0:T(8,128)S(1)}, f32[336,1536]{1,0:T(8,128)S(1)}, f32[336,1]{...) custom-call(s32[2]{0:T(128)S(1)} %pad_add_fusion.scal, s32[336,1]{1,0:T(8,128)S(1)} %fusion.15.slot_ref, ...), custom_call_target="tpu_custom_call" | custom-call | flops 2000000000 | bytes 3515720 | tf_op jit(solution)/shard_map/gate/pallas_call | solution.py:425
  74.6 8.7 %spatial.1 = (bf16[336,512]{1,0:T(8,128)(2,1)S(1)}, bf16[336,336]{1,0:T(8,128)(2,1)S(1)}, bf16[336,1536]{1,0:T(8,128)(2,1)S(1)}, bf16[336,1536]{1,0:T(8,128)(2,1...) custom-call(s32[2]{0:T(128)S(1)} %pad_add_fusion.scal, s32[336,1]{1,0:T(8,128)S(1)} %fusion.15.slot_ref, ...), custom_call_target="tpu_custom_call" | custom-call | flops 4000000000 | bytes 8295048 | tf_op jit(solution)/shard_map/spatial/pallas_call | solution.py:425
  83.5 3.3 %back.1 = (bf16[336,1536]{1,0:T(8,128)(2,1)S(1)}, bf16[4,192,512]{2,1,0:T(8,128)(2,1)S(1)}, bf16[4,192,512]{2,1,0:T(8,128)(2,1)S(1)}, f32[6,512]{1,0:T(8,128)S(1)}) custom-call(s32[336,1]{1,0:T(8,128)S(1)} %fusion.15.slot_ref, bf16[512,336]{1,0:T(8,128)(2,1)S(1)} %get-tuple-element.82.xt_ref, bf16[336,336]{1,0:T(8,128)(2,1)S(1)} %get-tuple-element.89.mix_ref, ...), custom_call_target="tpu_custom_call" | custom-call | flops 2000000000 | bytes 5739648 | tf_op jit(solution)/shard_map/back/pallas_call | solution.py:425
  87.4 1.1 core_a.1
  88.5 3.9 %token_grad.1 = (bf16[2,81,512]{2,1,0:T(8,128)(2,1)S(1)}, bf16[2,81,512]{2,1,0:T(8,128)(2,1)S(1)}, bf16[2,81,512]{2,1,0:T(8,128)(2,1)S(1)}, bf16[2,81,512]{2,1,0:T(8,128)(2,1)S(1)}, f32[16,512]{1,0:T(8,128)S(1)}) custom-call(s32[336,1]{1,0:T(8,128)S(1)} %fusion.15.slot_ref, s32[1,336]{1,0:T(1,128)S(1)} %and_select_fusion.1.slot_row, ...), custom_call_target="tpu_custom_call" | custom-call | flops 2000000000 | bytes 7750272 | tf_op jit(solution)/shard_map/token_grad/pallas_call | solution.py:425
  92.5 1.1 collective-permute-done.34.vec_got
  93.8 1.6 collective-permute-start.35
  95.4 6.3 %collective-permute-start.24 = (bf16[2,81,512]{2,1,0:T(8,128)(2,1)S(1)}, bf16[2,81,512]{2,1,0:T(8,128)(2,1)S(1)}, u32[]{:S(2)}, u32[]{:S(2)}) collective-permute-start(bf16[2,81,512]{2,1,0:T(8,128)(2,1)S(1)} %get-tuple-element.101), channel_id=1, source_target_pairs={{0,3},{1,0},{2,1},{3,2},{4,7},{5,4},{6,5},{7,6},{8,11},{9,8},{10,9... | collective-permute-start | bytes 497672 | tf_op jit(solution)/shard_map/ppermute | solution.py:40
  102.2 1.4 collective-permute-start.37
  103.7 1.5 collective-permute-start.27
  106.1 1.4 collective-permute-start.29
  107.6 7.5 %collective-permute-done.36.g2 = bf16[224,512]{1,0:T(8,128)(2,1)S(1)} collective-permute-done((bf16[224,512]{1,0:T(8,128)(2,1)S(1)}, bf16[224,512]{1,0:T(8,128)(2,1)S(1)}, u32[]{:S(2)}, u32[]{:S(2)}) %collective-permute-start.36) | collective-permute-done | bytes 229408 | tf_op jit(solution)/shard_map/ppermute | solution.py:45
  115.2 9.7 %collective-permute-done.25.h2 = bf16[2,81,512]{2,1,0:T(8,128)(2,1)S(1)} collective-permute-done((bf16[2,81,512]{2,1,0:T(8,128)(2,1)S(1)}, bf16[2,81,512]{2,1,0:T(8,128)(2,1)S(1)}, u32[]{:S(2)}, u32[]{:S(2)}) %collective-permute-start.25) | collective-permute-done | bytes 165920 | tf_op jit(solution)/shard_map/ppermute | solution.py:40
  124.8 1.0 collective-permute-start.39
  125.9 6.1 %collective-permute-done.38.g1 = bf16[80,512]{1,0:T(8,128)(2,1)S(1)} collective-permute-done((bf16[80,512]{1,0:T(8,128)(2,1)S(1)}, bf16[80,512]{1,0:T(8,128)(2,1)S(1)}, u32[]{:S(2)}, u32[]{:S(2)}) %collective-permute-start.38) | collective-permute-done | bytes 81952 | tf_op jit(solution)/shard_map/ppermute | solution.py:40
  132.7 0.9 copy.55
  133.6 1.5 copy.56
  135.1 1.4 collective-permute-done.40.g3
  137.2 1.2 plane_a.1
  139.1 1.7 %collective-permute-start.31 = (bf16[112,512]{1,0:T(8,128)(2,1)S(1)}, bf16[112,512]{1,0:T(8,128)(2,1)S(1)}, u32[]{:S(2)}, u32[]{:S(2)}) collective-permute-start(bf16[112,512]{1,0:T(8,128)(2,1)S(1)} %get-tuple-element.111), channel_id=1, source_target_pairs={{0,2},{1,3},{2,0},{3,1},{4,6},{5,7},{6,4},{7,5},{8,10},{9,11},{10,... | collective-permute-start | bytes 344072 | tf_op jit(solution)/shard_map/ppermute | solution.py:40
  140.8 1.5 collective-permute-start.32
  143.0 9.0 %all-gather.1 = bf16[384,512]{1,0:T(8,128)(2,1)S(1)} all-gather(bf16[48,512]{1,0:T(8,128)(2,1)S(1)} %get-tuple-element.126), channel_id=3, replica_groups={{0,4,8,12,16,20,24,28},{1,5,9,13,17,21,25,29},{2,6,10,14,18,22,26,30},{..., dimensions={0}, use_global_device_ids=true | all-gather | bytes 442368 | tf_op jit(solution)/shard_map/all_gather | solution.py:448
  152.5 10.3 %all-gather = bf16[896,512]{1,0:T(8,128)(2,1)S(1)} all-gather(bf16[112,512]{1,0:T(8,128)(2,1)S(1)} %patch_a.1), channel_id=2, replica_groups={{0,4,8,12,16,20,24,28},{1,5,9,13,17,21,25,29},{2,6,10,14,18,22,26,30},{..., dimensions={0}, use_global_device_ids=true | all-gather | bytes 1032192 | tf_op jit(solution)/shard_map/all_gather | solution.py:448
  164.6 1.7 multiply_add_fusion.1
  166.4 0.9 copy-done.6
  167.8 2.7 %multiply_add_fusion = (f32[128,3072]{1,0:T(8,128)}, f32[128,3072]{1,0:T(8,128)}, f32[128,3072]{1,0:T(8,128)}) fusion(f32[128,3072]{1,0:T(8,128)S(1)} %copy-done.6, f32[128,3072]{1,0:T(8,128)S(1)} %copy-done.5, bf16[128,1536]{1,0:T(8,128)(2,1)S(1)} %bitcast.63, bf16[128,1536]{1,0:T(8,128)(2,1)S(1)} %bitcast.64, f32[128,3072]{1,0:T(8,128)S(1)} %copy-done.7), kind=kLoop, calls=%fused_computation.4 | loop fusion | flops 5111808 | bytes 10223616 | tf_op jit(solution)/shard_map/add | solution.py:34
  (122 shorter events, 13.7 us)
Async XLA Ops:
  0.6 46.2 %copy-start = (s32[4,1,324]{2,1,0:T(1,128)S(1)}, s32[4,1,324]{2,1,0:T(1,128)}, u32[]{:S(2)}) copy-start(s32[4,1,324]{2,1,0:T(1,128)} %param.19) | copy-start | bytes 15556
  0.7 8.5 %copy-start.2 = (f32[81,324]{1,0:T(8,128)S(1)}, f32[81,324]{1,0:T(8,128)}, u32[]{:S(2)}) copy-start(f32[81,324]{1,0:T(8,128)} %mix.1) | copy-start | bytes 314932
  0.7 8.5 %copy-start.1 = (f32[384,512]{1,0:T(8,128)S(1)}, f32[384,512]{1,0:T(8,128)}, u32[]{:S(2)}) copy-start(f32[384,512]{1,0:T(8,128)} %weight.1) | copy-start | bytes 2359300
  1.7 11.5 %collective-permute-start.8 = (bf16[16,3072]{1,0:T(8,128)(2,1)S(1)}, bf16[16,3072]{1,0:T(8,128)(2,1)S(1)}, u32[]{:S(2)}, u32[]{:S(2)}) collective-permute-start(bf16[16,3072]{1,0:T(8,128)(2,1)S(1)} %dynamic-slice_convert_fusion), channel_id=1, source_target_pairs={{0,3},{1,0},{2,1},{3,2},{4,7},{5,4},{6,5},{7,6},{8,11},{9,8},{10,9... | collective-permute-start | bytes 294920 | tf_op jit(solution)/shard_map/ppermute | solution.py:40
  6.8 13.2 %collective-permute-start.7 = (bf16[16,3072]{1,0:T(8,128)(2,1)S(1)}, bf16[16,3072]{1,0:T(8,128)(2,1)S(1)}, u32[]{:S(2)}, u32[]{:S(2)}) collective-permute-start(bf16[16,3072]{1,0:T(8,128)(2,1)S(1)} %dynamic-slice_convert_fusion), channel_id=1, source_target_pairs={{0,2},{1,3},{2,0},{3,1},{4,6},{5,7},{6,4},{7,5},{8,10},{9,11},{10,... | collective-permute-start | bytes 294920 | tf_op jit(solution)/shard_map/ppermute | solution.py:40
  6.8 13.2 %collective-permute-start.6 = (bf16[16,3072]{1,0:T(8,128)(2,1)S(1)}, bf16[16,3072]{1,0:T(8,128)(2,1)S(1)}, u32[]{:S(2)}, u32[]{:S(2)}) collective-permute-start(bf16[16,3072]{1,0:T(8,128)(2,1)S(1)} %dynamic-slice_convert_fusion), channel_id=1, source_target_pairs={{0,1},{1,2},{2,3},{3,0},{4,5},{5,6},{6,7},{7,4},{8,9},{9,10},{10,1... | collective-permute-start | bytes 294920 | tf_op jit(solution)/shard_map/ppermute | solution.py:40
  9.0 32.3 %copy-start.10 = (f32[8004]{0:T(1024)S(1)}, f32[8004]{0:T(1024)}, u32[]{:S(2)}) copy-start(f32[8004]{0:T(1024)} %param.29) | copy-start | bytes 96052
  9.1 32.3 %copy-start.15 = (s32[4,1]{0,1:T(1,128)S(1)}, s32[4,1]{0,1:T(1,128)}, u32[]{:S(2)}) copy-start(s32[4,1]{0,1:T(1,128)} %param.18) | copy-start | bytes 52
  9.8 31.1 %copy-start.3 = (bf16[128,512]{1,0:T(8,128)(2,1)}, bf16[128,512]{1,0:T(8,128)(2,1)S(1)}, u32[]{:S(2)}) copy-start(bf16[128,512]{1,0:T(8,128)(2,1)S(1)} %get-tuple-element.87.mx_own) | copy-start | bytes 393220
  9.8 29.5 %collective-permute-start.3 = (bf16[81,512]{1,0:T(8,128)(2,1)S(1)}, bf16[81,512]{1,0:T(8,128)(2,1)S(1)}, u32[]{:S(2)}, u32[]{:S(2)}) collective-permute-start(bf16[81,512]{1,0:T(8,128)(2,1)S(1)} %get-tuple-element.77), channel_id=1, source_target_pairs={{0,1},{1,2},{2,3},{3,0},{4,5},{5,6},{6,7},{7,4},{8,9},{9,10},{10,1... | collective-permute-start | bytes 248840 | tf_op jit(solution)/shard_map/ppermute | solution.py:40
  12.3 28.5 %collective-permute-start.4 = (bf16[81,512]{1,0:T(8,128)(2,1)S(1)}, bf16[81,512]{1,0:T(8,128)(2,1)S(1)}, u32[]{:S(2)}, u32[]{:S(2)}) collective-permute-start(bf16[81,512]{1,0:T(8,128)(2,1)S(1)} %get-tuple-element.78), channel_id=1, source_target_pairs={{0,2},{1,3},{2,0},{3,1},{4,6},{5,7},{6,4},{7,5},{8,10},{9,11},{10,... | collective-permute-start | bytes 248840 | tf_op jit(solution)/shard_map/ppermute | solution.py:40
  13.3 32.0 %collective-permute-start.5 = (bf16[81,512]{1,0:T(8,128)(2,1)S(1)}, bf16[81,512]{1,0:T(8,128)(2,1)S(1)}, u32[]{:S(2)}, u32[]{:S(2)}) collective-permute-start(bf16[81,512]{1,0:T(8,128)(2,1)S(1)} %get-tuple-element.79), channel_id=1, source_target_pairs={{0,3},{1,0},{2,1},{3,2},{4,7},{5,4},{6,5},{7,6},{8,11},{9,8},{10,9... | collective-permute-start | bytes 248840 | tf_op jit(solution)/shard_map/ppermute | solution.py:40
  20.0 8.4 %collective-permute-start = (bf16[145,512]{1,0:T(8,128)(2,1)S(1)}, bf16[145,512]{1,0:T(8,128)(2,1)S(1)}, u32[]{:S(2)}, u32[]{:S(2)}) collective-permute-start(bf16[145,512]{1,0:T(8,128)(2,1)S(1)} %get-tuple-element.72), channel_id=1, source_target_pairs={{0,1},{1,2},{2,3},{3,0},{4,5},{5,6},{6,7},{7,4},{8,9},{9,10},{10,1... | collective-permute-start | bytes 445448 | tf_op jit(solution)/shard_map/ppermute | solution.py:40
  20.0 13.4 %collective-permute-start.1 = (bf16[145,512]{1,0:T(8,128)(2,1)S(1)}, bf16[145,512]{1,0:T(8,128)(2,1)S(1)}, u32[]{:S(2)}, u32[]{:S(2)}) collective-permute-start(bf16[145,512]{1,0:T(8,128)(2,1)S(1)} %get-tuple-element.73), channel_id=1, source_target_pairs={{0,2},{1,3},{2,0},{3,1},{4,6},{5,7},{6,4},{7,5},{8,10},{9,11},{10,... | collective-permute-start | bytes 445448 | tf_op jit(solution)/shard_map/ppermute | solution.py:40
  28.5 9.3 %collective-permute-start.2 = (bf16[145,512]{1,0:T(8,128)(2,1)S(1)}, bf16[145,512]{1,0:T(8,128)(2,1)S(1)}, u32[]{:S(2)}, u32[]{:S(2)}) collective-permute-start(bf16[145,512]{1,0:T(8,128)(2,1)S(1)} %get-tuple-element.74), channel_id=1, source_target_pairs={{0,3},{1,0},{2,1},{3,2},{4,7},{5,4},{6,5},{7,6},{8,11},{9,8},{10,9... | collective-permute-start | bytes 445448 | tf_op jit(solution)/shard_map/ppermute | solution.py:40
  33.4 19.9 %collective-permute-start.14 = (bf16[3,16,3072]{2,1,0:T(8,128)(2,1)S(1)}, bf16[3,16,3072]{2,1,0:T(8,128)(2,1)S(1)}, u32[]{:S(2)}, u32[]{:S(2)}) collective-permute-start(bf16[3,16,3072]{2,1,0:T(8,128)(2,1)S(1)} %pad_maximum_fusion.1.rest_0_), channel_id=1, source_target_pairs={{0,24},{4,28},{8,16},{12,20},{16,8},{20,12},{24,0},{28,4},{1,25},{... | collective-permute-start | bytes 884744 | tf_op jit(solution)/shard_map/ppermute | solution.py:45
  37.8 16.1 %collective-permute-start.12 = (bf16[3,16,3072]{2,1,0:T(8,128)(2,1)S(1)}, bf16[3,16,3072]{2,1,0:T(8,128)(2,1)}, u32[]{:S(2)}, u32[]{:S(2)}) collective-permute-start(bf16[3,16,3072]{2,1,0:T(8,128)(2,1)S(1)} %pad_maximum_fusion.1.rest_0_), channel_id=1, source_target_pairs={{0,16},{4,20},{8,24},{12,28},{16,0},{20,4},{24,8},{28,12},{1,17},{... | collective-permute-start | bytes 884744 | tf_op jit(solution)/shard_map/ppermute | solution.py:45
  39.3 16.9 %slice-start = ((f32[8004]{0:T(1024)}), f32[324]{0:T(512)S(1)}, s32[]{:S(2)}) async-start(f32[8004]{0:T(1024)} %param.29), calls=%async_computation | async-start | bytes 4096 | tf_op jit(solution)/shard_map/slice | solution.py:526
  39.3 14.6 %collective-permute-start.10 = (bf16[3,16,3072]{2,1,0:T(8,128)(2,1)S(1)}, bf16[3,16,3072]{2,1,0:T(8,128)(2,1)}, u32[]{:S(2)}, u32[]{:S(2)}) collective-permute-start(bf16[3,16,3072]{2,1,0:T(8,128)(2,1)S(1)} %pad_maximum_fusion.1.rest_0_), channel_id=1, source_target_pairs={{0,8},{4,12},{8,0},{12,4},{16,24},{20,28},{24,16},{28,20},{1,9},{5... | collective-permute-start | bytes 884744 | tf_op jit(solution)/shard_map/ppermute | solution.py:45
  40.9 12.4 %collective-permute-start.21 = (bf16[3,64,512]{2,1,0:T(8,128)(2,1)S(1)}, bf16[3,64,512]{2,1,0:T(8,128)(2,1)S(1)}, u32[]{:S(2)}, u32[]{:S(2)}) collective-permute-start(bf16[3,64,512]{2,1,0:T(8,128)(2,1)S(1)} %pad_maximum_fusion.2.rest_0_), channel_id=1, source_target_pairs={{0,24},{4,28},{8,16},{12,20},{16,8},{20,12},{24,0},{28,4},{1,25},{... | collective-permute-start | bytes 589832 | tf_op jit(solution)/shard_map/ppermute | solution.py:45
  45.2 12.2 %collective-permute-start.19 = (bf16[3,64,512]{2,1,0:T(8,128)(2,1)S(1)}, bf16[3,64,512]{2,1,0:T(8,128)(2,1)S(1)}, u32[]{:S(2)}, u32[]{:S(2)}) collective-permute-start(bf16[3,64,512]{2,1,0:T(8,128)(2,1)S(1)} %pad_maximum_fusion.2.rest_0_), channel_id=1, source_target_pairs={{0,16},{4,20},{8,24},{12,28},{16,0},{20,4},{24,8},{28,12},{1,17},{... | collective-permute-start | bytes 589832 | tf_op jit(solution)/shard_map/ppermute | solution.py:45
  53.3 10.8 %collective-permute-start.9 = (bf16[3,16,3072]{2,1,0:T(8,128)(2,1)S(1)}, bf16[3,16,3072]{2,1,0:T(8,128)(2,1)S(1)}, u32[]{:S(2)}, u32[]{:S(2)}) collective-permute-start(bf16[3,16,3072]{2,1,0:T(8,128)(2,1)S(1)} %pad_maximum_fusion.1.rest_0_), channel_id=1, source_target_pairs={{0,4},{4,0},{8,12},{12,8},{16,20},{20,16},{24,28},{28,24},{1,5},{5... | collective-permute-start | bytes 884744 | tf_op jit(solution)/shard_map/ppermute | solution.py:45
  53.3 11.3 %collective-permute-start.15 = (bf16[3,16,3072]{2,1,0:T(8,128)(2,1)S(1)}, bf16[3,16,3072]{2,1,0:T(8,128)(2,1)S(1)}, u32[]{:S(2)}, u32[]{:S(2)}) collective-permute-start(bf16[3,16,3072]{2,1,0:T(8,128)(2,1)S(1)} %collective-permute-done.14.rest_6_), channel_id=1, source_target_pairs={{0,4},{4,0},{8,12},{12,8},{16,20},{20,16},{24,28},{28,24},{1,5},{5... | collective-permute-start | bytes 884744 | tf_op jit(solution)/shard_map/ppermute | solution.py:45
  53.8 10.9 %collective-permute-start.13 = (bf16[3,16,3072]{2,1,0:T(8,128)(2,1)}, bf16[3,16,3072]{2,1,0:T(8,128)(2,1)S(1)}, u32[]{:S(2)}, u32[]{:S(2)}) collective-permute-start(bf16[3,16,3072]{2,1,0:T(8,128)(2,1)} %collective-permute-done.12.rest_4_), channel_id=1, source_target_pairs={{0,4},{4,0},{8,12},{12,8},{16,20},{20,16},{24,28},{28,24},{1,5},{5... | collective-permute-start | bytes 884744 | tf_op jit(solution)/shard_map/ppermute | solution.py:45
  53.9 13.4 %collective-permute-start.11 = (bf16[3,16,3072]{2,1,0:T(8,128)(2,1)}, bf16[3,16,3072]{2,1,0:T(8,128)(2,1)S(1)}, u32[]{:S(2)}, u32[]{:S(2)}) collective-permute-start(bf16[3,16,3072]{2,1,0:T(8,128)(2,1)} %collective-permute-done.10.rest_2_), channel_id=1, source_target_pairs={{0,4},{4,0},{8,12},{12,8},{16,20},{20,16},{24,28},{28,24},{1,5},{5... | collective-permute-start | bytes 884744 | tf_op jit(solution)/shard_map/ppermute | solution.py:45
  57.4 6.8 %collective-permute-start.17 = (bf16[3,64,512]{2,1,0:T(8,128)(2,1)S(1)}, bf16[3,64,512]{2,1,0:T(8,128)(2,1)S(1)}, u32[]{:S(2)}, u32[]{:S(2)}) collective-permute-start(bf16[3,64,512]{2,1,0:T(8,128)(2,1)S(1)} %pad_maximum_fusion.2.rest_0_), channel_id=1, source_target_pairs={{0,8},{4,12},{8,0},{12,4},{16,24},{20,28},{24,16},{28,20},{1,9},{5... | collective-permute-start | bytes 589832 | tf_op jit(solution)/shard_map/ppermute | solution.py:45
  64.2 10.4 %collective-permute-start.16 = (bf16[3,64,512]{2,1,0:T(8,128)(2,1)S(1)}, bf16[3,64,512]{2,1,0:T(8,128)(2,1)S(1)}, u32[]{:S(2)}, u32[]{:S(2)}) collective-permute-start(bf16[3,64,512]{2,1,0:T(8,128)(2,1)S(1)} %pad_maximum_fusion.2.rest_0_), channel_id=1, source_target_pairs={{0,4},{4,0},{8,12},{12,8},{16,20},{20,16},{24,28},{28,24},{1,5},{5... | collective-permute-start | bytes 589832 | tf_op jit(solution)/shard_map/ppermute | solution.py:45
  64.2 10.4 %collective-permute-start.22 = (bf16[3,64,512]{2,1,0:T(8,128)(2,1)S(1)}, bf16[3,64,512]{2,1,0:T(8,128)(2,1)S(1)}, u32[]{:S(2)}, u32[]{:S(2)}) collective-permute-start(bf16[3,64,512]{2,1,0:T(8,128)(2,1)S(1)} %collective-permute-done.21.rest_6_), channel_id=1, source_target_pairs={{0,4},{4,0},{8,12},{12,8},{16,20},{20,16},{24,28},{28,24},{1,5},{5... | collective-permute-start | bytes 589832 | tf_op jit(solution)/shard_map/ppermute | solution.py:45
  64.7 9.9 %collective-permute-start.20 = (bf16[3,64,512]{2,1,0:T(8,128)(2,1)S(1)}, bf16[3,64,512]{2,1,0:T(8,128)(2,1)S(1)}, u32[]{:S(2)}, u32[]{:S(2)}) collective-permute-start(bf16[3,64,512]{2,1,0:T(8,128)(2,1)S(1)} %collective-permute-done.19.rest_4_), channel_id=1, source_target_pairs={{0,4},{4,0},{8,12},{12,8},{16,20},{20,16},{24,28},{28,24},{1,5},{5... | collective-permute-start | bytes 589832 | tf_op jit(solution)/shard_map/ppermute | solution.py:45
  64.7 9.9 %collective-permute-start.18 = (bf16[3,64,512]{2,1,0:T(8,128)(2,1)S(1)}, bf16[3,64,512]{2,1,0:T(8,128)(2,1)S(1)}, u32[]{:S(2)}, u32[]{:S(2)}) collective-permute-start(bf16[3,64,512]{2,1,0:T(8,128)(2,1)S(1)} %collective-permute-done.17.rest_2_), channel_id=1, source_target_pairs={{0,4},{4,0},{8,12},{12,8},{16,20},{20,16},{24,28},{28,24},{1,5},{5... | collective-permute-start | bytes 589832 | tf_op jit(solution)/shard_map/ppermute | solution.py:45
  83.3 4.0 %collective-permute-start.23 = (bf16[4,448,512]{2,1,0:T(8,128)(2,1)S(1)}, bf16[4,448,512]{2,1,0:T(8,128)(2,1)S(1)}, u32[]{:S(2)}, u32[]{:S(2)}) collective-permute-start(bf16[4,448,512]{2,1,0:T(8,128)(2,1)S(1)} %get-tuple-element.98), channel_id=1, source_target_pairs={{0,4},{4,0},{8,12},{12,8},{16,20},{20,16},{24,28},{28,24},{1,5},{5... | collective-permute-start | bytes 5505032 | tf_op jit(solution)/shard_map/ppermute | solution.py:45
  86.8 5.7 %collective-permute-start.33 = (bf16[4,192,512]{2,1,0:T(8,128)(2,1)S(1)}, bf16[4,192,512]{2,1,0:T(8,128)(2,1)S(1)}, u32[]{:S(2)}, u32[]{:S(2)}) collective-permute-start(bf16[4,192,512]{2,1,0:T(8,128)(2,1)S(1)} %get-tuple-element.114), channel_id=1, source_target_pairs={{0,4},{4,0},{8,12},{12,8},{16,20},{20,16},{24,28},{28,24},{1,5},{5... | collective-permute-start | bytes 2359304 | tf_op jit(solution)/shard_map/ppermute | solution.py:45
  92.4 1.2 collective-permute-start.34
  93.8 12.3 %collective-permute-start.35 = (bf16[224,512]{1,0:T(8,128)(2,1)S(1)}, bf16[224,512]{1,0:T(8,128)(2,1)S(1)}, u32[]{:S(2)}, u32[]{:S(2)}) collective-permute-start(bf16[224,512]{1,0:T(8,128)(2,1)S(1)} %get-tuple-element.118), channel_id=1, source_target_pairs={{0,8},{4,12},{8,0},{12,4},{16,24},{20,28},{24,16},{28,20},{1,9},{5... | collective-permute-start | bytes 688136 | tf_op jit(solution)/shard_map/ppermute | solution.py:45
  95.4 10.2 %collective-permute-start.24 = (bf16[2,81,512]{2,1,0:T(8,128)(2,1)S(1)}, bf16[2,81,512]{2,1,0:T(8,128)(2,1)S(1)}, u32[]{:S(2)}, u32[]{:S(2)}) collective-permute-start(bf16[2,81,512]{2,1,0:T(8,128)(2,1)S(1)} %get-tuple-element.101), channel_id=1, source_target_pairs={{0,3},{1,0},{2,1},{3,2},{4,7},{5,4},{6,5},{7,6},{8,11},{9,8},{10,9... | collective-permute-start | bytes 497672 | tf_op jit(solution)/shard_map/ppermute | solution.py:40
  101.7 13.4 %collective-permute-start.36 = (bf16[224,512]{1,0:T(8,128)(2,1)S(1)}, bf16[224,512]{1,0:T(8,128)(2,1)S(1)}, u32[]{:S(2)}, u32[]{:S(2)}) collective-permute-start(bf16[224,512]{1,0:T(8,128)(2,1)S(1)} %get-tuple-element.119), channel_id=1, source_target_pairs={{0,16},{4,20},{8,24},{12,28},{16,0},{20,4},{24,8},{28,12},{1,17},{... | collective-permute-start | bytes 688136 | tf_op jit(solution)/shard_map/ppermute | solution.py:45
  102.2 12.8 %collective-permute-start.37 = (bf16[224,512]{1,0:T(8,128)(2,1)S(1)}, bf16[224,512]{1,0:T(8,128)(2,1)S(1)}, u32[]{:S(2)}, u32[]{:S(2)}) collective-permute-start(bf16[224,512]{1,0:T(8,128)(2,1)S(1)} %get-tuple-element.120), channel_id=1, source_target_pairs={{0,24},{4,28},{8,16},{12,20},{16,8},{20,12},{24,0},{28,4},{1,25},{... | collective-permute-start | bytes 688136 | tf_op jit(solution)/shard_map/ppermute | solution.py:45
  103.7 33.5 %collective-permute-start.27 = (bf16[448,512]{1,0:T(8,128)(2,1)}, bf16[448,512]{1,0:T(8,128)(2,1)S(1)}, u32[]{:S(2)}, u32[]{:S(2)}) collective-permute-start(bf16[448,512]{1,0:T(8,128)(2,1)} %get-tuple-element.107), channel_id=1, source_target_pairs={{0,8},{4,12},{8,0},{12,4},{16,24},{20,28},{24,16},{28,20},{1,9},{5... | collective-permute-start | bytes 1376264 | tf_op jit(solution)/shard_map/ppermute | solution.py:45
  105.5 31.7 %collective-permute-start.28 = (bf16[448,512]{1,0:T(8,128)(2,1)}, bf16[448,512]{1,0:T(8,128)(2,1)S(1)}, u32[]{:S(2)}, u32[]{:S(2)}) collective-permute-start(bf16[448,512]{1,0:T(8,128)(2,1)} %get-tuple-element.108), channel_id=1, source_target_pairs={{0,16},{4,20},{8,24},{12,28},{16,0},{20,4},{24,8},{28,12},{1,17},{... | collective-permute-start | bytes 1376264 | tf_op jit(solution)/shard_map/ppermute | solution.py:45
  106.1 31.1 %collective-permute-start.29 = (bf16[448,512]{1,0:T(8,128)(2,1)S(1)}, bf16[448,512]{1,0:T(8,128)(2,1)}, u32[]{:S(2)}, u32[]{:S(2)}) collective-permute-start(bf16[448,512]{1,0:T(8,128)(2,1)S(1)} %get-tuple-element.99.rest_0_), channel_id=1, source_target_pairs={{0,24},{4,28},{8,16},{12,20},{16,8},{20,12},{24,0},{28,4},{1,25},{... | collective-permute-start | bytes 1376264 | tf_op jit(solution)/shard_map/ppermute | solution.py:45
  115.0 9.8 %collective-permute-start.25 = (bf16[2,81,512]{2,1,0:T(8,128)(2,1)S(1)}, bf16[2,81,512]{2,1,0:T(8,128)(2,1)S(1)}, u32[]{:S(2)}, u32[]{:S(2)}) collective-permute-start(bf16[2,81,512]{2,1,0:T(8,128)(2,1)S(1)} %get-tuple-element.102), channel_id=1, source_target_pairs={{0,2},{1,3},{2,0},{3,1},{4,6},{5,7},{6,4},{7,5},{8,10},{9,11},{10,... | collective-permute-start | bytes 497672 | tf_op jit(solution)/shard_map/ppermute | solution.py:40
  115.0 9.8 %collective-permute-start.26 = (bf16[2,81,512]{2,1,0:T(8,128)(2,1)S(1)}, bf16[2,81,512]{2,1,0:T(8,128)(2,1)S(1)}, u32[]{:S(2)}, u32[]{:S(2)}) collective-permute-start(bf16[2,81,512]{2,1,0:T(8,128)(2,1)S(1)} %get-tuple-element.103), channel_id=1, source_target_pairs={{0,1},{1,2},{2,3},{3,0},{4,5},{5,6},{6,7},{7,4},{8,9},{9,10},{10,1... | collective-permute-start | bytes 497672 | tf_op jit(solution)/shard_map/ppermute | solution.py:40
  124.8 7.2 %collective-permute-start.38 = (bf16[80,512]{1,0:T(8,128)(2,1)S(1)}, bf16[80,512]{1,0:T(8,128)(2,1)S(1)}, u32[]{:S(2)}, u32[]{:S(2)}) collective-permute-start(bf16[80,512]{1,0:T(8,128)(2,1)S(1)} %get-tuple-element.123), channel_id=1, source_target_pairs={{0,1},{1,2},{2,3},{3,0},{4,5},{5,6},{6,7},{7,4},{8,9},{9,10},{10,1... | collective-permute-start | bytes 245768 | tf_op jit(solution)/shard_map/ppermute | solution.py:40
  124.8 10.2 %collective-permute-start.39 = (bf16[80,512]{1,0:T(8,128)(2,1)S(1)}, bf16[80,512]{1,0:T(8,128)(2,1)S(1)}, u32[]{:S(2)}, u32[]{:S(2)}) collective-permute-start(bf16[80,512]{1,0:T(8,128)(2,1)S(1)} %get-tuple-element.124), channel_id=1, source_target_pairs={{0,2},{1,3},{2,0},{3,1},{4,6},{5,7},{6,4},{7,5},{8,10},{9,11},{10,... | collective-permute-start | bytes 245768 | tf_op jit(solution)/shard_map/ppermute | solution.py:40
  132.0 4.4 %collective-permute-start.40 = (bf16[80,512]{1,0:T(8,128)(2,1)S(1)}, bf16[80,512]{1,0:T(8,128)(2,1)S(1)}, u32[]{:S(2)}, u32[]{:S(2)}) collective-permute-start(bf16[80,512]{1,0:T(8,128)(2,1)S(1)} %get-tuple-element.125), channel_id=1, source_target_pairs={{0,3},{1,0},{2,1},{3,2},{4,7},{5,4},{6,5},{7,6},{8,11},{9,8},{10,9... | collective-permute-start | bytes 245768 | tf_op jit(solution)/shard_map/ppermute | solution.py:40
  138.4 14.0 %collective-permute-start.30 = (bf16[112,512]{1,0:T(8,128)(2,1)S(1)}, bf16[112,512]{1,0:T(8,128)(2,1)S(1)}, u32[]{:S(2)}, u32[]{:S(2)}) collective-permute-start(bf16[112,512]{1,0:T(8,128)(2,1)S(1)} %get-tuple-element.110), channel_id=1, source_target_pairs={{0,1},{1,2},{2,3},{3,0},{4,5},{5,6},{6,7},{7,4},{8,9},{9,10},{10,1... | collective-permute-start | bytes 344072 | tf_op jit(solution)/shard_map/ppermute | solution.py:40
  139.1 13.3 %collective-permute-start.31 = (bf16[112,512]{1,0:T(8,128)(2,1)S(1)}, bf16[112,512]{1,0:T(8,128)(2,1)S(1)}, u32[]{:S(2)}, u32[]{:S(2)}) collective-permute-start(bf16[112,512]{1,0:T(8,128)(2,1)S(1)} %get-tuple-element.111), channel_id=1, source_target_pairs={{0,2},{1,3},{2,0},{3,1},{4,6},{5,7},{6,4},{7,5},{8,10},{9,11},{10,... | collective-permute-start | bytes 344072 | tf_op jit(solution)/shard_map/ppermute | solution.py:40
  140.8 11.6 %collective-permute-start.32 = (bf16[112,512]{1,0:T(8,128)(2,1)S(1)}, bf16[112,512]{1,0:T(8,128)(2,1)S(1)}, u32[]{:S(2)}, u32[]{:S(2)}) collective-permute-start(bf16[112,512]{1,0:T(8,128)(2,1)S(1)} %get-tuple-element.112), channel_id=1, source_target_pairs={{0,3},{1,0},{2,1},{3,2},{4,7},{5,4},{6,5},{7,6},{8,11},{9,8},{10,9... | collective-permute-start | bytes 344072 | tf_op jit(solution)/shard_map/ppermute | solution.py:40
  (10 other events, 34.7 us)

commit v3 on v2

--- a/solution.py
+++ b/solution.py
@@ -17,6 +17,8 @@
 CORE, XBIT, YBIT = 1, 2, 4
 LANE = 512
 STEP = 16
+ROWS = 81
+HALF = 96
 
 
 def step_rates(images, model_width, gate_width, cell_count):
@@ -72,44 +74,110 @@
     return jnp.sum(v, axis=-1, keepdims=True) * (1.0 / v.shape[-1])
 
 
+def slot_kernel(grid, scal, counts, crops, col_ref, row_ref):
+    own = scal[0]
+    lane = lax.broadcasted_iota(I32, counts.shape, 1)
+    count = jnp.sum(jnp.where(lane == own, counts[...], 0), axis=1, keepdims=True)
+    start = crops[own][:, 0:1]
+    cells = grid * grid
+    side = jnp.zeros_like(count)
+    top = jnp.zeros_like(count)
+    for k in range(1, grid + 1):
+        side = jnp.where(count == k * k, k, side)
+        top = top + jnp.where(start >= k * grid, 1, 0)
+    quarter = count >> 2
+    left = start - top * grid
+    for ref, dim in ((col_ref, 0), (row_ref, 1)):
+        place = lax.broadcasted_iota(I32, ref.shape, dim)
+        row = jnp.zeros(ref.shape, I32)
+        for k in range(1, grid):
+            row = row + jnp.where(place >= k * grid, 1, 0)
+        drow = row - top
+        dcol = place - row * grid - left
+        inside = (drow >= 0) & (drow < side) & (dcol >= 0) & (dcol < side) & (place < cells)
+        order = drow * side + dcol
+        block = jnp.zeros(ref.shape, I32)
+        for k in (1, 2, 3):
+            block = block + jnp.where(order >= k * quarter, 1, 0)
+        slot = ((own - block) & 3) * ROWS + order - block * quarter
+        ref[...] = jnp.where(inside, slot, -1)
+
+
 def onehot(slot, lanes, base):
     lane = lax.broadcasted_iota(I32, (slot.shape[0], lanes), 1) + base
     return jnp.where(slot == lane, 1.0, 0.0).astype(BF)
 
 
-def prep_kernel(scal, tok, cot, weight, mix, m1, m2, m3, tok_own, c1, c2, c3, cot_own, wo_own, mx_own):
+class Copies:
+    def __init__(self, sems):
+        self.sems, self.all = sems, []
+
+    def bring(self, src, dst):
+        copy = pltpu.make_async_copy(src, dst, self.sems.at[len(self.all)])
+        copy.start()
+        self.all.append(copy)
+
+    def wait(self):
+        for copy in self.all:
+            copy.wait()
+
+
+def prep_kernel(scal, tok, cot, w_out, mix, m1, m2, m3, tok_own, cot_own, held, strip, sems):
     own, unit = scal[0], scal[1]
-    rows = weight.shape[0] // 8
-    wo_own[...] = weight[...].astype(BF)
-    mx_own[...] = jnp.zeros_like(mx_own)
-    mx_own[0 : mix.shape[0], 0 : mix.shape[1]] = mix[...].astype(BF)
-    piece = weight[pl.ds(aligned(unit * rows, STEP), rows), :].astype(BF)
-    strip = mx_own[pl.ds(aligned(unit * STEP, STEP), STEP), :]
-    for r, (msg, out) in enumerate(((m1, c1), (m2, c2), (m3, c3)), 1):
+    rows = held.shape[0]
+    low = rows + STEP
+    count = tok.shape[1]
+    copies = Copies(sems)
+    copies.bring(w_out.at[pl.ds(aligned(unit * rows, STEP), rows), :], held)
+    strip[...] = jnp.zeros_like(strip)
+    strip[0 : mix.shape[0], 0 : mix.shape[1]] = mix[...].astype(BF)
+    copies.wait()
+    for r, msg in enumerate((m1, m2, m3), 1):
         to = lax.rem(own + r, 4)
-        msg[0:rows, :] = piece
-        msg[rows : rows + STEP, :] = strip
-        msg[rows + STEP :, :] = tok[to]
-        out[...] = cot[to]
+        msg[0:rows, :] = held[...].astype(BF)
+        msg[rows:low, :] = strip[pl.ds(aligned(unit * STEP, STEP), STEP), :]
+        msg[low : low + count, :] = tok[to]
+        msg[low + HALF : low + HALF + count, :] = cot[to]
     tok_own[...] = tok[own]
     cot_own[...] = cot[own]
 
 
-def place_kernel(slot_ref, b0, b1, b2, b3, pos_ref):
+def hold_kernel(src, tie, dst):
+    dst[...] = src[...]
+
+
+def stack_tied_kernel(m1, m2, m3, tie, out):
+    stack_kernel(m1, m2, m3, out)
+
+
+def join_kernel(p0, p1, p2, p3, tie, out):
+    for e, part in enumerate((p0, p1, p2, p3)):
+        out[e] = part[...]
+
+
+def stack_kernel(m1, m2, m3, out):
+    for r, msg in enumerate((m1, m2, m3)):
+        out[r] = msg[0 : out.shape[1], :]
+
+
+def place(slot_ref, own, others, at, pos_ref):
     slot = slot_ref[...]
-    lanes = b0.shape[0]
-    total = None
-    for r, blk in enumerate((b0, b1, b2, b3)):
-        part = dot(onehot(slot, lanes, r * lanes), blk[blk.shape[0] - lanes :, :])
-        total = part if total is None else total + part
+    lanes = own.shape[0]
+    total = dot(onehot(slot, lanes, 0), own[...])
+    for r, msg in enumerate(others, 1):
+        total = total + dot(onehot(slot, lanes, r * lanes), msg[at : at + lanes, :])
     pos_ref[...] = total.astype(BF)
 
 
+def place_kernel(at, slot_ref, own, m1, m2, m3, tie, pos_ref):
+    place(slot_ref, own, (m1, m2, m3), at, pos_ref)
+
+
 ORDER = [(c, y, x, r) for c in (0, 1) for y in (0, 1) for x in (0, 1) for r in range(4)]
 
 
-def norm_kernel(scal, slot_ref, b0, b1, b2, b3, gain, shift, pos_ref, xn_ref, xt_ref, turned):
-    place_kernel(slot_ref, b0, b1, b2, b3, pos_ref)
+def norm_kernel(at, scal, slot_ref, own_blk, m1, m2, m3, gain, shift, pos_ref, xn_ref, xt_ref, turned):
+    place(slot_ref, own_blk, (m1, m2, m3), at, pos_ref)
     own, unit = scal[0], scal[1]
 
     @each_tile(pos_ref.shape[0])
@@ -127,34 +195,23 @@
         xt_ref[k * STEP : (k + 1) * STEP, :] = turned[pl.ds(aligned(src, STEP), STEP), :]
 
 
-class Copies:
-    def __init__(self, sems):
-        self.sems, self.all = sems, []
-
-    def bring(self, src, dst):
-        copy = pltpu.make_async_copy(src, dst, self.sems.at[len(self.all)])
-        copy.start()
-        self.all.append(copy)
-
-    def wait(self):
-        for copy in self.all:
-            copy.wait()
-
-
-def gate_kernel(scal, slot_ref, xn_ref, b_in, g_two, s_two, wi_own, *rest):
+def right_kernel(scal, slot_ref, xn_ref, b_in, g_two, s_two, wi_own, *rest):
     wi, rest = rest[:8], rest[8:]
-    win, u_ref, slope_u, vhat_ref, rstd_ref, slope_v, vn_ref, pre, sems = rest
+    win, vhat_ref, rstd_ref, slope_v, vn_ref, pre, held, sems = rest
     own, unit = scal[0], scal[1]
     n, gate = vhat_ref.shape
     tiles = gate // LANE
     copies = Copies(sems)
-    copies.bring(wi_own, win.at[pl.ds(aligned(own * 128, 128), 128), :])
+    copies.bring(wi_own, held)
     for e in range(8):
         for r in (1, 2, 3):
             who = lax.rem(own + (4 - r), 4)
             at = who * 128 + (unit ^ e) * STEP
             copies.bring(wi[e].at[r - 1], win.at[pl.ds(aligned(at, STEP), STEP), :])
-    copies.wait()
+    copies.all[0].wait()
+    win[pl.ds(aligned(own * 128, 128), 128), :] = held[...].astype(BF)
+    for copy in copies.all[1:]:
+        copy.wait()
 
     xn = xn_ref[...]
     for k in range(tiles):
@@ -175,7 +232,12 @@
         vn = jnp.where(slot_ref[rows, :] >= 0, vhat * g_two[...] + s_two[...], 0.0)
         vn_ref[rows, :] = vn.astype(BF)
 
-    for k in range(tiles):
+
+def left_kernel(xn_ref, b_in, win, *rest):
+    u_ref, slope_u, pre = rest[-3:]
+    n, gate = u_ref.shape
+    xn = xn_ref[...]
+    for k in range(gate // LANE):
         cols = slice(k * LANE, (k + 1) * LANE)
         pre[:, cols] = dot(xn, win[:, cols]) + b_in[:, cols]
 
@@ -187,26 +249,31 @@
         slope_u[rows, :] = slope
 
 
-def spatial_kernel(scal, slot_ref, pos_ref, xt_ref, cot_ref, u_ref, slope_u, vn_ref, b_mix, b_out, wo_own, mx_own, *rest):
-    wo, rest = rest[:8], rest[8:]
-    out_ref, mix_ref, pre_u, sg_ref, keep, send, *rest = rest
-    wout, mixp, spat, gated, gtmp, sems = rest
+def spatial_kernel(scal, xt_ref, cot_ref, u_ref, slope_u, vn_ref, b_mix, mix_own, wo_own, *rest):
+    wo, rest = rest[:2], rest[2:]
+    mix_ref, pre_u, sg_ref, gated, wout, keep, send, *rest = rest
+    mixp, spat, gtmp, held, sems = rest
     own, unit = scal[0], scal[1]
     n, gate = u_ref.shape
     tiles = gate // LANE
     out_unit = wout.shape[0] // 32
     copies = Copies(sems)
-    copies.bring(wo_own, wout.at[pl.ds(aligned(own * 8 * out_unit, STEP), 8 * out_unit), :])
-    copies.bring(mx_own, mixp.at[pl.ds(aligned(own * 128, 128), 128), :])
+    copies.bring(wo_own, held)
     for e in range(8):
         for r in (1, 2, 3):
             who = lax.rem(own + (4 - r), 4)
             at = (who * 8 + (unit ^ e)) * out_unit
-            copies.bring(wo[e].at[r - 1, pl.ds(0, out_unit)], wout.at[pl.ds(aligned(at, STEP), out_unit), :])
+            copies.bring(wo[e % 2].at[e // 2, r - 1, pl.ds(0, out_unit)], wout.at[pl.ds(aligned(at, STEP), out_unit), :])
             at = who * 128 + (unit ^ e) * STEP
-            copies.bring(wo[e].at[r - 1, pl.ds(out_unit, STEP)], mixp.at[pl.ds(aligned(at, STEP), STEP), :])
-    copies.wait()
-    per = 81
+            copies.bring(wo[e % 2].at[e // 2, r - 1, pl.ds(out_unit, STEP)], mixp.at[pl.ds(aligned(at, STEP), STEP), :])
+    per, cells = mix_own.shape
+    mine = aligned(own * 128, 128)
+    mixp[pl.ds(mine, 128), :] = jnp.zeros((128, LANE), BF)
+    mixp[pl.ds(mine, per), 0:cells] = mix_own[...].astype(BF)
+    copies.all[0].wait()
+    wout[pl.ds(aligned(own * 8 * out_unit, STEP), 8 * out_unit), :] = held[...].astype(BF)
+    for copy in copies.all[1:]:
+        copy.wait()
     cell = lax.broadcasted_iota(I32, (n, mixp.shape[0]), 0)
     lane = lax.broadcasted_iota(I32, (n, mixp.shape[0]), 1)
     part = jnp.where(cell >= per, 1, 0) + jnp.where(cell >= 2 * per, 1, 0) + jnp.where(cell >= 3 * per, 1, 0)
@@ -256,9 +323,6 @@
         for j, (c, y, x, r) in enumerate(ORDER):
             to = r * height + low + k * STEP
             (send if c else keep)[x + 2 * y, to : to + STEP, :] = part[j * STEP : (j + 1) * STEP, :]
-    branch = dot(gated[...], wout[...]) + b_out[...]
-    live = slot_ref[...] >= 0
-    out_ref[...] = jnp.where(live, pos_ref[...].astype(F32) + branch, 0.0).astype(BF)
 
 
 def back_kernel(slot_ref, xt_ref, mix_ref, sg_ref, vhat_ref, rstd_ref, slope_v, g_two, pre_v, keep, send, rows_ref, vng, gain, shift):
@@ -293,8 +357,8 @@
         rows_ref[tiles + k : tiles + k + 1, :] = jnp.sum(shift[:, cols], 0, keepdims=True)
 
 
-def token_kernel(slot_ref, slot_row, pos_ref, cot_ref, win, pre_u, pre_v, sg_ref, out_ref, g_one, rows_ref, *rest):
-    _, o0, o1, o2, o3, vec, xg, in_ref, gain, shift = rest
+def token_kernel(slot_ref, slot_row, pos_ref, cot_ref, win, pre_u, pre_v, sg_ref, gated, wout, g_one, b_out, rows_ref, *rest):
+    _, h0, h1, h2, h3, vec, xg, out_ref, in_ref, gain, shift = rest
     n, gate = pre_u.shape
     xg[...] = dot(pre_u[...], win[:, :gate], 1, 1) + dot(pre_v[...], win[:, gate:], 1, 1)
     gain[...] = jnp.zeros_like(gain)
@@ -316,12 +380,13 @@
         total = cot_ref[rows, :].astype(F32) + x_grad
         in_ref[rows, :] = jnp.where(slot_ref[rows, :] >= 0, total, 0.0).astype(BF)
 
-    count = o0.shape[1]
-    for r, dst in enumerate((o0, o1, o2, o3)):
-        spot = lax.broadcasted_iota(I32, (count, n), 0) + r * count
+    branch = dot(gated[...], wout[...]) + b_out[...]
+    out_ref[...] = jnp.where(slot_ref[...] >= 0, pos_ref[...].astype(F32) + branch, 0.0).astype(BF)
+    for r, dst in enumerate((h0, h1, h2, h3)):
+        spot = lax.broadcasted_iota(I32, (ROWS, n), 0) + r * ROWS
         pick = jnp.where(slot_row[...] == spot, 1.0, 0.0).astype(BF)
-        dst[0] = dot(pick, out_ref[...]).astype(BF)
-        dst[1] = dot(pick, in_ref[...]).astype(BF)
+        dst[0:ROWS, :] = dot(pick, out_ref[...]).astype(BF)
+        dst[HALF : HALF + ROWS, :] = dot(pick, in_ref[...]).astype(BF)
 
     ones = jnp.ones((8, n), BF)
     tiles = gate // LANE
@@ -334,9 +399,12 @@
     at = 2 + 2 * tiles
     vec[at : at + 2 * tiles, :] = rows_ref[...]
     at += 2 * tiles
-    vec[at : at + 1, :] = dot(ones, cot_ref[...])[0:1]
-    vec[at + 1 : at + 2, :] = jnp.zeros((1, LANE), F32)
-    vec[at + 1 : at + 2, 0:n] = dot(jnp.ones((8, gate), BF), sg_ref[...], 1, 1)[0:1]
+    cells = 4 * ROWS
+    lane = lax.broadcasted_iota(I32, (1, LANE), 1)
+    last = pltpu.roll(dot(ones, cot_ref[...])[0:1], cells, 1)
+    vec[at : at + 1, 0:n] = dot(jnp.ones((8, gate), BF), sg_ref[...], 1, 1)[0:1]
+    vec[at : at + 1, :] = jnp.where(lane < cells, vec[at : at + 1, :], last)
+    vec[at + 1 : at + 2, :] = jnp.where(lane < cells, last, 0.0)
 
 
 def split_low(v):
@@ -359,7 +427,7 @@
         dst[...] = (keep[e].astype(F32) + got[e].astype(F32)).astype(dst.dtype)
 
 
-def core_vec_kernel(keep, got, vec, vec_got, own, s1, s2, s3, vec_own):
+def core_vec_kernel(keep, got, vec, vec_got, tie, own, s1, s2, s3, vec_own):
     rows = own.shape[0]
     total = vec[...] + vec_got[...]
     put_vec(vec_own, 0, total)
@@ -377,7 +445,7 @@
         dst[...] = total.astype(dst.dtype)
 
 
-def plane_vec_kernel(own, vec_own, g1, g2, g3, z0, z1, z2, z3, vec_out):
+def plane_vec_kernel(own, vec_own, g1, g2, g3, tie, z0, z1, z2, z3, vec_out):
     rows, at = z0.shape[0], own.shape[0]
     vec = (get_vec(vec_own, 0) + get_vec(g1, at)) + (get_vec(g2, at) + get_vec(g3, at))
     put_vec(vec_out, 0, vec)
@@ -397,7 +465,7 @@
     out[...] = total.astype(out.dtype)
 
 
-def patch_vec_kernel(scal, own, vec_own, g1, g2, g3, out, vec_out, held):
+def patch_vec_kernel(scal, own, vec_own, g1, g2, g3, tie, tie_home, out, vec_out, held):
     patch_kernel(own, g1, g2, g3, out)
     rows = own.shape[0]
     me = scal[0]
@@ -407,12 +475,54 @@
     vec_out[...] = (held[0] + held[1]) + (held[2] + held[3])
 
 
-def home_kernel(scal, h0, h1, h2, h3, out_ref, grad_ref):
-    own = scal[0]
+def home_kernel(scal, h0, h1, h2, h3, out_ref, grad_ref, held):
     for r, h in enumerate((h0, h1, h2, h3)):
-        m = lax.rem(own + r, 4)
-        out_ref[m] = h[0]
-        grad_ref[m] = h[1].astype(F32)
+        m = lax.rem(scal[0] + r, 4)
+        held[m] = h[0:ROWS, :]
+        grad_ref[m, :, 0, :] = h[HALF : HALF + ROWS, :].astype(F32)
+    for m in range(4):
+        out_ref[:, m, :] = held[m]
+
+
+def update_kernel(rates, first, second, *rest):
+    olds, rest = rest[:9], rest[9:]
+    news, rest = rest[:9], rest[9:]
+    made, sems = rest[:9], rest[9]
+    copies = Copies(sems)
+    out_unit = olds[3].shape[0] // 8
+    low = out_unit + STEP
+
+    def step(which, rows, cols, grads):
+        old, new = olds[3 * which : 3 * which + 3], made[3 * which : 3 * which + 3]
+        at = (slice(*rows), slice(*cols))
+        fresh = nesterov(old[0][at], grads.astype(F32), old[1][at], old[2][at], rates[which])
+        for ref, value in zip(new, fresh):
+            ref[at] = value
+
+    def send(which):
+        for j in range(3 * which, 3 * which + 3):
+            copies.bring(made[j], news[j])
+
+    width = olds[3].shape[1]
+    for u in range(8):
+        step(1, (u * out_unit, (u + 1) * out_unit), (0, width), first[u, 0:out_unit, :])
+    send(1)
+    mix_rows, cells = olds[6].shape
+    for u in range(-(-mix_rows // STEP)):
+        rows = min(STEP, mix_rows - u * STEP)
+        step(2, (u * STEP, u * STEP + rows), (0, cells), first[u, out_unit : out_unit + rows, 0:cells])
+    send(2)
+    tiles = olds[0].shape[1] // LANE
+    for u in range(8):
+        for k in range(tiles):
+            if k < tiles // 2:
+                grads = first[u, low + k * STEP : low + (k + 1) * STEP, :]
+            else:
+                j = k - tiles // 2
+                grads = second[u, j * STEP : (j + 1) * STEP, :]
+            step(0, (u * STEP, (u + 1) * STEP), (k * LANE, (k + 1) * LANE), grads)
+    send(0)
+    copies.wait()
 
 
 VM = pl.BlockSpec(memory_space=pltpu.VMEM)
@@ -420,13 +530,13 @@
 ANY = pl.BlockSpec(memory_space=pl.ANY)
 
 
-def call(body, ins, outs, scratch=(), specs=None, flops=100_000_000, limit=16, name=None):
+def call(body, ins, outs, scratch=(), specs=None, out_specs=None, flops=100_000_000, limit=16, name=None):
     moved = sum(math.prod(a.shape) * a.dtype.itemsize for a in ins)
     return pl.pallas_call(
         body,
         out_shape=[jax.ShapeDtypeStruct(s, d) for s, d in outs],
         in_specs=specs or [VM] * len(ins),
-        out_specs=[VM] * len(outs),
+        out_specs=out_specs or [VM] * len(outs),
         scratch_shapes=list(scratch),
         compiler_params=pltpu.CompilerParams(vmem_limit_bytes=limit * 2**20),
         cost_estimate=pl.CostEstimate(flops=flops, bytes_accessed=moved, transcendentals=0),
@@ -490,34 +600,39 @@
         return found
 
     wi_piece = lax.dynamic_slice_in_dim(in_weight, unit * in_unit, in_unit, 0).astype(BF)
-    wi = over_plane(jnp.stack([turn(wi_piece, r) for r in (1, 2, 3)]))
-    wi_own = in_weight.astype(BF)
 
     blk = ((row_count, width), BF)
-    msg = ((low + row_count, width), BF)
-    m1, m2, m3, tok_own, c1, c2, c3, cot_own, wo_own, mx_own = call(
+    msg = ((low + HALF + row_count, width), BF)
+    m1, m2, m3, tok_own, cot_own = call(
         prep_kernel,
         [scal, tokens.reshape(4, row_count, width), cotangent.reshape(4, row_count, width), out_weight, spatial_weight],
-        [msg, msg, msg, blk, blk, blk, blk, blk, (out_weight.shape, BF), ((128, LANE), BF)],
-        specs=[SM] + [VM] * 4,
+        [msg, msg, msg, blk, blk],
+        [pltpu.VMEM((out_unit, width), F32), pltpu.VMEM((128, LANE), BF), pltpu.SemaphoreType.DMA((1,))],
+        specs=[SM, VM, VM, ANY, VM],
+        limit=8,
         name="prep",
     )
+    (base_in,) = call(
+        stack_tied_kernel,
+        [turn(wi_piece, r) for r in (1, 2, 3)] + [m1],
+        [((3, in_unit, hidden), BF)],
+        specs=[VM] * 3 + [ANY],
+        limit=8,
+        name="stack_i",
+    )
+    wi = over_plane(base_in)
     got = [turn(m, r) for r, m in enumerate((m1, m2, m3), 1)]
-    cot = [cot_own] + [turn(c, r) for r, c in enumerate((c1, c2, c3), 1)]
-    wo = over_plane(jnp.stack([g[:low] for g in got]))
-
-    count = lax.dynamic_index_in_dim(patch_count, p, 0, keepdims=False)[0]
-    start = lax.dynamic_index_in_dim(crop_index, p, 0, keepdims=False)[0, 0]
-    quarter = count // 4
-    side = jnp.round(jnp.sqrt(count.astype(F32))).astype(I32)
-    place = jnp.arange(n, dtype=I32)
-    drow = place // grid - start // grid
-    dcol = place % grid - start % grid
-    inside = (drow >= 0) & (drow < side) & (dcol >= 0) & (dcol < side) & (place < cells)
-    order = drow * side + dcol
-    block = (order >= quarter).astype(I32) + (order >= 2 * quarter).astype(I32) + (order >= 3 * quarter).astype(I32)
-    slot = jnp.where(inside, ((p - block) % 4) * row_count + order - block * quarter, -1)
-    slot_col, slot_row = slot[:, None], slot[None, :]
+    (base,) = call(stack_tied_kernel, [*got, wi[2]], [((3, low, LANE), BF)], specs=[VM] * 3 + [ANY], limit=8, name="stack_o")
+    plane_out = [base] + [swap(base, m) for m in (2, 4, 6)]
+
+    slot_col, slot_row = call(
+        functools.partial(slot_kernel, grid),
+        [scal, patch_count.reshape(1, 4), crop_index],
+        [((n, 1), I32), ((1, n), I32)],
+        specs=[SM, VM, VM],
+        limit=8,
+        name="slots",
+    )
 
     bounds = [width, width, hidden, gate, gate, cells, width]
     pieces = []
@@ -529,39 +644,57 @@
     b_mix = jnp.pad(b_mix[0], (0, n - cells))[:, None]
 
     pos, xn, xt = call(
-        norm_kernel,
+        functools.partial(norm_kernel, low),
         [scal, slot_col, tok_own, *got, g_one, s_one],
         [((n, width), BF), ((n, width), BF), ((width, n), BF)],
         [pltpu.VMEM((width, n), BF)],
         specs=[SM] + [VM] * 7,
         name="norm_in",
     )
-    (cot_pos,) = call(place_kernel, [slot_col, *cot], [((n, width), BF)], name="place_cot")
     sized = lambda kind: ((n, gate), kind)
-    win, u, slope_u, vhat, rstd, slope_v, vn = call(
-        gate_kernel,
-        [scal, slot_col, xn, b_in, g_two, s_two, wi_own, *wi],
-        [((width, hidden), BF), sized(F32), sized(F32), sized(F32), ((n, 1), F32), sized(F32), sized(BF)],
-        [pltpu.VMEM((n, gate), F32), pltpu.SemaphoreType.DMA((25,))],
+    win, vhat, rstd, slope_v, vn = call(
+        right_kernel,
+        [scal, slot_col, xn, b_in, g_two, s_two, in_weight, *wi],
+        [((width, hidden), BF), sized(F32), ((n, 1), F32), sized(F32), sized(BF)],
+        [pltpu.VMEM((n, gate), F32), pltpu.VMEM(in_weight.shape, F32), pltpu.SemaphoreType.DMA((25,))],
         specs=[SM] + [VM] * 5 + [ANY] * 9,
-        flops=2_000_000_000,
-        limit=24,
-        name="gate",
+        flops=1_500_000_000,
+        limit=20,
+        name="right",
+    )
+    (joined,) = call(
+        join_kernel, [*plane_out, vn], [((4, 3, low, LANE), BF)], specs=[VM] * 4 + [ANY], limit=8, name="join"
+    )
+    (cot_pos,) = call(
+        functools.partial(place_kernel, low + HALF),
+        [slot_col, cot_own, *got, joined],
+        [((n, width), BF)],
+        specs=[VM] * 5 + [ANY],
+        name="place_cot",
+    )
+    u, slope_u = call(
+        left_kernel,
+        [xn, b_in, win, cot_pos],
+        [sized(F32), sized(F32)],
+        [pltpu.VMEM((n, gate), F32)],
+        specs=[VM] * 3 + [ANY],
+        flops=1_000_000_000,
+        limit=16,
+        name="left",
     )
     packed = ((4, 4 * (low + side_rows), LANE), BF)
-    out_pos, mix, pre_u, sg, keep_a, send_a = call(
+    mix, pre_u, sg, gated, wout, keep_a, send_a = call(
         spatial_kernel,
-        [scal, slot_col, pos, xt, cot_pos, u, slope_u, vn, b_mix, b_out, wo_own, mx_own, *wo],
-        [((n, width), BF), ((n, n), BF), sized(BF), sized(BF), packed, packed],
+        [scal, xt, cot_pos, u, slope_u, vn, b_mix, spatial_weight, out_weight, joined, swap(joined, CORE)],
+        [((n, n), BF), sized(BF), sized(BF), sized(BF), ((gate, width), BF), packed, packed],
         [
-            pltpu.VMEM((gate, width), BF),
             pltpu.VMEM((512, LANE), BF),
             pltpu.VMEM((n, gate), F32),
-            pltpu.VMEM((n, gate), BF),
             pltpu.VMEM((gate, width), BF),
+            pltpu.VMEM(out_weight.shape, F32),
             pltpu.SemaphoreType.DMA((50,)),
         ],
-        specs=[SM] + [VM] * 9 + [ANY] * 10,
+        specs=[SM] + [VM] * 7 + [ANY] * 3,
         flops=4_000_000_000,
         limit=24,
         name="spatial",
@@ -583,18 +716,18 @@
         core_kernel, [keep_a, core_a], [((rows_a, LANE), F32)] + [((rows_a, LANE), BF)] * 3, limit=12, name="core_a"
     )
     plane_a = [swap(s, m) for s, m in zip(send_a, (2, 4, 6))]
-    pair = ((2, row_count, width), BF)
-    h0, h1, h2, h3, vec = call(
+    *home, vec = call(
         token_kernel,
-        [slot_col, slot_row, pos, cot_pos, win, pre_u, pre_v, sg, out_pos, g_one, rows_b, send_a[2]],
-        [pair, pair, pair, pair, ((STEP, LANE), F32)],
+        [slot_col, slot_row, pos, cot_pos, win, pre_u, pre_v, sg, gated, wout, g_one, b_out, rows_b, send_a[2]],
+        [((HALF + row_count, width), BF)] * 4 + [((STEP, LANE), F32)],
         [
             pltpu.VMEM((n, width), F32),
+            pltpu.VMEM((n, width), BF),
             pltpu.VMEM((n, width), BF),
             pltpu.VMEM((8, width), F32),
             pltpu.VMEM((8, width), F32),
         ],
-        specs=[VM] * 11 + [ANY],
+        specs=[VM] * 13 + [ANY],
         flops=2_000_000_000,
         limit=20,
         name="token_grad",
@@ -602,17 +735,20 @@
     vec_got = swap(vec, CORE)
     own_b, *send_b, vec_own = call(
         core_vec_kernel,
-        [keep_b, core_b, vec, vec_got],
+        [keep_b, core_b, vec, vec_got, send_a[0]],
         [((rows_b4, LANE), F32)] + [((rows_b4 + 2 * STEP, LANE), BF)] * 3 + [((2 * STEP, LANE), BF)],
+        specs=[VM] * 4 + [ANY],
         name="core_b",
     )
     plane_b = [swap(s, m) for s, m in zip(send_b, (2, 4, 6))]
-    home = [h0] + [turn(h, -r) for r, h in enumerate((h1, h2, h3), 1)]
+    home = [home[0]] + [turn(h, -r) for r, h in enumerate(home[1:], 1)]
     out_tokens, in_grad = call(
         home_kernel,
         [scal, *home],
-        [((4, row_count, width), BF), ((4, row_count, width), F32)],
+        [((row_count, 4, width), BF), ((4, row_count, 1, width), F32)],
+        [pltpu.VMEM((4, row_count, width), BF)],
         specs=[SM] + [VM] * 4,
+        limit=8,
         name="home",
     )
     z_rows = low + side_rows
@@ -622,44 +758,44 @@
     got_a = [turn(z, r) for r, z in enumerate(patch_a, 1)]
     own_b, *patch_b, vec_own = call(
         plane_vec_kernel,
-        [own_b, vec_own, *plane_b],
+        [own_b, vec_own, *plane_b, patch_a[0]],
         [((side_rows, LANE), F32)] + [((side_rows + 2 * STEP, LANE), BF)] * 3 + [((2 * STEP, LANE), BF)],
+        specs=[VM] * 5 + [ANY],
         name="plane_b",
     )
     got_b = [turn(z, r) for r, z in enumerate(patch_b, 1)]
     kind = BF if lax.axis_size("img") == 8 else F32
     (first,) = call(patch_kernel, [own_a, *got_a], [((z_rows, LANE), kind)], name="patch_a")
+    first = img_gather(rest_of_img(first).astype(BF))
     second, vec_sum = call(
         patch_vec_kernel,
-        [scal, own_b, vec_own, *got_b],
+        [scal, own_b, vec_own, *got_b, first, in_grad],
         [((side_rows, LANE), kind), ((STEP, LANE), F32)],
         [pltpu.VMEM((4, STEP, LANE), F32)],
-        specs=[SM] + [VM] * 5,
+        specs=[SM] + [VM] * 5 + [ANY] * 2,
         name="patch_b",
     )
-    first = img_gather(rest_of_img(first).astype(BF))
     second = img_gather(rest_of_img(second).astype(BF))
     vec_sum = rest_of_img(vec_sum).reshape(STEP * LANE)
 
-    def unpack(arr):
-        arr = arr.reshape(8, gate // LANE, in_unit, LANE).transpose(0, 2, 1, 3)
-        return arr.reshape(8 * in_unit, gate)
-
-    out_share = first[:, :out_unit].reshape(8 * out_unit, width).astype(F32)
-    mix_share = first[:, out_unit:low].reshape(128, LANE)[:mix_rows, :cells].astype(F32)
-    in_share = jnp.concatenate([unpack(first[:, low:]), unpack(second)], axis=1).astype(F32)
-    head_len = 2 * width + hidden + 2 * gate
-    vec_sum = jnp.concatenate(
-        [vec_sum[:head_len], vec_sum[head_len + width : head_len + width + cells], vec_sum[head_len : head_len + width]]
-    )
+    vec_sum = vec_sum[: vectors.shape[0]]
 
     images = micro_count * slot_count * lax.axis_size("img")
     rate_in, rate_out, rate_mix, rate_vec = step_rates(images, width, gate, cells)
-    in_new = nesterov(in_weight, in_share, in_moment, in_average, rate_in)
-    out_new = nesterov(out_weight, out_share, out_moment, out_average, rate_out)
-    mix_new = nesterov(spatial_weight, mix_share, spatial_moment, spatial_average, rate_mix)
+    olds = [in_weight, in_moment, in_average, out_weight, out_moment, out_average]
+    olds += [spatial_weight, spatial_moment, spatial_average]
+    news = call(
+        functools.partial(update_kernel, (rate_in, rate_out, rate_mix)),
+        [first, second, *olds],
+        [(a.shape, F32) for a in olds],
+        [pltpu.VMEM(a.shape, F32) for a in olds] + [pltpu.SemaphoreType.DMA((9,))],
+        specs=[VM] * 11,
+        out_specs=[ANY] * 9,
+        limit=20,
+        name="update",
+    )
     vec_new = nesterov(vectors, vec_sum, vector_moment, vector_average, rate_vec)
-    return (out_tokens.reshape(tokens.shape), in_grad.reshape(tokens.shape), *in_new, *out_new, *mix_new, *vec_new)
+    return (out_tokens.transpose(1, 0, 2).reshape(tokens.shape), in_grad.transpose(0, 2, 1, 3), *news, *vec_new)
 
 
 def solution(mesh):

time: 171 us -> 139 us (0.81)
  waiting for transfers between devices: 53.8 us -> 39.6 us
  other arithmetic: 7.76 us -> 0.72 us
  starting transfers between devices: 43.8 us -> 37.5 us
  between operations: 6.42 us -> 1.22 us
  local copies, waits for them, and re-layouts: 8.99 us -> 3.91 us
  Pallas kernels: 30.4 us -> 34.6 us
    ppermute x23 -> x20, waiting for transfers between devices: 18.3 us -> 10.3 us  [swap(): return lax.ppermute(arr, 'img', [(k, k ^ mask) for k in range(n)])]
    ppermute x18 -> x15, waiting for transfers between devices: 35.5 us -> 29.3 us  [turn(): return lax.ppermute(arr, 'patch', [(s, (s + r) % n) for s in range(n)])]
    add x4 -> x1, other arithmetic: 5.81 us -> 0.65 us  [nesterov(): average_new = AVG_DECAY * average + (1.0 - AVG_DECAY) * weight_new]
    ppermute x23 -> x20, starting transfers between devices: 19 us -> 14 us  [swap(): return lax.ppermute(arr, 'img', [(k, k ^ mask) for k in range(n)])]
    pallas_call x14 -> x20, Pallas kernels: 30.4 us -> 34.6 us  [call(): pl.pallas_call(body, out_shape=[jax.ShapeDtypeStruct(s, d) for s, d in ou...]
    unnamed x37 -> x33, local copies, waits for them, and re-layouts: 4.62 us -> 0.99 us
    ppermute x18 -> x15, starting transfers between devices: 24.9 us -> 23.6 us  [turn(): return lax.ppermute(arr, 'patch', [(s, (s + r) % n) for s in range(n)])]
  transfers between devices with their start and end apart: 41 -> 35, of which waited for: 13 -> 10; matrix products, arithmetic and copies ran while one was open for 5% -> 1% of each run, Pallas kernels for 12% -> 17%
where the time goes in v3:
time: 139 us; the launch traced here: 137 us
  waiting for transfers between devices  39.6 us (28%)
  starting transfers between devices  37.5 us (27%)
  Pallas kernels  34.6 us (25%)
  blocking collectives  19.5 us (14%)
  local copies, waits for them, and re-layouts  3.91 us (3%)
    pallas_call x20, Pallas kernels, call(): pl.pallas_call(body, out_shape=[jax.ShapeDtypeStruct(s, d) for s, d in ou...  34.6 us
    ppermute x15, waiting for transfers between devices, turn(): return lax.ppermute(arr, 'patch', [(s, (s + r) % n) for s in range(n)])  29.3 us
    ppermute x15, starting transfers between devices, turn(): return lax.ppermute(arr, 'patch', [(s, (s + r) % n) for s in range(n)])  23.6 us
    all_gather x2, blocking collectives, img_gather(): return lax.all_gather(arr, 'img', axis_index_groups=groups)  19.5 us
    ppermute x20, starting transfers between devices, swap(): return lax.ppermute(arr, 'img', [(k, k ^ mask) for k in range(n)])  14 us
    ppermute x20, waiting for transfers between devices, swap(): return lax.ppermute(arr, 'img', [(k, k ^ mask) for k in range(n)])  10.3 us
  transfers between devices with their start and end apart: 35, of which 10 were waited for; matrix products, arithmetic and copies ran while one was open for 1% of the time, Pallas kernels for 17%

profile of v3, /device:TPU:0, one launch (start us, length us, event | category | flops | bytes accessed | tf_op | source)
XLA Modules:
  0.0 137.1 jit_solution(11537226170988369263)
XLA Ops:
  0.7 1.0 dynamic-slice_convert_fusion
  1.7 5.1 %collective-permute-start.5 = (bf16[16,3072]{1,0:T(8,128)(2,1)S(1)}, bf16[16,3072]{1,0:T(8,128)(2,1)S(1)}, u32[]{:S(2)}, u32[]{:S(2)}) collective-permute-start(bf16[16,3072]{1,0:T(8,128)(2,1)S(1)} %dynamic-slice_convert_fusion), channel_id=1, source_target_pairs={{0,3},{1,0},{2,1},{3,2},{4,7},{5,4},{6,5},{7,6},{8,11},{9,8},{10,9... | collective-permute-start | bytes 294920 | tf_op jit(solution)/shard_map/ppermute | solution.py:42
  6.8 1.0 collective-permute-start.3
  7.8 1.2 copy_bitcast_fusion
  9.1 0.9 copy-done.7
  10.0 0.8 prep.1
  10.8 4.7 %collective-permute-done.4.m2 = bf16[16,3072]{1,0:T(8,128)(2,1)S(1)} collective-permute-done((bf16[16,3072]{1,0:T(8,128)(2,1)S(1)}, bf16[16,3072]{1,0:T(8,128)(2,1)S(1)}, u32[]{:S(2)}, u32[]{:S(2)}) %collective-permute-start.4) | collective-permute-done | bytes 98336 | tf_op jit(solution)/shard_map/ppermute | solution.py:42
  15.6 2.5 %collective-permute-start.14 = (bf16[3,16,3072]{2,1,0:T(8,128)(2,1)S(1)}, bf16[3,16,3072]{2,1,0:T(8,128)(2,1)S(1)}, u32[]{:S(2)}, u32[]{:S(2)}) collective-permute-start(bf16[3,16,3072]{2,1,0:T(8,128)(2,1)S(1)} %stack_i.1.rest_0_), channel_id=1, source_target_pairs={{0,24},{4,28},{8,16},{12,20},{16,8},{20,12},{24,0},{28,4},{1,25},{... | collective-permute-start | bytes 884744 | tf_op jit(solution)/shard_map/ppermute | solution.py:47
  18.1 2.3 %collective-permute-start.1 = (bf16[241,512]{1,0:T(8,128)(2,1)S(1)}, bf16[241,512]{1,0:T(8,128)(2,1)S(1)}, u32[]{:S(2)}, u32[]{:S(2)}) collective-permute-start(bf16[241,512]{1,0:T(8,128)(2,1)S(1)} %get-tuple-element.82), channel_id=1, source_target_pairs={{0,2},{1,3},{2,0},{3,1},{4,6},{5,7},{6,4},{7,5},{8,10},{9,11},{10,... | collective-permute-start | bytes 740360 | tf_op jit(solution)/shard_map/ppermute | solution.py:42
  20.9 0.5 collective-permute-start.6
  21.8 9.5 %collective-permute-done.1.m2 = bf16[241,512]{1,0:T(8,128)(2,1)S(1)} collective-permute-done((bf16[241,512]{1,0:T(8,128)(2,1)S(1)}, bf16[241,512]{1,0:T(8,128)(2,1)S(1)}, u32[]{:S(2)}, u32[]{:S(2)}) %collective-permute-start.1) | collective-permute-done | bytes 246816 | tf_op jit(solution)/shard_map/ppermute | solution.py:42
  31.9 1.0 collective-permute-done.2.m3
  32.9 4.4 %collective-permute-start = (bf16[241,512]{1,0:T(8,128)(2,1)S(1)}, bf16[241,512]{1,0:T(8,128)(2,1)S(1)}, u32[]{:S(2)}, u32[]{:S(2)}) collective-permute-start(bf16[241,512]{1,0:T(8,128)(2,1)S(1)} %get-tuple-element.81.tie), channel_id=1, source_target_pairs={{0,1},{1,2},{2,3},{3,0},{4,5},{5,6},{6,7},{7,4},{8,9},{9,10},{10,1... | collective-permute-start | bytes 740360 | tf_op jit(solution)/shard_map/ppermute | solution.py:42
  37.8 6.8 %collective-permute-done.m1 = bf16[241,512]{1,0:T(8,128)(2,1)S(1)} collective-permute-done((bf16[241,512]{1,0:T(8,128)(2,1)S(1)}, bf16[241,512]{1,0:T(8,128)(2,1)S(1)}, u32[]{:S(2)}, u32[]{:S(2)}) %collective-permute-start) | collective-permute-done | bytes 246816 | tf_op jit(solution)/shard_map/ppermute | solution.py:42
  44.6 0.5 collective-permute-start.9
  45.2 1.5 %collective-permute-start.8 = (bf16[3,64,512]{2,1,0:T(8,128)(2,1)S(1)}, bf16[3,64,512]{2,1,0:T(8,128)(2,1)S(1)}, u32[]{:S(2)}, u32[]{:S(2)}) collective-permute-start(bf16[3,64,512]{2,1,0:T(8,128)(2,1)S(1)} %stack_o.1.p0), channel_id=1, source_target_pairs={{0,16},{4,20},{8,24},{12,28},{16,0},{20,4},{24,8},{28,12},{1,17},{... | collective-permute-start | bytes 589832 | tf_op jit(solution)/shard_map/ppermute | solution.py:47
  46.7 1.5 %collective-permute-start.7 = (bf16[3,64,512]{2,1,0:T(8,128)(2,1)S(1)}, bf16[3,64,512]{2,1,0:T(8,128)(2,1)S(1)}, u32[]{:S(2)}, u32[]{:S(2)}) collective-permute-start(bf16[3,64,512]{2,1,0:T(8,128)(2,1)S(1)} %stack_o.1.p0), channel_id=1, source_target_pairs={{0,8},{4,12},{8,0},{12,4},{16,24},{20,28},{24,16},{28,20},{1,9},{5... | collective-permute-start | bytes 589832 | tf_op jit(solution)/shard_map/ppermute | solution.py:47
  48.3 0.8 slots.1
  49.1 1.9 %norm_in.1 = (bf16[336,512]{1,0:T(8,128)(2,1)S(1)}, bf16[336,512]{1,0:T(8,128)(2,1)S(1)}, bf16[512,336]{1,0:T(8,128)(2,1)S(1)}) custom-call(s32[2]{0:T(128)S(1)} %pad_add_fusion.scal, s32[336,1]{1,0:T(8,128)S(1)} %get-tuple-element.78.slot_ref, bf16[81,512]{1,0:T(8,128)(2,1)S(1)} %get-tuple-element.80.own_blk, bf16[241,512]{1,0:T(8,128)(2,1)S(1)} %collective-permute-done.m1, ...), custom_call_target="tpu_custom_call" | custom-call | flops 100000000 | bytes 828744 | tf_op jit(solution)/shard_map/norm_in/pallas_call | solution.py:535
  51.1 6.4 %right.1 = (bf16[512,3072]{1,0:T(8,128)(2,1)S(1)}, f32[336,1536]{1,0:T(8,128)S(1)}, f32[336,1]{1,0:T(8,128)S(1)}, f32[336,1536]{1,0:T(8,128)S(1)}, bf16[336,1536]{1,0:T(8,128)(2,1)S(1)}) custom-call(s32[2]{0:T(128)S(1)} %pad_add_fusion.scal, s32[336,1]{1,0:T(8,128)S(1)} %get-tuple-element.78.slot_ref, bf16[336,512]{1,0:T(8,128)(2,1)S(1)} %get-tuple-element.86.xn_ref, ...), custom_call_target="tpu_custom_call" | custom-call | flops 1500000000 | bytes 4302152 | tf_op jit(solution)/shard_map/right/pallas_call | solution.py:535
  58.3 0.6 place_cot.1.rest_0_.cot_ref
  58.9 1.7 %left.1 = (f32[336,1536]{1,0:T(8,128)S(1)}, f32[336,1536]{1,0:T(8,128)S(1)}) custom-call(bf16[336,512]{1,0:T(8,128)(2,1)S(1)} %get-tuple-element.86.xn_ref, f32[1,3072]{1,0:T(1,128)S(1)} %bitcast.24, bf16[512,3072]{1,0:T(8,128)(2,1)S(1)} %get-tuple-element.88.win, bf16[336,512]{1,0:T(8,128)(2,1)S(1)} %place_cot.1.rest_0_.cot_ref), custom_call_target="tpu_custom_call" | custom-call | flops 1000000000 | bytes 3846144 | tf_op jit(solution)/shard_map/left/pallas_call | solution.py:535
  60.7 7.8 %spatial.1 = (bf16[336,336]{1,0:T(8,128)(2,1)S(1)}, bf16[336,1536]{1,0:T(8,128)(2,1)S(1)}, bf16[336,1536]{1,0:T(8,128)(2,1)S(1)}, bf16[336,1536]{1,0:T(8,128)(2,...) custom-call(s32[2]{0:T(128)S(1)} %pad_add_fusion.scal, ...), custom_call_target="tpu_custom_call" | custom-call | flops 4000000000 | bytes 8314712 | tf_op jit(solution)/shard_map/spatial/pallas_call | solution.py:535
  68.6 3.3 %back.1 = (bf16[336,1536]{1,0:T(8,128)(2,1)S(1)}, bf16[4,192,512]{2,1,0:T(8,128)(2,1)S(1)}, bf16[4,192,512]{2,1,0:T(8,128)(2,1)S(1)}, f32[6,512]{1,0:T(8,128)S(1)}) custom-call(s32[336,1]{1,0:T(8,128)S(1)} %get-tuple-element.78.slot_ref, bf16[512,336]{1,0:T(8,128)(2,1)S(1)} %get-tuple-element.89.xt_ref, bf16[336,336]{1,0:T(8,128)(2,1)S(1)} %get-tuple-element.93.mix_ref, ...), custom_call_target="tpu_custom_call" | custom-call | flops 2000000000 | bytes 5739648 | tf_op jit(solution)/shard_map/back/pallas_call | solution.py:535
  71.9 0.6 collective-permute-start.27
  72.9 0.6 collective-permute-start.22
  73.4 1.5 %collective-permute-start.23 = (bf16[448,512]{1,0:T(8,128)(2,1)S(1)}, bf16[448,512]{1,0:T(8,128)(2,1)S(1)}, u32[]{:S(2)}, u32[]{:S(2)}) collective-permute-start(bf16[448,512]{1,0:T(8,128)(2,1)S(1)} %get-tuple-element.104.rest_0_), channel_id=1, source_target_pairs={{0,24},{4,28},{8,16},{12,20},{16,8},{20,12},{24,0},{28,4},{1,25},{... | collective-permute-start | bytes 1376264 | tf_op jit(solution)/shard_map/ppermute | solution.py:47
  74.9 1.5 %collective-permute-start.21 = (bf16[448,512]{1,0:T(8,128)(2,1)S(1)}, bf16[448,512]{1,0:T(8,128)(2,1)S(1)}, u32[]{:S(2)}, u32[]{:S(2)}) collective-permute-start(bf16[448,512]{1,0:T(8,128)(2,1)S(1)} %get-tuple-element.112.tie), channel_id=1, source_target_pairs={{0,8},{4,12},{8,0},{12,4},{16,24},{20,28},{24,16},{28,20},{1,9},{5... | collective-permute-start | bytes 1376264 | tf_op jit(solution)/shard_map/ppermute | solution.py:47
  76.4 4.5 %token_grad.1 = (bf16[177,512]{1,0:T(8,128)(2,1)S(1)}, bf16[177,512]{1,0:T(8,128)(2,1)S(1)}, bf16[177,512]{1,0:T(8,128)(2,1)S(1)}, bf16[177,512]{1,0:T(8,128)(2,1)S(1)}, f32[16,512]{1,0:T(8,128)S(1)}) custom-call(s32[336,1]{1,0:T(8,128)S(1)} %get-tuple-element.78.slot_ref, s32[1,336]{1,0:T(1,128)S(1)} %get-tuple-element.79.slot_row, ...), custom_call_target="tpu_custom_call" | custom-call | flops 2000000000 | bytes 10013312 | tf_op jit(solution)/shard_map/token_grad/pallas_call | solution.py:535
  81.0 1.8 %collective-permute-start.18 = (bf16[177,512]{1,0:T(8,128)(2,1)S(1)}, bf16[177,512]{1,0:T(8,128)(2,1)S(1)}, u32[]{:S(2)}, u32[]{:S(2)}) collective-permute-start(bf16[177,512]{1,0:T(8,128)(2,1)S(1)} %get-tuple-element.106), channel_id=1, source_target_pairs={{0,3},{1,0},{2,1},{3,2},{4,7},{5,4},{6,5},{7,6},{8,11},{9,8},{10,9... | collective-permute-start | bytes 543752 | tf_op jit(solution)/shard_map/ppermute | solution.py:42
  82.7 1.2 collective-permute-done.28.vec_got
  84.1 0.6 collective-permute-start.29
  84.7 2.1 %collective-permute-done.18.h1 = bf16[177,512]{1,0:T(8,128)(2,1)S(1)} collective-permute-done((bf16[177,512]{1,0:T(8,128)(2,1)S(1)}, bf16[177,512]{1,0:T(8,128)(2,1)S(1)}, u32[]{:S(2)}, u32[]{:S(2)}) %collective-permute-start.18) | collective-permute-done | bytes 181280 | tf_op jit(solution)/shard_map/ppermute | solution.py:42
  86.8 0.5 collective-permute-start.19
  87.4 7.8 %collective-permute-done.22.g2 = bf16[448,512]{1,0:T(8,128)(2,1)S(1)} collective-permute-done((bf16[448,512]{1,0:T(8,128)(2,1)S(1)}, bf16[448,512]{1,0:T(8,128)(2,1)S(1)}, u32[]{:S(2)}, u32[]{:S(2)}) %collective-permute-start.22) | collective-permute-done | bytes 458784 | tf_op jit(solution)/shard_map/ppermute | solution.py:47
  95.2 0.7 collective-permute-start.20
  96.4 1.2 collective-permute-done.21.g1
  98.3 1.5 %collective-permute-start.25 = (bf16[112,512]{1,0:T(8,128)(2,1)S(1)}, bf16[112,512]{1,0:T(8,128)(2,1)S(1)}, u32[]{:S(2)}, u32[]{:S(2)}) collective-permute-start(bf16[112,512]{1,0:T(8,128)(2,1)S(1)} %get-tuple-element.116), channel_id=1, source_target_pairs={{0,2},{1,3},{2,0},{3,1},{4,6},{5,7},{6,4},{7,5},{8,10},{9,11},{10,... | collective-permute-start | bytes 344072 | tf_op jit(solution)/shard_map/ppermute | solution.py:42
  99.8 5.0 %collective-permute-done.20.h3 = bf16[177,512]{1,0:T(8,128)(2,1)S(1)} collective-permute-done((bf16[177,512]{1,0:T(8,128)(2,1)S(1)}, bf16[177,512]{1,0:T(8,128)(2,1)S(1)}, u32[]{:S(2)}, u32[]{:S(2)}) %collective-permute-start.20) | collective-permute-done | bytes 181280 | tf_op jit(solution)/shard_map/ppermute | solution.py:42
  104.8 2.0 %collective-permute-start.24 = (bf16[112,512]{1,0:T(8,128)(2,1)S(1)}, bf16[112,512]{1,0:T(8,128)(2,1)S(1)}, u32[]{:S(2)}, u32[]{:S(2)}) collective-permute-start(bf16[112,512]{1,0:T(8,128)(2,1)S(1)} %get-tuple-element.115.tie), channel_id=1, source_target_pairs={{0,1},{1,2},{2,3},{3,0},{4,5},{5,6},{6,7},{7,4},{8,9},{9,10},{10,1... | collective-permute-start | bytes 344072 | tf_op jit(solution)/shard_map/ppermute | solution.py:42
  106.8 1.7 %home.1 = (bf16[81,4,512]{2,1,0:T(4,128)(2,1)}, f32[4,81,1,512]{3,2,1,0:T(1,128)}) custom-call(s32[2]{0:T(128)S(1)} %pad_add_fusion.scal, bf16[177,512]{1,0:T(8,128)(2,1)S(1)} %get-tuple-element.105.h0, bf16[177,512]{1,0:T(8,128)(2,1)S(1)} %collective-permute-done.18.h1, bf16[177,512]{1,0:T(8,128)(2,1)S(1)} %collective-permute-done.19.h2, ...), custom_call_target="tpu_custom_call" | custom-call | flops 100000000 | bytes 725000 | tf_op jit(solution)/shard_map/home/pallas_call | solution.py:535
  108.8 2.3 %collective-permute-start.33 = (bf16[80,512]{1,0:T(8,128)(2,1)S(1)}, bf16[80,512]{1,0:T(8,128)(2,1)S(1)}, u32[]{:S(2)}, u32[]{:S(2)}) collective-permute-start(bf16[80,512]{1,0:T(8,128)(2,1)S(1)} %get-tuple-element.129), channel_id=1, source_target_pairs={{0,2},{1,3},{2,0},{3,1},{4,6},{5,7},{6,4},{7,5},{8,10},{9,11},{10,... | collective-permute-start | bytes 245768 | tf_op jit(solution)/shard_map/ppermute | solution.py:42
  111.1 1.5 %collective-permute-start.34 = (bf16[80,512]{1,0:T(8,128)(2,1)S(1)}, bf16[80,512]{1,0:T(8,128)(2,1)S(1)}, u32[]{:S(2)}, u32[]{:S(2)}) collective-permute-start(bf16[80,512]{1,0:T(8,128)(2,1)S(1)} %get-tuple-element.130), channel_id=1, source_target_pairs={{0,3},{1,0},{2,1},{3,2},{4,7},{5,4},{6,5},{7,6},{8,11},{9,8},{10,9... | collective-permute-start | bytes 245768 | tf_op jit(solution)/shard_map/ppermute | solution.py:42
  112.8 9.9 %all-gather = bf16[896,512]{1,0:T(8,128)(2,1)S(1)} all-gather(bf16[112,512]{1,0:T(8,128)(2,1)S(1)} %patch_a.1), channel_id=2, replica_groups={{0,4,8,12,16,20,24,28},{1,5,9,13,17,21,25,29},{2,6,10,14,18,22,26,30},{..., dimensions={0}, use_global_device_ids=true | all-gather | bytes 1032192 | tf_op jit(solution)/shard_map/all_gather | solution.py:558
  122.7 0.6 patch_b.1
  123.3 9.6 %all-gather.1 = bf16[384,512]{1,0:T(8,128)(2,1)S(1)} all-gather(bf16[48,512]{1,0:T(8,128)(2,1)S(1)} %get-tuple-element.131), channel_id=3, replica_groups={{0,4,8,12,16,20,24,28},{1,5,9,13,17,21,25,29},{2,6,10,14,18,22,26,30},{..., dimensions={0}, use_global_device_ids=true | all-gather | bytes 442368 | tf_op jit(solution)/shard_map/all_gather | solution.py:558
  132.9 0.6 multiply_add_fusion
  133.6 3.3 %update.1 = (f32[128,3072]{1,0:T(8,128)}, f32[128,3072]{1,0:T(8,128)}, f32[128,3072]{1,0:T(8,128)}, f32[384,512]{1,0:T(8,128)}, f32[384,512]{1,0:T(8,128)}, /*in...) custom-call(bf16[8,112,512]{2,1,0:T(8,128)(2,1)S(1)} %bitcast.20, ...), custom_call_target="tpu_custom_call" | custom-call | flops 100000000 | bytes 8703536 | tf_op jit(solution)/shard_map/update/pallas_call | solution.py:535
  (90 shorter events, 5.2 us)
Async XLA Ops:
  1.7 9.1 %collective-permute-start.5 = (bf16[16,3072]{1,0:T(8,128)(2,1)S(1)}, bf16[16,3072]{1,0:T(8,128)(2,1)S(1)}, u32[]{:S(2)}, u32[]{:S(2)}) collective-permute-start(bf16[16,3072]{1,0:T(8,128)(2,1)S(1)} %dynamic-slice_convert_fusion), channel_id=1, source_target_pairs={{0,3},{1,0},{2,1},{3,2},{4,7},{5,4},{6,5},{7,6},{8,11},{9,8},{10,9... | collective-permute-start | bytes 294920 | tf_op jit(solution)/shard_map/ppermute | solution.py:42
  6.8 8.7 %collective-permute-start.4 = (bf16[16,3072]{1,0:T(8,128)(2,1)S(1)}, bf16[16,3072]{1,0:T(8,128)(2,1)S(1)}, u32[]{:S(2)}, u32[]{:S(2)}) collective-permute-start(bf16[16,3072]{1,0:T(8,128)(2,1)S(1)} %dynamic-slice_convert_fusion), channel_id=1, source_target_pairs={{0,2},{1,3},{2,0},{3,1},{4,6},{5,7},{6,4},{7,5},{8,10},{9,11},{10,... | collective-permute-start | bytes 294920 | tf_op jit(solution)/shard_map/ppermute | solution.py:42
  6.8 8.7 %collective-permute-start.3 = (bf16[16,3072]{1,0:T(8,128)(2,1)S(1)}, bf16[16,3072]{1,0:T(8,128)(2,1)S(1)}, u32[]{:S(2)}, u32[]{:S(2)}) collective-permute-start(bf16[16,3072]{1,0:T(8,128)(2,1)S(1)} %dynamic-slice_convert_fusion), channel_id=1, source_target_pairs={{0,1},{1,2},{2,3},{3,0},{4,5},{5,6},{6,7},{7,4},{8,9},{9,10},{10,1... | collective-permute-start | bytes 294920 | tf_op jit(solution)/shard_map/ppermute | solution.py:42
  7.8 30.0 %copy-start.13 = (f32[8004]{0:T(1024)S(1)}, f32[8004]{0:T(1024)}, u32[]{:S(2)}) copy-start(f32[8004]{0:T(1024)} %param.29) | copy-start | bytes 96052
  10.0 38.3 %copy-start.11 = (s32[4,1,324]{2,1,0:T(1,128)S(1)}, s32[4,1,324]{2,1,0:T(1,128)}, u32[]{:S(2)}) copy-start(s32[4,1,324]{2,1,0:T(1,128)} %crops.1) | copy-start | bytes 15556
  10.0 38.3 %copy-start.12 = (s32[4,1]{0,1:T(1,128)S(1)}, s32[4,1]{0,1:T(1,128)}, u32[]{:S(2)}) copy-start(s32[4,1]{0,1:T(1,128)} %param.18) | copy-start | bytes 52
  10.8 40.3 %copy-start.1 = (f32[128,3072]{1,0:T(8,128)S(1)}, f32[128,3072]{1,0:T(8,128)}, u32[]{:S(2)}) copy-start(f32[128,3072]{1,0:T(8,128)} %rest_0_.1) | copy-start | bytes 4718596
  15.6 15.8 %collective-permute-start.14 = (bf16[3,16,3072]{2,1,0:T(8,128)(2,1)S(1)}, bf16[3,16,3072]{2,1,0:T(8,128)(2,1)S(1)}, u32[]{:S(2)}, u32[]{:S(2)}) collective-permute-start(bf16[3,16,3072]{2,1,0:T(8,128)(2,1)S(1)} %stack_i.1.rest_0_), channel_id=1, source_target_pairs={{0,24},{4,28},{8,16},{12,20},{16,8},{20,12},{24,0},{28,4},{1,25},{... | collective-permute-start | bytes 884744 | tf_op jit(solution)/shard_map/ppermute | solution.py:47
  18.1 13.3 %collective-permute-start.1 = (bf16[241,512]{1,0:T(8,128)(2,1)S(1)}, bf16[241,512]{1,0:T(8,128)(2,1)S(1)}, u32[]{:S(2)}, u32[]{:S(2)}) collective-permute-start(bf16[241,512]{1,0:T(8,128)(2,1)S(1)} %get-tuple-element.82), channel_id=1, source_target_pairs={{0,2},{1,3},{2,0},{3,1},{4,6},{5,7},{6,4},{7,5},{8,10},{9,11},{10,... | collective-permute-start | bytes 740360 | tf_op jit(solution)/shard_map/ppermute | solution.py:42
  20.4 16.9 %collective-permute-start.12 = (bf16[3,16,3072]{2,1,0:T(8,128)(2,1)S(1)}, bf16[3,16,3072]{2,1,0:T(8,128)(2,1)S(1)}, u32[]{:S(2)}, u32[]{:S(2)}) collective-permute-start(bf16[3,16,3072]{2,1,0:T(8,128)(2,1)S(1)} %stack_i.1.rest_0_), channel_id=1, source_target_pairs={{0,16},{4,20},{8,24},{12,28},{16,0},{20,4},{24,8},{28,12},{1,17},{... | collective-permute-start | bytes 884744 | tf_op jit(solution)/shard_map/ppermute | solution.py:47
  20.9 16.4 %collective-permute-start.6 = (bf16[3,16,3072]{2,1,0:T(8,128)(2,1)S(1)}, bf16[3,16,3072]{2,1,0:T(8,128)(2,1)S(1)}, u32[]{:S(2)}, u32[]{:S(2)}) collective-permute-start(bf16[3,16,3072]{2,1,0:T(8,128)(2,1)S(1)} %stack_i.1.rest_0_), channel_id=1, source_target_pairs={{0,8},{4,12},{8,0},{12,4},{16,24},{20,28},{24,16},{28,20},{1,9},{5... | collective-permute-start | bytes 884744 | tf_op jit(solution)/shard_map/ppermute | solution.py:47
  21.4 11.5 %collective-permute-start.2 = (bf16[241,512]{1,0:T(8,128)(2,1)S(1)}, bf16[241,512]{1,0:T(8,128)(2,1)S(1)}, u32[]{:S(2)}, u32[]{:S(2)}) collective-permute-start(bf16[241,512]{1,0:T(8,128)(2,1)S(1)} %get-tuple-element.83), channel_id=1, source_target_pairs={{0,3},{1,0},{2,1},{3,2},{4,7},{5,4},{6,5},{7,6},{8,11},{9,8},{10,9... | collective-permute-start | bytes 740360 | tf_op jit(solution)/shard_map/ppermute | solution.py:42
  31.3 13.8 %collective-permute-start.10 = (bf16[3,16,3072]{2,1,0:T(8,128)(2,1)S(1)}, bf16[3,16,3072]{2,1,0:T(8,128)(2,1)S(1)}, u32[]{:S(2)}, u32[]{:S(2)}) collective-permute-start(bf16[3,16,3072]{2,1,0:T(8,128)(2,1)S(1)} %stack_i.1.rest_0_), channel_id=1, source_target_pairs={{0,4},{4,0},{8,12},{12,8},{16,20},{20,16},{24,28},{28,24},{1,5},{5... | collective-permute-start | bytes 884744 | tf_op jit(solution)/shard_map/ppermute | solution.py:47
  31.3 15.3 %collective-permute-start.15 = (bf16[3,16,3072]{2,1,0:T(8,128)(2,1)S(1)}, bf16[3,16,3072]{2,1,0:T(8,128)(2,1)S(1)}, u32[]{:S(2)}, u32[]{:S(2)}) collective-permute-start(bf16[3,16,3072]{2,1,0:T(8,128)(2,1)S(1)} %collective-permute-done.14.rest_6_), channel_id=1, source_target_pairs={{0,4},{4,0},{8,12},{12,8},{16,20},{20,16},{24,28},{28,24},{1,5},{5... | collective-permute-start | bytes 884744 | tf_op jit(solution)/shard_map/ppermute | solution.py:47
  32.9 11.7 %collective-permute-start = (bf16[241,512]{1,0:T(8,128)(2,1)S(1)}, bf16[241,512]{1,0:T(8,128)(2,1)S(1)}, u32[]{:S(2)}, u32[]{:S(2)}) collective-permute-start(bf16[241,512]{1,0:T(8,128)(2,1)S(1)} %get-tuple-element.81.tie), channel_id=1, source_target_pairs={{0,1},{1,2},{2,3},{3,0},{4,5},{5,6},{6,7},{7,4},{8,9},{9,10},{10,1... | collective-permute-start | bytes 740360 | tf_op jit(solution)/shard_map/ppermute | solution.py:42
  37.3 13.8 %collective-permute-start.13 = (bf16[3,16,3072]{2,1,0:T(8,128)(2,1)S(1)}, bf16[3,16,3072]{2,1,0:T(8,128)(2,1)S(1)}, u32[]{:S(2)}, u32[]{:S(2)}) collective-permute-start(bf16[3,16,3072]{2,1,0:T(8,128)(2,1)S(1)} %collective-permute-done.12.rest_4_), channel_id=1, source_target_pairs={{0,4},{4,0},{8,12},{12,8},{16,20},{20,16},{24,28},{28,24},{1,5},{5... | collective-permute-start | bytes 884744 | tf_op jit(solution)/shard_map/ppermute | solution.py:47
  37.3 13.8 %collective-permute-start.11 = (bf16[3,16,3072]{2,1,0:T(8,128)(2,1)S(1)}, bf16[3,16,3072]{2,1,0:T(8,128)(2,1)S(1)}, u32[]{:S(2)}, u32[]{:S(2)}) collective-permute-start(bf16[3,16,3072]{2,1,0:T(8,128)(2,1)S(1)} %collective-permute-done.6.tie.rest_2_), channel_id=1, source_target_pairs={{0,4},{4,0},{8,12},{12,8},{16,20},{20,16},{24,28},{28,24},{1,5},{5... | collective-permute-start | bytes 884744 | tf_op jit(solution)/shard_map/ppermute | solution.py:47
  44.6 12.9 %collective-permute-start.9 = (bf16[3,64,512]{2,1,0:T(8,128)(2,1)S(1)}, bf16[3,64,512]{2,1,0:T(8,128)(2,1)S(1)}, u32[]{:S(2)}, u32[]{:S(2)}) collective-permute-start(bf16[3,64,512]{2,1,0:T(8,128)(2,1)S(1)} %stack_o.1.p0), channel_id=1, source_target_pairs={{0,24},{4,28},{8,16},{12,20},{16,8},{20,12},{24,0},{28,4},{1,25},{... | collective-permute-start | bytes 589832 | tf_op jit(solution)/shard_map/ppermute | solution.py:47
  45.2 12.4 %collective-permute-start.8 = (bf16[3,64,512]{2,1,0:T(8,128)(2,1)S(1)}, bf16[3,64,512]{2,1,0:T(8,128)(2,1)S(1)}, u32[]{:S(2)}, u32[]{:S(2)}) collective-permute-start(bf16[3,64,512]{2,1,0:T(8,128)(2,1)S(1)} %stack_o.1.p0), channel_id=1, source_target_pairs={{0,16},{4,20},{8,24},{12,28},{16,0},{20,4},{24,8},{28,12},{1,17},{... | collective-permute-start | bytes 589832 | tf_op jit(solution)/shard_map/ppermute | solution.py:47
  46.7 10.9 %collective-permute-start.7 = (bf16[3,64,512]{2,1,0:T(8,128)(2,1)S(1)}, bf16[3,64,512]{2,1,0:T(8,128)(2,1)S(1)}, u32[]{:S(2)}, u32[]{:S(2)}) collective-permute-start(bf16[3,64,512]{2,1,0:T(8,128)(2,1)S(1)} %stack_o.1.p0), channel_id=1, source_target_pairs={{0,8},{4,12},{8,0},{12,4},{16,24},{20,28},{24,16},{28,20},{1,9},{5... | collective-permute-start | bytes 589832 | tf_op jit(solution)/shard_map/ppermute | solution.py:47
  57.6 3.0 %collective-permute-start.16 = (bf16[4,3,64,512]{3,2,1,0:T(8,128)(2,1)S(1)}, bf16[4,3,64,512]{3,2,1,0:T(8,128)(2,1)S(1)}, u32[]{:S(2)}, u32[]{:S(2)}) collective-permute-start(bf16[4,3,64,512]{3,2,1,0:T(8,128)(2,1)S(1)} %join.1.tie.rest_0_), channel_id=1, source_target_pairs={{0,4},{4,0},{8,12},{12,8},{16,20},{20,16},{24,28},{28,24},{1,5},{5... | collective-permute-start | bytes 2359304 | tf_op jit(solution)/shard_map/ppermute | solution.py:47
  68.5 4.0 %collective-permute-start.17 = (bf16[4,448,512]{2,1,0:T(8,128)(2,1)S(1)}, bf16[4,448,512]{2,1,0:T(8,128)(2,1)S(1)}, u32[]{:S(2)}, u32[]{:S(2)}) collective-permute-start(bf16[4,448,512]{2,1,0:T(8,128)(2,1)S(1)} %get-tuple-element.103), channel_id=1, source_target_pairs={{0,4},{4,0},{8,12},{12,8},{16,20},{20,16},{24,28},{28,24},{1,5},{5... | collective-permute-start | bytes 5505032 | tf_op jit(solution)/shard_map/ppermute | solution.py:47
  71.9 10.8 %collective-permute-start.27 = (bf16[4,192,512]{2,1,0:T(8,128)(2,1)S(1)}, bf16[4,192,512]{2,1,0:T(8,128)(2,1)S(1)}, u32[]{:S(2)}, u32[]{:S(2)}) collective-permute-start(bf16[4,192,512]{2,1,0:T(8,128)(2,1)S(1)} %get-tuple-element.119), channel_id=1, source_target_pairs={{0,4},{4,0},{8,12},{12,8},{16,20},{20,16},{24,28},{28,24},{1,5},{5... | collective-permute-start | bytes 2359304 | tf_op jit(solution)/shard_map/ppermute | solution.py:47
  72.9 22.4 %collective-permute-start.22 = (bf16[448,512]{1,0:T(8,128)(2,1)S(1)}, bf16[448,512]{1,0:T(8,128)(2,1)S(1)}, u32[]{:S(2)}, u32[]{:S(2)}) collective-permute-start(bf16[448,512]{1,0:T(8,128)(2,1)S(1)} %get-tuple-element.113), channel_id=1, source_target_pairs={{0,16},{4,20},{8,24},{12,28},{16,0},{20,4},{24,8},{28,12},{1,17},{... | collective-permute-start | bytes 1376264 | tf_op jit(solution)/shard_map/ppermute | solution.py:47
  73.4 22.5 %collective-permute-start.23 = (bf16[448,512]{1,0:T(8,128)(2,1)S(1)}, bf16[448,512]{1,0:T(8,128)(2,1)S(1)}, u32[]{:S(2)}, u32[]{:S(2)}) collective-permute-start(bf16[448,512]{1,0:T(8,128)(2,1)S(1)} %get-tuple-element.104.rest_0_), channel_id=1, source_target_pairs={{0,24},{4,28},{8,16},{12,20},{16,8},{20,12},{24,0},{28,4},{1,25},{... | collective-permute-start | bytes 1376264 | tf_op jit(solution)/shard_map/ppermute | solution.py:47
  74.9 22.7 %collective-permute-start.21 = (bf16[448,512]{1,0:T(8,128)(2,1)S(1)}, bf16[448,512]{1,0:T(8,128)(2,1)S(1)}, u32[]{:S(2)}, u32[]{:S(2)}) collective-permute-start(bf16[448,512]{1,0:T(8,128)(2,1)S(1)} %get-tuple-element.112.tie), channel_id=1, source_target_pairs={{0,8},{4,12},{8,0},{12,4},{16,24},{20,28},{24,16},{28,20},{1,9},{5... | collective-permute-start | bytes 1376264 | tf_op jit(solution)/shard_map/ppermute | solution.py:47
  81.0 5.9 %collective-permute-start.18 = (bf16[177,512]{1,0:T(8,128)(2,1)S(1)}, bf16[177,512]{1,0:T(8,128)(2,1)S(1)}, u32[]{:S(2)}, u32[]{:S(2)}) collective-permute-start(bf16[177,512]{1,0:T(8,128)(2,1)S(1)} %get-tuple-element.106), channel_id=1, source_target_pairs={{0,3},{1,0},{2,1},{3,2},{4,7},{5,4},{6,5},{7,6},{8,11},{9,8},{10,9... | collective-permute-start | bytes 543752 | tf_op jit(solution)/shard_map/ppermute | solution.py:42
  82.7 1.2 collective-permute-start.28
  84.1 20.7 %collective-permute-start.29 = (bf16[224,512]{1,0:T(8,128)(2,1)S(1)}, bf16[224,512]{1,0:T(8,128)(2,1)S(1)}, u32[]{:S(2)}, u32[]{:S(2)}) collective-permute-start(bf16[224,512]{1,0:T(8,128)(2,1)S(1)} %get-tuple-element.123), channel_id=1, source_target_pairs={{0,8},{4,12},{8,0},{12,4},{16,24},{20,28},{24,16},{28,20},{1,9},{5... | collective-permute-start | bytes 688136 | tf_op jit(solution)/shard_map/ppermute | solution.py:47
  86.8 11.5 %collective-permute-start.19 = (bf16[177,512]{1,0:T(8,128)(2,1)S(1)}, bf16[177,512]{1,0:T(8,128)(2,1)S(1)}, u32[]{:S(2)}, u32[]{:S(2)}) collective-permute-start(bf16[177,512]{1,0:T(8,128)(2,1)S(1)} %get-tuple-element.107), channel_id=1, source_target_pairs={{0,2},{1,3},{2,0},{3,1},{4,6},{5,7},{6,4},{7,5},{8,10},{9,11},{10,... | collective-permute-start | bytes 543752 | tf_op jit(solution)/shard_map/ppermute | solution.py:42
  95.2 9.6 %collective-permute-start.20 = (bf16[177,512]{1,0:T(8,128)(2,1)S(1)}, bf16[177,512]{1,0:T(8,128)(2,1)S(1)}, u32[]{:S(2)}, u32[]{:S(2)}) collective-permute-start(bf16[177,512]{1,0:T(8,128)(2,1)S(1)} %get-tuple-element.108), channel_id=1, source_target_pairs={{0,1},{1,2},{2,3},{3,0},{4,5},{5,6},{6,7},{7,4},{8,9},{9,10},{10,1... | collective-permute-start | bytes 543752 | tf_op jit(solution)/shard_map/ppermute | solution.py:42
  95.9 12.7 %collective-permute-start.30 = (bf16[224,512]{1,0:T(8,128)(2,1)S(1)}, bf16[224,512]{1,0:T(8,128)(2,1)S(1)}, u32[]{:S(2)}, u32[]{:S(2)}) collective-permute-start(bf16[224,512]{1,0:T(8,128)(2,1)S(1)} %get-tuple-element.124), channel_id=1, source_target_pairs={{0,16},{4,20},{8,24},{12,28},{16,0},{20,4},{24,8},{28,12},{1,17},{... | collective-permute-start | bytes 688136 | tf_op jit(solution)/shard_map/ppermute | solution.py:47
  97.6 10.9 %collective-permute-start.31 = (bf16[224,512]{1,0:T(8,128)(2,1)S(1)}, bf16[224,512]{1,0:T(8,128)(2,1)S(1)}, u32[]{:S(2)}, u32[]{:S(2)}) collective-permute-start(bf16[224,512]{1,0:T(8,128)(2,1)S(1)} %get-tuple-element.125), channel_id=1, source_target_pairs={{0,24},{4,28},{8,16},{12,20},{16,8},{20,12},{24,0},{28,4},{1,25},{... | collective-permute-start | bytes 688136 | tf_op jit(solution)/shard_map/ppermute | solution.py:47
  98.3 12.8 %collective-permute-start.25 = (bf16[112,512]{1,0:T(8,128)(2,1)S(1)}, bf16[112,512]{1,0:T(8,128)(2,1)S(1)}, u32[]{:S(2)}, u32[]{:S(2)}) collective-permute-start(bf16[112,512]{1,0:T(8,128)(2,1)S(1)} %get-tuple-element.116), channel_id=1, source_target_pairs={{0,2},{1,3},{2,0},{3,1},{4,6},{5,7},{6,4},{7,5},{8,10},{9,11},{10,... | collective-permute-start | bytes 344072 | tf_op jit(solution)/shard_map/ppermute | solution.py:42
  104.8 7.8 %collective-permute-start.26 = (bf16[112,512]{1,0:T(8,128)(2,1)S(1)}, bf16[112,512]{1,0:T(8,128)(2,1)S(1)}, u32[]{:S(2)}, u32[]{:S(2)}) collective-permute-start(bf16[112,512]{1,0:T(8,128)(2,1)S(1)} %get-tuple-element.117), channel_id=1, source_target_pairs={{0,3},{1,0},{2,1},{3,2},{4,7},{5,4},{6,5},{7,6},{8,11},{9,8},{10,9... | collective-permute-start | bytes 344072 | tf_op jit(solution)/shard_map/ppermute | solution.py:42
  104.8 7.8 %collective-permute-start.24 = (bf16[112,512]{1,0:T(8,128)(2,1)S(1)}, bf16[112,512]{1,0:T(8,128)(2,1)S(1)}, u32[]{:S(2)}, u32[]{:S(2)}) collective-permute-start(bf16[112,512]{1,0:T(8,128)(2,1)S(1)} %get-tuple-element.115.tie), channel_id=1, source_target_pairs={{0,1},{1,2},{2,3},{3,0},{4,5},{5,6},{6,7},{7,4},{8,9},{9,10},{10,1... | collective-permute-start | bytes 344072 | tf_op jit(solution)/shard_map/ppermute | solution.py:42
  106.8 26.1 %copy-start.14 = (f32[8004]{0:T(1024)S(1)}, f32[8004]{0:T(1024)}, u32[]{:S(2)}) copy-start(f32[8004]{0:T(1024)} %param.31) | copy-start | bytes 96052
  106.8 26.1 %copy-start.15 = (f32[8004]{0:T(1024)S(1)}, f32[8004]{0:T(1024)}, u32[]{:S(2)}) copy-start(f32[8004]{0:T(1024)} %param.30) | copy-start | bytes 96052
  108.5 14.1 %copy-start.6 = (f32[4,81,1,512]{3,2,1,0:T(1,128)S(1)}, f32[4,81,1,512]{3,2,1,0:T(1,128)}, u32[]{:S(2)}) copy-start(f32[4,81,1,512]{3,2,1,0:T(1,128)} %get-tuple-element.110.tie_home) | copy-start | bytes 1990660
  108.6 25.0 %copy-start.5 = (f32[384,512]{1,0:T(8,128)S(1)}, f32[384,512]{1,0:T(8,128)}, u32[]{:S(2)}) copy-start(f32[384,512]{1,0:T(8,128)} %rest_5_.1) | copy-start | bytes 2359300
  108.7 14.0 %collective-permute-start.32 = (bf16[80,512]{1,0:T(8,128)(2,1)S(1)}, bf16[80,512]{1,0:T(8,128)(2,1)S(1)}, u32[]{:S(2)}, u32[]{:S(2)}) collective-permute-start(bf16[80,512]{1,0:T(8,128)(2,1)S(1)} %get-tuple-element.128), channel_id=1, source_target_pairs={{0,1},{1,2},{2,3},{3,0},{4,5},{5,6},{6,7},{7,4},{8,9},{9,10},{10,1... | collective-permute-start | bytes 245768 | tf_op jit(solution)/shard_map/ppermute | solution.py:42
  108.8 13.9 %collective-permute-start.33 = (bf16[80,512]{1,0:T(8,128)(2,1)S(1)}, bf16[80,512]{1,0:T(8,128)(2,1)S(1)}, u32[]{:S(2)}, u32[]{:S(2)}) collective-permute-start(bf16[80,512]{1,0:T(8,128)(2,1)S(1)} %get-tuple-element.129), channel_id=1, source_target_pairs={{0,2},{1,3},{2,0},{3,1},{4,6},{5,7},{6,4},{7,5},{8,10},{9,11},{10,... | collective-permute-start | bytes 245768 | tf_op jit(solution)/shard_map/ppermute | solution.py:42
  111.1 11.6 %collective-permute-start.34 = (bf16[80,512]{1,0:T(8,128)(2,1)S(1)}, bf16[80,512]{1,0:T(8,128)(2,1)S(1)}, u32[]{:S(2)}, u32[]{:S(2)}) collective-permute-start(bf16[80,512]{1,0:T(8,128)(2,1)S(1)} %get-tuple-element.130), channel_id=1, source_target_pairs={{0,3},{1,0},{2,1},{3,2},{4,7},{5,4},{6,5},{7,6},{8,11},{9,8},{10,9... | collective-permute-start | bytes 245768 | tf_op jit(solution)/shard_map/ppermute | solution.py:42
  112.6 20.9 %copy-start.4 = (f32[384,512]{1,0:T(8,128)S(1)}, f32[384,512]{1,0:T(8,128)}, u32[]{:S(2)}) copy-start(f32[384,512]{1,0:T(8,128)} %rest_4_.1) | copy-start | bytes 2359300
  112.7 20.9 %copy-start.2 = (f32[128,3072]{1,0:T(8,128)S(1)}, f32[128,3072]{1,0:T(8,128)}, u32[]{:S(2)}) copy-start(f32[128,3072]{1,0:T(8,128)} %rest_1_.1) | copy-start | bytes 4718596
  112.7 20.9 %copy-start.3 = (f32[128,3072]{1,0:T(8,128)S(1)}, f32[128,3072]{1,0:T(8,128)}, u32[]{:S(2)}) copy-start(f32[128,3072]{1,0:T(8,128)} %rest_2_.1) | copy-start | bytes 4718596
  112.7 20.9 %copy-start.9 = (f32[81,324]{1,0:T(8,128)S(1)}, f32[81,324]{1,0:T(8,128)}, u32[]{:S(2)}) copy-start(f32[81,324]{1,0:T(8,128)} %rest_7_.1) | copy-start | bytes 314932
  112.7 20.9 %copy-start.10 = (f32[81,324]{1,0:T(8,128)S(1)}, f32[81,324]{1,0:T(8,128)}, u32[]{:S(2)}) copy-start(f32[81,324]{1,0:T(8,128)} %rest_8_.1) | copy-start | bytes 314932
  (4 other events, 11.8 us)

commit v4 on v3

--- a/solution.py
+++ b/solution.py
@@ -122,13 +122,14 @@
             copy.wait()
 
 
-def prep_kernel(scal, tok, cot, w_out, mix, m1, m2, m3, tok_own, cot_own, held, strip, sems):
+def prep_kernel(grid, scal, counts, crops, tok, w_out, mix, m1, m2, m3, tok_own, col_ref, row_ref, held, strip, sems):
     own, unit = scal[0], scal[1]
     rows = held.shape[0]
     low = rows + STEP
     count = tok.shape[1]
     copies = Copies(sems)
     copies.bring(w_out.at[pl.ds(aligned(unit * rows, STEP), rows), :], held)
+    slot_kernel(grid, scal, counts, crops, col_ref, row_ref)
     strip[...] = jnp.zeros_like(strip)
     strip[0 : mix.shape[0], 0 : mix.shape[1]] = mix[...].astype(BF)
     copies.wait()
@@ -137,9 +138,12 @@
         msg[0:rows, :] = held[...].astype(BF)
         msg[rows:low, :] = strip[pl.ds(aligned(unit * STEP, STEP), STEP), :]
         msg[low : low + count, :] = tok[to]
-        msg[low + HALF : low + HALF + count, :] = cot[to]
     tok_own[...] = tok[own]
-    cot_own[...] = cot[own]
+
+
+def cot_kernel(scal, cot, tie, c0, c1, c2, c3):
+    for r, out in enumerate((c0, c1, c2, c3)):
+        out[...] = cot[lax.rem(scal[0] + r, 4)]
 
 
 def hold_kernel(src, tie, dst):
@@ -196,22 +200,17 @@
 
 
 def right_kernel(scal, slot_ref, xn_ref, b_in, g_two, s_two, wi_own, *rest):
-    wi, rest = rest[:8], rest[8:]
-    win, vhat_ref, rstd_ref, slope_v, vn_ref, pre, held, sems = rest
+    wi, rest = rest[:8], rest[9:]
+    win, vhat_ref, rstd_ref, slope_v, vn_ref, pre = rest
     own, unit = scal[0], scal[1]
     n, gate = vhat_ref.shape
     tiles = gate // LANE
-    copies = Copies(sems)
-    copies.bring(wi_own, held)
+    win[pl.ds(aligned(own * 128, 128), 128), :] = wi_own[...].astype(BF)
     for e in range(8):
         for r in (1, 2, 3):
             who = lax.rem(own + (4 - r), 4)
             at = who * 128 + (unit ^ e) * STEP
-            copies.bring(wi[e].at[r - 1], win.at[pl.ds(aligned(at, STEP), STEP), :])
-    copies.all[0].wait()
-    win[pl.ds(aligned(own * 128, 128), 128), :] = held[...].astype(BF)
-    for copy in copies.all[1:]:
-        copy.wait()
+            win[pl.ds(aligned(at, STEP), STEP), :] = wi[e][r - 1]
 
     xn = xn_ref[...]
     for k in range(tiles):
@@ -252,28 +251,23 @@
 def spatial_kernel(scal, xt_ref, cot_ref, u_ref, slope_u, vn_ref, b_mix, mix_own, wo_own, *rest):
     wo, rest = rest[:2], rest[2:]
     mix_ref, pre_u, sg_ref, gated, wout, keep, send, *rest = rest
-    mixp, spat, gtmp, held, sems = rest
+    mixp, spat, gtmp = rest
     own, unit = scal[0], scal[1]
     n, gate = u_ref.shape
     tiles = gate // LANE
     out_unit = wout.shape[0] // 32
-    copies = Copies(sems)
-    copies.bring(wo_own, held)
+    wout[pl.ds(aligned(own * 8 * out_unit, STEP), 8 * out_unit), :] = wo_own[...].astype(BF)
     for e in range(8):
         for r in (1, 2, 3):
             who = lax.rem(own + (4 - r), 4)
             at = (who * 8 + (unit ^ e)) * out_unit
-            copies.bring(wo[e % 2].at[e // 2, r - 1, pl.ds(0, out_unit)], wout.at[pl.ds(aligned(at, STEP), out_unit), :])
+            wout[pl.ds(aligned(at, STEP), out_unit), :] = wo[e % 2][e // 2, r - 1, 0:out_unit, :]
             at = who * 128 + (unit ^ e) * STEP
-            copies.bring(wo[e % 2].at[e // 2, r - 1, pl.ds(out_unit, STEP)], mixp.at[pl.ds(aligned(at, STEP), STEP), :])
+            mixp[pl.ds(aligned(at, STEP), STEP), :] = wo[e % 2][e // 2, r - 1, out_unit:, :]
     per, cells = mix_own.shape
     mine = aligned(own * 128, 128)
     mixp[pl.ds(mine, 128), :] = jnp.zeros((128, LANE), BF)
     mixp[pl.ds(mine, per), 0:cells] = mix_own[...].astype(BF)
-    copies.all[0].wait()
-    wout[pl.ds(aligned(own * 8 * out_unit, STEP), 8 * out_unit), :] = held[...].astype(BF)
-    for copy in copies.all[1:]:
-        copy.wait()
     cell = lax.broadcasted_iota(I32, (n, mixp.shape[0]), 0)
     lane = lax.broadcasted_iota(I32, (n, mixp.shape[0]), 1)
     part = jnp.where(cell >= per, 1, 0) + jnp.where(cell >= 2 * per, 1, 0) + jnp.where(cell >= 3 * per, 1, 0)
@@ -593,7 +587,8 @@
     scal = jnp.stack([p, unit]).astype(I32)
 
     def over_plane(base):
-        chips = [base] + [swap(base, m) for m in (2, 4, 6)]
+        near = swap(base, XBIT)
+        chips = [base, near, swap(base, YBIT), swap(near, YBIT)]
         found = []
         for arr in chips:
             found += [arr, swap(arr, CORE)]
@@ -602,13 +597,13 @@
     wi_piece = lax.dynamic_slice_in_dim(in_weight, unit * in_unit, in_unit, 0).astype(BF)
 
     blk = ((row_count, width), BF)
-    msg = ((low + HALF + row_count, width), BF)
-    m1, m2, m3, tok_own, cot_own = call(
-        prep_kernel,
-        [scal, tokens.reshape(4, row_count, width), cotangent.reshape(4, row_count, width), out_weight, spatial_weight],
-        [msg, msg, msg, blk, blk],
+    msg = ((low + row_count, width), BF)
+    m1, m2, m3, tok_own, slot_col, slot_row = call(
+        functools.partial(prep_kernel, grid),
+        [scal, patch_count.reshape(1, 4), crop_index, tokens.reshape(4, row_count, width), out_weight, spatial_weight],
+        [msg, msg, msg, blk, ((n, 1), I32), ((1, n), I32)],
         [pltpu.VMEM((out_unit, width), F32), pltpu.VMEM((128, LANE), BF), pltpu.SemaphoreType.DMA((1,))],
-        specs=[SM, VM, VM, ANY, VM],
+        specs=[SM, VM, VM, VM, ANY, VM],
         limit=8,
         name="prep",
     )
@@ -623,16 +618,16 @@
     wi = over_plane(base_in)
     got = [turn(m, r) for r, m in enumerate((m1, m2, m3), 1)]
     (base,) = call(stack_tied_kernel, [*got, wi[2]], [((3, low, LANE), BF)], specs=[VM] * 3 + [ANY], limit=8, name="stack_o")
+    cot = call(
+        cot_kernel,
+        [scal, cotangent.reshape(4, row_count, width), base],
+        [blk] * 4,
+        specs=[SM, VM, ANY],
+        limit=8,
+        name="prep_cot",
+    )
+    cot = [cot[0]] + [turn(c, r) for r, c in enumerate(cot[1:], 1)]
     plane_out = [base] + [swap(base, m) for m in (2, 4, 6)]
-
-    slot_col, slot_row = call(
-        functools.partial(slot_kernel, grid),
-        [scal, patch_count.reshape(1, 4), crop_index],
-        [((n, 1), I32), ((1, n), I32)],
-        specs=[SM, VM, VM],
-        limit=8,
-        name="slots",
-    )
 
     bounds = [width, width, hidden, gate, gate, cells, width]
     pieces = []
@@ -652,12 +647,19 @@
         name="norm_in",
     )
     sized = lambda kind: ((n, gate), kind)
+    (cot_pos,) = call(
+        functools.partial(place_kernel, 0),
+        [slot_col, *cot, xn],
+        [((n, width), BF)],
+        specs=[VM] * 5 + [ANY],
+        name="place_cot",
+    )
     win, vhat, rstd, slope_v, vn = call(
         right_kernel,
-        [scal, slot_col, xn, b_in, g_two, s_two, in_weight, *wi],
+        [scal, slot_col, xn, b_in, g_two, s_two, in_weight, *wi, cot_pos],
         [((width, hidden), BF), sized(F32), ((n, 1), F32), sized(F32), sized(BF)],
-        [pltpu.VMEM((n, gate), F32), pltpu.VMEM(in_weight.shape, F32), pltpu.SemaphoreType.DMA((25,))],
-        specs=[SM] + [VM] * 5 + [ANY] * 9,
+        [pltpu.VMEM((n, gate), F32)],
+        specs=[SM] + [VM] * 14 + [ANY],
         flops=1_500_000_000,
         limit=20,
         name="right",
@@ -665,16 +667,9 @@
     (joined,) = call(
         join_kernel, [*plane_out, vn], [((4, 3, low, LANE), BF)], specs=[VM] * 4 + [ANY], limit=8, name="join"
     )
-    (cot_pos,) = call(
-        functools.partial(place_kernel, low + HALF),
-        [slot_col, cot_own, *got, joined],
-        [((n, width), BF)],
-        specs=[VM] * 5 + [ANY],
-        name="place_cot",
-    )
     u, slope_u = call(
         left_kernel,
-        [xn, b_in, win, cot_pos],
+        [xn, b_in, win, joined],
         [sized(F32), sized(F32)],
         [pltpu.VMEM((n, gate), F32)],
         specs=[VM] * 3 + [ANY],
@@ -691,10 +686,8 @@
             pltpu.VMEM((512, LANE), BF),
             pltpu.VMEM((n, gate), F32),
             pltpu.VMEM((gate, width), BF),
-            pltpu.VMEM(out_weight.shape, F32),
-            pltpu.SemaphoreType.DMA((50,)),
         ],
-        specs=[SM] + [VM] * 7 + [ANY] * 3,
+        specs=[SM] + [VM] * 10,
         flops=4_000_000_000,
         limit=24,
         name="spatial",

time: 139 us -> 135 us (0.971)
  starting transfers between devices: 37.5 us -> 48.5 us
  waiting for transfers between devices: 39.6 us -> 29.5 us
  Pallas kernels: 34.6 us -> 28.7 us
  local copies, waits for them, and re-layouts: 3.91 us -> 5.75 us
    ppermute x15 -> x18, waiting for transfers between devices: 29.3 us -> 17.9 us  [turn(): return lax.ppermute(arr, 'patch', [(s, (s + r) % n) for s in range(n)])]
    ppermute x15 -> x18, starting transfers between devices: 23.6 us -> 32.2 us  [turn(): return lax.ppermute(arr, 'patch', [(s, (s + r) % n) for s in range(n)])]
    pallas_call x20, Pallas kernels: 34.6 us -> 28.7 us  [call(): pl.pallas_call(body, out_shape=[jax.ShapeDtypeStruct(s, d) for s, d in ou...]
    unnamed x33 -> x39, local copies, waits for them, and re-layouts: 0.99 us -> 4.56 us
    ppermute x20, starting transfers between devices: 14 us -> 16.3 us  [swap(): return lax.ppermute(arr, 'img', [(k, k ^ mask) for k in range(n)])]
  transfers between devices with their start and end apart: 35 -> 38, of which waited for: 10 -> 12; matrix products, arithmetic and copies ran while one was open for 1% -> 1% of each run, Pallas kernels for 17% -> 15%
where the time goes in v4:
time: 135 us; the launch traced here: 134 us
  starting transfers between devices  48.5 us (36%)
  waiting for transfers between devices  29.5 us (22%)
  Pallas kernels  28.7 us (21%)
  blocking collectives  19.6 us (15%)
  local copies, waits for them, and re-layouts  5.75 us (4%)
    ppermute x18, starting transfers between devices, turn(): return lax.ppermute(arr, 'patch', [(s, (s + r) % n) for s in range(n)])  32.2 us
    pallas_call x20, Pallas kernels, call(): pl.pallas_call(body, out_shape=[jax.ShapeDtypeStruct(s, d) for s, d in ou...  28.7 us
    all_gather x2, blocking collectives, img_gather(): return lax.all_gather(arr, 'img', axis_index_groups=groups)  19.6 us
    ppermute x18, waiting for transfers between devices, turn(): return lax.ppermute(arr, 'patch', [(s, (s + r) % n) for s in range(n)])  17.9 us
    ppermute x20, starting transfers between devices, swap(): return lax.ppermute(arr, 'img', [(k, k ^ mask) for k in range(n)])  16.3 us
    ppermute x20, waiting for transfers between devices, swap(): return lax.ppermute(arr, 'img', [(k, k ^ mask) for k in range(n)])  11.5 us
    unnamed x39, local copies, waits for them, and re-layouts  4.56 us
  transfers between devices with their start and end apart: 38, of which 12 were waited for; matrix products, arithmetic and copies ran while one was open for 1% of the time, Pallas kernels for 15%

profile of v4, /device:TPU:0, one launch (start us, length us, event | category | flops | bytes accessed | tf_op | source)
XLA Modules:
  0.0 133.9 jit_solution(8077866674979937445)
XLA Ops:
  0.7 1.0 dynamic-slice_convert_fusion
  1.7 5.1 %collective-permute-start.5 = (bf16[16,3072]{1,0:T(8,128)(2,1)S(1)}, bf16[16,3072]{1,0:T(8,128)(2,1)S(1)}, u32[]{:S(2)}, u32[]{:S(2)}) collective-permute-start(bf16[16,3072]{1,0:T(8,128)(2,1)S(1)} %dynamic-slice_convert_fusion), channel_id=1, source_target_pairs={{0,3},{1,0},{2,1},{3,2},{4,7},{5,4},{6,5},{7,6},{8,11},{9,8},{10,9... | collective-permute-start | bytes 294920 | tf_op jit(solution)/shard_map/ppermute | solution.py:42
  6.8 1.0 collective-permute-start.3
  7.8 1.0 copy.39
  8.9 1.1 copy-done
  12.3 1.0 prep.1
  13.3 2.2 %collective-permute-done.4.m2 = bf16[16,3072]{1,0:T(8,128)(2,1)S(1)} collective-permute-done((bf16[16,3072]{1,0:T(8,128)(2,1)S(1)}, bf16[16,3072]{1,0:T(8,128)(2,1)S(1)}, u32[]{:S(2)}, u32[]{:S(2)}) %collective-permute-start.4) | collective-permute-done | bytes 98336 | tf_op jit(solution)/shard_map/ppermute | solution.py:42
  15.5 1.6 %collective-permute-start.6 = (bf16[3,16,3072]{2,1,0:T(8,128)(2,1)S(1)}, bf16[3,16,3072]{2,1,0:T(8,128)(2,1)S(1)}, u32[]{:S(2)}, u32[]{:S(2)}) collective-permute-start(bf16[3,16,3072]{2,1,0:T(8,128)(2,1)S(1)} %stack_i.1.rest_0_), channel_id=1, source_target_pairs={{0,8},{4,12},{8,0},{12,4},{16,24},{20,28},{24,16},{28,20},{1,9},{5... | collective-permute-start | bytes 884744 | tf_op jit(solution)/shard_map/ppermute | solution.py:47
  17.1 2.3 %collective-permute-start.1 = (bf16[145,512]{1,0:T(8,128)(2,1)S(1)}, bf16[145,512]{1,0:T(8,128)(2,1)S(1)}, u32[]{:S(2)}, u32[]{:S(2)}) collective-permute-start(bf16[145,512]{1,0:T(8,128)(2,1)S(1)} %get-tuple-element.85), channel_id=1, source_target_pairs={{0,2},{1,3},{2,0},{3,1},{4,6},{5,7},{6,4},{7,5},{8,10},{9,11},{10,... | collective-permute-start | bytes 445448 | tf_op jit(solution)/shard_map/ppermute | solution.py:42
  19.4 1.5 %collective-permute-start.12 = (bf16[3,16,3072]{2,1,0:T(8,128)(2,1)S(1)}, bf16[3,16,3072]{2,1,0:T(8,128)(2,1)S(1)}, u32[]{:S(2)}, u32[]{:S(2)}) collective-permute-start(bf16[3,16,3072]{2,1,0:T(8,128)(2,1)S(1)} %stack_i.1.rest_0_), channel_id=1, source_target_pairs={{0,16},{4,20},{8,24},{12,28},{16,0},{20,4},{24,8},{28,12},{1,17},{... | collective-permute-start | bytes 884744 | tf_op jit(solution)/shard_map/ppermute | solution.py:47
  20.9 3.2 %collective-permute-done.6.tie.rest_2_ = bf16[3,16,3072]{2,1,0:T(8,128)(2,1)S(1)} collective-permute-done((bf16[3,16,3072]{2,1,0:T(8,128)(2,1)S(1)}, bf16[3,16,3072]{2,1,0:T(8,128)(2,1)S(1)}, u32[]{:S(2)}, u32[]{:S(2)}) %collective-permute-start.6) | collective-permute-done | bytes 294944 | tf_op jit(solution)/shard_map/ppermute | solution.py:47
  24.0 1.5 %collective-permute-start.14 = (bf16[3,16,3072]{2,1,0:T(8,128)(2,1)S(1)}, bf16[3,16,3072]{2,1,0:T(8,128)(2,1)S(1)}, u32[]{:S(2)}, u32[]{:S(2)}) collective-permute-start(bf16[3,16,3072]{2,1,0:T(8,128)(2,1)S(1)} %collective-permute-done.6.tie.rest_2_), channel_id=1, source_target_pairs={{0,16},{4,20},{8,24},{12,28},{16,0},{20,4},{24,8},{28,12},{1,17},{... | collective-permute-start | bytes 884744 | tf_op jit(solution)/shard_map/ppermute | solution.py:47
  26.2 1.4 %collective-permute-start = (bf16[145,512]{1,0:T(8,128)(2,1)S(1)}, bf16[145,512]{1,0:T(8,128)(2,1)S(1)}, u32[]{:S(2)}, u32[]{:S(2)}) collective-permute-start(bf16[145,512]{1,0:T(8,128)(2,1)S(1)} %get-tuple-element.84.tie), channel_id=1, source_target_pairs={{0,1},{1,2},{2,3},{3,0},{4,5},{5,6},{6,7},{7,4},{8,9},{9,10},{10,1... | collective-permute-start | bytes 445448 | tf_op jit(solution)/shard_map/ppermute | solution.py:42
  27.7 4.2 %collective-permute-done.2.m3 = bf16[145,512]{1,0:T(8,128)(2,1)S(1)} collective-permute-done((bf16[145,512]{1,0:T(8,128)(2,1)S(1)}, bf16[145,512]{1,0:T(8,128)(2,1)S(1)}, u32[]{:S(2)}, u32[]{:S(2)}) %collective-permute-start.2) | collective-permute-done | bytes 148512 | tf_op jit(solution)/shard_map/ppermute | solution.py:42
  31.9 3.2 %collective-permute-done.m1 = bf16[145,512]{1,0:T(8,128)(2,1)S(1)} collective-permute-done((bf16[145,512]{1,0:T(8,128)(2,1)S(1)}, bf16[145,512]{1,0:T(8,128)(2,1)S(1)}, u32[]{:S(2)}, u32[]{:S(2)}) %collective-permute-start) | collective-permute-done | bytes 148512 | tf_op jit(solution)/shard_map/ppermute | solution.py:42
  36.6 3.0 %collective-permute-start.9 = (bf16[81,512]{1,0:T(8,128)(2,1)S(1)}, bf16[81,512]{1,0:T(8,128)(2,1)S(1)}, u32[]{:S(2)}, u32[]{:S(2)}) collective-permute-start(bf16[81,512]{1,0:T(8,128)(2,1)S(1)} %get-tuple-element.91), channel_id=1, source_target_pairs={{0,3},{1,0},{2,1},{3,2},{4,7},{5,4},{6,5},{7,6},{8,11},{9,8},{10,9... | collective-permute-start | bytes 248840 | tf_op jit(solution)/shard_map/ppermute | solution.py:42
  39.7 3.5 %collective-permute-done.7.m1 = bf16[81,512]{1,0:T(8,128)(2,1)S(1)} collective-permute-done((bf16[81,512]{1,0:T(8,128)(2,1)S(1)}, bf16[81,512]{1,0:T(8,128)(2,1)S(1)}, u32[]{:S(2)}, u32[]{:S(2)}) %collective-permute-start.7) | collective-permute-done | bytes 82976 | tf_op jit(solution)/shard_map/ppermute | solution.py:42
  43.7 1.4 %collective-permute-done.8.m2 = bf16[81,512]{1,0:T(8,128)(2,1)S(1)} collective-permute-done((bf16[81,512]{1,0:T(8,128)(2,1)S(1)}, bf16[81,512]{1,0:T(8,128)(2,1)S(1)}, u32[]{:S(2)}, u32[]{:S(2)}) %collective-permute-start.8) | collective-permute-done | bytes 82976 | tf_op jit(solution)/shard_map/ppermute | solution.py:42
  45.1 1.5 %collective-permute-start.18 = (bf16[3,64,512]{2,1,0:T(8,128)(2,1)S(1)}, bf16[3,64,512]{2,1,0:T(8,128)(2,1)S(1)}, u32[]{:S(2)}, u32[]{:S(2)}) collective-permute-start(bf16[3,64,512]{2,1,0:T(8,128)(2,1)S(1)} %stack_o.1.tie.p0), channel_id=1, source_target_pairs={{0,24},{4,28},{8,16},{12,20},{16,8},{20,12},{24,0},{28,4},{1,25},{... | collective-permute-start | bytes 589832 | tf_op jit(solution)/shard_map/ppermute | solution.py:47
  47.3 1.3 collective-permute-start.16
  48.7 2.1 %norm_in.1 = (bf16[336,512]{1,0:T(8,128)(2,1)S(1)}, bf16[336,512]{1,0:T(8,128)(2,1)S(1)}, bf16[512,336]{1,0:T(8,128)(2,1)S(1)}) custom-call(s32[2]{0:T(128)S(1)} %pad_add_fusion.scal, s32[336,1]{1,0:T(8,128)S(1)} %get-tuple-element.81.slot_ref, bf16[81,512]{1,0:T(8,128)(2,1)S(1)} %get-tuple-element.83.own_blk, bf16[145,512]{1,0:T(8,128)(2,1)S(1)} %collective-permute-done.m1, ...), custom_call_target="tpu_custom_call" | custom-call | flops 100000000 | bytes 533832 | tf_op jit(solution)/shard_map/norm_in/pallas_call | solution.py:529
  51.4 3.1 %right.1 = (bf16[512,3072]{1,0:T(8,128)(2,1)S(1)}, f32[336,1536]{1,0:T(8,128)S(1)}, f32[336,1]{1,0:T(8,128)S(1)}, f32[336,1536]{1,0:T(8,128)S(1)}, bf16[336,1536]{1,0:T(8,128)(2,1)S(1)}) custom-call(s32[2]{0:T(128)S(1)} %pad_add_fusion.scal, s32[336,1]{1,0:T(8,128)S(1)} %get-tuple-element.81.slot_ref, bf16[336,512]{1,0:T(8,128)(2,1)S(1)} %get-tuple-element.92.tie.xn_ref, ...), custom_call_target="tpu_custom_call" | custom-call | flops 1500000000 | bytes 4646216 | tf_op jit(solution)/shard_map/right/pallas_call | solution.py:529
  54.6 1.1 collective-permute-done.17.p2
  56.0 1.7 %left.1 = (f32[336,1536]{1,0:T(8,128)S(1)}, f32[336,1536]{1,0:T(8,128)S(1)}) custom-call(bf16[336,512]{1,0:T(8,128)(2,1)S(1)} %get-tuple-element.92.tie.xn_ref, f32[1,3072]{1,0:T(1,128)S(1)} %bitcast.28, bf16[512,3072]{1,0:T(8,128)(2,1)S(1)} %get-tuple-element.93.win, bf16[4,3,64,512]{3,2,1,0:T(8,128)(2,1)S(1)} %join.1.rest_0_), custom_call_target="tpu_custom_call" | custom-call | flops 1000000000 | bytes 4288512 | tf_op jit(solution)/shard_map/left/pallas_call | solution.py:529
  58.1 5.1 %spatial.1 = (bf16[336,336]{1,0:T(8,128)(2,1)S(1)}, bf16[336,1536]{1,0:T(8,128)(2,1)S(1)}, bf16[336,1536]{1,0:T(8,128)(2,1)S(1)}, bf16[336,1536]{1,0:T(8,128)(2,...) custom-call(s32[2]{0:T(128)S(1)} %pad_add_fusion.scal, ...), custom_call_target="tpu_custom_call" | custom-call | flops 4000000000 | bytes 8314712 | tf_op jit(solution)/shard_map/spatial/pallas_call | solution.py:529
  63.5 3.3 %back.1 = (bf16[336,1536]{1,0:T(8,128)(2,1)S(1)}, bf16[4,192,512]{2,1,0:T(8,128)(2,1)S(1)}, bf16[4,192,512]{2,1,0:T(8,128)(2,1)S(1)}, f32[6,512]{1,0:T(8,128)S(1)}) custom-call(s32[336,1]{1,0:T(8,128)S(1)} %get-tuple-element.81.slot_ref, bf16[512,336]{1,0:T(8,128)(2,1)S(1)} %get-tuple-element.94.xt_ref, bf16[336,336]{1,0:T(8,128)(2,1)S(1)} %get-tuple-element.99.mix_ref, ...), custom_call_target="tpu_custom_call" | custom-call | flops 2000000000 | bytes 5739648 | tf_op jit(solution)/shard_map/back/pallas_call | solution.py:529
  67.7 1.1 collective-permute-start.25
  68.7 1.2 collective-permute-start.26
  69.9 1.3 collective-permute-start.24
  71.2 4.4 %token_grad.1 = (bf16[177,512]{1,0:T(8,128)(2,1)S(1)}, bf16[177,512]{1,0:T(8,128)(2,1)S(1)}, bf16[177,512]{1,0:T(8,128)(2,1)S(1)}, bf16[177,512]{1,0:T(8,128)(2,1)S(1)}, f32[16,512]{1,0:T(8,128)S(1)}) custom-call(s32[336,1]{1,0:T(8,128)S(1)} %get-tuple-element.81.slot_ref, s32[1,336]{1,0:T(1,128)S(1)} %get-tuple-element.82.slot_row, ...), custom_call_target="tpu_custom_call" | custom-call | flops 2000000000 | bytes 10013312 | tf_op jit(solution)/shard_map/token_grad/pallas_call | solution.py:529
  75.6 4.2 %collective-permute-start.21 = (bf16[177,512]{1,0:T(8,128)(2,1)S(1)}, bf16[177,512]{1,0:T(8,128)(2,1)S(1)}, u32[]{:S(2)}, u32[]{:S(2)}) collective-permute-start(bf16[177,512]{1,0:T(8,128)(2,1)S(1)} %get-tuple-element.112), channel_id=1, source_target_pairs={{0,3},{1,0},{2,1},{3,2},{4,7},{5,4},{6,5},{7,6},{8,11},{9,8},{10,9... | collective-permute-start | bytes 543752 | tf_op jit(solution)/shard_map/ppermute | solution.py:42
  79.8 1.2 collective-permute-done.31.vec_got
  81.2 0.9 collective-permute-start.32
  82.1 1.1 collective-permute-done.21.h1
  83.2 1.3 collective-permute-start.22
  84.5 5.6 %collective-permute-done.25.g2 = bf16[448,512]{1,0:T(8,128)(2,1)S(1)} collective-permute-done((bf16[448,512]{1,0:T(8,128)(2,1)S(1)}, bf16[448,512]{1,0:T(8,128)(2,1)S(1)}, u32[]{:S(2)}, u32[]{:S(2)}) %collective-permute-start.25) | collective-permute-done | bytes 458784 | tf_op jit(solution)/shard_map/ppermute | solution.py:47
  90.1 1.3 collective-permute-start.23
  91.5 1.0 collective-permute-start.33
  92.4 1.5 %collective-permute-start.34 = (bf16[224,512]{1,0:T(8,128)(2,1)S(1)}, bf16[224,512]{1,0:T(8,128)(2,1)S(1)}, u32[]{:S(2)}, u32[]{:S(2)}) collective-permute-start(bf16[224,512]{1,0:T(8,128)(2,1)S(1)} %get-tuple-element.131), channel_id=1, source_target_pairs={{0,24},{4,28},{8,16},{12,20},{16,8},{20,12},{24,0},{28,4},{1,25},{... | collective-permute-start | bytes 688136 | tf_op jit(solution)/shard_map/ppermute | solution.py:47
  94.2 3.3 %collective-permute-start.28 = (bf16[112,512]{1,0:T(8,128)(2,1)S(1)}, bf16[112,512]{1,0:T(8,128)(2,1)S(1)}, u32[]{:S(2)}, u32[]{:S(2)}) collective-permute-start(bf16[112,512]{1,0:T(8,128)(2,1)S(1)} %get-tuple-element.122), channel_id=1, source_target_pairs={{0,2},{1,3},{2,0},{3,1},{4,6},{5,7},{6,4},{7,5},{8,10},{9,11},{10,... | collective-permute-start | bytes 344072 | tf_op jit(solution)/shard_map/ppermute | solution.py:42
  97.5 2.3 %collective-permute-done.23.h3 = bf16[177,512]{1,0:T(8,128)(2,1)S(1)} collective-permute-done((bf16[177,512]{1,0:T(8,128)(2,1)S(1)}, bf16[177,512]{1,0:T(8,128)(2,1)S(1)}, u32[]{:S(2)}, u32[]{:S(2)}) %collective-permute-start.23) | collective-permute-done | bytes 181280 | tf_op jit(solution)/shard_map/ppermute | solution.py:42
  99.8 1.2 collective-permute-start.29
  101.8 1.7 %home.1 = (bf16[81,4,512]{2,1,0:T(4,128)(2,1)}, f32[4,81,1,512]{3,2,1,0:T(1,128)}) custom-call(s32[2]{0:T(128)S(1)} %pad_add_fusion.scal, bf16[177,512]{1,0:T(8,128)(2,1)S(1)} %get-tuple-element.111.h0, bf16[177,512]{1,0:T(8,128)(2,1)S(1)} %collective-permute-done.21.h1, bf16[177,512]{1,0:T(8,128)(2,1)S(1)} %collective-permute-done.22.h2, ...), custom_call_target="tpu_custom_call" | custom-call | flops 100000000 | bytes 725000 | tf_op jit(solution)/shard_map/home/pallas_call | solution.py:529
  103.7 3.5 %collective-permute-start.36 = (bf16[80,512]{1,0:T(8,128)(2,1)S(1)}, bf16[80,512]{1,0:T(8,128)(2,1)S(1)}, u32[]{:S(2)}, u32[]{:S(2)}) collective-permute-start(bf16[80,512]{1,0:T(8,128)(2,1)S(1)} %get-tuple-element.135), channel_id=1, source_target_pairs={{0,2},{1,3},{2,0},{3,1},{4,6},{5,7},{6,4},{7,5},{8,10},{9,11},{10,... | collective-permute-start | bytes 245768 | tf_op jit(solution)/shard_map/ppermute | solution.py:42
  107.3 2.1 %collective-permute-start.37 = (bf16[80,512]{1,0:T(8,128)(2,1)S(1)}, bf16[80,512]{1,0:T(8,128)(2,1)S(1)}, u32[]{:S(2)}, u32[]{:S(2)}) collective-permute-start(bf16[80,512]{1,0:T(8,128)(2,1)S(1)} %get-tuple-element.136), channel_id=1, source_target_pairs={{0,3},{1,0},{2,1},{3,2},{4,7},{5,4},{6,5},{7,6},{8,11},{9,8},{10,9... | collective-permute-start | bytes 245768 | tf_op jit(solution)/shard_map/ppermute | solution.py:42
  109.5 10.4 %all-gather = bf16[896,512]{1,0:T(8,128)(2,1)S(1)} all-gather(bf16[112,512]{1,0:T(8,128)(2,1)S(1)} %patch_a.1), channel_id=2, replica_groups={{0,4,8,12,16,20,24,28},{1,5,9,13,17,21,25,29},{2,6,10,14,18,22,26,30},{..., dimensions={0}, use_global_device_ids=true | all-gather | bytes 1032192 | tf_op jit(solution)/shard_map/all_gather | solution.py:552
  120.5 9.2 %all-gather.1 = bf16[384,512]{1,0:T(8,128)(2,1)S(1)} all-gather(bf16[48,512]{1,0:T(8,128)(2,1)S(1)} %get-tuple-element.137), channel_id=3, replica_groups={{0,4,8,12,16,20,24,28},{1,5,9,13,17,21,25,29},{2,6,10,14,18,22,26,30},{..., dimensions={0}, use_global_device_ids=true | all-gather | bytes 442368 | tf_op jit(solution)/shard_map/all_gather | solution.py:552
  130.4 3.3 %update.1 = (f32[128,3072]{1,0:T(8,128)}, f32[128,3072]{1,0:T(8,128)}, f32[128,3072]{1,0:T(8,128)}, f32[384,512]{1,0:T(8,128)}, f32[384,512]{1,0:T(8,128)}, /*in...) custom-call(bf16[8,112,512]{2,1,0:T(8,128)(2,1)S(1)} %bitcast.22, ...), custom_call_target="tpu_custom_call" | custom-call | flops 100000000 | bytes 8703536 | tf_op jit(solution)/shard_map/update/pallas_call | solution.py:529
  (101 shorter events, 10.9 us)
Async XLA Ops:
  0.6 27.0 %copy-start.14 = (bf16[4,1,81,512]{3,0,2,1:T(4,128)(2,1)S(1)}, bf16[4,1,81,512]{3,0,2,1:T(4,128)(2,1)}, u32[]{:S(2)}) copy-start(bf16[4,1,81,512]{3,0,2,1:T(4,128)(2,1)} %param.17) | copy-start | bytes 995332
  1.7 11.7 %collective-permute-start.5 = (bf16[16,3072]{1,0:T(8,128)(2,1)S(1)}, bf16[16,3072]{1,0:T(8,128)(2,1)S(1)}, u32[]{:S(2)}, u32[]{:S(2)}) collective-permute-start(bf16[16,3072]{1,0:T(8,128)(2,1)S(1)} %dynamic-slice_convert_fusion), channel_id=1, source_target_pairs={{0,3},{1,0},{2,1},{3,2},{4,7},{5,4},{6,5},{7,6},{8,11},{9,8},{10,9... | collective-permute-start | bytes 294920 | tf_op jit(solution)/shard_map/ppermute | solution.py:42
  6.8 8.7 %collective-permute-start.4 = (bf16[16,3072]{1,0:T(8,128)(2,1)S(1)}, bf16[16,3072]{1,0:T(8,128)(2,1)S(1)}, u32[]{:S(2)}, u32[]{:S(2)}) collective-permute-start(bf16[16,3072]{1,0:T(8,128)(2,1)S(1)} %dynamic-slice_convert_fusion), channel_id=1, source_target_pairs={{0,2},{1,3},{2,0},{3,1},{4,6},{5,7},{6,4},{7,5},{8,10},{9,11},{10,... | collective-permute-start | bytes 294920 | tf_op jit(solution)/shard_map/ppermute | solution.py:42
  6.8 8.7 %collective-permute-start.3 = (bf16[16,3072]{1,0:T(8,128)(2,1)S(1)}, bf16[16,3072]{1,0:T(8,128)(2,1)S(1)}, u32[]{:S(2)}, u32[]{:S(2)}) collective-permute-start(bf16[16,3072]{1,0:T(8,128)(2,1)S(1)} %dynamic-slice_convert_fusion), channel_id=1, source_target_pairs={{0,1},{1,2},{2,3},{3,0},{4,5},{5,6},{6,7},{7,4},{8,9},{9,10},{10,1... | collective-permute-start | bytes 294920 | tf_op jit(solution)/shard_map/ppermute | solution.py:42
  12.3 31.4 %copy-start.15 = (f32[8004]{0:T(1024)S(1)}, f32[8004]{0:T(1024)}, u32[]{:S(2)}) copy-start(f32[8004]{0:T(1024)} %param.29) | copy-start | bytes 96052
  15.5 8.5 %collective-permute-start.6 = (bf16[3,16,3072]{2,1,0:T(8,128)(2,1)S(1)}, bf16[3,16,3072]{2,1,0:T(8,128)(2,1)S(1)}, u32[]{:S(2)}, u32[]{:S(2)}) collective-permute-start(bf16[3,16,3072]{2,1,0:T(8,128)(2,1)S(1)} %stack_i.1.rest_0_), channel_id=1, source_target_pairs={{0,8},{4,12},{8,0},{12,4},{16,24},{20,28},{24,16},{28,20},{1,9},{5... | collective-permute-start | bytes 884744 | tf_op jit(solution)/shard_map/ppermute | solution.py:47
  17.1 9.1 %collective-permute-start.1 = (bf16[145,512]{1,0:T(8,128)(2,1)S(1)}, bf16[145,512]{1,0:T(8,128)(2,1)S(1)}, u32[]{:S(2)}, u32[]{:S(2)}) collective-permute-start(bf16[145,512]{1,0:T(8,128)(2,1)S(1)} %get-tuple-element.85), channel_id=1, source_target_pairs={{0,2},{1,3},{2,0},{3,1},{4,6},{5,7},{6,4},{7,5},{8,10},{9,11},{10,... | collective-permute-start | bytes 445448 | tf_op jit(solution)/shard_map/ppermute | solution.py:42
  19.4 16.4 %collective-permute-start.12 = (bf16[3,16,3072]{2,1,0:T(8,128)(2,1)S(1)}, bf16[3,16,3072]{2,1,0:T(8,128)(2,1)S(1)}, u32[]{:S(2)}, u32[]{:S(2)}) collective-permute-start(bf16[3,16,3072]{2,1,0:T(8,128)(2,1)S(1)} %stack_i.1.rest_0_), channel_id=1, source_target_pairs={{0,16},{4,20},{8,24},{12,28},{16,0},{20,4},{24,8},{28,12},{1,17},{... | collective-permute-start | bytes 884744 | tf_op jit(solution)/shard_map/ppermute | solution.py:47
  20.9 15.7 %collective-permute-start.10 = (bf16[3,16,3072]{2,1,0:T(8,128)(2,1)S(1)}, bf16[3,16,3072]{2,1,0:T(8,128)(2,1)S(1)}, u32[]{:S(2)}, u32[]{:S(2)}) collective-permute-start(bf16[3,16,3072]{2,1,0:T(8,128)(2,1)S(1)} %stack_i.1.rest_0_), channel_id=1, source_target_pairs={{0,4},{4,0},{8,12},{12,8},{16,20},{20,16},{24,28},{28,24},{1,5},{5... | collective-permute-start | bytes 884744 | tf_op jit(solution)/shard_map/ppermute | solution.py:47
  24.0 19.2 %collective-permute-start.14 = (bf16[3,16,3072]{2,1,0:T(8,128)(2,1)S(1)}, bf16[3,16,3072]{2,1,0:T(8,128)(2,1)S(1)}, u32[]{:S(2)}, u32[]{:S(2)}) collective-permute-start(bf16[3,16,3072]{2,1,0:T(8,128)(2,1)S(1)} %collective-permute-done.6.tie.rest_2_), channel_id=1, source_target_pairs={{0,16},{4,20},{8,24},{12,28},{16,0},{20,4},{24,8},{28,12},{1,17},{... | collective-permute-start | bytes 884744 | tf_op jit(solution)/shard_map/ppermute | solution.py:47
  25.6 6.3 %collective-permute-start.2 = (bf16[145,512]{1,0:T(8,128)(2,1)S(1)}, bf16[145,512]{1,0:T(8,128)(2,1)S(1)}, u32[]{:S(2)}, u32[]{:S(2)}) collective-permute-start(bf16[145,512]{1,0:T(8,128)(2,1)S(1)} %get-tuple-element.86), channel_id=1, source_target_pairs={{0,3},{1,0},{2,1},{3,2},{4,7},{5,4},{6,5},{7,6},{8,11},{9,8},{10,9... | collective-permute-start | bytes 445448 | tf_op jit(solution)/shard_map/ppermute | solution.py:42
  26.2 8.9 %collective-permute-start = (bf16[145,512]{1,0:T(8,128)(2,1)S(1)}, bf16[145,512]{1,0:T(8,128)(2,1)S(1)}, u32[]{:S(2)}, u32[]{:S(2)}) collective-permute-start(bf16[145,512]{1,0:T(8,128)(2,1)S(1)} %get-tuple-element.84.tie), channel_id=1, source_target_pairs={{0,1},{1,2},{2,3},{3,0},{4,5},{5,6},{6,7},{7,4},{8,9},{9,10},{10,1... | collective-permute-start | bytes 445448 | tf_op jit(solution)/shard_map/ppermute | solution.py:42
  27.7 23.8 %copy-start.2 = (f32[128,3072]{1,0:T(8,128)S(1)}, f32[128,3072]{1,0:T(8,128)}, u32[]{:S(2)}) copy-start(f32[128,3072]{1,0:T(8,128)} %rest_0_.1) | copy-start | bytes 4718596
  35.7 7.5 %collective-permute-start.7 = (bf16[81,512]{1,0:T(8,128)(2,1)S(1)}, bf16[81,512]{1,0:T(8,128)(2,1)S(1)}, u32[]{:S(2)}, u32[]{:S(2)}) collective-permute-start(bf16[81,512]{1,0:T(8,128)(2,1)S(1)} %get-tuple-element.89), channel_id=1, source_target_pairs={{0,1},{1,2},{2,3},{3,0},{4,5},{5,6},{6,7},{7,4},{8,9},{9,10},{10,1... | collective-permute-start | bytes 248840 | tf_op jit(solution)/shard_map/ppermute | solution.py:42
  35.8 11.5 %collective-permute-start.13 = (bf16[3,16,3072]{2,1,0:T(8,128)(2,1)S(1)}, bf16[3,16,3072]{2,1,0:T(8,128)(2,1)S(1)}, u32[]{:S(2)}, u32[]{:S(2)}) collective-permute-start(bf16[3,16,3072]{2,1,0:T(8,128)(2,1)S(1)} %collective-permute-done.12.rest_4_), channel_id=1, source_target_pairs={{0,4},{4,0},{8,12},{12,8},{16,20},{20,16},{24,28},{28,24},{1,5},{5... | collective-permute-start | bytes 884744 | tf_op jit(solution)/shard_map/ppermute | solution.py:47
  35.9 9.3 %collective-permute-start.8 = (bf16[81,512]{1,0:T(8,128)(2,1)S(1)}, bf16[81,512]{1,0:T(8,128)(2,1)S(1)}, u32[]{:S(2)}, u32[]{:S(2)}) collective-permute-start(bf16[81,512]{1,0:T(8,128)(2,1)S(1)} %get-tuple-element.90), channel_id=1, source_target_pairs={{0,2},{1,3},{2,0},{3,1},{4,6},{5,7},{6,4},{7,5},{8,10},{9,11},{10,... | collective-permute-start | bytes 248840 | tf_op jit(solution)/shard_map/ppermute | solution.py:42
  36.6 10.0 %collective-permute-start.9 = (bf16[81,512]{1,0:T(8,128)(2,1)S(1)}, bf16[81,512]{1,0:T(8,128)(2,1)S(1)}, u32[]{:S(2)}, u32[]{:S(2)}) collective-permute-start(bf16[81,512]{1,0:T(8,128)(2,1)S(1)} %get-tuple-element.91), channel_id=1, source_target_pairs={{0,3},{1,0},{2,1},{3,2},{4,7},{5,4},{6,5},{7,6},{8,11},{9,8},{10,9... | collective-permute-start | bytes 248840 | tf_op jit(solution)/shard_map/ppermute | solution.py:42
  43.2 8.2 %collective-permute-start.11 = (bf16[3,16,3072]{2,1,0:T(8,128)(2,1)S(1)}, bf16[3,16,3072]{2,1,0:T(8,128)(2,1)S(1)}, u32[]{:S(2)}, u32[]{:S(2)}) collective-permute-start(bf16[3,16,3072]{2,1,0:T(8,128)(2,1)S(1)} %collective-permute-done.6.tie.rest_2_), channel_id=1, source_target_pairs={{0,4},{4,0},{8,12},{12,8},{16,20},{20,16},{24,28},{28,24},{1,5},{5... | collective-permute-start | bytes 884744 | tf_op jit(solution)/shard_map/ppermute | solution.py:47
  43.2 8.2 %collective-permute-start.15 = (bf16[3,16,3072]{2,1,0:T(8,128)(2,1)S(1)}, bf16[3,16,3072]{2,1,0:T(8,128)(2,1)S(1)}, u32[]{:S(2)}, u32[]{:S(2)}) collective-permute-start(bf16[3,16,3072]{2,1,0:T(8,128)(2,1)S(1)} %collective-permute-done.14.rest_6_), channel_id=1, source_target_pairs={{0,4},{4,0},{8,12},{12,8},{16,20},{20,16},{24,28},{28,24},{1,5},{5... | collective-permute-start | bytes 884744 | tf_op jit(solution)/shard_map/ppermute | solution.py:47
  45.1 9.4 %collective-permute-start.18 = (bf16[3,64,512]{2,1,0:T(8,128)(2,1)S(1)}, bf16[3,64,512]{2,1,0:T(8,128)(2,1)S(1)}, u32[]{:S(2)}, u32[]{:S(2)}) collective-permute-start(bf16[3,64,512]{2,1,0:T(8,128)(2,1)S(1)} %stack_o.1.tie.p0), channel_id=1, source_target_pairs={{0,24},{4,28},{8,16},{12,20},{16,8},{20,12},{24,0},{28,4},{1,25},{... | collective-permute-start | bytes 589832 | tf_op jit(solution)/shard_map/ppermute | solution.py:47
  46.6 9.1 %collective-permute-start.17 = (bf16[3,64,512]{2,1,0:T(8,128)(2,1)S(1)}, bf16[3,64,512]{2,1,0:T(8,128)(2,1)S(1)}, u32[]{:S(2)}, u32[]{:S(2)}) collective-permute-start(bf16[3,64,512]{2,1,0:T(8,128)(2,1)S(1)} %stack_o.1.tie.p0), channel_id=1, source_target_pairs={{0,16},{4,20},{8,24},{12,28},{16,0},{20,4},{24,8},{28,12},{1,17},{... | collective-permute-start | bytes 589832 | tf_op jit(solution)/shard_map/ppermute | solution.py:47
  47.3 8.4 %collective-permute-start.16 = (bf16[3,64,512]{2,1,0:T(8,128)(2,1)S(1)}, bf16[3,64,512]{2,1,0:T(8,128)(2,1)S(1)}, u32[]{:S(2)}, u32[]{:S(2)}) collective-permute-start(bf16[3,64,512]{2,1,0:T(8,128)(2,1)S(1)} %stack_o.1.tie.p0), channel_id=1, source_target_pairs={{0,8},{4,12},{8,0},{12,4},{16,24},{20,28},{24,16},{28,20},{1,9},{5... | collective-permute-start | bytes 589832 | tf_op jit(solution)/shard_map/ppermute | solution.py:47
  55.8 2.4 %collective-permute-start.19 = (bf16[4,3,64,512]{3,2,1,0:T(8,128)(2,1)S(1)}, bf16[4,3,64,512]{3,2,1,0:T(8,128)(2,1)S(1)}, u32[]{:S(2)}, u32[]{:S(2)}) collective-permute-start(bf16[4,3,64,512]{3,2,1,0:T(8,128)(2,1)S(1)} %join.1.rest_0_), channel_id=1, source_target_pairs={{0,4},{4,0},{8,12},{12,8},{16,20},{20,16},{24,28},{28,24},{1,5},{5... | collective-permute-start | bytes 2359304 | tf_op jit(solution)/shard_map/ppermute | solution.py:47
  63.3 4.0 %collective-permute-start.20 = (bf16[4,448,512]{2,1,0:T(8,128)(2,1)S(1)}, bf16[4,448,512]{2,1,0:T(8,128)(2,1)S(1)}, u32[]{:S(2)}, u32[]{:S(2)}) collective-permute-start(bf16[4,448,512]{2,1,0:T(8,128)(2,1)S(1)} %get-tuple-element.109), channel_id=1, source_target_pairs={{0,4},{4,0},{8,12},{12,8},{16,20},{20,16},{24,28},{28,24},{1,5},{5... | collective-permute-start | bytes 5505032 | tf_op jit(solution)/shard_map/ppermute | solution.py:47
  66.8 12.9 %collective-permute-start.30 = (bf16[4,192,512]{2,1,0:T(8,128)(2,1)S(1)}, bf16[4,192,512]{2,1,0:T(8,128)(2,1)S(1)}, u32[]{:S(2)}, u32[]{:S(2)}) collective-permute-start(bf16[4,192,512]{2,1,0:T(8,128)(2,1)S(1)} %get-tuple-element.125), channel_id=1, source_target_pairs={{0,4},{4,0},{8,12},{12,8},{16,20},{20,16},{24,28},{28,24},{1,5},{5... | collective-permute-start | bytes 2359304 | tf_op jit(solution)/shard_map/ppermute | solution.py:47
  67.7 22.5 %collective-permute-start.25 = (bf16[448,512]{1,0:T(8,128)(2,1)S(1)}, bf16[448,512]{1,0:T(8,128)(2,1)S(1)}, u32[]{:S(2)}, u32[]{:S(2)}) collective-permute-start(bf16[448,512]{1,0:T(8,128)(2,1)S(1)} %get-tuple-element.119), channel_id=1, source_target_pairs={{0,16},{4,20},{8,24},{12,28},{16,0},{20,4},{24,8},{28,12},{1,17},{... | collective-permute-start | bytes 1376264 | tf_op jit(solution)/shard_map/ppermute | solution.py:47
  68.7 22.7 %collective-permute-start.26 = (bf16[448,512]{1,0:T(8,128)(2,1)S(1)}, bf16[448,512]{1,0:T(8,128)(2,1)S(1)}, u32[]{:S(2)}, u32[]{:S(2)}) collective-permute-start(bf16[448,512]{1,0:T(8,128)(2,1)S(1)} %get-tuple-element.110.rest_0_), channel_id=1, source_target_pairs={{0,24},{4,28},{8,16},{12,20},{16,8},{20,12},{24,0},{28,4},{1,25},{... | collective-permute-start | bytes 1376264 | tf_op jit(solution)/shard_map/ppermute | solution.py:47
  69.9 22.5 %collective-permute-start.24 = (bf16[448,512]{1,0:T(8,128)(2,1)S(1)}, bf16[448,512]{1,0:T(8,128)(2,1)S(1)}, u32[]{:S(2)}, u32[]{:S(2)}) collective-permute-start(bf16[448,512]{1,0:T(8,128)(2,1)S(1)} %get-tuple-element.118.tie), channel_id=1, source_target_pairs={{0,8},{4,12},{8,0},{12,4},{16,24},{20,28},{24,16},{28,20},{1,9},{5... | collective-permute-start | bytes 1376264 | tf_op jit(solution)/shard_map/ppermute | solution.py:47
  75.6 7.6 %collective-permute-start.21 = (bf16[177,512]{1,0:T(8,128)(2,1)S(1)}, bf16[177,512]{1,0:T(8,128)(2,1)S(1)}, u32[]{:S(2)}, u32[]{:S(2)}) collective-permute-start(bf16[177,512]{1,0:T(8,128)(2,1)S(1)} %get-tuple-element.112), channel_id=1, source_target_pairs={{0,3},{1,0},{2,1},{3,2},{4,7},{5,4},{6,5},{7,6},{8,11},{9,8},{10,9... | collective-permute-start | bytes 543752 | tf_op jit(solution)/shard_map/ppermute | solution.py:42
  79.8 1.2 collective-permute-start.31
  81.2 19.8 %collective-permute-start.32 = (bf16[224,512]{1,0:T(8,128)(2,1)S(1)}, bf16[224,512]{1,0:T(8,128)(2,1)S(1)}, u32[]{:S(2)}, u32[]{:S(2)}) collective-permute-start(bf16[224,512]{1,0:T(8,128)(2,1)S(1)} %get-tuple-element.129), channel_id=1, source_target_pairs={{0,8},{4,12},{8,0},{12,4},{16,24},{20,28},{24,16},{28,20},{1,9},{5... | collective-permute-start | bytes 688136 | tf_op jit(solution)/shard_map/ppermute | solution.py:47
  83.2 10.9 %collective-permute-start.22 = (bf16[177,512]{1,0:T(8,128)(2,1)S(1)}, bf16[177,512]{1,0:T(8,128)(2,1)S(1)}, u32[]{:S(2)}, u32[]{:S(2)}) collective-permute-start(bf16[177,512]{1,0:T(8,128)(2,1)S(1)} %get-tuple-element.113), channel_id=1, source_target_pairs={{0,2},{1,3},{2,0},{3,1},{4,6},{5,7},{6,4},{7,5},{8,10},{9,11},{10,... | collective-permute-start | bytes 543752 | tf_op jit(solution)/shard_map/ppermute | solution.py:42
  90.1 9.7 %collective-permute-start.23 = (bf16[177,512]{1,0:T(8,128)(2,1)S(1)}, bf16[177,512]{1,0:T(8,128)(2,1)S(1)}, u32[]{:S(2)}, u32[]{:S(2)}) collective-permute-start(bf16[177,512]{1,0:T(8,128)(2,1)S(1)} %get-tuple-element.114), channel_id=1, source_target_pairs={{0,1},{1,2},{2,3},{3,0},{4,5},{5,6},{6,7},{7,4},{8,9},{9,10},{10,1... | collective-permute-start | bytes 543752 | tf_op jit(solution)/shard_map/ppermute | solution.py:42
  91.5 12.1 %collective-permute-start.33 = (bf16[224,512]{1,0:T(8,128)(2,1)S(1)}, bf16[224,512]{1,0:T(8,128)(2,1)S(1)}, u32[]{:S(2)}, u32[]{:S(2)}) collective-permute-start(bf16[224,512]{1,0:T(8,128)(2,1)S(1)} %get-tuple-element.130), channel_id=1, source_target_pairs={{0,16},{4,20},{8,24},{12,28},{16,0},{20,4},{24,8},{28,12},{1,17},{... | collective-permute-start | bytes 688136 | tf_op jit(solution)/shard_map/ppermute | solution.py:47
  92.4 11.1 %collective-permute-start.34 = (bf16[224,512]{1,0:T(8,128)(2,1)S(1)}, bf16[224,512]{1,0:T(8,128)(2,1)S(1)}, u32[]{:S(2)}, u32[]{:S(2)}) collective-permute-start(bf16[224,512]{1,0:T(8,128)(2,1)S(1)} %get-tuple-element.131), channel_id=1, source_target_pairs={{0,24},{4,28},{8,16},{12,20},{16,8},{20,12},{24,0},{28,4},{1,25},{... | collective-permute-start | bytes 688136 | tf_op jit(solution)/shard_map/ppermute | solution.py:47
  94.2 13.1 %collective-permute-start.28 = (bf16[112,512]{1,0:T(8,128)(2,1)S(1)}, bf16[112,512]{1,0:T(8,128)(2,1)S(1)}, u32[]{:S(2)}, u32[]{:S(2)}) collective-permute-start(bf16[112,512]{1,0:T(8,128)(2,1)S(1)} %get-tuple-element.122), channel_id=1, source_target_pairs={{0,2},{1,3},{2,0},{3,1},{4,6},{5,7},{6,4},{7,5},{8,10},{9,11},{10,... | collective-permute-start | bytes 344072 | tf_op jit(solution)/shard_map/ppermute | solution.py:42
  99.8 9.6 %collective-permute-start.29 = (bf16[112,512]{1,0:T(8,128)(2,1)S(1)}, bf16[112,512]{1,0:T(8,128)(2,1)S(1)}, u32[]{:S(2)}, u32[]{:S(2)}) collective-permute-start(bf16[112,512]{1,0:T(8,128)(2,1)S(1)} %get-tuple-element.123), channel_id=1, source_target_pairs={{0,3},{1,0},{2,1},{3,2},{4,7},{5,4},{6,5},{7,6},{8,11},{9,8},{10,9... | collective-permute-start | bytes 344072 | tf_op jit(solution)/shard_map/ppermute | solution.py:42
  101.0 8.4 %collective-permute-start.27 = (bf16[112,512]{1,0:T(8,128)(2,1)S(1)}, bf16[112,512]{1,0:T(8,128)(2,1)S(1)}, u32[]{:S(2)}, u32[]{:S(2)}) collective-permute-start(bf16[112,512]{1,0:T(8,128)(2,1)S(1)} %get-tuple-element.121.tie), channel_id=1, source_target_pairs={{0,1},{1,2},{2,3},{3,0},{4,5},{5,6},{6,7},{7,4},{8,9},{9,10},{10,1... | collective-permute-start | bytes 344072 | tf_op jit(solution)/shard_map/ppermute | solution.py:42
  101.8 27.9 %copy-start.16 = (f32[8004]{0:T(1024)S(1)}, f32[8004]{0:T(1024)}, u32[]{:S(2)}) copy-start(f32[8004]{0:T(1024)} %param.31) | copy-start | bytes 96052
  101.8 27.9 %copy-start.17 = (f32[8004]{0:T(1024)S(1)}, f32[8004]{0:T(1024)}, u32[]{:S(2)}) copy-start(f32[8004]{0:T(1024)} %param.30) | copy-start | bytes 96052
  103.5 26.8 %copy-start.6 = (f32[384,512]{1,0:T(8,128)S(1)}, f32[384,512]{1,0:T(8,128)}, u32[]{:S(2)}) copy-start(f32[384,512]{1,0:T(8,128)} %rest_5_.1) | copy-start | bytes 2359300
  103.7 16.2 %collective-permute-start.35 = (bf16[80,512]{1,0:T(8,128)(2,1)S(1)}, bf16[80,512]{1,0:T(8,128)(2,1)S(1)}, u32[]{:S(2)}, u32[]{:S(2)}) collective-permute-start(bf16[80,512]{1,0:T(8,128)(2,1)S(1)} %get-tuple-element.134), channel_id=1, source_target_pairs={{0,1},{1,2},{2,3},{3,0},{4,5},{5,6},{6,7},{7,4},{8,9},{9,10},{10,1... | collective-permute-start | bytes 245768 | tf_op jit(solution)/shard_map/ppermute | solution.py:42
  103.7 16.2 %collective-permute-start.36 = (bf16[80,512]{1,0:T(8,128)(2,1)S(1)}, bf16[80,512]{1,0:T(8,128)(2,1)S(1)}, u32[]{:S(2)}, u32[]{:S(2)}) collective-permute-start(bf16[80,512]{1,0:T(8,128)(2,1)S(1)} %get-tuple-element.135), channel_id=1, source_target_pairs={{0,2},{1,3},{2,0},{3,1},{4,6},{5,7},{6,4},{7,5},{8,10},{9,11},{10,... | collective-permute-start | bytes 245768 | tf_op jit(solution)/shard_map/ppermute | solution.py:42
  107.3 12.6 %collective-permute-start.37 = (bf16[80,512]{1,0:T(8,128)(2,1)S(1)}, bf16[80,512]{1,0:T(8,128)(2,1)S(1)}, u32[]{:S(2)}, u32[]{:S(2)}) collective-permute-start(bf16[80,512]{1,0:T(8,128)(2,1)S(1)} %get-tuple-element.136), channel_id=1, source_target_pairs={{0,3},{1,0},{2,1},{3,2},{4,7},{5,4},{6,5},{7,6},{8,11},{9,8},{10,9... | collective-permute-start | bytes 245768 | tf_op jit(solution)/shard_map/ppermute | solution.py:42
  109.4 21.0 %copy-start.5 = (f32[384,512]{1,0:T(8,128)S(1)}, f32[384,512]{1,0:T(8,128)}, u32[]{:S(2)}) copy-start(f32[384,512]{1,0:T(8,128)} %rest_4_.1) | copy-start | bytes 2359300
  109.5 20.9 %copy-start.3 = (f32[128,3072]{1,0:T(8,128)S(1)}, f32[128,3072]{1,0:T(8,128)}, u32[]{:S(2)}) copy-start(f32[128,3072]{1,0:T(8,128)} %rest_1_.1) | copy-start | bytes 4718596
  109.5 20.9 %copy-start.4 = (f32[128,3072]{1,0:T(8,128)S(1)}, f32[128,3072]{1,0:T(8,128)}, u32[]{:S(2)}) copy-start(f32[128,3072]{1,0:T(8,128)} %rest_2_.1) | copy-start | bytes 4718596
  109.5 20.9 %copy-start.10 = (f32[81,324]{1,0:T(8,128)S(1)}, f32[81,324]{1,0:T(8,128)}, u32[]{:S(2)}) copy-start(f32[81,324]{1,0:T(8,128)} %rest_7_.1) | copy-start | bytes 314932
  (9 other events, 46.3 us)

commit v5 on v4

--- a/solution.py
+++ b/solution.py
@@ -108,6 +108,17 @@
     return jnp.where(slot == lane, 1.0, 0.0).astype(BF)
 
 
+def side_kernel(scal, slot_ref, m0, m1, m2, m3, xn_ref, tie, pos_ref, xt_ref, turned):
+    place_kernel(slot_ref, m0, m1, m2, m3, pos_ref)
+    own, unit = scal[0], scal[1]
+    turned[...] = xn_ref[...].T
+    for k, (c, y, x, r) in enumerate(ORDER):
+        who = lax.rem(own + r, 4)
+        e = c + 2 * x + 4 * y
+        src = who * 128 + (unit ^ e) * STEP
+        xt_ref[k * STEP : (k + 1) * STEP, :] = turned[pl.ds(aligned(src, STEP), STEP), :]
+
+
 class Copies:
     def __init__(self, sems):
         self.sems, self.all = sems, []
@@ -122,28 +133,24 @@
             copy.wait()
 
 
-def prep_kernel(grid, scal, counts, crops, tok, w_out, mix, m1, m2, m3, tok_own, col_ref, row_ref, held, strip, sems):
-    own, unit = scal[0], scal[1]
+def out_kernel(grid, scal, counts, crops, w_out, mix, msg, col_ref, row_ref, held, strip, sems):
+    unit = scal[1]
     rows = held.shape[0]
-    low = rows + STEP
-    count = tok.shape[1]
     copies = Copies(sems)
     copies.bring(w_out.at[pl.ds(aligned(unit * rows, STEP), rows), :], held)
     slot_kernel(grid, scal, counts, crops, col_ref, row_ref)
     strip[...] = jnp.zeros_like(strip)
     strip[0 : mix.shape[0], 0 : mix.shape[1]] = mix[...].astype(BF)
     copies.wait()
-    for r, msg in enumerate((m1, m2, m3), 1):
-        to = lax.rem(own + r, 4)
-        msg[0:rows, :] = held[...].astype(BF)
-        msg[rows:low, :] = strip[pl.ds(aligned(unit * STEP, STEP), STEP), :]
-        msg[low : low + count, :] = tok[to]
-    tok_own[...] = tok[own]
-
-
-def cot_kernel(scal, cot, tie, c0, c1, c2, c3):
-    for r, out in enumerate((c0, c1, c2, c3)):
-        out[...] = cot[lax.rem(scal[0] + r, 4)]
+    msg[0:rows, :] = held[...].astype(BF)
+    msg[rows:, :] = strip[pl.ds(aligned(unit * STEP, STEP), STEP), :]
+
+
+def rows_kernel(scal, tok, cot, tie, m0, m1, m2, m3):
+    for r, msg in enumerate((m0, m1, m2, m3)):
+        to = lax.rem(scal[0] + r, 4)
+        msg[0:ROWS, :] = tok[to]
+        msg[HALF : HALF + ROWS, :] = cot[to]
 
 
 def hold_kernel(src, tie, dst):
@@ -154,9 +161,13 @@
     stack_kernel(m1, m2, m3, out)
 
 
-def join_kernel(p0, p1, p2, p3, tie, out):
+def join_kernel(p0, p1, p2, p3, out):
     for e, part in enumerate((p0, p1, p2, p3)):
         out[e] = part[...]
+
+
+def join_tied_kernel(p0, p1, p2, p3, tie, out):
+    join_kernel(p0, p1, p2, p3, out)
 
 
 def stack_kernel(m1, m2, m3, out):
@@ -164,26 +175,24 @@
         out[r] = msg[0 : out.shape[1], :]
 
 
-def place(slot_ref, own, others, at, pos_ref):
+def place(slot_ref, blocks, at, pos_ref):
     slot = slot_ref[...]
-    lanes = own.shape[0]
-    total = dot(onehot(slot, lanes, 0), own[...])
-    for r, msg in enumerate(others, 1):
-        total = total + dot(onehot(slot, lanes, r * lanes), msg[at : at + lanes, :])
+    total = None
+    for r, msg in enumerate(blocks):
+        part = dot(onehot(slot, ROWS, r * ROWS), msg[at : at + ROWS, :])
+        total = part if total is None else total + part
     pos_ref[...] = total.astype(BF)
 
 
-def place_kernel(at, slot_ref, own, m1, m2, m3, tie, pos_ref):
-    place(slot_ref, own, (m1, m2, m3), at, pos_ref)
+def place_kernel(slot_ref, m0, m1, m2, m3, pos_ref):
+    place(slot_ref, (m0, m1, m2, m3), HALF, pos_ref)
 
 
 ORDER = [(c, y, x, r) for c in (0, 1) for y in (0, 1) for x in (0, 1) for r in range(4)]
 
 
-def norm_kernel(at, scal, slot_ref, own_blk, m1, m2, m3, gain, shift, pos_ref, xn_ref, xt_ref, turned):
-    place(slot_ref, own_blk, (m1, m2, m3), at, pos_ref)
-    own, unit = scal[0], scal[1]
-
+def norm_kernel(slot_ref, m0, m1, m2, m3, gain, shift, pos_ref, xn_ref):
+    place(slot_ref, (m0, m1, m2, m3), 0, pos_ref)
     @each_tile(pos_ref.shape[0])
     def _(i):
         x = pos_ref[rows_of(i), :].astype(F32)
@@ -191,16 +200,9 @@
         rstd = lax.rsqrt(mean_rows(cen * cen) + EPS)
         xn_ref[rows_of(i), :] = (cen * rstd * gain[...] + shift[...]).astype(BF)
 
-    turned[...] = xn_ref[...].T
-    for k, (c, y, x, r) in enumerate(ORDER):
-        who = lax.rem(own + r, 4)
-        e = c + 2 * x + 4 * y
-        src = who * 128 + (unit ^ e) * STEP
-        xt_ref[k * STEP : (k + 1) * STEP, :] = turned[pl.ds(aligned(src, STEP), STEP), :]
-
 
 def right_kernel(scal, slot_ref, xn_ref, b_in, g_two, s_two, wi_own, *rest):
-    wi, rest = rest[:8], rest[9:]
+    wi, rest = rest[:8], rest[8:]
     win, vhat_ref, rstd_ref, slope_v, vn_ref, pre = rest
     own, unit = scal[0], scal[1]
     n, gate = vhat_ref.shape
@@ -257,13 +259,15 @@
     tiles = gate // LANE
     out_unit = wout.shape[0] // 32
     wout[pl.ds(aligned(own * 8 * out_unit, STEP), 8 * out_unit), :] = wo_own[...].astype(BF)
-    for e in range(8):
-        for r in (1, 2, 3):
-            who = lax.rem(own + (4 - r), 4)
-            at = (who * 8 + (unit ^ e)) * out_unit
-            wout[pl.ds(aligned(at, STEP), out_unit), :] = wo[e % 2][e // 2, r - 1, 0:out_unit, :]
-            at = who * 128 + (unit ^ e) * STEP
-            mixp[pl.ds(aligned(at, STEP), STEP), :] = wo[e % 2][e // 2, r - 1, out_unit:, :]
+    for k in range(4):
+        for c in (0, 1):
+            piece = 2 * k + ((unit & 1) ^ c)
+            for r in (1, 2, 3):
+                who = lax.rem(own + (4 - r), 4)
+                at = (who * 8 + piece) * out_unit
+                wout[pl.ds(aligned(at, STEP), out_unit), :] = wo[c][k, r - 1, 0:out_unit, :]
+                at = who * 128 + piece * STEP
+                mixp[pl.ds(aligned(at, STEP), STEP), :] = wo[c][k, r - 1, out_unit:, :]
     per, cells = mix_own.shape
     mine = aligned(own * 128, 128)
     mixp[pl.ds(mine, 128), :] = jnp.zeros((128, LANE), BF)
@@ -401,19 +405,12 @@
     vec[at + 1 : at + 2, :] = jnp.where(lane < cells, last, 0.0)
 
 
-def split_low(v):
-    high = v.astype(BF)
-    return high, (v - high.astype(F32)).astype(BF)
-
-
 def put_vec(ref, at, v):
-    high, low = split_low(v)
-    ref[at : at + STEP, :] = high
-    ref[at + STEP : at + 2 * STEP, :] = low
+    ref[at : at + STEP, :] = v.astype(BF)
 
 
 def get_vec(ref, at):
-    return ref[at : at + STEP, :].astype(F32) + ref[at + STEP : at + 2 * STEP, :].astype(F32)
+    return ref[at : at + STEP, :].astype(F32)
 
 
 def core_kernel(keep, got, own, s1, s2, s3):
@@ -588,46 +585,50 @@
 
     def over_plane(base):
         near = swap(base, XBIT)
-        chips = [base, near, swap(base, YBIT), swap(near, YBIT)]
-        found = []
-        for arr in chips:
-            found += [arr, swap(arr, CORE)]
-        return found
+        return [base, near, swap(base, YBIT), swap(near, YBIT)]
 
     wi_piece = lax.dynamic_slice_in_dim(in_weight, unit * in_unit, in_unit, 0).astype(BF)
 
-    blk = ((row_count, width), BF)
-    msg = ((low + row_count, width), BF)
-    m1, m2, m3, tok_own, slot_col, slot_row = call(
-        functools.partial(prep_kernel, grid),
-        [scal, patch_count.reshape(1, 4), crop_index, tokens.reshape(4, row_count, width), out_weight, spatial_weight],
-        [msg, msg, msg, blk, ((n, 1), I32), ((1, n), I32)],
+    msg, slot_col, slot_row = call(
+        functools.partial(out_kernel, grid),
+        [scal, patch_count.reshape(1, 4), crop_index, out_weight, spatial_weight],
+        [((low, LANE), BF), ((n, 1), I32), ((1, n), I32)],
         [pltpu.VMEM((out_unit, width), F32), pltpu.VMEM((128, LANE), BF), pltpu.SemaphoreType.DMA((1,))],
-        specs=[SM, VM, VM, VM, ANY, VM],
+        specs=[SM, VM, VM, ANY, VM],
         limit=8,
-        name="prep",
+        name="prep_out",
     )
     (base_in,) = call(
         stack_tied_kernel,
-        [turn(wi_piece, r) for r in (1, 2, 3)] + [m1],
+        [turn(wi_piece, r) for r in (1, 2, 3)] + [msg],
         [((3, in_unit, hidden), BF)],
         specs=[VM] * 3 + [ANY],
         limit=8,
         name="stack_i",
     )
-    wi = over_plane(base_in)
-    got = [turn(m, r) for r, m in enumerate((m1, m2, m3), 1)]
-    (base,) = call(stack_tied_kernel, [*got, wi[2]], [((3, low, LANE), BF)], specs=[VM] * 3 + [ANY], limit=8, name="stack_o")
-    cot = call(
-        cot_kernel,
-        [scal, cotangent.reshape(4, row_count, width), base],
-        [blk] * 4,
-        specs=[SM, VM, ANY],
+    plane_in = over_plane(base_in)
+    wi = [arr for part in plane_in for arr in (part, swap(part, CORE))]
+    (base,) = call(
+        stack_tied_kernel,
+        [turn(msg, r) for r in (1, 2, 3)] + [base_in],
+        [((3, low, LANE), BF)],
+        specs=[VM] * 3 + [ANY],
         limit=8,
-        name="prep_cot",
-    )
-    cot = [cot[0]] + [turn(c, r) for r, c in enumerate(cot[1:], 1)]
-    plane_out = [base] + [swap(base, m) for m in (2, 4, 6)]
+        name="stack_o",
+    )
+    got = call(
+        rows_kernel,
+        [scal, tokens.reshape(4, row_count, width), cotangent.reshape(4, row_count, width), base],
+        [((HALF + row_count, width), BF)] * 4,
+        specs=[SM, VM, VM, ANY],
+        limit=8,
+        name="prep_rows",
+    )
+    got = [got[0]] + [turn(m, r) for r, m in enumerate(got[1:], 1)]
+    (held,) = call(hold_kernel, [base, plane_in[2]], [((3, low, LANE), BF)], specs=[VM, ANY], limit=8, name="hold_out")
+    planes = [[8 * g + c + 2 * k for k in range(4)] for g in range(lax.axis_size("img") // 8) for c in (0, 1)]
+    joined = lax.all_gather(held, "img", axis_index_groups=planes)
+    joined_got = swap(joined, CORE)
 
     bounds = [width, width, hidden, gate, gate, cells, width]
     pieces = []
@@ -638,38 +639,34 @@
     g_one, s_one, b_in, g_two, s_two, b_mix, b_out = pieces
     b_mix = jnp.pad(b_mix[0], (0, n - cells))[:, None]
 
-    pos, xn, xt = call(
-        functools.partial(norm_kernel, low),
-        [scal, slot_col, tok_own, *got, g_one, s_one],
-        [((n, width), BF), ((n, width), BF), ((width, n), BF)],
-        [pltpu.VMEM((width, n), BF)],
-        specs=[SM] + [VM] * 7,
+    pos, xn = call(
+        norm_kernel,
+        [slot_col, *got, g_one, s_one],
+        [((n, width), BF), ((n, width), BF)],
         name="norm_in",
     )
     sized = lambda kind: ((n, gate), kind)
-    (cot_pos,) = call(
-        functools.partial(place_kernel, 0),
-        [slot_col, *cot, xn],
-        [((n, width), BF)],
-        specs=[VM] * 5 + [ANY],
-        name="place_cot",
-    )
     win, vhat, rstd, slope_v, vn = call(
         right_kernel,
-        [scal, slot_col, xn, b_in, g_two, s_two, in_weight, *wi, cot_pos],
+        [scal, slot_col, xn, b_in, g_two, s_two, in_weight, *wi],
         [((width, hidden), BF), sized(F32), ((n, 1), F32), sized(F32), sized(BF)],
         [pltpu.VMEM((n, gate), F32)],
-        specs=[SM] + [VM] * 14 + [ANY],
+        specs=[SM] + [VM] * 14,
         flops=1_500_000_000,
         limit=20,
         name="right",
     )
-    (joined,) = call(
-        join_kernel, [*plane_out, vn], [((4, 3, low, LANE), BF)], specs=[VM] * 4 + [ANY], limit=8, name="join"
+    cot_pos, xt = call(
+        side_kernel,
+        [scal, slot_col, *got, xn, vn],
+        [((n, width), BF), ((width, n), BF)],
+        [pltpu.VMEM((width, n), BF)],
+        specs=[SM] + [VM] * 6 + [ANY],
+        name="place_cot",
     )
     u, slope_u = call(
         left_kernel,
-        [xn, b_in, win, joined],
+        [xn, b_in, win, joined_got],
         [sized(F32), sized(F32)],
         [pltpu.VMEM((n, gate), F32)],
         specs=[VM] * 3 + [ANY],
@@ -680,7 +677,7 @@
     packed = ((4, 4 * (low + side_rows), LANE), BF)
     mix, pre_u, sg, gated, wout, keep_a, send_a = call(
         spatial_kernel,
-        [scal, xt, cot_pos, u, slope_u, vn, b_mix, spatial_weight, out_weight, joined, swap(joined, CORE)],
+        [scal, xt, cot_pos, u, slope_u, vn, b_mix, spatial_weight, out_weight, joined, joined_got],
         [((n, n), BF), sized(BF), sized(BF), sized(BF), ((gate, width), BF), packed, packed],
         [
             pltpu.VMEM((512, LANE), BF),
@@ -729,7 +726,7 @@
     own_b, *send_b, vec_own = call(
         core_vec_kernel,
         [keep_b, core_b, vec, vec_got, send_a[0]],
-        [((rows_b4, LANE), F32)] + [((rows_b4 + 2 * STEP, LANE), BF)] * 3 + [((2 * STEP, LANE), BF)],
+        [((rows_b4, LANE), F32)] + [((rows_b4 + STEP, LANE), BF)] * 3 + [((STEP, LANE), BF)],
         specs=[VM] * 4 + [ANY],
         name="core_b",
     )
@@ -752,7 +749,7 @@
     own_b, *patch_b, vec_own = call(
         plane_vec_kernel,
         [own_b, vec_own, *plane_b, patch_a[0]],
-        [((side_rows, LANE), F32)] + [((side_rows + 2 * STEP, LANE), BF)] * 3 + [((2 * STEP, LANE), BF)],
+        [((side_rows, LANE), F32)] + [((side_rows + STEP, LANE), BF)] * 3 + [((STEP, LANE), BF)],
         specs=[VM] * 5 + [ANY],
         name="plane_b",
     )

time: 135 us -> 131 us (0.970)
  blocking collectives: 19.6 us -> 33.3 us
  starting transfers between devices: 48.5 us -> 39.7 us
  waiting for transfers between devices: 29.5 us -> 20.8 us
    all_gather x0 -> x1, blocking collectives: none -> 13.8 us  [shards(): joined = lax.all_gather(held, 'img', axis_index_groups=planes)]
    ppermute x18, waiting for transfers between devices: 17.9 us -> 11.3 us  [turn(): return lax.ppermute(arr, 'patch', [(s, (s + r) % n) for s in range(n)])]
    ppermute x18, starting transfers between devices: 32.2 us -> 26.3 us  [turn(): return lax.ppermute(arr, 'patch', [(s, (s + r) % n) for s in range(n)])]
    ppermute x20 -> x17, starting transfers between devices: 16.3 us -> 13.4 us  [swap(): return lax.ppermute(arr, 'img', [(k, k ^ mask) for k in range(n)])]
    ppermute x20 -> x17, waiting for transfers between devices: 11.5 us -> 9.51 us  [swap(): return lax.ppermute(arr, 'img', [(k, k ^ mask) for k in range(n)])]
    unnamed x39 -> x35, local copies, waits for them, and re-layouts: 4.56 us -> 3.46 us
  transfers between devices with their start and end apart: 38 -> 35, of which waited for: 12 -> 11; matrix products, arithmetic and copies ran while one was open for 1% -> 1% of each run, Pallas kernels for 15% -> 14%
where the time goes in v5:
time: 131 us; the launch traced here: 130 us
  starting transfers between devices  39.7 us (30%)
  blocking collectives  33.3 us (25%)
  Pallas kernels  28.5 us (22%)
  waiting for transfers between devices  20.8 us (16%)
  local copies, waits for them, and re-layouts  5.81 us (4%)
    pallas_call x20, Pallas kernels, call(): pl.pallas_call(body, out_shape=[jax.ShapeDtypeStruct(s, d) for s, d in ou...  28.5 us
    ppermute x18, starting transfers between devices, turn(): return lax.ppermute(arr, 'patch', [(s, (s + r) % n) for s in range(n)])  26.3 us
    all_gather x2, blocking collectives, img_gather(): return lax.all_gather(arr, 'img', axis_index_groups=groups)  19.6 us
    all_gather x1, blocking collectives, shards(): joined = lax.all_gather(held, 'img', axis_index_groups=planes)  13.8 us
    ppermute x17, starting transfers between devices, swap(): return lax.ppermute(arr, 'img', [(k, k ^ mask) for k in range(n)])  13.4 us
    ppermute x18, waiting for transfers between devices, turn(): return lax.ppermute(arr, 'patch', [(s, (s + r) % n) for s in range(n)])  11.3 us
    ppermute x17, waiting for transfers between devices, swap(): return lax.ppermute(arr, 'img', [(k, k ^ mask) for k in range(n)])  9.51 us
    unnamed x35, local copies, waits for them, and re-layouts  3.46 us
  transfers between devices with their start and end apart: 35, of which 11 were waited for; matrix products, arithmetic and copies ran while one was open for 1% of the time, Pallas kernels for 14%

profile of v5, /device:TPU:0, one launch (start us, length us, event | category | flops | bytes accessed | tf_op | source)
XLA Modules:
  0.0 130.1 jit_solution(11122178817751361159)
XLA Ops:
  0.7 0.9 dynamic-slice_convert_fusion
  1.6 5.1 %collective-permute-start.5 = (bf16[16,3072]{1,0:T(8,128)(2,1)S(1)}, bf16[16,3072]{1,0:T(8,128)(2,1)S(1)}, u32[]{:S(2)}, u32[]{:S(2)}) collective-permute-start(bf16[16,3072]{1,0:T(8,128)(2,1)S(1)} %dynamic-slice_convert_fusion), channel_id=1, source_target_pairs={{0,3},{1,0},{2,1},{3,2},{4,7},{5,4},{6,5},{7,6},{8,11},{9,8},{10,9... | collective-permute-start | bytes 294920 | tf_op jit(solution)/shard_map/ppermute | solution.py:42
  6.7 1.0 collective-permute-start.3
  7.8 1.1 copy-done
  8.9 0.9 copy-done.8
  9.8 0.7 copy-done.12
  10.5 0.7 copy-done.13
  11.2 1.0 prep_out.1
  12.2 3.3 %collective-permute-done.4.m2 = bf16[16,3072]{1,0:T(8,128)(2,1)S(1)} collective-permute-done((bf16[16,3072]{1,0:T(8,128)(2,1)S(1)}, bf16[16,3072]{1,0:T(8,128)(2,1)S(1)}, u32[]{:S(2)}, u32[]{:S(2)}) %collective-permute-start.4) | collective-permute-done | bytes 98336 | tf_op jit(solution)/shard_map/ppermute | solution.py:42
  15.5 1.6 %collective-permute-start.12 = (bf16[3,16,3072]{2,1,0:T(8,128)(2,1)S(1)}, bf16[3,16,3072]{2,1,0:T(8,128)(2,1)S(1)}, u32[]{:S(2)}, u32[]{:S(2)}) collective-permute-start(bf16[3,16,3072]{2,1,0:T(8,128)(2,1)S(1)} %stack_i.1.tie.rest_0_), channel_id=1, source_target_pairs={{0,16},{4,20},{8,24},{12,28},{16,0},{20,4},{24,8},{28,12},{1,17},{... | collective-permute-start | bytes 884744 | tf_op jit(solution)/shard_map/ppermute | solution.py:47
  17.1 1.5 %collective-permute-start.10 = (bf16[3,16,3072]{2,1,0:T(8,128)(2,1)S(1)}, bf16[3,16,3072]{2,1,0:T(8,128)(2,1)S(1)}, u32[]{:S(2)}, u32[]{:S(2)}) collective-permute-start(bf16[3,16,3072]{2,1,0:T(8,128)(2,1)S(1)} %stack_i.1.tie.rest_0_), channel_id=1, source_target_pairs={{0,8},{4,12},{8,0},{12,4},{16,24},{20,28},{24,16},{28,20},{1,9},{5... | collective-permute-start | bytes 884744 | tf_op jit(solution)/shard_map/ppermute | solution.py:47
  18.6 1.9 %collective-permute-start.2 = (bf16[64,512]{1,0:T(8,128)(2,1)S(1)}, bf16[64,512]{1,0:T(8,128)(2,1)S(1)}, u32[]{:S(2)}, u32[]{:S(2)}) collective-permute-start(bf16[64,512]{1,0:T(8,128)(2,1)S(1)} %get-tuple-element.81.tie), channel_id=1, source_target_pairs={{0,3},{1,0},{2,1},{3,2},{4,7},{5,4},{6,5},{7,6},{8,11},{9,8},{10,9... | collective-permute-start | bytes 196616 | tf_op jit(solution)/shard_map/ppermute | solution.py:42
  20.8 2.0 %collective-permute-start = (bf16[64,512]{1,0:T(8,128)(2,1)S(1)}, bf16[64,512]{1,0:T(8,128)(2,1)S(1)}, u32[]{:S(2)}, u32[]{:S(2)}) collective-permute-start(bf16[64,512]{1,0:T(8,128)(2,1)S(1)} %get-tuple-element.81.tie), channel_id=1, source_target_pairs={{0,1},{1,2},{2,3},{3,0},{4,5},{5,6},{6,7},{7,4},{8,9},{9,10},{10,1... | collective-permute-start | bytes 196616 | tf_op jit(solution)/shard_map/ppermute | solution.py:42
  22.9 1.2 copy_bitcast_fusion
  24.1 3.0 %collective-permute-done.1.m2 = bf16[64,512]{1,0:T(8,128)(2,1)S(1)} collective-permute-done((bf16[64,512]{1,0:T(8,128)(2,1)S(1)}, bf16[64,512]{1,0:T(8,128)(2,1)S(1)}, u32[]{:S(2)}, u32[]{:S(2)}) %collective-permute-start.1) | collective-permute-done | bytes 65568 | tf_op jit(solution)/shard_map/ppermute | solution.py:42
  27.1 0.6 prep_rows.1
  27.8 1.6 %collective-permute-start.7 = (bf16[177,512]{1,0:T(8,128)(2,1)S(1)}, bf16[177,512]{1,0:T(8,128)(2,1)S(1)}, u32[]{:S(2)}, u32[]{:S(2)}) collective-permute-start(bf16[177,512]{1,0:T(8,128)(2,1)S(1)} %get-tuple-element.84), channel_id=1, source_target_pairs={{0,2},{1,3},{2,0},{3,1},{4,6},{5,7},{6,4},{7,5},{8,10},{9,11},{10,... | collective-permute-start | bytes 543752 | tf_op jit(solution)/shard_map/ppermute | solution.py:42
  29.4 2.2 %collective-permute-start.8 = (bf16[177,512]{1,0:T(8,128)(2,1)S(1)}, bf16[177,512]{1,0:T(8,128)(2,1)S(1)}, u32[]{:S(2)}, u32[]{:S(2)}) collective-permute-start(bf16[177,512]{1,0:T(8,128)(2,1)S(1)} %get-tuple-element.85), channel_id=1, source_target_pairs={{0,3},{1,0},{2,1},{3,2},{4,7},{5,4},{6,5},{7,6},{8,11},{9,8},{10,9... | collective-permute-start | bytes 543752 | tf_op jit(solution)/shard_map/ppermute | solution.py:42
  32.2 13.8 %all-gather = bf16[12,64,512]{2,1,0:T(8,128)(2,1)S(1)} all-gather(bf16[3,64,512]{2,1,0:T(8,128)(2,1)S(1)} %hold_out.1), channel_id=2, replica_groups={{0,8,16,24},{4,12,20,28},{1,9,17,25},{5,13,21,29},{2,10,18,26},{6,14,22..., dimensions={0}, use_global_device_ids=true | all-gather | bytes 983040 | tf_op jit(solution)/shard_map/all_gather | solution.py:630
  47.4 1.4 %norm_in.1 = (bf16[336,512]{1,0:T(8,128)(2,1)S(1)}, bf16[336,512]{1,0:T(8,128)(2,1)S(1)}) custom-call(s32[336,1]{1,0:T(8,128)S(1)} %get-tuple-element.79.slot_ref, bf16[177,512]{1,0:T(8,128)(2,1)S(1)} %get-tuple-element.82.m0, bf16[177,512]{1,0:T(8,128)(2,1)S(1)} %collective-permute-done.6.m1, bf16[177,512]{1,0:T(8,128)(2,1)S(1)} %collective-permute-done.7.m2, ...), custom_call_target="tpu_custom_call" | custom-call | flops 100000000 | bytes 730432 | tf_op jit(solution)/shard_map/norm_in/pallas_call | solution.py:526
  50.0 3.1 %right.1 = (bf16[512,3072]{1,0:T(8,128)(2,1)S(1)}, f32[336,1536]{1,0:T(8,128)S(1)}, f32[336,1]{1,0:T(8,128)S(1)}, f32[336,1536]{1,0:T(8,128)S(1)}, bf16[336,1536]{1,0:T(8,128)(2,1)S(1)}) custom-call(s32[2]{0:T(128)S(1)} %pad_add_fusion.scal, s32[336,1]{1,0:T(8,128)S(1)} %get-tuple-element.79.slot_ref, bf16[336,512]{1,0:T(8,128)(2,1)S(1)} %get-tuple-element.87.xn_ref, ...), custom_call_target="tpu_custom_call" | custom-call | flops 1500000000 | bytes 4302152 | tf_op jit(solution)/shard_map/right/pallas_call | solution.py:526
  53.1 1.1 place_cot.1
  54.2 1.7 %left.1 = (f32[336,1536]{1,0:T(8,128)S(1)}, f32[336,1536]{1,0:T(8,128)S(1)}) custom-call(bf16[336,512]{1,0:T(8,128)(2,1)S(1)} %get-tuple-element.87.xn_ref, f32[1,3072]{1,0:T(1,128)S(1)} %bitcast.27, bf16[512,3072]{1,0:T(8,128)(2,1)S(1)} %get-tuple-element.90.win, bf16[4,3,64,512]{3,2,1,0:T(8,128)(2,1)S(1)} %collective-permute-done.16.rest_0_.rest_1_), custom_call_target="tpu_custom_call" | custom-call | flops 1000000000 | bytes 4288512 | tf_op jit(solution)/shard_map/left/pallas_call | solution.py:526
  56.0 5.2 %spatial.1 = (bf16[336,336]{1,0:T(8,128)(2,1)S(1)}, bf16[336,1536]{1,0:T(8,128)(2,1)S(1)}, bf16[336,1536]{1,0:T(8,128)(2,1)S(1)}, bf16[336,1536]{1,0:T(8,128)(2,...) custom-call(s32[2]{0:T(128)S(1)} %pad_add_fusion.scal, ...), custom_call_target="tpu_custom_call" | custom-call | flops 4000000000 | bytes 8314712 | tf_op jit(solution)/shard_map/spatial/pallas_call | solution.py:526
  61.4 3.3 %back.1 = (bf16[336,1536]{1,0:T(8,128)(2,1)S(1)}, bf16[4,192,512]{2,1,0:T(8,128)(2,1)S(1)}, bf16[4,192,512]{2,1,0:T(8,128)(2,1)S(1)}, f32[6,512]{1,0:T(8,128)S(1)}) custom-call(s32[336,1]{1,0:T(8,128)S(1)} %get-tuple-element.79.slot_ref, bf16[512,336]{1,0:T(8,128)(2,1)S(1)} %get-tuple-element.91.xt_ref, bf16[336,336]{1,0:T(8,128)(2,1)S(1)} %get-tuple-element.95.mix_ref, ...), custom_call_target="tpu_custom_call" | custom-call | flops 2000000000 | bytes 5739648 | tf_op jit(solution)/shard_map/back/pallas_call | solution.py:526
  65.6 1.6 %collective-permute-start.22 = (bf16[448,512]{1,0:T(8,128)(2,1)S(1)}, bf16[448,512]{1,0:T(8,128)(2,1)S(1)}, u32[]{:S(2)}, u32[]{:S(2)}) collective-permute-start(bf16[448,512]{1,0:T(8,128)(2,1)S(1)} %get-tuple-element.115), channel_id=1, source_target_pairs={{0,16},{4,20},{8,24},{12,28},{16,0},{20,4},{24,8},{28,12},{1,17},{... | collective-permute-start | bytes 1376264 | tf_op jit(solution)/shard_map/ppermute | solution.py:47
  67.1 1.5 %collective-permute-start.23 = (bf16[448,512]{1,0:T(8,128)(2,1)S(1)}, bf16[448,512]{1,0:T(8,128)(2,1)S(1)}, u32[]{:S(2)}, u32[]{:S(2)}) collective-permute-start(bf16[448,512]{1,0:T(8,128)(2,1)S(1)} %get-tuple-element.106.rest_0_), channel_id=1, source_target_pairs={{0,24},{4,28},{8,16},{12,20},{16,8},{20,12},{24,0},{28,4},{1,25},{... | collective-permute-start | bytes 1376264 | tf_op jit(solution)/shard_map/ppermute | solution.py:47
  69.1 4.4 %token_grad.1 = (bf16[177,512]{1,0:T(8,128)(2,1)S(1)}, bf16[177,512]{1,0:T(8,128)(2,1)S(1)}, bf16[177,512]{1,0:T(8,128)(2,1)S(1)}, bf16[177,512]{1,0:T(8,128)(2,1)S(1)}, f32[16,512]{1,0:T(8,128)S(1)}) custom-call(s32[336,1]{1,0:T(8,128)S(1)} %get-tuple-element.79.slot_ref, s32[1,336]{1,0:T(1,128)S(1)} %get-tuple-element.80.slot_row, ...), custom_call_target="tpu_custom_call" | custom-call | flops 2000000000 | bytes 10013312 | tf_op jit(solution)/shard_map/token_grad/pallas_call | solution.py:526
  73.5 0.7 collective-permute-start.18
  74.2 1.2 collective-permute-done.28.vec_got
  75.6 1.5 %collective-permute-start.29 = (bf16[208,512]{1,0:T(8,128)(2,1)S(1)}, bf16[208,512]{1,0:T(8,128)(2,1)S(1)}, u32[]{:S(2)}, u32[]{:S(2)}) collective-permute-start(bf16[208,512]{1,0:T(8,128)(2,1)S(1)} %get-tuple-element.125), channel_id=1, source_target_pairs={{0,8},{4,12},{8,0},{12,4},{16,24},{20,28},{24,16},{28,20},{1,9},{5... | collective-permute-start | bytes 638984 | tf_op jit(solution)/shard_map/ppermute | solution.py:47
  77.1 2.4 %collective-permute-done.18.h1 = bf16[177,512]{1,0:T(8,128)(2,1)S(1)} collective-permute-done((bf16[177,512]{1,0:T(8,128)(2,1)S(1)}, bf16[177,512]{1,0:T(8,128)(2,1)S(1)}, u32[]{:S(2)}, u32[]{:S(2)}) %collective-permute-start.18) | collective-permute-done | bytes 181280 | tf_op jit(solution)/shard_map/ppermute | solution.py:42
  79.5 1.8 %collective-permute-start.19 = (bf16[177,512]{1,0:T(8,128)(2,1)S(1)}, bf16[177,512]{1,0:T(8,128)(2,1)S(1)}, u32[]{:S(2)}, u32[]{:S(2)}) collective-permute-start(bf16[177,512]{1,0:T(8,128)(2,1)S(1)} %get-tuple-element.109), channel_id=1, source_target_pairs={{0,2},{1,3},{2,0},{3,1},{4,6},{5,7},{6,4},{7,5},{8,10},{9,11},{10,... | collective-permute-start | bytes 543752 | tf_op jit(solution)/shard_map/ppermute | solution.py:42
  81.2 6.8 %collective-permute-done.22.g2 = bf16[448,512]{1,0:T(8,128)(2,1)S(1)} collective-permute-done((bf16[448,512]{1,0:T(8,128)(2,1)S(1)}, bf16[448,512]{1,0:T(8,128)(2,1)S(1)}, u32[]{:S(2)}, u32[]{:S(2)}) %collective-permute-start.22) | collective-permute-done | bytes 458784 | tf_op jit(solution)/shard_map/ppermute | solution.py:47
  88.6 1.5 %collective-permute-start.30 = (bf16[208,512]{1,0:T(8,128)(2,1)S(1)}, bf16[208,512]{1,0:T(8,128)(2,1)S(1)}, u32[]{:S(2)}, u32[]{:S(2)}) collective-permute-start(bf16[208,512]{1,0:T(8,128)(2,1)S(1)} %get-tuple-element.126), channel_id=1, source_target_pairs={{0,16},{4,20},{8,24},{12,28},{16,0},{20,4},{24,8},{28,12},{1,17},{... | collective-permute-start | bytes 638984 | tf_op jit(solution)/shard_map/ppermute | solution.py:47
  90.3 1.5 %collective-permute-start.31 = (bf16[208,512]{1,0:T(8,128)(2,1)S(1)}, bf16[208,512]{1,0:T(8,128)(2,1)S(1)}, u32[]{:S(2)}, u32[]{:S(2)}) collective-permute-start(bf16[208,512]{1,0:T(8,128)(2,1)S(1)} %get-tuple-element.127), channel_id=1, source_target_pairs={{0,24},{4,28},{8,16},{12,20},{16,8},{20,12},{24,0},{28,4},{1,25},{... | collective-permute-start | bytes 638984 | tf_op jit(solution)/shard_map/ppermute | solution.py:47
  92.0 1.9 %collective-permute-start.25 = (bf16[112,512]{1,0:T(8,128)(2,1)S(1)}, bf16[112,512]{1,0:T(8,128)(2,1)S(1)}, u32[]{:S(2)}, u32[]{:S(2)}) collective-permute-start(bf16[112,512]{1,0:T(8,128)(2,1)S(1)} %get-tuple-element.118), channel_id=1, source_target_pairs={{0,2},{1,3},{2,0},{3,1},{4,6},{5,7},{6,4},{7,5},{8,10},{9,11},{10,... | collective-permute-start | bytes 344072 | tf_op jit(solution)/shard_map/ppermute | solution.py:42
  93.9 2.6 %collective-permute-done.20.h3 = bf16[177,512]{1,0:T(8,128)(2,1)S(1)} collective-permute-done((bf16[177,512]{1,0:T(8,128)(2,1)S(1)}, bf16[177,512]{1,0:T(8,128)(2,1)S(1)}, u32[]{:S(2)}, u32[]{:S(2)}) %collective-permute-start.20) | collective-permute-done | bytes 181280 | tf_op jit(solution)/shard_map/ppermute | solution.py:42
  96.5 2.0 %collective-permute-start.24 = (bf16[112,512]{1,0:T(8,128)(2,1)S(1)}, bf16[112,512]{1,0:T(8,128)(2,1)S(1)}, u32[]{:S(2)}, u32[]{:S(2)}) collective-permute-start(bf16[112,512]{1,0:T(8,128)(2,1)S(1)} %get-tuple-element.117.tie), channel_id=1, source_target_pairs={{0,1},{1,2},{2,3},{3,0},{4,5},{5,6},{6,7},{7,4},{8,9},{9,10},{10,1... | collective-permute-start | bytes 344072 | tf_op jit(solution)/shard_map/ppermute | solution.py:42
  98.5 1.7 %home.1 = (bf16[81,4,512]{2,1,0:T(4,128)(2,1)}, f32[4,81,1,512]{3,2,1,0:T(1,128)}) custom-call(s32[2]{0:T(128)S(1)} %pad_add_fusion.scal, bf16[177,512]{1,0:T(8,128)(2,1)S(1)} %get-tuple-element.107.h0, bf16[177,512]{1,0:T(8,128)(2,1)S(1)} %collective-permute-done.18.h1, bf16[177,512]{1,0:T(8,128)(2,1)S(1)} %collective-permute-done.19.h2, ...), custom_call_target="tpu_custom_call" | custom-call | flops 100000000 | bytes 725000 | tf_op jit(solution)/shard_map/home/pallas_call | solution.py:526
  100.4 0.9 collective-permute-start.32
  101.3 2.1 %collective-permute-start.33 = (bf16[64,512]{1,0:T(8,128)(2,1)S(1)}, bf16[64,512]{1,0:T(8,128)(2,1)S(1)}, u32[]{:S(2)}, u32[]{:S(2)}) collective-permute-start(bf16[64,512]{1,0:T(8,128)(2,1)S(1)} %get-tuple-element.131), channel_id=1, source_target_pairs={{0,2},{1,3},{2,0},{3,1},{4,6},{5,7},{6,4},{7,5},{8,10},{9,11},{10,... | collective-permute-start | bytes 196616 | tf_op jit(solution)/shard_map/ppermute | solution.py:42
  103.3 2.2 %collective-permute-start.34 = (bf16[64,512]{1,0:T(8,128)(2,1)S(1)}, bf16[64,512]{1,0:T(8,128)(2,1)S(1)}, u32[]{:S(2)}, u32[]{:S(2)}) collective-permute-start(bf16[64,512]{1,0:T(8,128)(2,1)S(1)} %get-tuple-element.132), channel_id=1, source_target_pairs={{0,3},{1,0},{2,1},{3,2},{4,7},{5,4},{6,5},{7,6},{8,11},{9,8},{10,9... | collective-permute-start | bytes 196616 | tf_op jit(solution)/shard_map/ppermute | solution.py:42
  105.7 10.8 %all-gather.1 = bf16[896,512]{1,0:T(8,128)(2,1)S(1)} all-gather(bf16[112,512]{1,0:T(8,128)(2,1)S(1)} %patch_a.1), channel_id=3, replica_groups={{0,4,8,12,16,20,24,28},{1,5,9,13,17,21,25,29},{2,6,10,14,18,22,26,30},{..., dimensions={0}, use_global_device_ids=true | all-gather | bytes 1032192 | tf_op jit(solution)/shard_map/all_gather | solution.py:549
  116.5 0.6 patch_b.1
  117.1 8.8 %all-gather.2 = bf16[384,512]{1,0:T(8,128)(2,1)S(1)} all-gather(bf16[48,512]{1,0:T(8,128)(2,1)S(1)} %get-tuple-element.133), channel_id=4, replica_groups={{0,4,8,12,16,20,24,28},{1,5,9,13,17,21,25,29},{2,6,10,14,18,22,26,30},{..., dimensions={0}, use_global_device_ids=true | all-gather | bytes 442368 | tf_op jit(solution)/shard_map/all_gather | solution.py:549
  125.9 0.6 multiply_add_fusion
  126.5 3.4 %update.1 = (f32[128,3072]{1,0:T(8,128)}, f32[128,3072]{1,0:T(8,128)}, f32[128,3072]{1,0:T(8,128)}, f32[384,512]{1,0:T(8,128)}, f32[384,512]{1,0:T(8,128)}, /*in...) custom-call(bf16[8,112,512]{2,1,0:T(8,128)(2,1)S(1)} %bitcast.21, ...), custom_call_target="tpu_custom_call" | custom-call | flops 100000000 | bytes 8703536 | tf_op jit(solution)/shard_map/update/pallas_call | solution.py:526
  (93 shorter events, 6.8 us)
Async XLA Ops:
  1.6 10.6 %collective-permute-start.5 = (bf16[16,3072]{1,0:T(8,128)(2,1)S(1)}, bf16[16,3072]{1,0:T(8,128)(2,1)S(1)}, u32[]{:S(2)}, u32[]{:S(2)}) collective-permute-start(bf16[16,3072]{1,0:T(8,128)(2,1)S(1)} %dynamic-slice_convert_fusion), channel_id=1, source_target_pairs={{0,3},{1,0},{2,1},{3,2},{4,7},{5,4},{6,5},{7,6},{8,11},{9,8},{10,9... | collective-permute-start | bytes 294920 | tf_op jit(solution)/shard_map/ppermute | solution.py:42
  6.7 8.7 %collective-permute-start.4 = (bf16[16,3072]{1,0:T(8,128)(2,1)S(1)}, bf16[16,3072]{1,0:T(8,128)(2,1)S(1)}, u32[]{:S(2)}, u32[]{:S(2)}) collective-permute-start(bf16[16,3072]{1,0:T(8,128)(2,1)S(1)} %dynamic-slice_convert_fusion), channel_id=1, source_target_pairs={{0,2},{1,3},{2,0},{3,1},{4,6},{5,7},{6,4},{7,5},{8,10},{9,11},{10,... | collective-permute-start | bytes 294920 | tf_op jit(solution)/shard_map/ppermute | solution.py:42
  6.7 8.7 %collective-permute-start.3 = (bf16[16,3072]{1,0:T(8,128)(2,1)S(1)}, bf16[16,3072]{1,0:T(8,128)(2,1)S(1)}, u32[]{:S(2)}, u32[]{:S(2)}) collective-permute-start(bf16[16,3072]{1,0:T(8,128)(2,1)S(1)} %dynamic-slice_convert_fusion), channel_id=1, source_target_pairs={{0,1},{1,2},{2,3},{3,0},{4,5},{5,6},{6,7},{7,4},{8,9},{9,10},{10,1... | collective-permute-start | bytes 294920 | tf_op jit(solution)/shard_map/ppermute | solution.py:42
  15.5 16.1 %collective-permute-start.12 = (bf16[3,16,3072]{2,1,0:T(8,128)(2,1)S(1)}, bf16[3,16,3072]{2,1,0:T(8,128)(2,1)S(1)}, u32[]{:S(2)}, u32[]{:S(2)}) collective-permute-start(bf16[3,16,3072]{2,1,0:T(8,128)(2,1)S(1)} %stack_i.1.tie.rest_0_), channel_id=1, source_target_pairs={{0,16},{4,20},{8,24},{12,28},{16,0},{20,4},{24,8},{28,12},{1,17},{... | collective-permute-start | bytes 884744 | tf_op jit(solution)/shard_map/ppermute | solution.py:47
  17.1 14.6 %collective-permute-start.10 = (bf16[3,16,3072]{2,1,0:T(8,128)(2,1)S(1)}, bf16[3,16,3072]{2,1,0:T(8,128)(2,1)S(1)}, u32[]{:S(2)}, u32[]{:S(2)}) collective-permute-start(bf16[3,16,3072]{2,1,0:T(8,128)(2,1)S(1)} %stack_i.1.tie.rest_0_), channel_id=1, source_target_pairs={{0,8},{4,12},{8,0},{12,4},{16,24},{20,28},{24,16},{28,20},{1,9},{5... | collective-permute-start | bytes 884744 | tf_op jit(solution)/shard_map/ppermute | solution.py:47
  18.6 5.5 %collective-permute-start.2 = (bf16[64,512]{1,0:T(8,128)(2,1)S(1)}, bf16[64,512]{1,0:T(8,128)(2,1)S(1)}, u32[]{:S(2)}, u32[]{:S(2)}) collective-permute-start(bf16[64,512]{1,0:T(8,128)(2,1)S(1)} %get-tuple-element.81.tie), channel_id=1, source_target_pairs={{0,3},{1,0},{2,1},{3,2},{4,7},{5,4},{6,5},{7,6},{8,11},{9,8},{10,9... | collective-permute-start | bytes 196616 | tf_op jit(solution)/shard_map/ppermute | solution.py:42
  20.5 6.6 %collective-permute-start.1 = (bf16[64,512]{1,0:T(8,128)(2,1)S(1)}, bf16[64,512]{1,0:T(8,128)(2,1)S(1)}, u32[]{:S(2)}, u32[]{:S(2)}) collective-permute-start(bf16[64,512]{1,0:T(8,128)(2,1)S(1)} %get-tuple-element.81.tie), channel_id=1, source_target_pairs={{0,2},{1,3},{2,0},{3,1},{4,6},{5,7},{6,4},{7,5},{8,10},{9,11},{10,... | collective-permute-start | bytes 196616 | tf_op jit(solution)/shard_map/ppermute | solution.py:42
  20.8 6.2 %collective-permute-start = (bf16[64,512]{1,0:T(8,128)(2,1)S(1)}, bf16[64,512]{1,0:T(8,128)(2,1)S(1)}, u32[]{:S(2)}, u32[]{:S(2)}) collective-permute-start(bf16[64,512]{1,0:T(8,128)(2,1)S(1)} %get-tuple-element.81.tie), channel_id=1, source_target_pairs={{0,1},{1,2},{2,3},{3,0},{4,5},{5,6},{6,7},{7,4},{8,9},{9,10},{10,1... | collective-permute-start | bytes 196616 | tf_op jit(solution)/shard_map/ppermute | solution.py:42
  24.1 23.0 %copy-start.14 = (f32[8004]{0:T(1024)S(1)}, f32[8004]{0:T(1024)}, u32[]{:S(2)}) copy-start(f32[8004]{0:T(1024)} %param.29) | copy-start | bytes 96052
  24.1 23.1 %slice-start = ((f32[8004]{0:T(1024)}), f32[324]{0:T(512)S(1)}, s32[]{:S(2)}) async-start(f32[8004]{0:T(1024)} %param.29), calls=%async_computation | async-start | bytes 4096 | tf_op jit(solution)/shard_map/slice | solution.py:637
  27.1 22.9 %copy-start.2 = (f32[128,3072]{1,0:T(8,128)S(1)}, f32[128,3072]{1,0:T(8,128)}, u32[]{:S(2)}) copy-start(f32[128,3072]{1,0:T(8,128)} %rest_0_.1) | copy-start | bytes 4718596
  27.7 18.3 %collective-permute-start.6 = (bf16[177,512]{1,0:T(8,128)(2,1)S(1)}, bf16[177,512]{1,0:T(8,128)(2,1)S(1)}, u32[]{:S(2)}, u32[]{:S(2)}) collective-permute-start(bf16[177,512]{1,0:T(8,128)(2,1)S(1)} %get-tuple-element.83), channel_id=1, source_target_pairs={{0,1},{1,2},{2,3},{3,0},{4,5},{5,6},{6,7},{7,4},{8,9},{9,10},{10,1... | collective-permute-start | bytes 543752 | tf_op jit(solution)/shard_map/ppermute | solution.py:42
  27.8 18.7 %collective-permute-start.7 = (bf16[177,512]{1,0:T(8,128)(2,1)S(1)}, bf16[177,512]{1,0:T(8,128)(2,1)S(1)}, u32[]{:S(2)}, u32[]{:S(2)}) collective-permute-start(bf16[177,512]{1,0:T(8,128)(2,1)S(1)} %get-tuple-element.84), channel_id=1, source_target_pairs={{0,2},{1,3},{2,0},{3,1},{4,6},{5,7},{6,4},{7,5},{8,10},{9,11},{10,... | collective-permute-start | bytes 543752 | tf_op jit(solution)/shard_map/ppermute | solution.py:42
  29.4 17.2 %collective-permute-start.8 = (bf16[177,512]{1,0:T(8,128)(2,1)S(1)}, bf16[177,512]{1,0:T(8,128)(2,1)S(1)}, u32[]{:S(2)}, u32[]{:S(2)}) collective-permute-start(bf16[177,512]{1,0:T(8,128)(2,1)S(1)} %get-tuple-element.85), channel_id=1, source_target_pairs={{0,3},{1,0},{2,1},{3,2},{4,7},{5,4},{6,5},{7,6},{8,11},{9,8},{10,9... | collective-permute-start | bytes 543752 | tf_op jit(solution)/shard_map/ppermute | solution.py:42
  31.6 15.4 %collective-permute-start.14 = (bf16[3,16,3072]{2,1,0:T(8,128)(2,1)S(1)}, bf16[3,16,3072]{2,1,0:T(8,128)(2,1)S(1)}, u32[]{:S(2)}, u32[]{:S(2)}) collective-permute-start(bf16[3,16,3072]{2,1,0:T(8,128)(2,1)S(1)} %collective-permute-done.10.rest_2_), channel_id=1, source_target_pairs={{0,16},{4,20},{8,24},{12,28},{16,0},{20,4},{24,8},{28,12},{1,17},{... | collective-permute-start | bytes 884744 | tf_op jit(solution)/shard_map/ppermute | solution.py:47
  46.0 8.2 %collective-permute-start.16 = (bf16[4,3,64,512]{3,2,1,0:T(8,128)(2,1)S(1)}, bf16[4,3,64,512]{3,2,1,0:T(8,128)(2,1)S(1)}, u32[]{:S(2)}, u32[]{:S(2)}) collective-permute-start(bf16[4,3,64,512]{3,2,1,0:T(8,128)(2,1)S(1)} %bitcast.23), channel_id=1, source_target_pairs={{0,4},{4,0},{8,12},{12,8},{16,20},{20,16},{24,28},{28,24},{1,5},{5... | collective-permute-start | bytes 2359304 | tf_op jit(solution)/shard_map/ppermute | solution.py:47
  46.0 2.7 %collective-permute-start.9 = (bf16[3,16,3072]{2,1,0:T(8,128)(2,1)S(1)}, bf16[3,16,3072]{2,1,0:T(8,128)(2,1)S(1)}, u32[]{:S(2)}, u32[]{:S(2)}) collective-permute-start(bf16[3,16,3072]{2,1,0:T(8,128)(2,1)S(1)} %stack_i.1.tie.rest_0_), channel_id=1, source_target_pairs={{0,4},{4,0},{8,12},{12,8},{16,20},{20,16},{24,28},{28,24},{1,5},{5... | collective-permute-start | bytes 884744 | tf_op jit(solution)/shard_map/ppermute | solution.py:47
  46.5 2.6 %collective-permute-start.13 = (bf16[3,16,3072]{2,1,0:T(8,128)(2,1)S(1)}, bf16[3,16,3072]{2,1,0:T(8,128)(2,1)S(1)}, u32[]{:S(2)}, u32[]{:S(2)}) collective-permute-start(bf16[3,16,3072]{2,1,0:T(8,128)(2,1)S(1)} %collective-permute-done.12.rest_4_.tie), channel_id=1, source_target_pairs={{0,4},{4,0},{8,12},{12,8},{16,20},{20,16},{24,28},{28,24},{1,5},{5... | collective-permute-start | bytes 884744 | tf_op jit(solution)/shard_map/ppermute | solution.py:47
  46.6 3.0 %collective-permute-start.11 = (bf16[3,16,3072]{2,1,0:T(8,128)(2,1)S(1)}, bf16[3,16,3072]{2,1,0:T(8,128)(2,1)S(1)}, u32[]{:S(2)}, u32[]{:S(2)}) collective-permute-start(bf16[3,16,3072]{2,1,0:T(8,128)(2,1)S(1)} %collective-permute-done.10.rest_2_), channel_id=1, source_target_pairs={{0,4},{4,0},{8,12},{12,8},{16,20},{20,16},{24,28},{28,24},{1,5},{5... | collective-permute-start | bytes 884744 | tf_op jit(solution)/shard_map/ppermute | solution.py:47
  47.0 2.9 %collective-permute-start.15 = (bf16[3,16,3072]{2,1,0:T(8,128)(2,1)S(1)}, bf16[3,16,3072]{2,1,0:T(8,128)(2,1)S(1)}, u32[]{:S(2)}, u32[]{:S(2)}) collective-permute-start(bf16[3,16,3072]{2,1,0:T(8,128)(2,1)S(1)} %collective-permute-done.14.rest_6_), channel_id=1, source_target_pairs={{0,4},{4,0},{8,12},{12,8},{16,20},{20,16},{24,28},{28,24},{1,5},{5... | collective-permute-start | bytes 884744 | tf_op jit(solution)/shard_map/ppermute | solution.py:47
  54.2 1.8 %copy-start.1 = (f32[384,512]{1,0:T(8,128)S(1)}, f32[384,512]{1,0:T(8,128)}, u32[]{:S(2)}) copy-start(f32[384,512]{1,0:T(8,128)} %rest_3_.1) | copy-start | bytes 2359300
  61.2 4.0 %collective-permute-start.17 = (bf16[4,448,512]{2,1,0:T(8,128)(2,1)S(1)}, bf16[4,448,512]{2,1,0:T(8,128)(2,1)S(1)}, u32[]{:S(2)}, u32[]{:S(2)}) collective-permute-start(bf16[4,448,512]{2,1,0:T(8,128)(2,1)S(1)} %get-tuple-element.105), channel_id=1, source_target_pairs={{0,4},{4,0},{8,12},{12,8},{16,20},{20,16},{24,28},{28,24},{1,5},{5... | collective-permute-start | bytes 5505032 | tf_op jit(solution)/shard_map/ppermute | solution.py:47
  64.7 9.5 %collective-permute-start.27 = (bf16[4,192,512]{2,1,0:T(8,128)(2,1)S(1)}, bf16[4,192,512]{2,1,0:T(8,128)(2,1)S(1)}, u32[]{:S(2)}, u32[]{:S(2)}) collective-permute-start(bf16[4,192,512]{2,1,0:T(8,128)(2,1)S(1)} %get-tuple-element.121), channel_id=1, source_target_pairs={{0,4},{4,0},{8,12},{12,8},{16,20},{20,16},{24,28},{28,24},{1,5},{5... | collective-permute-start | bytes 2359304 | tf_op jit(solution)/shard_map/ppermute | solution.py:47
  65.6 22.5 %collective-permute-start.22 = (bf16[448,512]{1,0:T(8,128)(2,1)S(1)}, bf16[448,512]{1,0:T(8,128)(2,1)S(1)}, u32[]{:S(2)}, u32[]{:S(2)}) collective-permute-start(bf16[448,512]{1,0:T(8,128)(2,1)S(1)} %get-tuple-element.115), channel_id=1, source_target_pairs={{0,16},{4,20},{8,24},{12,28},{16,0},{20,4},{24,8},{28,12},{1,17},{... | collective-permute-start | bytes 1376264 | tf_op jit(solution)/shard_map/ppermute | solution.py:47
  67.1 21.5 %collective-permute-start.23 = (bf16[448,512]{1,0:T(8,128)(2,1)S(1)}, bf16[448,512]{1,0:T(8,128)(2,1)S(1)}, u32[]{:S(2)}, u32[]{:S(2)}) collective-permute-start(bf16[448,512]{1,0:T(8,128)(2,1)S(1)} %get-tuple-element.106.rest_0_), channel_id=1, source_target_pairs={{0,24},{4,28},{8,16},{12,20},{16,8},{20,12},{24,0},{28,4},{1,25},{... | collective-permute-start | bytes 1376264 | tf_op jit(solution)/shard_map/ppermute | solution.py:47
  68.6 21.7 %collective-permute-start.21 = (bf16[448,512]{1,0:T(8,128)(2,1)S(1)}, bf16[448,512]{1,0:T(8,128)(2,1)S(1)}, u32[]{:S(2)}, u32[]{:S(2)}) collective-permute-start(bf16[448,512]{1,0:T(8,128)(2,1)S(1)} %get-tuple-element.114.tie), channel_id=1, source_target_pairs={{0,8},{4,12},{8,0},{12,4},{16,24},{20,28},{24,16},{28,20},{1,9},{5... | collective-permute-start | bytes 1376264 | tf_op jit(solution)/shard_map/ppermute | solution.py:47
  73.5 6.0 %collective-permute-start.18 = (bf16[177,512]{1,0:T(8,128)(2,1)S(1)}, bf16[177,512]{1,0:T(8,128)(2,1)S(1)}, u32[]{:S(2)}, u32[]{:S(2)}) collective-permute-start(bf16[177,512]{1,0:T(8,128)(2,1)S(1)} %get-tuple-element.108), channel_id=1, source_target_pairs={{0,3},{1,0},{2,1},{3,2},{4,7},{5,4},{6,5},{7,6},{8,11},{9,8},{10,9... | collective-permute-start | bytes 543752 | tf_op jit(solution)/shard_map/ppermute | solution.py:42
  74.2 1.2 collective-permute-start.28
  75.6 20.9 %collective-permute-start.29 = (bf16[208,512]{1,0:T(8,128)(2,1)S(1)}, bf16[208,512]{1,0:T(8,128)(2,1)S(1)}, u32[]{:S(2)}, u32[]{:S(2)}) collective-permute-start(bf16[208,512]{1,0:T(8,128)(2,1)S(1)} %get-tuple-element.125), channel_id=1, source_target_pairs={{0,8},{4,12},{8,0},{12,4},{16,24},{20,28},{24,16},{28,20},{1,9},{5... | collective-permute-start | bytes 638984 | tf_op jit(solution)/shard_map/ppermute | solution.py:47
  79.5 12.5 %collective-permute-start.19 = (bf16[177,512]{1,0:T(8,128)(2,1)S(1)}, bf16[177,512]{1,0:T(8,128)(2,1)S(1)}, u32[]{:S(2)}, u32[]{:S(2)}) collective-permute-start(bf16[177,512]{1,0:T(8,128)(2,1)S(1)} %get-tuple-element.109), channel_id=1, source_target_pairs={{0,2},{1,3},{2,0},{3,1},{4,6},{5,7},{6,4},{7,5},{8,10},{9,11},{10,... | collective-permute-start | bytes 543752 | tf_op jit(solution)/shard_map/ppermute | solution.py:42
  88.0 8.5 %collective-permute-start.20 = (bf16[177,512]{1,0:T(8,128)(2,1)S(1)}, bf16[177,512]{1,0:T(8,128)(2,1)S(1)}, u32[]{:S(2)}, u32[]{:S(2)}) collective-permute-start(bf16[177,512]{1,0:T(8,128)(2,1)S(1)} %get-tuple-element.110), channel_id=1, source_target_pairs={{0,1},{1,2},{2,3},{3,0},{4,5},{5,6},{6,7},{7,4},{8,9},{9,10},{10,1... | collective-permute-start | bytes 543752 | tf_op jit(solution)/shard_map/ppermute | solution.py:42
  88.6 11.7 %collective-permute-start.30 = (bf16[208,512]{1,0:T(8,128)(2,1)S(1)}, bf16[208,512]{1,0:T(8,128)(2,1)S(1)}, u32[]{:S(2)}, u32[]{:S(2)}) collective-permute-start(bf16[208,512]{1,0:T(8,128)(2,1)S(1)} %get-tuple-element.126), channel_id=1, source_target_pairs={{0,16},{4,20},{8,24},{12,28},{16,0},{20,4},{24,8},{28,12},{1,17},{... | collective-permute-start | bytes 638984 | tf_op jit(solution)/shard_map/ppermute | solution.py:47
  90.3 9.9 %collective-permute-start.31 = (bf16[208,512]{1,0:T(8,128)(2,1)S(1)}, bf16[208,512]{1,0:T(8,128)(2,1)S(1)}, u32[]{:S(2)}, u32[]{:S(2)}) collective-permute-start(bf16[208,512]{1,0:T(8,128)(2,1)S(1)} %get-tuple-element.127), channel_id=1, source_target_pairs={{0,24},{4,28},{8,16},{12,20},{16,8},{20,12},{24,0},{28,4},{1,25},{... | collective-permute-start | bytes 638984 | tf_op jit(solution)/shard_map/ppermute | solution.py:47
  92.0 11.3 %collective-permute-start.25 = (bf16[112,512]{1,0:T(8,128)(2,1)S(1)}, bf16[112,512]{1,0:T(8,128)(2,1)S(1)}, u32[]{:S(2)}, u32[]{:S(2)}) collective-permute-start(bf16[112,512]{1,0:T(8,128)(2,1)S(1)} %get-tuple-element.118), channel_id=1, source_target_pairs={{0,2},{1,3},{2,0},{3,1},{4,6},{5,7},{6,4},{7,5},{8,10},{9,11},{10,... | collective-permute-start | bytes 344072 | tf_op jit(solution)/shard_map/ppermute | solution.py:42
  96.5 9.1 %collective-permute-start.26 = (bf16[112,512]{1,0:T(8,128)(2,1)S(1)}, bf16[112,512]{1,0:T(8,128)(2,1)S(1)}, u32[]{:S(2)}, u32[]{:S(2)}) collective-permute-start(bf16[112,512]{1,0:T(8,128)(2,1)S(1)} %get-tuple-element.119), channel_id=1, source_target_pairs={{0,3},{1,0},{2,1},{3,2},{4,7},{5,4},{6,5},{7,6},{8,11},{9,8},{10,9... | collective-permute-start | bytes 344072 | tf_op jit(solution)/shard_map/ppermute | solution.py:42
  96.5 9.0 %collective-permute-start.24 = (bf16[112,512]{1,0:T(8,128)(2,1)S(1)}, bf16[112,512]{1,0:T(8,128)(2,1)S(1)}, u32[]{:S(2)}, u32[]{:S(2)}) collective-permute-start(bf16[112,512]{1,0:T(8,128)(2,1)S(1)} %get-tuple-element.117.tie), channel_id=1, source_target_pairs={{0,1},{1,2},{2,3},{3,0},{4,5},{5,6},{6,7},{7,4},{8,9},{9,10},{10,1... | collective-permute-start | bytes 344072 | tf_op jit(solution)/shard_map/ppermute | solution.py:42
  98.5 27.3 %copy-start.15 = (f32[8004]{0:T(1024)S(1)}, f32[8004]{0:T(1024)}, u32[]{:S(2)}) copy-start(f32[8004]{0:T(1024)} %param.31) | copy-start | bytes 96052
  98.5 27.3 %copy-start.16 = (f32[8004]{0:T(1024)S(1)}, f32[8004]{0:T(1024)}, u32[]{:S(2)}) copy-start(f32[8004]{0:T(1024)} %param.30) | copy-start | bytes 96052
  98.5 28.0 %copy-start.11 = (f32[81,324]{1,0:T(8,128)S(1)}, f32[81,324]{1,0:T(8,128)}, u32[]{:S(2)}) copy-start(f32[81,324]{1,0:T(8,128)} %rest_8_.1) | copy-start | bytes 314932
  100.3 16.2 %copy-start.7 = (f32[4,81,1,512]{3,2,1,0:T(1,128)S(1)}, f32[4,81,1,512]{3,2,1,0:T(1,128)}, u32[]{:S(2)}) copy-start(f32[4,81,1,512]{3,2,1,0:T(1,128)} %get-tuple-element.112.tie_home) | copy-start | bytes 1990660
  100.3 26.3 %copy-start.6 = (f32[384,512]{1,0:T(8,128)S(1)}, f32[384,512]{1,0:T(8,128)}, u32[]{:S(2)}) copy-start(f32[384,512]{1,0:T(8,128)} %rest_5_.1) | copy-start | bytes 2359300
  100.4 16.1 %collective-permute-start.32 = (bf16[64,512]{1,0:T(8,128)(2,1)S(1)}, bf16[64,512]{1,0:T(8,128)(2,1)S(1)}, u32[]{:S(2)}, u32[]{:S(2)}) collective-permute-start(bf16[64,512]{1,0:T(8,128)(2,1)S(1)} %get-tuple-element.130), channel_id=1, source_target_pairs={{0,1},{1,2},{2,3},{3,0},{4,5},{5,6},{6,7},{7,4},{8,9},{9,10},{10,1... | collective-permute-start | bytes 196616 | tf_op jit(solution)/shard_map/ppermute | solution.py:42
  101.3 15.2 %collective-permute-start.33 = (bf16[64,512]{1,0:T(8,128)(2,1)S(1)}, bf16[64,512]{1,0:T(8,128)(2,1)S(1)}, u32[]{:S(2)}, u32[]{:S(2)}) collective-permute-start(bf16[64,512]{1,0:T(8,128)(2,1)S(1)} %get-tuple-element.131), channel_id=1, source_target_pairs={{0,2},{1,3},{2,0},{3,1},{4,6},{5,7},{6,4},{7,5},{8,10},{9,11},{10,... | collective-permute-start | bytes 196616 | tf_op jit(solution)/shard_map/ppermute | solution.py:42
  103.3 13.1 %collective-permute-start.34 = (bf16[64,512]{1,0:T(8,128)(2,1)S(1)}, bf16[64,512]{1,0:T(8,128)(2,1)S(1)}, u32[]{:S(2)}, u32[]{:S(2)}) collective-permute-start(bf16[64,512]{1,0:T(8,128)(2,1)S(1)} %get-tuple-element.132), channel_id=1, source_target_pairs={{0,3},{1,0},{2,1},{3,2},{4,7},{5,4},{6,5},{7,6},{8,11},{9,8},{10,9... | collective-permute-start | bytes 196616 | tf_op jit(solution)/shard_map/ppermute | solution.py:42
  105.6 21.0 %copy-start.5 = (f32[384,512]{1,0:T(8,128)S(1)}, f32[384,512]{1,0:T(8,128)}, u32[]{:S(2)}) copy-start(f32[384,512]{1,0:T(8,128)} %rest_4_.1) | copy-start | bytes 2359300
  105.6 20.9 %copy-start.3 = (f32[128,3072]{1,0:T(8,128)S(1)}, f32[128,3072]{1,0:T(8,128)}, u32[]{:S(2)}) copy-start(f32[128,3072]{1,0:T(8,128)} %rest_1_.1) | copy-start | bytes 4718596
  105.6 20.9 %copy-start.4 = (f32[128,3072]{1,0:T(8,128)S(1)}, f32[128,3072]{1,0:T(8,128)}, u32[]{:S(2)}) copy-start(f32[128,3072]{1,0:T(8,128)} %rest_2_.1) | copy-start | bytes 4718596
  105.7 20.9 %copy-start.10 = (f32[81,324]{1,0:T(8,128)S(1)}, f32[81,324]{1,0:T(8,128)}, u32[]{:S(2)}) copy-start(f32[81,324]{1,0:T(8,128)} %rest_7_.1) | copy-start | bytes 314932
  (5 other events, 5.2 us)

commit v6 on v5

--- a/solution.py
+++ b/solution.py
@@ -133,12 +133,26 @@
             copy.wait()
 
 
-def out_kernel(grid, scal, counts, crops, w_out, mix, msg, col_ref, row_ref, held, strip, sems):
+def pick_kernel(per, own, unit, pick_ref, pack_ref):
+    n = pick_ref.shape[0]
+    cell = lax.broadcasted_iota(I32, (n, pick_ref.shape[1]), 0)
+    lane = lax.broadcasted_iota(I32, (n, pick_ref.shape[1]), 1)
+    part = jnp.where(cell >= per, 1, 0) + jnp.where(cell >= 2 * per, 1, 0) + jnp.where(cell >= 3 * per, 1, 0)
+    pick_ref[...] = jnp.where(lane == cell + part * (128 - per), 1.0, 0.0).astype(BF)
+    big = lax.broadcasted_iota(I32, (512, n), 0)
+    lane = lax.broadcasted_iota(I32, (512, n), 1)
+    within = ((big >> 6) ^ unit) * STEP + (big & 15)
+    a = (((big >> 4) + own) & 3) * per + within
+    pack_ref[...] = jnp.where((lane == a) & (within < per), 1.0, 0.0).astype(BF)
+
+
+def out_kernel(grid, scal, counts, crops, w_out, mix, msg, col_ref, row_ref, pick_ref, pack_ref, held, strip, sems):
     unit = scal[1]
     rows = held.shape[0]
     copies = Copies(sems)
     copies.bring(w_out.at[pl.ds(aligned(unit * rows, STEP), rows), :], held)
     slot_kernel(grid, scal, counts, crops, col_ref, row_ref)
+    pick_kernel(mix.shape[0], scal[0], unit, pick_ref, pack_ref)
     strip[...] = jnp.zeros_like(strip)
     strip[0 : mix.shape[0], 0 : mix.shape[1]] = mix[...].astype(BF)
     copies.wait()
@@ -250,7 +264,7 @@
         slope_u[rows, :] = slope
 
 
-def spatial_kernel(scal, xt_ref, cot_ref, u_ref, slope_u, vn_ref, b_mix, mix_own, wo_own, *rest):
+def spatial_kernel(scal, pick_ref, pack_ref, xt_ref, cot_ref, u_ref, slope_u, vn_ref, b_mix, mix_own, wo_own, *rest):
     wo, rest = rest[:2], rest[2:]
     mix_ref, pre_u, sg_ref, gated, wout, keep, send, *rest = rest
     mixp, spat, gtmp = rest
@@ -272,11 +286,7 @@
     mine = aligned(own * 128, 128)
     mixp[pl.ds(mine, 128), :] = jnp.zeros((128, LANE), BF)
     mixp[pl.ds(mine, per), 0:cells] = mix_own[...].astype(BF)
-    cell = lax.broadcasted_iota(I32, (n, mixp.shape[0]), 0)
-    lane = lax.broadcasted_iota(I32, (n, mixp.shape[0]), 1)
-    part = jnp.where(cell >= per, 1, 0) + jnp.where(cell >= 2 * per, 1, 0) + jnp.where(cell >= 3 * per, 1, 0)
-    pick = jnp.where(lane == cell + part * (128 - per), 1.0, 0.0).astype(BF)
-    mix_ref[...] = dot(pick, mixp[:, :n]).astype(BF)
+    mix_ref[...] = dot(pick_ref[...], mixp[:, :n]).astype(BF)
     mix = mix_ref[...]
     for k in range(tiles):
         cols = slice(k * LANE, (k + 1) * LANE)
@@ -302,12 +312,7 @@
                 at = (lax.rem(own + r, 4) * 8 + (unit ^ (c + 2 * e))) * out_unit
                 dst[e, r * height : r * height + out_unit, :] = gtmp[pl.ds(aligned(at, STEP), out_unit), :]
     gmix = dot(sg_ref[...], vn_ref[...], 1, 1).astype(BF)
-    big = lax.broadcasted_iota(I32, (512, n), 0)
-    lane = lax.broadcasted_iota(I32, (512, n), 1)
-    within = ((big >> 6) ^ unit) * STEP + (big & 15)
-    a = (((big >> 4) + own) & 3) * per + within
-    pick = jnp.where((lane == a) & (within < per), 1.0, 0.0).astype(BF)
-    padded = dot(pick, gmix).astype(BF)
+    padded = dot(pack_ref[...], gmix).astype(BF)
     for c, dst in ((0, keep), (1, send)):
         for e in range(4):
             for r in range(4):
@@ -589,10 +594,10 @@
 
     wi_piece = lax.dynamic_slice_in_dim(in_weight, unit * in_unit, in_unit, 0).astype(BF)
 
-    msg, slot_col, slot_row = call(
+    msg, slot_col, slot_row, pick, pack = call(
         functools.partial(out_kernel, grid),
         [scal, patch_count.reshape(1, 4), crop_index, out_weight, spatial_weight],
-        [((low, LANE), BF), ((n, 1), I32), ((1, n), I32)],
+        [((low, LANE), BF), ((n, 1), I32), ((1, n), I32), ((n, 512), BF), ((512, n), BF)],
         [pltpu.VMEM((out_unit, width), F32), pltpu.VMEM((128, LANE), BF), pltpu.SemaphoreType.DMA((1,))],
         specs=[SM, VM, VM, ANY, VM],
         limit=8,
@@ -618,7 +623,7 @@
     )
     got = call(
         rows_kernel,
-        [scal, tokens.reshape(4, row_count, width), cotangent.reshape(4, row_count, width), base],
+        [scal, tokens.reshape(4, row_count, width), cotangent.reshape(4, row_count, width), base_in],
         [((HALF + row_count, width), BF)] * 4,
         specs=[SM, VM, VM, ANY],
         limit=8,
@@ -677,14 +682,14 @@
     packed = ((4, 4 * (low + side_rows), LANE), BF)
     mix, pre_u, sg, gated, wout, keep_a, send_a = call(
         spatial_kernel,
-        [scal, xt, cot_pos, u, slope_u, vn, b_mix, spatial_weight, out_weight, joined, joined_got],
+        [scal, pick, pack, xt, cot_pos, u, slope_u, vn, b_mix, spatial_weight, out_weight, joined, joined_got],
         [((n, n), BF), sized(BF), sized(BF), sized(BF), ((gate, width), BF), packed, packed],
         [
             pltpu.VMEM((512, LANE), BF),
             pltpu.VMEM((n, gate), F32),
             pltpu.VMEM((gate, width), BF),
         ],
-        specs=[SM] + [VM] * 10,
+        specs=[SM] + [VM] * 12,
         flops=4_000_000_000,
         limit=24,
         name="spatial",

time: 131 us -> 131 us (level)
  no operation moved by 1% of the time
where the time goes in v6:
time: 131 us; the launch traced here: 130 us
  starting transfers between devices  40.2 us (31%)
  blocking collectives  32.3 us (25%)
  Pallas kernels  28.8 us (22%)
  waiting for transfers between devices  21.1 us (16%)
  local copies, waits for them, and re-layouts  5.81 us (4%)
    pallas_call x20, Pallas kernels, call(): pl.pallas_call(body, out_shape=[jax.ShapeDtypeStruct(s, d) for s, d in ou...  28.8 us
    ppermute x18, starting transfers between devices, turn(): return lax.ppermute(arr, 'patch', [(s, (s + r) % n) for s in range(n)])  26.8 us
    all_gather x2, blocking collectives, img_gather(): return lax.all_gather(arr, 'img', axis_index_groups=groups)  19.5 us
    ppermute x17, starting transfers between devices, swap(): return lax.ppermute(arr, 'img', [(k, k ^ mask) for k in range(n)])  13.4 us
    all_gather x1, blocking collectives, shards(): joined = lax.all_gather(held, 'img', axis_index_groups=planes)  12.7 us
    ppermute x18, waiting for transfers between devices, turn(): return lax.ppermute(arr, 'patch', [(s, (s + r) % n) for s in range(n)])  11.9 us
    ppermute x17, waiting for transfers between devices, swap(): return lax.ppermute(arr, 'img', [(k, k ^ mask) for k in range(n)])  9.22 us
    unnamed x35, local copies, waits for them, and re-layouts  3.46 us
  transfers between devices with their start and end apart: 35, of which 11 were waited for; matrix products, arithmetic and copies ran while one was open for 1% of the time, Pallas kernels for 14%

profile of v6, /device:TPU:0, one launch (start us, length us, event | category | flops | bytes accessed | tf_op | source)
XLA Modules:
  0.0 130.2 jit_solution(4124735063570452700)
XLA Ops:
  0.7 0.9 dynamic-slice_convert_fusion
  1.6 5.1 %collective-permute-start.2 = (bf16[16,3072]{1,0:T(8,128)(2,1)S(1)}, bf16[16,3072]{1,0:T(8,128)(2,1)S(1)}, u32[]{:S(2)}, u32[]{:S(2)}) collective-permute-start(bf16[16,3072]{1,0:T(8,128)(2,1)S(1)} %dynamic-slice_convert_fusion), channel_id=1, source_target_pairs={{0,3},{1,0},{2,1},{3,2},{4,7},{5,4},{6,5},{7,6},{8,11},{9,8},{10,9... | collective-permute-start | bytes 294920 | tf_op jit(solution)/shard_map/ppermute | solution.py:42
  6.7 1.0 collective-permute-start
  7.8 1.1 copy-done
  8.9 0.9 copy-done.8
  9.8 0.7 copy-done.12
  10.5 0.7 copy-done.13
  11.2 1.3 %prep_out.1 = (bf16[64,512]{1,0:T(8,128)(2,1)S(1)}, s32[336,1]{1,0:T(8,128)S(1)}, s32[1,336]{1,0:T(1,128)S(1)}, bf16[336,512]{1,0:T(8,128)(2,1)S(1)}, bf16[512,336]{1,0:T(8,128)(2,1)S(1)}) custom-call(s32[2]{0:T(128)S(1)} %pad_add_fusion.scal, s32[1,4]{1,0:T(1,128)S(1)} %bitcast.33, s32[4,1,324]{2,1,0:T(1,128)S(1)} %copy-done.12, f32[384,512]{1,0:T(8,128)S(1)} %copy-done, ...), custom_call_target="tpu_custom_call" | custom-call | flops 100000000 | bytes 896616 | tf_op jit(solution)/shard_map/prep_out/pallas_call | solution.py:531
  12.5 2.9 %collective-permute-done.1.m2 = bf16[16,3072]{1,0:T(8,128)(2,1)S(1)} collective-permute-done((bf16[16,3072]{1,0:T(8,128)(2,1)S(1)}, bf16[16,3072]{1,0:T(8,128)(2,1)S(1)}, u32[]{:S(2)}, u32[]{:S(2)}) %collective-permute-start.1) | collective-permute-done | bytes 98336 | tf_op jit(solution)/shard_map/ppermute | solution.py:42
  15.5 1.6 %collective-permute-start.7 = (bf16[3,16,3072]{2,1,0:T(8,128)(2,1)S(1)}, bf16[3,16,3072]{2,1,0:T(8,128)(2,1)S(1)}, u32[]{:S(2)}, u32[]{:S(2)}) collective-permute-start(bf16[3,16,3072]{2,1,0:T(8,128)(2,1)S(1)} %stack_i.1.tie.rest_0_), channel_id=1, source_target_pairs={{0,8},{4,12},{8,0},{12,4},{16,24},{20,28},{24,16},{28,20},{1,9},{5... | collective-permute-start | bytes 884744 | tf_op jit(solution)/shard_map/ppermute | solution.py:47
  17.0 1.5 %collective-permute-start.9 = (bf16[3,16,3072]{2,1,0:T(8,128)(2,1)S(1)}, bf16[3,16,3072]{2,1,0:T(8,128)(2,1)S(1)}, u32[]{:S(2)}, u32[]{:S(2)}) collective-permute-start(bf16[3,16,3072]{2,1,0:T(8,128)(2,1)S(1)} %stack_i.1.tie.rest_0_), channel_id=1, source_target_pairs={{0,16},{4,20},{8,24},{12,28},{16,0},{20,4},{24,8},{28,12},{1,17},{... | collective-permute-start | bytes 884744 | tf_op jit(solution)/shard_map/ppermute | solution.py:47
  18.6 1.9 %collective-permute-start.15 = (bf16[64,512]{1,0:T(8,128)(2,1)S(1)}, bf16[64,512]{1,0:T(8,128)(2,1)S(1)}, u32[]{:S(2)}, u32[]{:S(2)}) collective-permute-start(bf16[64,512]{1,0:T(8,128)(2,1)S(1)} %get-tuple-element.83.tie), channel_id=1, source_target_pairs={{0,3},{1,0},{2,1},{3,2},{4,7},{5,4},{6,5},{7,6},{8,11},{9,8},{10,9... | collective-permute-start | bytes 196616 | tf_op jit(solution)/shard_map/ppermute | solution.py:42
  20.8 2.0 %collective-permute-start.13 = (bf16[64,512]{1,0:T(8,128)(2,1)S(1)}, bf16[64,512]{1,0:T(8,128)(2,1)S(1)}, u32[]{:S(2)}, u32[]{:S(2)}) collective-permute-start(bf16[64,512]{1,0:T(8,128)(2,1)S(1)} %get-tuple-element.83.tie), channel_id=1, source_target_pairs={{0,1},{1,2},{2,3},{3,0},{4,5},{5,6},{6,7},{7,4},{8,9},{9,10},{10,1... | collective-permute-start | bytes 196616 | tf_op jit(solution)/shard_map/ppermute | solution.py:42
  22.9 1.2 copy_bitcast_fusion
  24.1 0.6 prep_rows.1
  24.7 1.2 collective-permute-start.3
  25.9 6.5 %collective-permute-done.14.m2 = bf16[64,512]{1,0:T(8,128)(2,1)S(1)} collective-permute-done((bf16[64,512]{1,0:T(8,128)(2,1)S(1)}, bf16[64,512]{1,0:T(8,128)(2,1)S(1)}, u32[]{:S(2)}, u32[]{:S(2)}) %collective-permute-start.14) | collective-permute-done | bytes 65568 | tf_op jit(solution)/shard_map/ppermute | solution.py:42
  33.1 12.7 %all-gather = bf16[12,64,512]{2,1,0:T(8,128)(2,1)S(1)} all-gather(bf16[3,64,512]{2,1,0:T(8,128)(2,1)S(1)} %hold_out.1), channel_id=2, replica_groups={{0,8,16,24},{4,12,20,28},{1,9,17,25},{5,13,21,29},{2,10,18,26},{6,14,22..., dimensions={0}, use_global_device_ids=true | all-gather | bytes 983040 | tf_op jit(solution)/shard_map/all_gather | solution.py:635
  47.2 1.4 %norm_in.1 = (bf16[336,512]{1,0:T(8,128)(2,1)S(1)}, bf16[336,512]{1,0:T(8,128)(2,1)S(1)}) custom-call(s32[336,1]{1,0:T(8,128)S(1)} %get-tuple-element.81.slot_ref, bf16[177,512]{1,0:T(8,128)(2,1)S(1)} %get-tuple-element.84.m0, bf16[177,512]{1,0:T(8,128)(2,1)S(1)} %collective-permute-done.3.m1, bf16[177,512]{1,0:T(8,128)(2,1)S(1)} %collective-permute-done.4.m2, ...), custom_call_target="tpu_custom_call" | custom-call | flops 100000000 | bytes 730432 | tf_op jit(solution)/shard_map/norm_in/pallas_call | solution.py:531
  49.8 3.1 %right.1 = (bf16[512,3072]{1,0:T(8,128)(2,1)S(1)}, f32[336,1536]{1,0:T(8,128)S(1)}, f32[336,1]{1,0:T(8,128)S(1)}, f32[336,1536]{1,0:T(8,128)S(1)}, bf16[336,1536]{1,0:T(8,128)(2,1)S(1)}) custom-call(s32[2]{0:T(128)S(1)} %pad_add_fusion.scal, s32[336,1]{1,0:T(8,128)S(1)} %get-tuple-element.81.slot_ref, bf16[336,512]{1,0:T(8,128)(2,1)S(1)} %get-tuple-element.89.xn_ref, ...), custom_call_target="tpu_custom_call" | custom-call | flops 1500000000 | bytes 4302152 | tf_op jit(solution)/shard_map/right/pallas_call | solution.py:531
  52.9 1.1 place_cot.1
  54.0 1.7 %left.1 = (f32[336,1536]{1,0:T(8,128)S(1)}, f32[336,1536]{1,0:T(8,128)S(1)}) custom-call(bf16[336,512]{1,0:T(8,128)(2,1)S(1)} %get-tuple-element.89.xn_ref, f32[1,3072]{1,0:T(1,128)S(1)} %bitcast.27, bf16[512,3072]{1,0:T(8,128)(2,1)S(1)} %get-tuple-element.92.win, bf16[4,3,64,512]{3,2,1,0:T(8,128)(2,1)S(1)} %collective-permute-done.16.rest_0_.rest_1_), custom_call_target="tpu_custom_call" | custom-call | flops 1000000000 | bytes 4288512 | tf_op jit(solution)/shard_map/left/pallas_call | solution.py:531
  55.8 5.2 %spatial.1 = (bf16[336,336]{1,0:T(8,128)(2,1)S(1)}, bf16[336,1536]{1,0:T(8,128)(2,1)S(1)}, bf16[336,1536]{1,0:T(8,128)(2,1)S(1)}, bf16[336,1536]{1,0:T(8,128)(2,...) custom-call(s32[2]{0:T(128)S(1)} %pad_add_fusion.scal, ...), custom_call_target="tpu_custom_call" | custom-call | flops 4000000000 | bytes 9002840 | tf_op jit(solution)/shard_map/spatial/pallas_call | solution.py:531
  61.2 3.3 %back.1 = (bf16[336,1536]{1,0:T(8,128)(2,1)S(1)}, bf16[4,192,512]{2,1,0:T(8,128)(2,1)S(1)}, bf16[4,192,512]{2,1,0:T(8,128)(2,1)S(1)}, f32[6,512]{1,0:T(8,128)S(1)}) custom-call(s32[336,1]{1,0:T(8,128)S(1)} %get-tuple-element.81.slot_ref, bf16[512,336]{1,0:T(8,128)(2,1)S(1)} %get-tuple-element.95.xt_ref, bf16[336,336]{1,0:T(8,128)(2,1)S(1)} %get-tuple-element.99.mix_ref, ...), custom_call_target="tpu_custom_call" | custom-call | flops 2000000000 | bytes 5739648 | tf_op jit(solution)/shard_map/back/pallas_call | solution.py:531
  65.4 0.6 collective-permute-start.22
  66.0 1.5 %collective-permute-start.23 = (bf16[448,512]{1,0:T(8,128)(2,1)S(1)}, bf16[448,512]{1,0:T(8,128)(2,1)S(1)}, u32[]{:S(2)}, u32[]{:S(2)}) collective-permute-start(bf16[448,512]{1,0:T(8,128)(2,1)S(1)} %get-tuple-element.110.rest_0_), channel_id=1, source_target_pairs={{0,24},{4,28},{8,16},{12,20},{16,8},{20,12},{24,0},{28,4},{1,25},{... | collective-permute-start | bytes 1376264 | tf_op jit(solution)/shard_map/ppermute | solution.py:47
  67.4 1.5 %collective-permute-start.21 = (bf16[448,512]{1,0:T(8,128)(2,1)S(1)}, bf16[448,512]{1,0:T(8,128)(2,1)S(1)}, u32[]{:S(2)}, u32[]{:S(2)}) collective-permute-start(bf16[448,512]{1,0:T(8,128)(2,1)S(1)} %get-tuple-element.118.tie), channel_id=1, source_target_pairs={{0,8},{4,12},{8,0},{12,4},{16,24},{20,28},{24,16},{28,20},{1,9},{5... | collective-permute-start | bytes 1376264 | tf_op jit(solution)/shard_map/ppermute | solution.py:47
  68.9 4.4 %token_grad.1 = (bf16[177,512]{1,0:T(8,128)(2,1)S(1)}, bf16[177,512]{1,0:T(8,128)(2,1)S(1)}, bf16[177,512]{1,0:T(8,128)(2,1)S(1)}, bf16[177,512]{1,0:T(8,128)(2,1)S(1)}, f32[16,512]{1,0:T(8,128)S(1)}) custom-call(s32[336,1]{1,0:T(8,128)S(1)} %get-tuple-element.81.slot_ref, s32[1,336]{1,0:T(1,128)S(1)} %get-tuple-element.82.slot_row, ...), custom_call_target="tpu_custom_call" | custom-call | flops 2000000000 | bytes 10013312 | tf_op jit(solution)/shard_map/token_grad/pallas_call | solution.py:531
  73.3 3.1 %collective-permute-start.18 = (bf16[177,512]{1,0:T(8,128)(2,1)S(1)}, bf16[177,512]{1,0:T(8,128)(2,1)S(1)}, u32[]{:S(2)}, u32[]{:S(2)}) collective-permute-start(bf16[177,512]{1,0:T(8,128)(2,1)S(1)} %get-tuple-element.112), channel_id=1, source_target_pairs={{0,3},{1,0},{2,1},{3,2},{4,7},{5,4},{6,5},{7,6},{8,11},{9,8},{10,9... | collective-permute-start | bytes 543752 | tf_op jit(solution)/shard_map/ppermute | solution.py:42
  76.4 1.2 collective-permute-done.28.vec_got
  77.8 1.6 %collective-permute-start.29 = (bf16[208,512]{1,0:T(8,128)(2,1)S(1)}, bf16[208,512]{1,0:T(8,128)(2,1)S(1)}, u32[]{:S(2)}, u32[]{:S(2)}) collective-permute-start(bf16[208,512]{1,0:T(8,128)(2,1)S(1)} %get-tuple-element.129), channel_id=1, source_target_pairs={{0,8},{4,12},{8,0},{12,4},{16,24},{20,28},{24,16},{28,20},{1,9},{5... | collective-permute-start | bytes 638984 | tf_op jit(solution)/shard_map/ppermute | solution.py:47
  79.9 1.3 %collective-permute-start.19 = (bf16[177,512]{1,0:T(8,128)(2,1)S(1)}, bf16[177,512]{1,0:T(8,128)(2,1)S(1)}, u32[]{:S(2)}, u32[]{:S(2)}) collective-permute-start(bf16[177,512]{1,0:T(8,128)(2,1)S(1)} %get-tuple-element.113), channel_id=1, source_target_pairs={{0,2},{1,3},{2,0},{3,1},{4,6},{5,7},{6,4},{7,5},{8,10},{9,11},{10,... | collective-permute-start | bytes 543752 | tf_op jit(solution)/shard_map/ppermute | solution.py:42
  81.2 6.7 %collective-permute-done.22.g2 = bf16[448,512]{1,0:T(8,128)(2,1)S(1)} collective-permute-done((bf16[448,512]{1,0:T(8,128)(2,1)S(1)}, bf16[448,512]{1,0:T(8,128)(2,1)S(1)}, u32[]{:S(2)}, u32[]{:S(2)}) %collective-permute-start.22) | collective-permute-done | bytes 458784 | tf_op jit(solution)/shard_map/ppermute | solution.py:47
  87.8 0.7 collective-permute-start.20
  88.5 1.5 %collective-permute-start.30 = (bf16[208,512]{1,0:T(8,128)(2,1)S(1)}, bf16[208,512]{1,0:T(8,128)(2,1)S(1)}, u32[]{:S(2)}, u32[]{:S(2)}) collective-permute-start(bf16[208,512]{1,0:T(8,128)(2,1)S(1)} %get-tuple-element.130), channel_id=1, source_target_pairs={{0,16},{4,20},{8,24},{12,28},{16,0},{20,4},{24,8},{28,12},{1,17},{... | collective-permute-start | bytes 638984 | tf_op jit(solution)/shard_map/ppermute | solution.py:47
  90.1 1.5 %collective-permute-start.31 = (bf16[208,512]{1,0:T(8,128)(2,1)S(1)}, bf16[208,512]{1,0:T(8,128)(2,1)S(1)}, u32[]{:S(2)}, u32[]{:S(2)}) collective-permute-start(bf16[208,512]{1,0:T(8,128)(2,1)S(1)} %get-tuple-element.131), channel_id=1, source_target_pairs={{0,24},{4,28},{8,16},{12,20},{16,8},{20,12},{24,0},{28,4},{1,25},{... | collective-permute-start | bytes 638984 | tf_op jit(solution)/shard_map/ppermute | solution.py:47
  91.8 2.9 %collective-permute-start.25 = (bf16[112,512]{1,0:T(8,128)(2,1)S(1)}, bf16[112,512]{1,0:T(8,128)(2,1)S(1)}, u32[]{:S(2)}, u32[]{:S(2)}) collective-permute-start(bf16[112,512]{1,0:T(8,128)(2,1)S(1)} %get-tuple-element.122), channel_id=1, source_target_pairs={{0,2},{1,3},{2,0},{3,1},{4,6},{5,7},{6,4},{7,5},{8,10},{9,11},{10,... | collective-permute-start | bytes 344072 | tf_op jit(solution)/shard_map/ppermute | solution.py:42
  94.7 1.8 %collective-permute-done.20.h3 = bf16[177,512]{1,0:T(8,128)(2,1)S(1)} collective-permute-done((bf16[177,512]{1,0:T(8,128)(2,1)S(1)}, bf16[177,512]{1,0:T(8,128)(2,1)S(1)}, u32[]{:S(2)}, u32[]{:S(2)}) %collective-permute-start.20) | collective-permute-done | bytes 181280 | tf_op jit(solution)/shard_map/ppermute | solution.py:42
  96.5 1.6 %collective-permute-start.26 = (bf16[112,512]{1,0:T(8,128)(2,1)S(1)}, bf16[112,512]{1,0:T(8,128)(2,1)S(1)}, u32[]{:S(2)}, u32[]{:S(2)}) collective-permute-start(bf16[112,512]{1,0:T(8,128)(2,1)S(1)} %get-tuple-element.123), channel_id=1, source_target_pairs={{0,3},{1,0},{2,1},{3,2},{4,7},{5,4},{6,5},{7,6},{8,11},{9,8},{10,9... | collective-permute-start | bytes 344072 | tf_op jit(solution)/shard_map/ppermute | solution.py:42
  98.5 1.7 %home.1 = (bf16[81,4,512]{2,1,0:T(4,128)(2,1)}, f32[4,81,1,512]{3,2,1,0:T(1,128)}) custom-call(s32[2]{0:T(128)S(1)} %pad_add_fusion.scal, bf16[177,512]{1,0:T(8,128)(2,1)S(1)} %get-tuple-element.111.h0, bf16[177,512]{1,0:T(8,128)(2,1)S(1)} %collective-permute-done.18.h1, bf16[177,512]{1,0:T(8,128)(2,1)S(1)} %collective-permute-done.19.h2, ...), custom_call_target="tpu_custom_call" | custom-call | flops 100000000 | bytes 725000 | tf_op jit(solution)/shard_map/home/pallas_call | solution.py:531
  100.4 0.6 collective-permute-start.32
  101.0 3.4 %collective-permute-start.33 = (bf16[64,512]{1,0:T(8,128)(2,1)S(1)}, bf16[64,512]{1,0:T(8,128)(2,1)S(1)}, u32[]{:S(2)}, u32[]{:S(2)}) collective-permute-start(bf16[64,512]{1,0:T(8,128)(2,1)S(1)} %get-tuple-element.135), channel_id=1, source_target_pairs={{0,2},{1,3},{2,0},{3,1},{4,6},{5,7},{6,4},{7,5},{8,10},{9,11},{10,... | collective-permute-start | bytes 196616 | tf_op jit(solution)/shard_map/ppermute | solution.py:42
  104.4 1.1 collective-permute-start.34
  105.8 10.6 %all-gather.1 = bf16[896,512]{1,0:T(8,128)(2,1)S(1)} all-gather(bf16[112,512]{1,0:T(8,128)(2,1)S(1)} %patch_a.1), channel_id=3, replica_groups={{0,4,8,12,16,20,24,28},{1,5,9,13,17,21,25,29},{2,6,10,14,18,22,26,30},{..., dimensions={0}, use_global_device_ids=true | all-gather | bytes 1032192 | tf_op jit(solution)/shard_map/all_gather | solution.py:554
  116.4 0.6 patch_b.1
  117.0 9.0 %all-gather.2 = bf16[384,512]{1,0:T(8,128)(2,1)S(1)} all-gather(bf16[48,512]{1,0:T(8,128)(2,1)S(1)} %get-tuple-element.137), channel_id=4, replica_groups={{0,4,8,12,16,20,24,28},{1,5,9,13,17,21,25,29},{2,6,10,14,18,22,26,30},{..., dimensions={0}, use_global_device_ids=true | all-gather | bytes 442368 | tf_op jit(solution)/shard_map/all_gather | solution.py:554
  126.0 0.6 multiply_add_fusion
  126.7 3.4 %update.1 = (f32[128,3072]{1,0:T(8,128)}, f32[128,3072]{1,0:T(8,128)}, f32[128,3072]{1,0:T(8,128)}, f32[384,512]{1,0:T(8,128)}, f32[384,512]{1,0:T(8,128)}, /*in...) custom-call(bf16[8,112,512]{2,1,0:T(8,128)(2,1)S(1)} %bitcast.21, ...), custom_call_target="tpu_custom_call" | custom-call | flops 100000000 | bytes 8703536 | tf_op jit(solution)/shard_map/update/pallas_call | solution.py:531
  (93 shorter events, 6.5 us)
Async XLA Ops:
  1.6 10.9 %collective-permute-start.2 = (bf16[16,3072]{1,0:T(8,128)(2,1)S(1)}, bf16[16,3072]{1,0:T(8,128)(2,1)S(1)}, u32[]{:S(2)}, u32[]{:S(2)}) collective-permute-start(bf16[16,3072]{1,0:T(8,128)(2,1)S(1)} %dynamic-slice_convert_fusion), channel_id=1, source_target_pairs={{0,3},{1,0},{2,1},{3,2},{4,7},{5,4},{6,5},{7,6},{8,11},{9,8},{10,9... | collective-permute-start | bytes 294920 | tf_op jit(solution)/shard_map/ppermute | solution.py:42
  6.7 8.7 %collective-permute-start.1 = (bf16[16,3072]{1,0:T(8,128)(2,1)S(1)}, bf16[16,3072]{1,0:T(8,128)(2,1)S(1)}, u32[]{:S(2)}, u32[]{:S(2)}) collective-permute-start(bf16[16,3072]{1,0:T(8,128)(2,1)S(1)} %dynamic-slice_convert_fusion), channel_id=1, source_target_pairs={{0,2},{1,3},{2,0},{3,1},{4,6},{5,7},{6,4},{7,5},{8,10},{9,11},{10,... | collective-permute-start | bytes 294920 | tf_op jit(solution)/shard_map/ppermute | solution.py:42
  6.7 8.7 %collective-permute-start = (bf16[16,3072]{1,0:T(8,128)(2,1)S(1)}, bf16[16,3072]{1,0:T(8,128)(2,1)S(1)}, u32[]{:S(2)}, u32[]{:S(2)}) collective-permute-start(bf16[16,3072]{1,0:T(8,128)(2,1)S(1)} %dynamic-slice_convert_fusion), channel_id=1, source_target_pairs={{0,1},{1,2},{2,3},{3,0},{4,5},{5,6},{6,7},{7,4},{8,9},{9,10},{10,1... | collective-permute-start | bytes 294920 | tf_op jit(solution)/shard_map/ppermute | solution.py:42
  15.5 17.0 %collective-permute-start.7 = (bf16[3,16,3072]{2,1,0:T(8,128)(2,1)S(1)}, bf16[3,16,3072]{2,1,0:T(8,128)(2,1)S(1)}, u32[]{:S(2)}, u32[]{:S(2)}) collective-permute-start(bf16[3,16,3072]{2,1,0:T(8,128)(2,1)S(1)} %stack_i.1.tie.rest_0_), channel_id=1, source_target_pairs={{0,8},{4,12},{8,0},{12,4},{16,24},{20,28},{24,16},{28,20},{1,9},{5... | collective-permute-start | bytes 884744 | tf_op jit(solution)/shard_map/ppermute | solution.py:47
  17.0 16.0 %collective-permute-start.9 = (bf16[3,16,3072]{2,1,0:T(8,128)(2,1)S(1)}, bf16[3,16,3072]{2,1,0:T(8,128)(2,1)S(1)}, u32[]{:S(2)}, u32[]{:S(2)}) collective-permute-start(bf16[3,16,3072]{2,1,0:T(8,128)(2,1)S(1)} %stack_i.1.tie.rest_0_), channel_id=1, source_target_pairs={{0,16},{4,20},{8,24},{12,28},{16,0},{20,4},{24,8},{28,12},{1,17},{... | collective-permute-start | bytes 884744 | tf_op jit(solution)/shard_map/ppermute | solution.py:47
  18.6 6.1 %collective-permute-start.15 = (bf16[64,512]{1,0:T(8,128)(2,1)S(1)}, bf16[64,512]{1,0:T(8,128)(2,1)S(1)}, u32[]{:S(2)}, u32[]{:S(2)}) collective-permute-start(bf16[64,512]{1,0:T(8,128)(2,1)S(1)} %get-tuple-element.83.tie), channel_id=1, source_target_pairs={{0,3},{1,0},{2,1},{3,2},{4,7},{5,4},{6,5},{7,6},{8,11},{9,8},{10,9... | collective-permute-start | bytes 196616 | tf_op jit(solution)/shard_map/ppermute | solution.py:42
  20.5 11.9 %collective-permute-start.14 = (bf16[64,512]{1,0:T(8,128)(2,1)S(1)}, bf16[64,512]{1,0:T(8,128)(2,1)S(1)}, u32[]{:S(2)}, u32[]{:S(2)}) collective-permute-start(bf16[64,512]{1,0:T(8,128)(2,1)S(1)} %get-tuple-element.83.tie), channel_id=1, source_target_pairs={{0,2},{1,3},{2,0},{3,1},{4,6},{5,7},{6,4},{7,5},{8,10},{9,11},{10,... | collective-permute-start | bytes 196616 | tf_op jit(solution)/shard_map/ppermute | solution.py:42
  20.8 11.6 %collective-permute-start.13 = (bf16[64,512]{1,0:T(8,128)(2,1)S(1)}, bf16[64,512]{1,0:T(8,128)(2,1)S(1)}, u32[]{:S(2)}, u32[]{:S(2)}) collective-permute-start(bf16[64,512]{1,0:T(8,128)(2,1)S(1)} %get-tuple-element.83.tie), channel_id=1, source_target_pairs={{0,1},{1,2},{2,3},{3,0},{4,5},{5,6},{6,7},{7,4},{8,9},{9,10},{10,1... | collective-permute-start | bytes 196616 | tf_op jit(solution)/shard_map/ppermute | solution.py:42
  24.1 22.8 %copy-start.14 = (f32[8004]{0:T(1024)S(1)}, f32[8004]{0:T(1024)}, u32[]{:S(2)}) copy-start(f32[8004]{0:T(1024)} %param.29) | copy-start | bytes 96052
  24.1 22.9 %slice-start = ((f32[8004]{0:T(1024)}), f32[324]{0:T(512)S(1)}, s32[]{:S(2)}) async-start(f32[8004]{0:T(1024)} %param.29), calls=%async_computation | async-start | bytes 4096 | tf_op jit(solution)/shard_map/slice | solution.py:642
  24.7 25.1 %copy-start.2 = (f32[128,3072]{1,0:T(8,128)S(1)}, f32[128,3072]{1,0:T(8,128)}, u32[]{:S(2)}) copy-start(f32[128,3072]{1,0:T(8,128)} %rest_0_.1) | copy-start | bytes 4718596
  24.7 21.1 %collective-permute-start.3 = (bf16[177,512]{1,0:T(8,128)(2,1)S(1)}, bf16[177,512]{1,0:T(8,128)(2,1)S(1)}, u32[]{:S(2)}, u32[]{:S(2)}) collective-permute-start(bf16[177,512]{1,0:T(8,128)(2,1)S(1)} %get-tuple-element.85), channel_id=1, source_target_pairs={{0,1},{1,2},{2,3},{3,0},{4,5},{5,6},{6,7},{7,4},{8,9},{9,10},{10,1... | collective-permute-start | bytes 543752 | tf_op jit(solution)/shard_map/ppermute | solution.py:42
  32.4 13.9 %collective-permute-start.4 = (bf16[177,512]{1,0:T(8,128)(2,1)S(1)}, bf16[177,512]{1,0:T(8,128)(2,1)S(1)}, u32[]{:S(2)}, u32[]{:S(2)}) collective-permute-start(bf16[177,512]{1,0:T(8,128)(2,1)S(1)} %get-tuple-element.86), channel_id=1, source_target_pairs={{0,2},{1,3},{2,0},{3,1},{4,6},{5,7},{6,4},{7,5},{8,10},{9,11},{10,... | collective-permute-start | bytes 543752 | tf_op jit(solution)/shard_map/ppermute | solution.py:42
  32.4 14.0 %collective-permute-start.5 = (bf16[177,512]{1,0:T(8,128)(2,1)S(1)}, bf16[177,512]{1,0:T(8,128)(2,1)S(1)}, u32[]{:S(2)}, u32[]{:S(2)}) collective-permute-start(bf16[177,512]{1,0:T(8,128)(2,1)S(1)} %get-tuple-element.87), channel_id=1, source_target_pairs={{0,3},{1,0},{2,1},{3,2},{4,7},{5,4},{6,5},{7,6},{8,11},{9,8},{10,9... | collective-permute-start | bytes 543752 | tf_op jit(solution)/shard_map/ppermute | solution.py:42
  32.5 14.4 %collective-permute-start.11 = (bf16[3,16,3072]{2,1,0:T(8,128)(2,1)S(1)}, bf16[3,16,3072]{2,1,0:T(8,128)(2,1)S(1)}, u32[]{:S(2)}, u32[]{:S(2)}) collective-permute-start(bf16[3,16,3072]{2,1,0:T(8,128)(2,1)S(1)} %collective-permute-done.7.rest_2_), channel_id=1, source_target_pairs={{0,16},{4,20},{8,24},{12,28},{16,0},{20,4},{24,8},{28,12},{1,17},{... | collective-permute-start | bytes 884744 | tf_op jit(solution)/shard_map/ppermute | solution.py:47
  45.8 8.2 %collective-permute-start.16 = (bf16[4,3,64,512]{3,2,1,0:T(8,128)(2,1)S(1)}, bf16[4,3,64,512]{3,2,1,0:T(8,128)(2,1)S(1)}, u32[]{:S(2)}, u32[]{:S(2)}) collective-permute-start(bf16[4,3,64,512]{3,2,1,0:T(8,128)(2,1)S(1)} %bitcast.23), channel_id=1, source_target_pairs={{0,4},{4,0},{8,12},{12,8},{16,20},{20,16},{24,28},{28,24},{1,5},{5... | collective-permute-start | bytes 2359304 | tf_op jit(solution)/shard_map/ppermute | solution.py:47
  45.8 2.7 %collective-permute-start.6 = (bf16[3,16,3072]{2,1,0:T(8,128)(2,1)S(1)}, bf16[3,16,3072]{2,1,0:T(8,128)(2,1)S(1)}, u32[]{:S(2)}, u32[]{:S(2)}) collective-permute-start(bf16[3,16,3072]{2,1,0:T(8,128)(2,1)S(1)} %stack_i.1.tie.rest_0_), channel_id=1, source_target_pairs={{0,4},{4,0},{8,12},{12,8},{16,20},{20,16},{24,28},{28,24},{1,5},{5... | collective-permute-start | bytes 884744 | tf_op jit(solution)/shard_map/ppermute | solution.py:47
  46.3 2.6 %collective-permute-start.10 = (bf16[3,16,3072]{2,1,0:T(8,128)(2,1)S(1)}, bf16[3,16,3072]{2,1,0:T(8,128)(2,1)S(1)}, u32[]{:S(2)}, u32[]{:S(2)}) collective-permute-start(bf16[3,16,3072]{2,1,0:T(8,128)(2,1)S(1)} %collective-permute-done.9.rest_4_.tie), channel_id=1, source_target_pairs={{0,4},{4,0},{8,12},{12,8},{16,20},{20,16},{24,28},{28,24},{1,5},{5... | collective-permute-start | bytes 884744 | tf_op jit(solution)/shard_map/ppermute | solution.py:47
  46.4 3.0 %collective-permute-start.8 = (bf16[3,16,3072]{2,1,0:T(8,128)(2,1)S(1)}, bf16[3,16,3072]{2,1,0:T(8,128)(2,1)S(1)}, u32[]{:S(2)}, u32[]{:S(2)}) collective-permute-start(bf16[3,16,3072]{2,1,0:T(8,128)(2,1)S(1)} %collective-permute-done.7.rest_2_), channel_id=1, source_target_pairs={{0,4},{4,0},{8,12},{12,8},{16,20},{20,16},{24,28},{28,24},{1,5},{5... | collective-permute-start | bytes 884744 | tf_op jit(solution)/shard_map/ppermute | solution.py:47
  46.8 2.9 %collective-permute-start.12 = (bf16[3,16,3072]{2,1,0:T(8,128)(2,1)S(1)}, bf16[3,16,3072]{2,1,0:T(8,128)(2,1)S(1)}, u32[]{:S(2)}, u32[]{:S(2)}) collective-permute-start(bf16[3,16,3072]{2,1,0:T(8,128)(2,1)S(1)} %collective-permute-done.11.rest_6_), channel_id=1, source_target_pairs={{0,4},{4,0},{8,12},{12,8},{16,20},{20,16},{24,28},{28,24},{1,5},{5... | collective-permute-start | bytes 884744 | tf_op jit(solution)/shard_map/ppermute | solution.py:47
  54.0 1.8 %copy-start.1 = (f32[384,512]{1,0:T(8,128)S(1)}, f32[384,512]{1,0:T(8,128)}, u32[]{:S(2)}) copy-start(f32[384,512]{1,0:T(8,128)} %rest_3_.1) | copy-start | bytes 2359300
  61.0 4.0 %collective-permute-start.17 = (bf16[4,448,512]{2,1,0:T(8,128)(2,1)S(1)}, bf16[4,448,512]{2,1,0:T(8,128)(2,1)S(1)}, u32[]{:S(2)}, u32[]{:S(2)}) collective-permute-start(bf16[4,448,512]{2,1,0:T(8,128)(2,1)S(1)} %get-tuple-element.109), channel_id=1, source_target_pairs={{0,4},{4,0},{8,12},{12,8},{16,20},{20,16},{24,28},{28,24},{1,5},{5... | collective-permute-start | bytes 5505032 | tf_op jit(solution)/shard_map/ppermute | solution.py:47
  64.5 11.9 %collective-permute-start.27 = (bf16[4,192,512]{2,1,0:T(8,128)(2,1)S(1)}, bf16[4,192,512]{2,1,0:T(8,128)(2,1)S(1)}, u32[]{:S(2)}, u32[]{:S(2)}) collective-permute-start(bf16[4,192,512]{2,1,0:T(8,128)(2,1)S(1)} %get-tuple-element.125), channel_id=1, source_target_pairs={{0,4},{4,0},{8,12},{12,8},{16,20},{20,16},{24,28},{28,24},{1,5},{5... | collective-permute-start | bytes 2359304 | tf_op jit(solution)/shard_map/ppermute | solution.py:47
  65.4 22.5 %collective-permute-start.22 = (bf16[448,512]{1,0:T(8,128)(2,1)S(1)}, bf16[448,512]{1,0:T(8,128)(2,1)S(1)}, u32[]{:S(2)}, u32[]{:S(2)}) collective-permute-start(bf16[448,512]{1,0:T(8,128)(2,1)S(1)} %get-tuple-element.119), channel_id=1, source_target_pairs={{0,16},{4,20},{8,24},{12,28},{16,0},{20,4},{24,8},{28,12},{1,17},{... | collective-permute-start | bytes 1376264 | tf_op jit(solution)/shard_map/ppermute | solution.py:47
  66.0 22.6 %collective-permute-start.23 = (bf16[448,512]{1,0:T(8,128)(2,1)S(1)}, bf16[448,512]{1,0:T(8,128)(2,1)S(1)}, u32[]{:S(2)}, u32[]{:S(2)}) collective-permute-start(bf16[448,512]{1,0:T(8,128)(2,1)S(1)} %get-tuple-element.110.rest_0_), channel_id=1, source_target_pairs={{0,24},{4,28},{8,16},{12,20},{16,8},{20,12},{24,0},{28,4},{1,25},{... | collective-permute-start | bytes 1376264 | tf_op jit(solution)/shard_map/ppermute | solution.py:47
  67.4 22.7 %collective-permute-start.21 = (bf16[448,512]{1,0:T(8,128)(2,1)S(1)}, bf16[448,512]{1,0:T(8,128)(2,1)S(1)}, u32[]{:S(2)}, u32[]{:S(2)}) collective-permute-start(bf16[448,512]{1,0:T(8,128)(2,1)S(1)} %get-tuple-element.118.tie), channel_id=1, source_target_pairs={{0,8},{4,12},{8,0},{12,4},{16,24},{20,28},{24,16},{28,20},{1,9},{5... | collective-permute-start | bytes 1376264 | tf_op jit(solution)/shard_map/ppermute | solution.py:47
  73.3 6.6 %collective-permute-start.18 = (bf16[177,512]{1,0:T(8,128)(2,1)S(1)}, bf16[177,512]{1,0:T(8,128)(2,1)S(1)}, u32[]{:S(2)}, u32[]{:S(2)}) collective-permute-start(bf16[177,512]{1,0:T(8,128)(2,1)S(1)} %get-tuple-element.112), channel_id=1, source_target_pairs={{0,3},{1,0},{2,1},{3,2},{4,7},{5,4},{6,5},{7,6},{8,11},{9,8},{10,9... | collective-permute-start | bytes 543752 | tf_op jit(solution)/shard_map/ppermute | solution.py:42
  76.4 1.2 collective-permute-start.28
  77.8 20.3 %collective-permute-start.29 = (bf16[208,512]{1,0:T(8,128)(2,1)S(1)}, bf16[208,512]{1,0:T(8,128)(2,1)S(1)}, u32[]{:S(2)}, u32[]{:S(2)}) collective-permute-start(bf16[208,512]{1,0:T(8,128)(2,1)S(1)} %get-tuple-element.129), channel_id=1, source_target_pairs={{0,8},{4,12},{8,0},{12,4},{16,24},{20,28},{24,16},{28,20},{1,9},{5... | collective-permute-start | bytes 638984 | tf_op jit(solution)/shard_map/ppermute | solution.py:47
  79.9 12.0 %collective-permute-start.19 = (bf16[177,512]{1,0:T(8,128)(2,1)S(1)}, bf16[177,512]{1,0:T(8,128)(2,1)S(1)}, u32[]{:S(2)}, u32[]{:S(2)}) collective-permute-start(bf16[177,512]{1,0:T(8,128)(2,1)S(1)} %get-tuple-element.113), channel_id=1, source_target_pairs={{0,2},{1,3},{2,0},{3,1},{4,6},{5,7},{6,4},{7,5},{8,10},{9,11},{10,... | collective-permute-start | bytes 543752 | tf_op jit(solution)/shard_map/ppermute | solution.py:42
  87.8 8.7 %collective-permute-start.20 = (bf16[177,512]{1,0:T(8,128)(2,1)S(1)}, bf16[177,512]{1,0:T(8,128)(2,1)S(1)}, u32[]{:S(2)}, u32[]{:S(2)}) collective-permute-start(bf16[177,512]{1,0:T(8,128)(2,1)S(1)} %get-tuple-element.114), channel_id=1, source_target_pairs={{0,1},{1,2},{2,3},{3,0},{4,5},{5,6},{6,7},{7,4},{8,9},{9,10},{10,1... | collective-permute-start | bytes 543752 | tf_op jit(solution)/shard_map/ppermute | solution.py:42
  88.5 11.7 %collective-permute-start.30 = (bf16[208,512]{1,0:T(8,128)(2,1)S(1)}, bf16[208,512]{1,0:T(8,128)(2,1)S(1)}, u32[]{:S(2)}, u32[]{:S(2)}) collective-permute-start(bf16[208,512]{1,0:T(8,128)(2,1)S(1)} %get-tuple-element.130), channel_id=1, source_target_pairs={{0,16},{4,20},{8,24},{12,28},{16,0},{20,4},{24,8},{28,12},{1,17},{... | collective-permute-start | bytes 638984 | tf_op jit(solution)/shard_map/ppermute | solution.py:47
  90.1 10.1 %collective-permute-start.31 = (bf16[208,512]{1,0:T(8,128)(2,1)S(1)}, bf16[208,512]{1,0:T(8,128)(2,1)S(1)}, u32[]{:S(2)}, u32[]{:S(2)}) collective-permute-start(bf16[208,512]{1,0:T(8,128)(2,1)S(1)} %get-tuple-element.131), channel_id=1, source_target_pairs={{0,24},{4,28},{8,16},{12,20},{16,8},{20,12},{24,0},{28,4},{1,25},{... | collective-permute-start | bytes 638984 | tf_op jit(solution)/shard_map/ppermute | solution.py:47
  91.8 12.5 %collective-permute-start.25 = (bf16[112,512]{1,0:T(8,128)(2,1)S(1)}, bf16[112,512]{1,0:T(8,128)(2,1)S(1)}, u32[]{:S(2)}, u32[]{:S(2)}) collective-permute-start(bf16[112,512]{1,0:T(8,128)(2,1)S(1)} %get-tuple-element.122), channel_id=1, source_target_pairs={{0,2},{1,3},{2,0},{3,1},{4,6},{5,7},{6,4},{7,5},{8,10},{9,11},{10,... | collective-permute-start | bytes 344072 | tf_op jit(solution)/shard_map/ppermute | solution.py:42
  96.5 9.0 %collective-permute-start.26 = (bf16[112,512]{1,0:T(8,128)(2,1)S(1)}, bf16[112,512]{1,0:T(8,128)(2,1)S(1)}, u32[]{:S(2)}, u32[]{:S(2)}) collective-permute-start(bf16[112,512]{1,0:T(8,128)(2,1)S(1)} %get-tuple-element.123), channel_id=1, source_target_pairs={{0,3},{1,0},{2,1},{3,2},{4,7},{5,4},{6,5},{7,6},{8,11},{9,8},{10,9... | collective-permute-start | bytes 344072 | tf_op jit(solution)/shard_map/ppermute | solution.py:42
  98.1 7.6 %collective-permute-start.24 = (bf16[112,512]{1,0:T(8,128)(2,1)S(1)}, bf16[112,512]{1,0:T(8,128)(2,1)S(1)}, u32[]{:S(2)}, u32[]{:S(2)}) collective-permute-start(bf16[112,512]{1,0:T(8,128)(2,1)S(1)} %get-tuple-element.121.tie), channel_id=1, source_target_pairs={{0,1},{1,2},{2,3},{3,0},{4,5},{5,6},{6,7},{7,4},{8,9},{9,10},{10,1... | collective-permute-start | bytes 344072 | tf_op jit(solution)/shard_map/ppermute | solution.py:42
  98.5 27.4 %copy-start.15 = (f32[8004]{0:T(1024)S(1)}, f32[8004]{0:T(1024)}, u32[]{:S(2)}) copy-start(f32[8004]{0:T(1024)} %param.31) | copy-start | bytes 96052
  98.5 27.4 %copy-start.16 = (f32[8004]{0:T(1024)S(1)}, f32[8004]{0:T(1024)}, u32[]{:S(2)}) copy-start(f32[8004]{0:T(1024)} %param.30) | copy-start | bytes 96052
  98.5 28.1 %copy-start.11 = (f32[81,324]{1,0:T(8,128)S(1)}, f32[81,324]{1,0:T(8,128)}, u32[]{:S(2)}) copy-start(f32[81,324]{1,0:T(8,128)} %rest_8_.1) | copy-start | bytes 314932
  100.2 16.1 %copy-start.7 = (f32[4,81,1,512]{3,2,1,0:T(1,128)S(1)}, f32[4,81,1,512]{3,2,1,0:T(1,128)}, u32[]{:S(2)}) copy-start(f32[4,81,1,512]{3,2,1,0:T(1,128)} %get-tuple-element.116.tie_home) | copy-start | bytes 1990660
  100.3 26.4 %copy-start.6 = (f32[384,512]{1,0:T(8,128)S(1)}, f32[384,512]{1,0:T(8,128)}, u32[]{:S(2)}) copy-start(f32[384,512]{1,0:T(8,128)} %rest_5_.1) | copy-start | bytes 2359300
  100.4 16.0 %collective-permute-start.32 = (bf16[64,512]{1,0:T(8,128)(2,1)S(1)}, bf16[64,512]{1,0:T(8,128)(2,1)S(1)}, u32[]{:S(2)}, u32[]{:S(2)}) collective-permute-start(bf16[64,512]{1,0:T(8,128)(2,1)S(1)} %get-tuple-element.134), channel_id=1, source_target_pairs={{0,1},{1,2},{2,3},{3,0},{4,5},{5,6},{6,7},{7,4},{8,9},{9,10},{10,1... | collective-permute-start | bytes 196616 | tf_op jit(solution)/shard_map/ppermute | solution.py:42
  101.0 15.4 %collective-permute-start.33 = (bf16[64,512]{1,0:T(8,128)(2,1)S(1)}, bf16[64,512]{1,0:T(8,128)(2,1)S(1)}, u32[]{:S(2)}, u32[]{:S(2)}) collective-permute-start(bf16[64,512]{1,0:T(8,128)(2,1)S(1)} %get-tuple-element.135), channel_id=1, source_target_pairs={{0,2},{1,3},{2,0},{3,1},{4,6},{5,7},{6,4},{7,5},{8,10},{9,11},{10,... | collective-permute-start | bytes 196616 | tf_op jit(solution)/shard_map/ppermute | solution.py:42
  104.4 12.0 %collective-permute-start.34 = (bf16[64,512]{1,0:T(8,128)(2,1)S(1)}, bf16[64,512]{1,0:T(8,128)(2,1)S(1)}, u32[]{:S(2)}, u32[]{:S(2)}) collective-permute-start(bf16[64,512]{1,0:T(8,128)(2,1)S(1)} %get-tuple-element.136), channel_id=1, source_target_pairs={{0,3},{1,0},{2,1},{3,2},{4,7},{5,4},{6,5},{7,6},{8,11},{9,8},{10,9... | collective-permute-start | bytes 196616 | tf_op jit(solution)/shard_map/ppermute | solution.py:42
  105.7 20.9 %copy-start.5 = (f32[384,512]{1,0:T(8,128)S(1)}, f32[384,512]{1,0:T(8,128)}, u32[]{:S(2)}) copy-start(f32[384,512]{1,0:T(8,128)} %rest_4_.1) | copy-start | bytes 2359300
  105.8 20.9 %copy-start.3 = (f32[128,3072]{1,0:T(8,128)S(1)}, f32[128,3072]{1,0:T(8,128)}, u32[]{:S(2)}) copy-start(f32[128,3072]{1,0:T(8,128)} %rest_1_.1) | copy-start | bytes 4718596
  105.8 20.9 %copy-start.4 = (f32[128,3072]{1,0:T(8,128)S(1)}, f32[128,3072]{1,0:T(8,128)}, u32[]{:S(2)}) copy-start(f32[128,3072]{1,0:T(8,128)} %rest_2_.1) | copy-start | bytes 4718596
  105.8 20.9 %copy-start.10 = (f32[81,324]{1,0:T(8,128)S(1)}, f32[81,324]{1,0:T(8,128)}, u32[]{:S(2)}) copy-start(f32[81,324]{1,0:T(8,128)} %rest_7_.1) | copy-start | bytes 314932
  (5 other events, 5.2 us)

commit v7 on v6

--- a/solution.py
+++ b/solution.py
@@ -99,7 +99,7 @@
         block = jnp.zeros(ref.shape, I32)
         for k in (1, 2, 3):
             block = block + jnp.where(order >= k * quarter, 1, 0)
-        slot = ((own - block) & 3) * ROWS + order - block * quarter
+        slot = ((block - own) & 3) * ROWS + order - block * quarter
         ref[...] = jnp.where(inside, slot, -1)
 
 
@@ -162,7 +162,7 @@
 
 def rows_kernel(scal, tok, cot, tie, m0, m1, m2, m3):
     for r, msg in enumerate((m0, m1, m2, m3)):
-        to = lax.rem(scal[0] + r, 4)
+        to = lax.rem(scal[0] + (4 - r), 4)
         msg[0:ROWS, :] = tok[to]
         msg[HALF : HALF + ROWS, :] = cot[to]
 
@@ -473,7 +473,7 @@
 
 def home_kernel(scal, h0, h1, h2, h3, out_ref, grad_ref, held):
     for r, h in enumerate((h0, h1, h2, h3)):
-        m = lax.rem(scal[0] + r, 4)
+        m = lax.rem(scal[0] + (4 - r), 4)
         held[m] = h[0:ROWS, :]
         grad_ref[m, :, 0, :] = h[HALF : HALF + ROWS, :].astype(F32)
     for m in range(4):
@@ -629,7 +629,7 @@
         limit=8,
         name="prep_rows",
     )
-    got = [got[0]] + [turn(m, r) for r, m in enumerate(got[1:], 1)]
+    got = [got[0]] + [turn(m, -r) for r, m in enumerate(got[1:], 1)]
     (held,) = call(hold_kernel, [base, plane_in[2]], [((3, low, LANE), BF)], specs=[VM, ANY], limit=8, name="hold_out")
     planes = [[8 * g + c + 2 * k for k in range(4)] for g in range(lax.axis_size("img") // 8) for c in (0, 1)]
     joined = lax.all_gather(held, "img", axis_index_groups=planes)
@@ -736,7 +736,7 @@
         name="core_b",
     )
     plane_b = [swap(s, m) for s, m in zip(send_b, (2, 4, 6))]
-    home = [home[0]] + [turn(h, -r) for r, h in enumerate(home[1:], 1)]
+    home = [home[0]] + [turn(h, r) for r, h in enumerate(home[1:], 1)]
     out_tokens, in_grad = call(
         home_kernel,
         [scal, *home],

time: 131 us -> 130 us (level)
  waiting for transfers between devices: 21.1 us -> 16.7 us
  blocking collectives: 32.3 us -> 34.2 us
  starting transfers between devices: 40.2 us -> 42.1 us
    ppermute x18, waiting for transfers between devices: 11.9 us -> 7.14 us  [turn(): return lax.ppermute(arr, 'patch', [(s, (s + r) % n) for s in range(n)])]
    ppermute x18, starting transfers between devices: 26.8 us -> 28.7 us  [turn(): return lax.ppermute(arr, 'patch', [(s, (s + r) % n) for s in range(n)])]
  transfers between devices with their start and end apart: 35 -> 35, of which waited for: 11 -> 10; matrix products, arithmetic and copies ran while one was open for 1% -> 1% of each run, Pallas kernels for 14% -> 14%
where the time goes in v7:
time: 130 us
  starting transfers between devices  42.1 us (32%)
  blocking collectives  34.2 us (26%)
  Pallas kernels  28.8 us (22%)
  waiting for transfers between devices  16.7 us (13%)
  local copies, waits for them, and re-layouts  5.81 us (4%)
    pallas_call x20, Pallas kernels, call(): pl.pallas_call(body, out_shape=[jax.ShapeDtypeStruct(s, d) for s, d in ou...  28.8 us
    ppermute x18, starting transfers between devices, turn(): return lax.ppermute(arr, 'patch', [(s, (s + r) % n) for s in range(n)])  28.7 us
    all_gather x2, blocking collectives, img_gather(): return lax.all_gather(arr, 'img', axis_index_groups=groups)  20.7 us
    all_gather x1, blocking collectives, shards(): joined = lax.all_gather(held, 'img', axis_index_groups=planes)  13.5 us
    ppermute x17, starting transfers between devices, swap(): return lax.ppermute(arr, 'img', [(k, k ^ mask) for k in range(n)])  13.4 us
    ppermute x17, waiting for transfers between devices, swap(): return lax.ppermute(arr, 'img', [(k, k ^ mask) for k in range(n)])  9.55 us
    ppermute x18, waiting for transfers between devices, turn(): return lax.ppermute(arr, 'patch', [(s, (s + r) % n) for s in range(n)])  7.14 us
    unnamed x35, local copies, waits for them, and re-layouts  3.47 us
  transfers between devices with their start and end apart: 35, of which 10 were waited for; matrix products, arithmetic and copies ran while one was open for 1% of the time, Pallas kernels for 14%

profile of v7, /device:TPU:0, one launch (start us, length us, event | category | flops | bytes accessed | tf_op | source)
XLA Modules:
  0.0 129.6 jit_solution(8679609849288345005)
XLA Ops:
  0.7 0.9 dynamic-slice_convert_fusion
  1.6 5.1 %collective-permute-start.2 = (bf16[16,3072]{1,0:T(8,128)(2,1)S(1)}, bf16[16,3072]{1,0:T(8,128)(2,1)S(1)}, u32[]{:S(2)}, u32[]{:S(2)}) collective-permute-start(bf16[16,3072]{1,0:T(8,128)(2,1)S(1)} %dynamic-slice_convert_fusion), channel_id=1, source_target_pairs={{0,3},{1,0},{2,1},{3,2},{4,7},{5,4},{6,5},{7,6},{8,11},{9,8},{10,9... | collective-permute-start | bytes 294920 | tf_op jit(solution)/shard_map/ppermute | solution.py:42
  6.7 1.0 collective-permute-start
  7.8 1.1 copy-done
  8.9 0.9 copy-done.8
  9.8 0.7 copy-done.12
  10.5 0.7 copy-done.13
  11.2 1.3 %prep_out.1 = (bf16[64,512]{1,0:T(8,128)(2,1)S(1)}, s32[336,1]{1,0:T(8,128)S(1)}, s32[1,336]{1,0:T(1,128)S(1)}, bf16[336,512]{1,0:T(8,128)(2,1)S(1)}, bf16[512,336]{1,0:T(8,128)(2,1)S(1)}) custom-call(s32[2]{0:T(128)S(1)} %pad_add_fusion.scal, s32[1,4]{1,0:T(1,128)S(1)} %bitcast.33, s32[4,1,324]{2,1,0:T(1,128)S(1)} %copy-done.12, f32[384,512]{1,0:T(8,128)S(1)} %copy-done, ...), custom_call_target="tpu_custom_call" | custom-call | flops 100000000 | bytes 896616 | tf_op jit(solution)/shard_map/prep_out/pallas_call | solution.py:531
  12.5 2.9 %collective-permute-done.1.m2 = bf16[16,3072]{1,0:T(8,128)(2,1)S(1)} collective-permute-done((bf16[16,3072]{1,0:T(8,128)(2,1)S(1)}, bf16[16,3072]{1,0:T(8,128)(2,1)S(1)}, u32[]{:S(2)}, u32[]{:S(2)}) %collective-permute-start.1) | collective-permute-done | bytes 98336 | tf_op jit(solution)/shard_map/ppermute | solution.py:42
  15.5 1.6 %collective-permute-start.7 = (bf16[3,16,3072]{2,1,0:T(8,128)(2,1)S(1)}, bf16[3,16,3072]{2,1,0:T(8,128)(2,1)S(1)}, u32[]{:S(2)}, u32[]{:S(2)}) collective-permute-start(bf16[3,16,3072]{2,1,0:T(8,128)(2,1)S(1)} %stack_i.1.tie.rest_0_), channel_id=1, source_target_pairs={{0,8},{4,12},{8,0},{12,4},{16,24},{20,28},{24,16},{28,20},{1,9},{5... | collective-permute-start | bytes 884744 | tf_op jit(solution)/shard_map/ppermute | solution.py:47
  17.0 1.5 %collective-permute-start.9 = (bf16[3,16,3072]{2,1,0:T(8,128)(2,1)S(1)}, bf16[3,16,3072]{2,1,0:T(8,128)(2,1)S(1)}, u32[]{:S(2)}, u32[]{:S(2)}) collective-permute-start(bf16[3,16,3072]{2,1,0:T(8,128)(2,1)S(1)} %stack_i.1.tie.rest_0_), channel_id=1, source_target_pairs={{0,16},{4,20},{8,24},{12,28},{16,0},{20,4},{24,8},{28,12},{1,17},{... | collective-permute-start | bytes 884744 | tf_op jit(solution)/shard_map/ppermute | solution.py:47
  18.6 1.9 %collective-permute-start.15 = (bf16[64,512]{1,0:T(8,128)(2,1)S(1)}, bf16[64,512]{1,0:T(8,128)(2,1)S(1)}, u32[]{:S(2)}, u32[]{:S(2)}) collective-permute-start(bf16[64,512]{1,0:T(8,128)(2,1)S(1)} %get-tuple-element.83.tie), channel_id=1, source_target_pairs={{0,3},{1,0},{2,1},{3,2},{4,7},{5,4},{6,5},{7,6},{8,11},{9,8},{10,9... | collective-permute-start | bytes 196616 | tf_op jit(solution)/shard_map/ppermute | solution.py:42
  20.8 2.0 %collective-permute-start.13 = (bf16[64,512]{1,0:T(8,128)(2,1)S(1)}, bf16[64,512]{1,0:T(8,128)(2,1)S(1)}, u32[]{:S(2)}, u32[]{:S(2)}) collective-permute-start(bf16[64,512]{1,0:T(8,128)(2,1)S(1)} %get-tuple-element.83.tie), channel_id=1, source_target_pairs={{0,1},{1,2},{2,3},{3,0},{4,5},{5,6},{6,7},{7,4},{8,9},{9,10},{10,1... | collective-permute-start | bytes 196616 | tf_op jit(solution)/shard_map/ppermute | solution.py:42
  22.9 1.2 copy_bitcast_fusion
  24.1 0.6 prep_rows.1
  24.7 2.1 %collective-permute-start.3 = (bf16[177,512]{1,0:T(8,128)(2,1)S(1)}, bf16[177,512]{1,0:T(8,128)(2,1)S(1)}, u32[]{:S(2)}, u32[]{:S(2)}) collective-permute-start(bf16[177,512]{1,0:T(8,128)(2,1)S(1)} %get-tuple-element.85), channel_id=1, source_target_pairs={{0,3},{1,0},{2,1},{3,2},{4,7},{5,4},{6,5},{7,6},{8,11},{9,8},{10,9... | collective-permute-start | bytes 543752 | tf_op jit(solution)/shard_map/ppermute | solution.py:42
  26.8 1.0 collective-permute-done.14.m2
  27.8 1.0 collective-permute-start.5
  29.4 13.5 %all-gather = bf16[12,64,512]{2,1,0:T(8,128)(2,1)S(1)} all-gather(bf16[3,64,512]{2,1,0:T(8,128)(2,1)S(1)} %hold_out.1), channel_id=2, replica_groups={{0,8,16,24},{4,12,20,28},{1,9,17,25},{5,13,21,29},{2,10,18,26},{6,14,22..., dimensions={0}, use_global_device_ids=true | all-gather | bytes 983040 | tf_op jit(solution)/shard_map/all_gather | solution.py:635
  44.3 1.4 %norm_in.1 = (bf16[336,512]{1,0:T(8,128)(2,1)S(1)}, bf16[336,512]{1,0:T(8,128)(2,1)S(1)}) custom-call(s32[336,1]{1,0:T(8,128)S(1)} %get-tuple-element.81.slot_ref, bf16[177,512]{1,0:T(8,128)(2,1)S(1)} %get-tuple-element.84.m0, bf16[177,512]{1,0:T(8,128)(2,1)S(1)} %collective-permute-done.3.m1, bf16[177,512]{1,0:T(8,128)(2,1)S(1)} %collective-permute-done.4.m2, ...), custom_call_target="tpu_custom_call" | custom-call | flops 100000000 | bytes 730432 | tf_op jit(solution)/shard_map/norm_in/pallas_call | solution.py:531
  46.9 3.1 %right.1 = (bf16[512,3072]{1,0:T(8,128)(2,1)S(1)}, f32[336,1536]{1,0:T(8,128)S(1)}, f32[336,1]{1,0:T(8,128)S(1)}, f32[336,1536]{1,0:T(8,128)S(1)}, bf16[336,1536]{1,0:T(8,128)(2,1)S(1)}) custom-call(s32[2]{0:T(128)S(1)} %pad_add_fusion.scal, s32[336,1]{1,0:T(8,128)S(1)} %get-tuple-element.81.slot_ref, bf16[336,512]{1,0:T(8,128)(2,1)S(1)} %get-tuple-element.89.xn_ref, ...), custom_call_target="tpu_custom_call" | custom-call | flops 1500000000 | bytes 4302152 | tf_op jit(solution)/shard_map/right/pallas_call | solution.py:531
  50.0 1.1 place_cot.1
  51.1 1.7 %left.1 = (f32[336,1536]{1,0:T(8,128)S(1)}, f32[336,1536]{1,0:T(8,128)S(1)}) custom-call(bf16[336,512]{1,0:T(8,128)(2,1)S(1)} %get-tuple-element.89.xn_ref, f32[1,3072]{1,0:T(1,128)S(1)} %bitcast.27, bf16[512,3072]{1,0:T(8,128)(2,1)S(1)} %get-tuple-element.92.win, bf16[4,3,64,512]{3,2,1,0:T(8,128)(2,1)S(1)} %collective-permute-done.16.rest_0_.rest_1_), custom_call_target="tpu_custom_call" | custom-call | flops 1000000000 | bytes 4288512 | tf_op jit(solution)/shard_map/left/pallas_call | solution.py:531
  52.9 5.2 %spatial.1 = (bf16[336,336]{1,0:T(8,128)(2,1)S(1)}, bf16[336,1536]{1,0:T(8,128)(2,1)S(1)}, bf16[336,1536]{1,0:T(8,128)(2,1)S(1)}, bf16[336,1536]{1,0:T(8,128)(2,...) custom-call(s32[2]{0:T(128)S(1)} %pad_add_fusion.scal, ...), custom_call_target="tpu_custom_call" | custom-call | flops 4000000000 | bytes 9002840 | tf_op jit(solution)/shard_map/spatial/pallas_call | solution.py:531
  58.3 3.3 %back.1 = (bf16[336,1536]{1,0:T(8,128)(2,1)S(1)}, bf16[4,192,512]{2,1,0:T(8,128)(2,1)S(1)}, bf16[4,192,512]{2,1,0:T(8,128)(2,1)S(1)}, f32[6,512]{1,0:T(8,128)S(1)}) custom-call(s32[336,1]{1,0:T(8,128)S(1)} %get-tuple-element.81.slot_ref, bf16[512,336]{1,0:T(8,128)(2,1)S(1)} %get-tuple-element.95.xt_ref, bf16[336,336]{1,0:T(8,128)(2,1)S(1)} %get-tuple-element.99.mix_ref, ...), custom_call_target="tpu_custom_call" | custom-call | flops 2000000000 | bytes 5739648 | tf_op jit(solution)/shard_map/back/pallas_call | solution.py:531
  62.5 1.6 %collective-permute-start.22 = (bf16[448,512]{1,0:T(8,128)(2,1)S(1)}, bf16[448,512]{1,0:T(8,128)(2,1)S(1)}, u32[]{:S(2)}, u32[]{:S(2)}) collective-permute-start(bf16[448,512]{1,0:T(8,128)(2,1)S(1)} %get-tuple-element.119), channel_id=1, source_target_pairs={{0,16},{4,20},{8,24},{12,28},{16,0},{20,4},{24,8},{28,12},{1,17},{... | collective-permute-start | bytes 1376264 | tf_op jit(solution)/shard_map/ppermute | solution.py:47
  64.0 1.5 %collective-permute-start.23 = (bf16[448,512]{1,0:T(8,128)(2,1)S(1)}, bf16[448,512]{1,0:T(8,128)(2,1)S(1)}, u32[]{:S(2)}, u32[]{:S(2)}) collective-permute-start(bf16[448,512]{1,0:T(8,128)(2,1)S(1)} %get-tuple-element.110.rest_0_), channel_id=1, source_target_pairs={{0,24},{4,28},{8,16},{12,20},{16,8},{20,12},{24,0},{28,4},{1,25},{... | collective-permute-start | bytes 1376264 | tf_op jit(solution)/shard_map/ppermute | solution.py:47
  66.0 4.4 %token_grad.1 = (bf16[177,512]{1,0:T(8,128)(2,1)S(1)}, bf16[177,512]{1,0:T(8,128)(2,1)S(1)}, bf16[177,512]{1,0:T(8,128)(2,1)S(1)}, bf16[177,512]{1,0:T(8,128)(2,1)S(1)}, f32[16,512]{1,0:T(8,128)S(1)}) custom-call(s32[336,1]{1,0:T(8,128)S(1)} %get-tuple-element.81.slot_ref, s32[1,336]{1,0:T(1,128)S(1)} %get-tuple-element.82.slot_row, ...), custom_call_target="tpu_custom_call" | custom-call | flops 2000000000 | bytes 10013312 | tf_op jit(solution)/shard_map/token_grad/pallas_call | solution.py:531
  70.4 2.6 %collective-permute-start.18 = (bf16[177,512]{1,0:T(8,128)(2,1)S(1)}, bf16[177,512]{1,0:T(8,128)(2,1)S(1)}, u32[]{:S(2)}, u32[]{:S(2)}) collective-permute-start(bf16[177,512]{1,0:T(8,128)(2,1)S(1)} %get-tuple-element.112), channel_id=1, source_target_pairs={{0,1},{1,2},{2,3},{3,0},{4,5},{5,6},{6,7},{7,4},{8,9},{9,10},{10,1... | collective-permute-start | bytes 543752 | tf_op jit(solution)/shard_map/ppermute | solution.py:42
  73.0 1.2 collective-permute-done.28.vec_got
  74.4 1.6 %collective-permute-start.29 = (bf16[208,512]{1,0:T(8,128)(2,1)S(1)}, bf16[208,512]{1,0:T(8,128)(2,1)S(1)}, u32[]{:S(2)}, u32[]{:S(2)}) collective-permute-start(bf16[208,512]{1,0:T(8,128)(2,1)S(1)} %get-tuple-element.129), channel_id=1, source_target_pairs={{0,8},{4,12},{8,0},{12,4},{16,24},{20,28},{24,16},{28,20},{1,9},{5... | collective-permute-start | bytes 638984 | tf_op jit(solution)/shard_map/ppermute | solution.py:47
  75.9 2.3 %collective-permute-done.18.h1 = bf16[177,512]{1,0:T(8,128)(2,1)S(1)} collective-permute-done((bf16[177,512]{1,0:T(8,128)(2,1)S(1)}, bf16[177,512]{1,0:T(8,128)(2,1)S(1)}, u32[]{:S(2)}, u32[]{:S(2)}) %collective-permute-start.18) | collective-permute-done | bytes 181280 | tf_op jit(solution)/shard_map/ppermute | solution.py:42
  78.6 6.3 %collective-permute-done.22.g2 = bf16[448,512]{1,0:T(8,128)(2,1)S(1)} collective-permute-done((bf16[448,512]{1,0:T(8,128)(2,1)S(1)}, bf16[448,512]{1,0:T(8,128)(2,1)S(1)}, u32[]{:S(2)}, u32[]{:S(2)}) %collective-permute-start.22) | collective-permute-done | bytes 458784 | tf_op jit(solution)/shard_map/ppermute | solution.py:47
  84.9 2.9 %collective-permute-start.20 = (bf16[177,512]{1,0:T(8,128)(2,1)S(1)}, bf16[177,512]{1,0:T(8,128)(2,1)S(1)}, u32[]{:S(2)}, u32[]{:S(2)}) collective-permute-start(bf16[177,512]{1,0:T(8,128)(2,1)S(1)} %get-tuple-element.114), channel_id=1, source_target_pairs={{0,3},{1,0},{2,1},{3,2},{4,7},{5,4},{6,5},{7,6},{8,11},{9,8},{10,9... | collective-permute-start | bytes 543752 | tf_op jit(solution)/shard_map/ppermute | solution.py:42
  87.8 1.5 %collective-permute-start.30 = (bf16[208,512]{1,0:T(8,128)(2,1)S(1)}, bf16[208,512]{1,0:T(8,128)(2,1)S(1)}, u32[]{:S(2)}, u32[]{:S(2)}) collective-permute-start(bf16[208,512]{1,0:T(8,128)(2,1)S(1)} %get-tuple-element.130), channel_id=1, source_target_pairs={{0,16},{4,20},{8,24},{12,28},{16,0},{20,4},{24,8},{28,12},{1,17},{... | collective-permute-start | bytes 638984 | tf_op jit(solution)/shard_map/ppermute | solution.py:47
  89.3 1.4 %collective-permute-start.31 = (bf16[208,512]{1,0:T(8,128)(2,1)S(1)}, bf16[208,512]{1,0:T(8,128)(2,1)S(1)}, u32[]{:S(2)}, u32[]{:S(2)}) collective-permute-start(bf16[208,512]{1,0:T(8,128)(2,1)S(1)} %get-tuple-element.131), channel_id=1, source_target_pairs={{0,24},{4,28},{8,16},{12,20},{16,8},{20,12},{24,0},{28,4},{1,25},{... | collective-permute-start | bytes 638984 | tf_op jit(solution)/shard_map/ppermute | solution.py:47
  91.0 1.2 collective-permute-start.25
  92.2 3.8 %collective-permute-start.26 = (bf16[112,512]{1,0:T(8,128)(2,1)S(1)}, bf16[112,512]{1,0:T(8,128)(2,1)S(1)}, u32[]{:S(2)}, u32[]{:S(2)}) collective-permute-start(bf16[112,512]{1,0:T(8,128)(2,1)S(1)} %get-tuple-element.123), channel_id=1, source_target_pairs={{0,3},{1,0},{2,1},{3,2},{4,7},{5,4},{6,5},{7,6},{8,11},{9,8},{10,9... | collective-permute-start | bytes 344072 | tf_op jit(solution)/shard_map/ppermute | solution.py:42
  96.1 1.7 %home.1 = (bf16[81,4,512]{2,1,0:T(4,128)(2,1)}, f32[4,81,1,512]{3,2,1,0:T(1,128)}) custom-call(s32[2]{0:T(128)S(1)} %pad_add_fusion.scal, bf16[177,512]{1,0:T(8,128)(2,1)S(1)} %get-tuple-element.111.h0, bf16[177,512]{1,0:T(8,128)(2,1)S(1)} %collective-permute-done.18.h1, bf16[177,512]{1,0:T(8,128)(2,1)S(1)} %collective-permute-done.19.h2, ...), custom_call_target="tpu_custom_call" | custom-call | flops 100000000 | bytes 725000 | tf_op jit(solution)/shard_map/home/pallas_call | solution.py:531
  97.8 0.8 collective-permute-done.30.g2
  98.9 3.4 %collective-permute-start.33 = (bf16[64,512]{1,0:T(8,128)(2,1)S(1)}, bf16[64,512]{1,0:T(8,128)(2,1)S(1)}, u32[]{:S(2)}, u32[]{:S(2)}) collective-permute-start(bf16[64,512]{1,0:T(8,128)(2,1)S(1)} %get-tuple-element.135), channel_id=1, source_target_pairs={{0,2},{1,3},{2,0},{3,1},{4,6},{5,7},{6,4},{7,5},{8,10},{9,11},{10,... | collective-permute-start | bytes 196616 | tf_op jit(solution)/shard_map/ppermute | solution.py:42
  102.3 0.7 collective-permute-start.34
  103.0 0.9 collective-permute-done.24.g1
  104.1 11.8 %all-gather.1 = bf16[896,512]{1,0:T(8,128)(2,1)S(1)} all-gather(bf16[112,512]{1,0:T(8,128)(2,1)S(1)} %patch_a.1), channel_id=3, replica_groups={{0,4,8,12,16,20,24,28},{1,5,9,13,17,21,25,29},{2,6,10,14,18,22,26,30},{..., dimensions={0}, use_global_device_ids=true | all-gather | bytes 1032192 | tf_op jit(solution)/shard_map/all_gather | solution.py:554
  115.8 0.6 patch_b.1
  116.5 8.9 %all-gather.2 = bf16[384,512]{1,0:T(8,128)(2,1)S(1)} all-gather(bf16[48,512]{1,0:T(8,128)(2,1)S(1)} %get-tuple-element.137), channel_id=4, replica_groups={{0,4,8,12,16,20,24,28},{1,5,9,13,17,21,25,29},{2,6,10,14,18,22,26,30},{..., dimensions={0}, use_global_device_ids=true | all-gather | bytes 442368 | tf_op jit(solution)/shard_map/all_gather | solution.py:554
  125.4 0.6 multiply_add_fusion
  126.1 3.4 %update.1 = (f32[128,3072]{1,0:T(8,128)}, f32[128,3072]{1,0:T(8,128)}, f32[128,3072]{1,0:T(8,128)}, f32[384,512]{1,0:T(8,128)}, f32[384,512]{1,0:T(8,128)}, /*in...) custom-call(bf16[8,112,512]{2,1,0:T(8,128)(2,1)S(1)} %bitcast.21, ...), custom_call_target="tpu_custom_call" | custom-call | flops 100000000 | bytes 8703536 | tf_op jit(solution)/shard_map/update/pallas_call | solution.py:531
  (93 shorter events, 6.5 us)
Async XLA Ops:
  1.6 10.9 %collective-permute-start.2 = (bf16[16,3072]{1,0:T(8,128)(2,1)S(1)}, bf16[16,3072]{1,0:T(8,128)(2,1)S(1)}, u32[]{:S(2)}, u32[]{:S(2)}) collective-permute-start(bf16[16,3072]{1,0:T(8,128)(2,1)S(1)} %dynamic-slice_convert_fusion), channel_id=1, source_target_pairs={{0,3},{1,0},{2,1},{3,2},{4,7},{5,4},{6,5},{7,6},{8,11},{9,8},{10,9... | collective-permute-start | bytes 294920 | tf_op jit(solution)/shard_map/ppermute | solution.py:42
  6.7 8.7 %collective-permute-start.1 = (bf16[16,3072]{1,0:T(8,128)(2,1)S(1)}, bf16[16,3072]{1,0:T(8,128)(2,1)S(1)}, u32[]{:S(2)}, u32[]{:S(2)}) collective-permute-start(bf16[16,3072]{1,0:T(8,128)(2,1)S(1)} %dynamic-slice_convert_fusion), channel_id=1, source_target_pairs={{0,2},{1,3},{2,0},{3,1},{4,6},{5,7},{6,4},{7,5},{8,10},{9,11},{10,... | collective-permute-start | bytes 294920 | tf_op jit(solution)/shard_map/ppermute | solution.py:42
  6.7 8.7 %collective-permute-start = (bf16[16,3072]{1,0:T(8,128)(2,1)S(1)}, bf16[16,3072]{1,0:T(8,128)(2,1)S(1)}, u32[]{:S(2)}, u32[]{:S(2)}) collective-permute-start(bf16[16,3072]{1,0:T(8,128)(2,1)S(1)} %dynamic-slice_convert_fusion), channel_id=1, source_target_pairs={{0,1},{1,2},{2,3},{3,0},{4,5},{5,6},{6,7},{7,4},{8,9},{9,10},{10,1... | collective-permute-start | bytes 294920 | tf_op jit(solution)/shard_map/ppermute | solution.py:42
  15.5 13.3 %collective-permute-start.7 = (bf16[3,16,3072]{2,1,0:T(8,128)(2,1)S(1)}, bf16[3,16,3072]{2,1,0:T(8,128)(2,1)S(1)}, u32[]{:S(2)}, u32[]{:S(2)}) collective-permute-start(bf16[3,16,3072]{2,1,0:T(8,128)(2,1)S(1)} %stack_i.1.tie.rest_0_), channel_id=1, source_target_pairs={{0,8},{4,12},{8,0},{12,4},{16,24},{20,28},{24,16},{28,20},{1,9},{5... | collective-permute-start | bytes 884744 | tf_op jit(solution)/shard_map/ppermute | solution.py:47
  17.0 12.3 %collective-permute-start.9 = (bf16[3,16,3072]{2,1,0:T(8,128)(2,1)S(1)}, bf16[3,16,3072]{2,1,0:T(8,128)(2,1)S(1)}, u32[]{:S(2)}, u32[]{:S(2)}) collective-permute-start(bf16[3,16,3072]{2,1,0:T(8,128)(2,1)S(1)} %stack_i.1.tie.rest_0_), channel_id=1, source_target_pairs={{0,16},{4,20},{8,24},{12,28},{16,0},{20,4},{24,8},{28,12},{1,17},{... | collective-permute-start | bytes 884744 | tf_op jit(solution)/shard_map/ppermute | solution.py:47
  18.6 6.1 %collective-permute-start.15 = (bf16[64,512]{1,0:T(8,128)(2,1)S(1)}, bf16[64,512]{1,0:T(8,128)(2,1)S(1)}, u32[]{:S(2)}, u32[]{:S(2)}) collective-permute-start(bf16[64,512]{1,0:T(8,128)(2,1)S(1)} %get-tuple-element.83.tie), channel_id=1, source_target_pairs={{0,3},{1,0},{2,1},{3,2},{4,7},{5,4},{6,5},{7,6},{8,11},{9,8},{10,9... | collective-permute-start | bytes 196616 | tf_op jit(solution)/shard_map/ppermute | solution.py:42
  20.5 7.3 %collective-permute-start.14 = (bf16[64,512]{1,0:T(8,128)(2,1)S(1)}, bf16[64,512]{1,0:T(8,128)(2,1)S(1)}, u32[]{:S(2)}, u32[]{:S(2)}) collective-permute-start(bf16[64,512]{1,0:T(8,128)(2,1)S(1)} %get-tuple-element.83.tie), channel_id=1, source_target_pairs={{0,2},{1,3},{2,0},{3,1},{4,6},{5,7},{6,4},{7,5},{8,10},{9,11},{10,... | collective-permute-start | bytes 196616 | tf_op jit(solution)/shard_map/ppermute | solution.py:42
  20.8 6.9 %collective-permute-start.13 = (bf16[64,512]{1,0:T(8,128)(2,1)S(1)}, bf16[64,512]{1,0:T(8,128)(2,1)S(1)}, u32[]{:S(2)}, u32[]{:S(2)}) collective-permute-start(bf16[64,512]{1,0:T(8,128)(2,1)S(1)} %get-tuple-element.83.tie), channel_id=1, source_target_pairs={{0,1},{1,2},{2,3},{3,0},{4,5},{5,6},{6,7},{7,4},{8,9},{9,10},{10,1... | collective-permute-start | bytes 196616 | tf_op jit(solution)/shard_map/ppermute | solution.py:42
  24.1 19.9 %copy-start.14 = (f32[8004]{0:T(1024)S(1)}, f32[8004]{0:T(1024)}, u32[]{:S(2)}) copy-start(f32[8004]{0:T(1024)} %param.29) | copy-start | bytes 96052
  24.1 20.0 %slice-start = ((f32[8004]{0:T(1024)}), f32[324]{0:T(512)S(1)}, s32[]{:S(2)}) async-start(f32[8004]{0:T(1024)} %param.29), calls=%async_computation | async-start | bytes 4096 | tf_op jit(solution)/shard_map/slice | solution.py:642
  24.7 22.2 %copy-start.2 = (f32[128,3072]{1,0:T(8,128)S(1)}, f32[128,3072]{1,0:T(8,128)}, u32[]{:S(2)}) copy-start(f32[128,3072]{1,0:T(8,128)} %rest_0_.1) | copy-start | bytes 4718596
  24.7 18.2 %collective-permute-start.3 = (bf16[177,512]{1,0:T(8,128)(2,1)S(1)}, bf16[177,512]{1,0:T(8,128)(2,1)S(1)}, u32[]{:S(2)}, u32[]{:S(2)}) collective-permute-start(bf16[177,512]{1,0:T(8,128)(2,1)S(1)} %get-tuple-element.85), channel_id=1, source_target_pairs={{0,3},{1,0},{2,1},{3,2},{4,7},{5,4},{6,5},{7,6},{8,11},{9,8},{10,9... | collective-permute-start | bytes 543752 | tf_op jit(solution)/shard_map/ppermute | solution.py:42
  27.8 15.6 %collective-permute-start.4 = (bf16[177,512]{1,0:T(8,128)(2,1)S(1)}, bf16[177,512]{1,0:T(8,128)(2,1)S(1)}, u32[]{:S(2)}, u32[]{:S(2)}) collective-permute-start(bf16[177,512]{1,0:T(8,128)(2,1)S(1)} %get-tuple-element.86), channel_id=1, source_target_pairs={{0,2},{1,3},{2,0},{3,1},{4,6},{5,7},{6,4},{7,5},{8,10},{9,11},{10,... | collective-permute-start | bytes 543752 | tf_op jit(solution)/shard_map/ppermute | solution.py:42
  27.8 15.7 %collective-permute-start.5 = (bf16[177,512]{1,0:T(8,128)(2,1)S(1)}, bf16[177,512]{1,0:T(8,128)(2,1)S(1)}, u32[]{:S(2)}, u32[]{:S(2)}) collective-permute-start(bf16[177,512]{1,0:T(8,128)(2,1)S(1)} %get-tuple-element.87), channel_id=1, source_target_pairs={{0,1},{1,2},{2,3},{3,0},{4,5},{5,6},{6,7},{7,4},{8,9},{9,10},{10,1... | collective-permute-start | bytes 543752 | tf_op jit(solution)/shard_map/ppermute | solution.py:42
  28.8 15.2 %collective-permute-start.11 = (bf16[3,16,3072]{2,1,0:T(8,128)(2,1)S(1)}, bf16[3,16,3072]{2,1,0:T(8,128)(2,1)S(1)}, u32[]{:S(2)}, u32[]{:S(2)}) collective-permute-start(bf16[3,16,3072]{2,1,0:T(8,128)(2,1)S(1)} %collective-permute-done.7.rest_2_), channel_id=1, source_target_pairs={{0,16},{4,20},{8,24},{12,28},{16,0},{20,4},{24,8},{28,12},{1,17},{... | collective-permute-start | bytes 884744 | tf_op jit(solution)/shard_map/ppermute | solution.py:47
  42.9 8.2 %collective-permute-start.16 = (bf16[4,3,64,512]{3,2,1,0:T(8,128)(2,1)S(1)}, bf16[4,3,64,512]{3,2,1,0:T(8,128)(2,1)S(1)}, u32[]{:S(2)}, u32[]{:S(2)}) collective-permute-start(bf16[4,3,64,512]{3,2,1,0:T(8,128)(2,1)S(1)} %bitcast.23), channel_id=1, source_target_pairs={{0,4},{4,0},{8,12},{12,8},{16,20},{20,16},{24,28},{28,24},{1,5},{5... | collective-permute-start | bytes 2359304 | tf_op jit(solution)/shard_map/ppermute | solution.py:47
  42.9 2.7 %collective-permute-start.6 = (bf16[3,16,3072]{2,1,0:T(8,128)(2,1)S(1)}, bf16[3,16,3072]{2,1,0:T(8,128)(2,1)S(1)}, u32[]{:S(2)}, u32[]{:S(2)}) collective-permute-start(bf16[3,16,3072]{2,1,0:T(8,128)(2,1)S(1)} %stack_i.1.tie.rest_0_), channel_id=1, source_target_pairs={{0,4},{4,0},{8,12},{12,8},{16,20},{20,16},{24,28},{28,24},{1,5},{5... | collective-permute-start | bytes 884744 | tf_op jit(solution)/shard_map/ppermute | solution.py:47
  43.4 2.6 %collective-permute-start.10 = (bf16[3,16,3072]{2,1,0:T(8,128)(2,1)S(1)}, bf16[3,16,3072]{2,1,0:T(8,128)(2,1)S(1)}, u32[]{:S(2)}, u32[]{:S(2)}) collective-permute-start(bf16[3,16,3072]{2,1,0:T(8,128)(2,1)S(1)} %collective-permute-done.9.rest_4_.tie), channel_id=1, source_target_pairs={{0,4},{4,0},{8,12},{12,8},{16,20},{20,16},{24,28},{28,24},{1,5},{5... | collective-permute-start | bytes 884744 | tf_op jit(solution)/shard_map/ppermute | solution.py:47
  43.5 3.0 %collective-permute-start.8 = (bf16[3,16,3072]{2,1,0:T(8,128)(2,1)S(1)}, bf16[3,16,3072]{2,1,0:T(8,128)(2,1)S(1)}, u32[]{:S(2)}, u32[]{:S(2)}) collective-permute-start(bf16[3,16,3072]{2,1,0:T(8,128)(2,1)S(1)} %collective-permute-done.7.rest_2_), channel_id=1, source_target_pairs={{0,4},{4,0},{8,12},{12,8},{16,20},{20,16},{24,28},{28,24},{1,5},{5... | collective-permute-start | bytes 884744 | tf_op jit(solution)/shard_map/ppermute | solution.py:47
  43.9 2.9 %collective-permute-start.12 = (bf16[3,16,3072]{2,1,0:T(8,128)(2,1)S(1)}, bf16[3,16,3072]{2,1,0:T(8,128)(2,1)S(1)}, u32[]{:S(2)}, u32[]{:S(2)}) collective-permute-start(bf16[3,16,3072]{2,1,0:T(8,128)(2,1)S(1)} %collective-permute-done.11.rest_6_), channel_id=1, source_target_pairs={{0,4},{4,0},{8,12},{12,8},{16,20},{20,16},{24,28},{28,24},{1,5},{5... | collective-permute-start | bytes 884744 | tf_op jit(solution)/shard_map/ppermute | solution.py:47
  51.1 1.8 %copy-start.1 = (f32[384,512]{1,0:T(8,128)S(1)}, f32[384,512]{1,0:T(8,128)}, u32[]{:S(2)}) copy-start(f32[384,512]{1,0:T(8,128)} %rest_3_.1) | copy-start | bytes 2359300
  58.1 4.0 %collective-permute-start.17 = (bf16[4,448,512]{2,1,0:T(8,128)(2,1)S(1)}, bf16[4,448,512]{2,1,0:T(8,128)(2,1)S(1)}, u32[]{:S(2)}, u32[]{:S(2)}) collective-permute-start(bf16[4,448,512]{2,1,0:T(8,128)(2,1)S(1)} %get-tuple-element.109), channel_id=1, source_target_pairs={{0,4},{4,0},{8,12},{12,8},{16,20},{20,16},{24,28},{28,24},{1,5},{5... | collective-permute-start | bytes 5505032 | tf_op jit(solution)/shard_map/ppermute | solution.py:47
  61.6 11.3 %collective-permute-start.27 = (bf16[4,192,512]{2,1,0:T(8,128)(2,1)S(1)}, bf16[4,192,512]{2,1,0:T(8,128)(2,1)S(1)}, u32[]{:S(2)}, u32[]{:S(2)}) collective-permute-start(bf16[4,192,512]{2,1,0:T(8,128)(2,1)S(1)} %get-tuple-element.125), channel_id=1, source_target_pairs={{0,4},{4,0},{8,12},{12,8},{16,20},{20,16},{24,28},{28,24},{1,5},{5... | collective-permute-start | bytes 2359304 | tf_op jit(solution)/shard_map/ppermute | solution.py:47
  62.5 22.5 %collective-permute-start.22 = (bf16[448,512]{1,0:T(8,128)(2,1)S(1)}, bf16[448,512]{1,0:T(8,128)(2,1)S(1)}, u32[]{:S(2)}, u32[]{:S(2)}) collective-permute-start(bf16[448,512]{1,0:T(8,128)(2,1)S(1)} %get-tuple-element.119), channel_id=1, source_target_pairs={{0,16},{4,20},{8,24},{12,28},{16,0},{20,4},{24,8},{28,12},{1,17},{... | collective-permute-start | bytes 1376264 | tf_op jit(solution)/shard_map/ppermute | solution.py:47
  64.0 23.8 %collective-permute-start.23 = (bf16[448,512]{1,0:T(8,128)(2,1)S(1)}, bf16[448,512]{1,0:T(8,128)(2,1)S(1)}, u32[]{:S(2)}, u32[]{:S(2)}) collective-permute-start(bf16[448,512]{1,0:T(8,128)(2,1)S(1)} %get-tuple-element.110.rest_0_), channel_id=1, source_target_pairs={{0,24},{4,28},{8,16},{12,20},{16,8},{20,12},{24,0},{28,4},{1,25},{... | collective-permute-start | bytes 1376264 | tf_op jit(solution)/shard_map/ppermute | solution.py:47
  65.5 23.8 %collective-permute-start.21 = (bf16[448,512]{1,0:T(8,128)(2,1)S(1)}, bf16[448,512]{1,0:T(8,128)(2,1)S(1)}, u32[]{:S(2)}, u32[]{:S(2)}) collective-permute-start(bf16[448,512]{1,0:T(8,128)(2,1)S(1)} %get-tuple-element.118.tie), channel_id=1, source_target_pairs={{0,8},{4,12},{8,0},{12,4},{16,24},{20,28},{24,16},{28,20},{1,9},{5... | collective-permute-start | bytes 1376264 | tf_op jit(solution)/shard_map/ppermute | solution.py:47
  70.4 7.8 %collective-permute-start.18 = (bf16[177,512]{1,0:T(8,128)(2,1)S(1)}, bf16[177,512]{1,0:T(8,128)(2,1)S(1)}, u32[]{:S(2)}, u32[]{:S(2)}) collective-permute-start(bf16[177,512]{1,0:T(8,128)(2,1)S(1)} %get-tuple-element.112), channel_id=1, source_target_pairs={{0,1},{1,2},{2,3},{3,0},{4,5},{5,6},{6,7},{7,4},{8,9},{9,10},{10,1... | collective-permute-start | bytes 543752 | tf_op jit(solution)/shard_map/ppermute | solution.py:42
  73.0 1.2 collective-permute-start.28
  74.4 21.7 %collective-permute-start.29 = (bf16[208,512]{1,0:T(8,128)(2,1)S(1)}, bf16[208,512]{1,0:T(8,128)(2,1)S(1)}, u32[]{:S(2)}, u32[]{:S(2)}) collective-permute-start(bf16[208,512]{1,0:T(8,128)(2,1)S(1)} %get-tuple-element.129), channel_id=1, source_target_pairs={{0,8},{4,12},{8,0},{12,4},{16,24},{20,28},{24,16},{28,20},{1,9},{5... | collective-permute-start | bytes 638984 | tf_op jit(solution)/shard_map/ppermute | solution.py:47
  78.2 12.8 %collective-permute-start.19 = (bf16[177,512]{1,0:T(8,128)(2,1)S(1)}, bf16[177,512]{1,0:T(8,128)(2,1)S(1)}, u32[]{:S(2)}, u32[]{:S(2)}) collective-permute-start(bf16[177,512]{1,0:T(8,128)(2,1)S(1)} %get-tuple-element.113), channel_id=1, source_target_pairs={{0,2},{1,3},{2,0},{3,1},{4,6},{5,7},{6,4},{7,5},{8,10},{9,11},{10,... | collective-permute-start | bytes 543752 | tf_op jit(solution)/shard_map/ppermute | solution.py:42
  84.9 7.3 %collective-permute-start.20 = (bf16[177,512]{1,0:T(8,128)(2,1)S(1)}, bf16[177,512]{1,0:T(8,128)(2,1)S(1)}, u32[]{:S(2)}, u32[]{:S(2)}) collective-permute-start(bf16[177,512]{1,0:T(8,128)(2,1)S(1)} %get-tuple-element.114), channel_id=1, source_target_pairs={{0,3},{1,0},{2,1},{3,2},{4,7},{5,4},{6,5},{7,6},{8,11},{9,8},{10,9... | collective-permute-start | bytes 543752 | tf_op jit(solution)/shard_map/ppermute | solution.py:42
  87.8 10.8 %collective-permute-start.30 = (bf16[208,512]{1,0:T(8,128)(2,1)S(1)}, bf16[208,512]{1,0:T(8,128)(2,1)S(1)}, u32[]{:S(2)}, u32[]{:S(2)}) collective-permute-start(bf16[208,512]{1,0:T(8,128)(2,1)S(1)} %get-tuple-element.130), channel_id=1, source_target_pairs={{0,16},{4,20},{8,24},{12,28},{16,0},{20,4},{24,8},{28,12},{1,17},{... | collective-permute-start | bytes 638984 | tf_op jit(solution)/shard_map/ppermute | solution.py:47
  89.3 9.3 %collective-permute-start.31 = (bf16[208,512]{1,0:T(8,128)(2,1)S(1)}, bf16[208,512]{1,0:T(8,128)(2,1)S(1)}, u32[]{:S(2)}, u32[]{:S(2)}) collective-permute-start(bf16[208,512]{1,0:T(8,128)(2,1)S(1)} %get-tuple-element.131), channel_id=1, source_target_pairs={{0,24},{4,28},{8,16},{12,20},{16,8},{20,12},{24,0},{28,4},{1,25},{... | collective-permute-start | bytes 638984 | tf_op jit(solution)/shard_map/ppermute | solution.py:47
  91.0 11.3 %collective-permute-start.25 = (bf16[112,512]{1,0:T(8,128)(2,1)S(1)}, bf16[112,512]{1,0:T(8,128)(2,1)S(1)}, u32[]{:S(2)}, u32[]{:S(2)}) collective-permute-start(bf16[112,512]{1,0:T(8,128)(2,1)S(1)} %get-tuple-element.122), channel_id=1, source_target_pairs={{0,2},{1,3},{2,0},{3,1},{4,6},{5,7},{6,4},{7,5},{8,10},{9,11},{10,... | collective-permute-start | bytes 344072 | tf_op jit(solution)/shard_map/ppermute | solution.py:42
  92.2 10.8 %collective-permute-start.26 = (bf16[112,512]{1,0:T(8,128)(2,1)S(1)}, bf16[112,512]{1,0:T(8,128)(2,1)S(1)}, u32[]{:S(2)}, u32[]{:S(2)}) collective-permute-start(bf16[112,512]{1,0:T(8,128)(2,1)S(1)} %get-tuple-element.123), channel_id=1, source_target_pairs={{0,3},{1,0},{2,1},{3,2},{4,7},{5,4},{6,5},{7,6},{8,11},{9,8},{10,9... | collective-permute-start | bytes 344072 | tf_op jit(solution)/shard_map/ppermute | solution.py:42
  96.1 7.9 %collective-permute-start.24 = (bf16[112,512]{1,0:T(8,128)(2,1)S(1)}, bf16[112,512]{1,0:T(8,128)(2,1)S(1)}, u32[]{:S(2)}, u32[]{:S(2)}) collective-permute-start(bf16[112,512]{1,0:T(8,128)(2,1)S(1)} %get-tuple-element.121.tie), channel_id=1, source_target_pairs={{0,1},{1,2},{2,3},{3,0},{4,5},{5,6},{6,7},{7,4},{8,9},{9,10},{10,1... | collective-permute-start | bytes 344072 | tf_op jit(solution)/shard_map/ppermute | solution.py:42
  96.1 29.3 %copy-start.15 = (f32[8004]{0:T(1024)S(1)}, f32[8004]{0:T(1024)}, u32[]{:S(2)}) copy-start(f32[8004]{0:T(1024)} %param.31) | copy-start | bytes 96052
  96.1 29.3 %copy-start.16 = (f32[8004]{0:T(1024)S(1)}, f32[8004]{0:T(1024)}, u32[]{:S(2)}) copy-start(f32[8004]{0:T(1024)} %param.30) | copy-start | bytes 96052
  96.1 30.0 %copy-start.11 = (f32[81,324]{1,0:T(8,128)S(1)}, f32[81,324]{1,0:T(8,128)}, u32[]{:S(2)}) copy-start(f32[81,324]{1,0:T(8,128)} %rest_8_.1) | copy-start | bytes 314932
  97.8 18.0 %copy-start.7 = (f32[4,81,1,512]{3,2,1,0:T(1,128)S(1)}, f32[4,81,1,512]{3,2,1,0:T(1,128)}, u32[]{:S(2)}) copy-start(f32[4,81,1,512]{3,2,1,0:T(1,128)} %get-tuple-element.116.tie_home) | copy-start | bytes 1990660
  98.6 27.5 %copy-start.6 = (f32[384,512]{1,0:T(8,128)S(1)}, f32[384,512]{1,0:T(8,128)}, u32[]{:S(2)}) copy-start(f32[384,512]{1,0:T(8,128)} %rest_5_.1) | copy-start | bytes 2359300
  98.7 17.1 %collective-permute-start.32 = (bf16[64,512]{1,0:T(8,128)(2,1)S(1)}, bf16[64,512]{1,0:T(8,128)(2,1)S(1)}, u32[]{:S(2)}, u32[]{:S(2)}) collective-permute-start(bf16[64,512]{1,0:T(8,128)(2,1)S(1)} %get-tuple-element.134), channel_id=1, source_target_pairs={{0,1},{1,2},{2,3},{3,0},{4,5},{5,6},{6,7},{7,4},{8,9},{9,10},{10,1... | collective-permute-start | bytes 196616 | tf_op jit(solution)/shard_map/ppermute | solution.py:42
  98.9 16.9 %collective-permute-start.33 = (bf16[64,512]{1,0:T(8,128)(2,1)S(1)}, bf16[64,512]{1,0:T(8,128)(2,1)S(1)}, u32[]{:S(2)}, u32[]{:S(2)}) collective-permute-start(bf16[64,512]{1,0:T(8,128)(2,1)S(1)} %get-tuple-element.135), channel_id=1, source_target_pairs={{0,2},{1,3},{2,0},{3,1},{4,6},{5,7},{6,4},{7,5},{8,10},{9,11},{10,... | collective-permute-start | bytes 196616 | tf_op jit(solution)/shard_map/ppermute | solution.py:42
  102.3 13.5 %collective-permute-start.34 = (bf16[64,512]{1,0:T(8,128)(2,1)S(1)}, bf16[64,512]{1,0:T(8,128)(2,1)S(1)}, u32[]{:S(2)}, u32[]{:S(2)}) collective-permute-start(bf16[64,512]{1,0:T(8,128)(2,1)S(1)} %get-tuple-element.136), channel_id=1, source_target_pairs={{0,3},{1,0},{2,1},{3,2},{4,7},{5,4},{6,5},{7,6},{8,11},{9,8},{10,9... | collective-permute-start | bytes 196616 | tf_op jit(solution)/shard_map/ppermute | solution.py:42
  104.0 22.1 %copy-start.5 = (f32[384,512]{1,0:T(8,128)S(1)}, f32[384,512]{1,0:T(8,128)}, u32[]{:S(2)}) copy-start(f32[384,512]{1,0:T(8,128)} %rest_4_.1) | copy-start | bytes 2359300
  104.0 22.0 %copy-start.3 = (f32[128,3072]{1,0:T(8,128)S(1)}, f32[128,3072]{1,0:T(8,128)}, u32[]{:S(2)}) copy-start(f32[128,3072]{1,0:T(8,128)} %rest_1_.1) | copy-start | bytes 4718596
  104.0 22.0 %copy-start.4 = (f32[128,3072]{1,0:T(8,128)S(1)}, f32[128,3072]{1,0:T(8,128)}, u32[]{:S(2)}) copy-start(f32[128,3072]{1,0:T(8,128)} %rest_2_.1) | copy-start | bytes 4718596
  104.1 22.0 %copy-start.10 = (f32[81,324]{1,0:T(8,128)S(1)}, f32[81,324]{1,0:T(8,128)}, u32[]{:S(2)}) copy-start(f32[81,324]{1,0:T(8,128)} %rest_7_.1) | copy-start | bytes 314932
  (5 other events, 5.2 us)

commit v8 on v7

--- a/solution.py
+++ b/solution.py
@@ -224,7 +224,7 @@
     win[pl.ds(aligned(own * 128, 128), 128), :] = wi_own[...].astype(BF)
     for e in range(8):
         for r in (1, 2, 3):
-            who = lax.rem(own + (4 - r), 4)
+            who = lax.rem(own + r, 4)
             at = who * 128 + (unit ^ e) * STEP
             win[pl.ds(aligned(at, STEP), STEP), :] = wi[e][r - 1]
 
@@ -605,7 +605,7 @@
     )
     (base_in,) = call(
         stack_tied_kernel,
-        [turn(wi_piece, r) for r in (1, 2, 3)] + [msg],
+        [turn(wi_piece, -r) for r in (1, 2, 3)] + [msg],
         [((3, in_unit, hidden), BF)],
         specs=[VM] * 3 + [ANY],
         limit=8,

time: 130 us -> 130 us (level)
  starting transfers between devices: 42.1 us -> 44.9 us
  waiting for transfers between devices: 16.7 us -> 14.4 us
    ppermute x18, starting transfers between devices: 28.7 us -> 31.5 us  [turn(): return lax.ppermute(arr, 'patch', [(s, (s + r) % n) for s in range(n)])]
    ppermute x18, waiting for transfers between devices: 7.14 us -> 5.24 us  [turn(): return lax.ppermute(arr, 'patch', [(s, (s + r) % n) for s in range(n)])]
  transfers between devices with their start and end apart: 35 -> 35, of which waited for: 10 -> 12; matrix products, arithmetic and copies ran while one was open for 1% -> 1% of each run, Pallas kernels for 14% -> 14%
where the time goes in v8:
time: 130 us
  starting transfers between devices  44.9 us (35%)
  blocking collectives  33.8 us (26%)
  Pallas kernels  28.8 us (22%)
  waiting for transfers between devices  14.4 us (11%)
  local copies, waits for them, and re-layouts  5.81 us (4%)
    ppermute x18, starting transfers between devices, turn(): return lax.ppermute(arr, 'patch', [(s, (s + r) % n) for s in range(n)])  31.5 us
    pallas_call x20, Pallas kernels, call(): pl.pallas_call(body, out_shape=[jax.ShapeDtypeStruct(s, d) for s, d in ou...  28.8 us
    all_gather x2, blocking collectives, img_gather(): return lax.all_gather(arr, 'img', axis_index_groups=groups)  20.2 us
    all_gather x1, blocking collectives, shards(): joined = lax.all_gather(held, 'img', axis_index_groups=planes)  13.6 us
    ppermute x17, starting transfers between devices, swap(): return lax.ppermute(arr, 'img', [(k, k ^ mask) for k in range(n)])  13.4 us
    ppermute x17, waiting for transfers between devices, swap(): return lax.ppermute(arr, 'img', [(k, k ^ mask) for k in range(n)])  9.18 us
    ppermute x18, waiting for transfers between devices, turn(): return lax.ppermute(arr, 'patch', [(s, (s + r) % n) for s in range(n)])  5.24 us
    unnamed x35, local copies, waits for them, and re-layouts  3.47 us
  transfers between devices with their start and end apart: 35, of which 12 were waited for; matrix products, arithmetic and copies ran while one was open for 1% of the time, Pallas kernels for 14%

profile of v8, /device:TPU:0, one launch (start us, length us, event | category | flops | bytes accessed | tf_op | source)
XLA Modules:
  0.0 129.7 jit_solution(12744391780829318234)
XLA Ops:
  0.7 0.9 dynamic-slice_convert_fusion
  1.6 3.1 %collective-permute-start.2 = (bf16[16,3072]{1,0:T(8,128)(2,1)S(1)}, bf16[16,3072]{1,0:T(8,128)(2,1)S(1)}, u32[]{:S(2)}, u32[]{:S(2)}) collective-permute-start(bf16[16,3072]{1,0:T(8,128)(2,1)S(1)} %dynamic-slice_convert_fusion), channel_id=1, source_target_pairs={{0,1},{1,2},{2,3},{3,0},{4,5},{5,6},{6,7},{7,4},{8,9},{9,10},{10,1... | collective-permute-start | bytes 294920 | tf_op jit(solution)/shard_map/ppermute | solution.py:42
  4.7 2.6 %collective-permute-start.1 = (bf16[16,3072]{1,0:T(8,128)(2,1)S(1)}, bf16[16,3072]{1,0:T(8,128)(2,1)S(1)}, u32[]{:S(2)}, u32[]{:S(2)}) collective-permute-start(bf16[16,3072]{1,0:T(8,128)(2,1)S(1)} %dynamic-slice_convert_fusion), channel_id=1, source_target_pairs={{0,2},{1,3},{2,0},{3,1},{4,6},{5,7},{6,4},{7,5},{8,10},{9,11},{10,... | collective-permute-start | bytes 294920 | tf_op jit(solution)/shard_map/ppermute | solution.py:42
  7.3 1.3 %collective-permute-start = (bf16[16,3072]{1,0:T(8,128)(2,1)S(1)}, bf16[16,3072]{1,0:T(8,128)(2,1)S(1)}, u32[]{:S(2)}, u32[]{:S(2)}) collective-permute-start(bf16[16,3072]{1,0:T(8,128)(2,1)S(1)} %dynamic-slice_convert_fusion), channel_id=1, source_target_pairs={{0,3},{1,0},{2,1},{3,2},{4,7},{5,4},{6,5},{7,6},{8,11},{9,8},{10,9... | collective-permute-start | bytes 294920 | tf_op jit(solution)/shard_map/ppermute | solution.py:42
  8.7 1.1 copy-done
  9.8 0.9 copy-done.8
  10.7 0.7 copy-done.12
  11.4 0.7 copy-done.13
  12.1 1.3 %prep_out.1 = (bf16[64,512]{1,0:T(8,128)(2,1)S(1)}, s32[336,1]{1,0:T(8,128)S(1)}, s32[1,336]{1,0:T(1,128)S(1)}, bf16[336,512]{1,0:T(8,128)(2,1)S(1)}, bf16[512,336]{1,0:T(8,128)(2,1)S(1)}) custom-call(s32[2]{0:T(128)S(1)} %pad_add_fusion.scal, s32[1,4]{1,0:T(1,128)S(1)} %bitcast.33, s32[4,1,324]{2,1,0:T(1,128)S(1)} %copy-done.12, f32[384,512]{1,0:T(8,128)S(1)} %copy-done, ...), custom_call_target="tpu_custom_call" | custom-call | flops 100000000 | bytes 896616 | tf_op jit(solution)/shard_map/prep_out/pallas_call | solution.py:531
  13.9 1.6 %collective-permute-start.7 = (bf16[3,16,3072]{2,1,0:T(8,128)(2,1)S(1)}, bf16[3,16,3072]{2,1,0:T(8,128)(2,1)S(1)}, u32[]{:S(2)}, u32[]{:S(2)}) collective-permute-start(bf16[3,16,3072]{2,1,0:T(8,128)(2,1)S(1)} %stack_i.1.tie.rest_0_), channel_id=1, source_target_pairs={{0,8},{4,12},{8,0},{12,4},{16,24},{20,28},{24,16},{28,20},{1,9},{5... | collective-permute-start | bytes 884744 | tf_op jit(solution)/shard_map/ppermute | solution.py:47
  15.5 1.5 %collective-permute-start.9 = (bf16[3,16,3072]{2,1,0:T(8,128)(2,1)S(1)}, bf16[3,16,3072]{2,1,0:T(8,128)(2,1)S(1)}, u32[]{:S(2)}, u32[]{:S(2)}) collective-permute-start(bf16[3,16,3072]{2,1,0:T(8,128)(2,1)S(1)} %stack_i.1.tie.rest_0_), channel_id=1, source_target_pairs={{0,16},{4,20},{8,24},{12,28},{16,0},{20,4},{24,8},{28,12},{1,17},{... | collective-permute-start | bytes 884744 | tf_op jit(solution)/shard_map/ppermute | solution.py:47
  17.0 3.6 %collective-permute-start.15 = (bf16[64,512]{1,0:T(8,128)(2,1)S(1)}, bf16[64,512]{1,0:T(8,128)(2,1)S(1)}, u32[]{:S(2)}, u32[]{:S(2)}) collective-permute-start(bf16[64,512]{1,0:T(8,128)(2,1)S(1)} %get-tuple-element.83.tie), channel_id=1, source_target_pairs={{0,3},{1,0},{2,1},{3,2},{4,7},{5,4},{6,5},{7,6},{8,11},{9,8},{10,9... | collective-permute-start | bytes 196616 | tf_op jit(solution)/shard_map/ppermute | solution.py:42
  21.2 1.2 copy_bitcast_fusion
  22.4 0.6 prep_rows.1
  23.0 3.8 %collective-permute-start.3 = (bf16[177,512]{1,0:T(8,128)(2,1)S(1)}, bf16[177,512]{1,0:T(8,128)(2,1)S(1)}, u32[]{:S(2)}, u32[]{:S(2)}) collective-permute-start(bf16[177,512]{1,0:T(8,128)(2,1)S(1)} %get-tuple-element.85), channel_id=1, source_target_pairs={{0,3},{1,0},{2,1},{3,2},{4,7},{5,4},{6,5},{7,6},{8,11},{9,8},{10,9... | collective-permute-start | bytes 543752 | tf_op jit(solution)/shard_map/ppermute | solution.py:42
  26.8 0.6 collective-permute-done.14.m2
  27.8 0.9 collective-permute-start.5
  28.7 0.6 collective-permute-start.11
  29.3 13.6 %all-gather = bf16[12,64,512]{2,1,0:T(8,128)(2,1)S(1)} all-gather(bf16[3,64,512]{2,1,0:T(8,128)(2,1)S(1)} %hold_out.1), channel_id=2, replica_groups={{0,8,16,24},{4,12,20,28},{1,9,17,25},{5,13,21,29},{2,10,18,26},{6,14,22..., dimensions={0}, use_global_device_ids=true | all-gather | bytes 983040 | tf_op jit(solution)/shard_map/all_gather | solution.py:635
  42.9 0.5 collective-permute-start.6
  44.2 1.4 %norm_in.1 = (bf16[336,512]{1,0:T(8,128)(2,1)S(1)}, bf16[336,512]{1,0:T(8,128)(2,1)S(1)}) custom-call(s32[336,1]{1,0:T(8,128)S(1)} %get-tuple-element.81.slot_ref, bf16[177,512]{1,0:T(8,128)(2,1)S(1)} %get-tuple-element.84.m0, bf16[177,512]{1,0:T(8,128)(2,1)S(1)} %collective-permute-done.3.m1, bf16[177,512]{1,0:T(8,128)(2,1)S(1)} %collective-permute-done.4.m2, ...), custom_call_target="tpu_custom_call" | custom-call | flops 100000000 | bytes 730432 | tf_op jit(solution)/shard_map/norm_in/pallas_call | solution.py:531
  46.8 3.1 %right.1 = (bf16[512,3072]{1,0:T(8,128)(2,1)S(1)}, f32[336,1536]{1,0:T(8,128)S(1)}, f32[336,1]{1,0:T(8,128)S(1)}, f32[336,1536]{1,0:T(8,128)S(1)}, bf16[336,1536]{1,0:T(8,128)(2,1)S(1)}) custom-call(s32[2]{0:T(128)S(1)} %pad_add_fusion.scal, s32[336,1]{1,0:T(8,128)S(1)} %get-tuple-element.81.slot_ref, bf16[336,512]{1,0:T(8,128)(2,1)S(1)} %get-tuple-element.89.xn_ref, ...), custom_call_target="tpu_custom_call" | custom-call | flops 1500000000 | bytes 4302152 | tf_op jit(solution)/shard_map/right/pallas_call | solution.py:531
  49.9 1.1 place_cot.1
  51.1 1.7 %left.1 = (f32[336,1536]{1,0:T(8,128)S(1)}, f32[336,1536]{1,0:T(8,128)S(1)}) custom-call(bf16[336,512]{1,0:T(8,128)(2,1)S(1)} %get-tuple-element.89.xn_ref, f32[1,3072]{1,0:T(1,128)S(1)} %bitcast.27, bf16[512,3072]{1,0:T(8,128)(2,1)S(1)} %get-tuple-element.92.win, bf16[4,3,64,512]{3,2,1,0:T(8,128)(2,1)S(1)} %collective-permute-done.16.rest_0_.rest_1_), custom_call_target="tpu_custom_call" | custom-call | flops 1000000000 | bytes 4288512 | tf_op jit(solution)/shard_map/left/pallas_call | solution.py:531
  52.9 5.2 %spatial.1 = (bf16[336,336]{1,0:T(8,128)(2,1)S(1)}, bf16[336,1536]{1,0:T(8,128)(2,1)S(1)}, bf16[336,1536]{1,0:T(8,128)(2,1)S(1)}, bf16[336,1536]{1,0:T(8,128)(2,...) custom-call(s32[2]{0:T(128)S(1)} %pad_add_fusion.scal, ...), custom_call_target="tpu_custom_call" | custom-call | flops 4000000000 | bytes 9002840 | tf_op jit(solution)/shard_map/spatial/pallas_call | solution.py:531
  58.2 3.3 %back.1 = (bf16[336,1536]{1,0:T(8,128)(2,1)S(1)}, bf16[4,192,512]{2,1,0:T(8,128)(2,1)S(1)}, bf16[4,192,512]{2,1,0:T(8,128)(2,1)S(1)}, f32[6,512]{1,0:T(8,128)S(1)}) custom-call(s32[336,1]{1,0:T(8,128)S(1)} %get-tuple-element.81.slot_ref, bf16[512,336]{1,0:T(8,128)(2,1)S(1)} %get-tuple-element.95.xt_ref, bf16[336,336]{1,0:T(8,128)(2,1)S(1)} %get-tuple-element.99.mix_ref, ...), custom_call_target="tpu_custom_call" | custom-call | flops 2000000000 | bytes 5739648 | tf_op jit(solution)/shard_map/back/pallas_call | solution.py:531
  62.4 1.6 %collective-permute-start.22 = (bf16[448,512]{1,0:T(8,128)(2,1)S(1)}, bf16[448,512]{1,0:T(8,128)(2,1)S(1)}, u32[]{:S(2)}, u32[]{:S(2)}) collective-permute-start(bf16[448,512]{1,0:T(8,128)(2,1)S(1)} %get-tuple-element.119), channel_id=1, source_target_pairs={{0,16},{4,20},{8,24},{12,28},{16,0},{20,4},{24,8},{28,12},{1,17},{... | collective-permute-start | bytes 1376264 | tf_op jit(solution)/shard_map/ppermute | solution.py:47
  64.0 1.5 %collective-permute-start.23 = (bf16[448,512]{1,0:T(8,128)(2,1)S(1)}, bf16[448,512]{1,0:T(8,128)(2,1)S(1)}, u32[]{:S(2)}, u32[]{:S(2)}) collective-permute-start(bf16[448,512]{1,0:T(8,128)(2,1)S(1)} %get-tuple-element.110.rest_0_), channel_id=1, source_target_pairs={{0,24},{4,28},{8,16},{12,20},{16,8},{20,12},{24,0},{28,4},{1,25},{... | collective-permute-start | bytes 1376264 | tf_op jit(solution)/shard_map/ppermute | solution.py:47
  65.4 0.5 collective-permute-start.21
  66.0 4.4 %token_grad.1 = (bf16[177,512]{1,0:T(8,128)(2,1)S(1)}, bf16[177,512]{1,0:T(8,128)(2,1)S(1)}, bf16[177,512]{1,0:T(8,128)(2,1)S(1)}, bf16[177,512]{1,0:T(8,128)(2,1)S(1)}, f32[16,512]{1,0:T(8,128)S(1)}) custom-call(s32[336,1]{1,0:T(8,128)S(1)} %get-tuple-element.81.slot_ref, s32[1,336]{1,0:T(1,128)S(1)} %get-tuple-element.82.slot_row, ...), custom_call_target="tpu_custom_call" | custom-call | flops 2000000000 | bytes 10013312 | tf_op jit(solution)/shard_map/token_grad/pallas_call | solution.py:531
  70.3 2.6 %collective-permute-start.18 = (bf16[177,512]{1,0:T(8,128)(2,1)S(1)}, bf16[177,512]{1,0:T(8,128)(2,1)S(1)}, u32[]{:S(2)}, u32[]{:S(2)}) collective-permute-start(bf16[177,512]{1,0:T(8,128)(2,1)S(1)} %get-tuple-element.112), channel_id=1, source_target_pairs={{0,1},{1,2},{2,3},{3,0},{4,5},{5,6},{6,7},{7,4},{8,9},{9,10},{10,1... | collective-permute-start | bytes 543752 | tf_op jit(solution)/shard_map/ppermute | solution.py:42
  72.9 1.2 collective-permute-done.28.vec_got
  74.3 1.6 %collective-permute-start.29 = (bf16[208,512]{1,0:T(8,128)(2,1)S(1)}, bf16[208,512]{1,0:T(8,128)(2,1)S(1)}, u32[]{:S(2)}, u32[]{:S(2)}) collective-permute-start(bf16[208,512]{1,0:T(8,128)(2,1)S(1)} %get-tuple-element.129), channel_id=1, source_target_pairs={{0,8},{4,12},{8,0},{12,4},{16,24},{20,28},{24,16},{28,20},{1,9},{5... | collective-permute-start | bytes 638984 | tf_op jit(solution)/shard_map/ppermute | solution.py:47
  75.9 2.2 %collective-permute-done.18.h1 = bf16[177,512]{1,0:T(8,128)(2,1)S(1)} collective-permute-done((bf16[177,512]{1,0:T(8,128)(2,1)S(1)}, bf16[177,512]{1,0:T(8,128)(2,1)S(1)}, u32[]{:S(2)}, u32[]{:S(2)}) %collective-permute-start.18) | collective-permute-done | bytes 181280 | tf_op jit(solution)/shard_map/ppermute | solution.py:42
  78.6 6.3 %collective-permute-done.22.g2 = bf16[448,512]{1,0:T(8,128)(2,1)S(1)} collective-permute-done((bf16[448,512]{1,0:T(8,128)(2,1)S(1)}, bf16[448,512]{1,0:T(8,128)(2,1)S(1)}, u32[]{:S(2)}, u32[]{:S(2)}) %collective-permute-start.22) | collective-permute-done | bytes 458784 | tf_op jit(solution)/shard_map/ppermute | solution.py:47
  84.9 3.2 %collective-permute-start.20 = (bf16[177,512]{1,0:T(8,128)(2,1)S(1)}, bf16[177,512]{1,0:T(8,128)(2,1)S(1)}, u32[]{:S(2)}, u32[]{:S(2)}) collective-permute-start(bf16[177,512]{1,0:T(8,128)(2,1)S(1)} %get-tuple-element.114), channel_id=1, source_target_pairs={{0,3},{1,0},{2,1},{3,2},{4,7},{5,4},{6,5},{7,6},{8,11},{9,8},{10,9... | collective-permute-start | bytes 543752 | tf_op jit(solution)/shard_map/ppermute | solution.py:42
  88.1 1.5 %collective-permute-start.30 = (bf16[208,512]{1,0:T(8,128)(2,1)S(1)}, bf16[208,512]{1,0:T(8,128)(2,1)S(1)}, u32[]{:S(2)}, u32[]{:S(2)}) collective-permute-start(bf16[208,512]{1,0:T(8,128)(2,1)S(1)} %get-tuple-element.130), channel_id=1, source_target_pairs={{0,16},{4,20},{8,24},{12,28},{16,0},{20,4},{24,8},{28,12},{1,17},{... | collective-permute-start | bytes 638984 | tf_op jit(solution)/shard_map/ppermute | solution.py:47
  89.6 1.5 %collective-permute-start.31 = (bf16[208,512]{1,0:T(8,128)(2,1)S(1)}, bf16[208,512]{1,0:T(8,128)(2,1)S(1)}, u32[]{:S(2)}, u32[]{:S(2)}) collective-permute-start(bf16[208,512]{1,0:T(8,128)(2,1)S(1)} %get-tuple-element.131), channel_id=1, source_target_pairs={{0,24},{4,28},{8,16},{12,20},{16,8},{20,12},{24,0},{28,4},{1,25},{... | collective-permute-start | bytes 638984 | tf_op jit(solution)/shard_map/ppermute | solution.py:47
  91.3 0.9 collective-permute-start.25
  92.4 4.3 %collective-permute-start.26 = (bf16[112,512]{1,0:T(8,128)(2,1)S(1)}, bf16[112,512]{1,0:T(8,128)(2,1)S(1)}, u32[]{:S(2)}, u32[]{:S(2)}) collective-permute-start(bf16[112,512]{1,0:T(8,128)(2,1)S(1)} %get-tuple-element.123), channel_id=1, source_target_pairs={{0,3},{1,0},{2,1},{3,2},{4,7},{5,4},{6,5},{7,6},{8,11},{9,8},{10,9... | collective-permute-start | bytes 344072 | tf_op jit(solution)/shard_map/ppermute | solution.py:42
  96.7 1.7 %home.1 = (bf16[81,4,512]{2,1,0:T(4,128)(2,1)}, f32[4,81,1,512]{3,2,1,0:T(1,128)}) custom-call(s32[2]{0:T(128)S(1)} %pad_add_fusion.scal, bf16[177,512]{1,0:T(8,128)(2,1)S(1)} %get-tuple-element.111.h0, bf16[177,512]{1,0:T(8,128)(2,1)S(1)} %collective-permute-done.18.h1, bf16[177,512]{1,0:T(8,128)(2,1)S(1)} %collective-permute-done.19.h2, ...), custom_call_target="tpu_custom_call" | custom-call | flops 100000000 | bytes 725000 | tf_op jit(solution)/shard_map/home/pallas_call | solution.py:531
  99.1 3.9 %collective-permute-start.33 = (bf16[64,512]{1,0:T(8,128)(2,1)S(1)}, bf16[64,512]{1,0:T(8,128)(2,1)S(1)}, u32[]{:S(2)}, u32[]{:S(2)}) collective-permute-start(bf16[64,512]{1,0:T(8,128)(2,1)S(1)} %get-tuple-element.135), channel_id=1, source_target_pairs={{0,2},{1,3},{2,0},{3,1},{4,6},{5,7},{6,4},{7,5},{8,10},{9,11},{10,... | collective-permute-start | bytes 196616 | tf_op jit(solution)/shard_map/ppermute | solution.py:42
  103.0 1.5 %collective-permute-done.24.g1 = bf16[112,512]{1,0:T(8,128)(2,1)S(1)} collective-permute-done((bf16[112,512]{1,0:T(8,128)(2,1)S(1)}, bf16[112,512]{1,0:T(8,128)(2,1)S(1)}, u32[]{:S(2)}, u32[]{:S(2)}) %collective-permute-start.24) | collective-permute-done | bytes 114720 | tf_op jit(solution)/shard_map/ppermute | solution.py:42
  104.6 11.4 %all-gather.1 = bf16[896,512]{1,0:T(8,128)(2,1)S(1)} all-gather(bf16[112,512]{1,0:T(8,128)(2,1)S(1)} %patch_a.1), channel_id=3, replica_groups={{0,4,8,12,16,20,24,28},{1,5,9,13,17,21,25,29},{2,6,10,14,18,22,26,30},{..., dimensions={0}, use_global_device_ids=true | all-gather | bytes 1032192 | tf_op jit(solution)/shard_map/all_gather | solution.py:554
  116.0 0.6 patch_b.1
  116.6 8.8 %all-gather.2 = bf16[384,512]{1,0:T(8,128)(2,1)S(1)} all-gather(bf16[48,512]{1,0:T(8,128)(2,1)S(1)} %get-tuple-element.137), channel_id=4, replica_groups={{0,4,8,12,16,20,24,28},{1,5,9,13,17,21,25,29},{2,6,10,14,18,22,26,30},{..., dimensions={0}, use_global_device_ids=true | all-gather | bytes 442368 | tf_op jit(solution)/shard_map/all_gather | solution.py:554
  125.5 0.6 multiply_add_fusion
  126.1 3.4 %update.1 = (f32[128,3072]{1,0:T(8,128)}, f32[128,3072]{1,0:T(8,128)}, f32[128,3072]{1,0:T(8,128)}, f32[384,512]{1,0:T(8,128)}, f32[384,512]{1,0:T(8,128)}, /*in...) custom-call(bf16[8,112,512]{2,1,0:T(8,128)(2,1)S(1)} %bitcast.21, ...), custom_call_target="tpu_custom_call" | custom-call | flops 100000000 | bytes 8703536 | tf_op jit(solution)/shard_map/update/pallas_call | solution.py:531
  (93 shorter events, 6.5 us)
Async XLA Ops:
  1.6 11.8 %collective-permute-start.2 = (bf16[16,3072]{1,0:T(8,128)(2,1)S(1)}, bf16[16,3072]{1,0:T(8,128)(2,1)S(1)}, u32[]{:S(2)}, u32[]{:S(2)}) collective-permute-start(bf16[16,3072]{1,0:T(8,128)(2,1)S(1)} %dynamic-slice_convert_fusion), channel_id=1, source_target_pairs={{0,1},{1,2},{2,3},{3,0},{4,5},{5,6},{6,7},{7,4},{8,9},{9,10},{10,1... | collective-permute-start | bytes 294920 | tf_op jit(solution)/shard_map/ppermute | solution.py:42
  4.7 9.2 %collective-permute-start.1 = (bf16[16,3072]{1,0:T(8,128)(2,1)S(1)}, bf16[16,3072]{1,0:T(8,128)(2,1)S(1)}, u32[]{:S(2)}, u32[]{:S(2)}) collective-permute-start(bf16[16,3072]{1,0:T(8,128)(2,1)S(1)} %dynamic-slice_convert_fusion), channel_id=1, source_target_pairs={{0,2},{1,3},{2,0},{3,1},{4,6},{5,7},{6,4},{7,5},{8,10},{9,11},{10,... | collective-permute-start | bytes 294920 | tf_op jit(solution)/shard_map/ppermute | solution.py:42
  7.3 6.6 %collective-permute-start = (bf16[16,3072]{1,0:T(8,128)(2,1)S(1)}, bf16[16,3072]{1,0:T(8,128)(2,1)S(1)}, u32[]{:S(2)}, u32[]{:S(2)}) collective-permute-start(bf16[16,3072]{1,0:T(8,128)(2,1)S(1)} %dynamic-slice_convert_fusion), channel_id=1, source_target_pairs={{0,3},{1,0},{2,1},{3,2},{4,7},{5,4},{6,5},{7,6},{8,11},{9,8},{10,9... | collective-permute-start | bytes 294920 | tf_op jit(solution)/shard_map/ppermute | solution.py:42
  13.9 14.7 %collective-permute-start.7 = (bf16[3,16,3072]{2,1,0:T(8,128)(2,1)S(1)}, bf16[3,16,3072]{2,1,0:T(8,128)(2,1)S(1)}, u32[]{:S(2)}, u32[]{:S(2)}) collective-permute-start(bf16[3,16,3072]{2,1,0:T(8,128)(2,1)S(1)} %stack_i.1.tie.rest_0_), channel_id=1, source_target_pairs={{0,8},{4,12},{8,0},{12,4},{16,24},{20,28},{24,16},{28,20},{1,9},{5... | collective-permute-start | bytes 884744 | tf_op jit(solution)/shard_map/ppermute | solution.py:47
  15.5 13.8 %collective-permute-start.9 = (bf16[3,16,3072]{2,1,0:T(8,128)(2,1)S(1)}, bf16[3,16,3072]{2,1,0:T(8,128)(2,1)S(1)}, u32[]{:S(2)}, u32[]{:S(2)}) collective-permute-start(bf16[3,16,3072]{2,1,0:T(8,128)(2,1)S(1)} %stack_i.1.tie.rest_0_), channel_id=1, source_target_pairs={{0,16},{4,20},{8,24},{12,28},{16,0},{20,4},{24,8},{28,12},{1,17},{... | collective-permute-start | bytes 884744 | tf_op jit(solution)/shard_map/ppermute | solution.py:47
  17.0 6.0 %collective-permute-start.15 = (bf16[64,512]{1,0:T(8,128)(2,1)S(1)}, bf16[64,512]{1,0:T(8,128)(2,1)S(1)}, u32[]{:S(2)}, u32[]{:S(2)}) collective-permute-start(bf16[64,512]{1,0:T(8,128)(2,1)S(1)} %get-tuple-element.83.tie), channel_id=1, source_target_pairs={{0,3},{1,0},{2,1},{3,2},{4,7},{5,4},{6,5},{7,6},{8,11},{9,8},{10,9... | collective-permute-start | bytes 196616 | tf_op jit(solution)/shard_map/ppermute | solution.py:42
  20.6 6.8 %collective-permute-start.14 = (bf16[64,512]{1,0:T(8,128)(2,1)S(1)}, bf16[64,512]{1,0:T(8,128)(2,1)S(1)}, u32[]{:S(2)}, u32[]{:S(2)}) collective-permute-start(bf16[64,512]{1,0:T(8,128)(2,1)S(1)} %get-tuple-element.83.tie), channel_id=1, source_target_pairs={{0,2},{1,3},{2,0},{3,1},{4,6},{5,7},{6,4},{7,5},{8,10},{9,11},{10,... | collective-permute-start | bytes 196616 | tf_op jit(solution)/shard_map/ppermute | solution.py:42
  21.0 6.8 %collective-permute-start.13 = (bf16[64,512]{1,0:T(8,128)(2,1)S(1)}, bf16[64,512]{1,0:T(8,128)(2,1)S(1)}, u32[]{:S(2)}, u32[]{:S(2)}) collective-permute-start(bf16[64,512]{1,0:T(8,128)(2,1)S(1)} %get-tuple-element.83.tie), channel_id=1, source_target_pairs={{0,1},{1,2},{2,3},{3,0},{4,5},{5,6},{6,7},{7,4},{8,9},{9,10},{10,1... | collective-permute-start | bytes 196616 | tf_op jit(solution)/shard_map/ppermute | solution.py:42
  22.4 21.6 %copy-start.14 = (f32[8004]{0:T(1024)S(1)}, f32[8004]{0:T(1024)}, u32[]{:S(2)}) copy-start(f32[8004]{0:T(1024)} %param.29) | copy-start | bytes 96052
  22.4 21.6 %slice-start = ((f32[8004]{0:T(1024)}), f32[324]{0:T(512)S(1)}, s32[]{:S(2)}) async-start(f32[8004]{0:T(1024)} %param.29), calls=%async_computation | async-start | bytes 4096 | tf_op jit(solution)/shard_map/slice | solution.py:642
  23.0 23.8 %copy-start.2 = (f32[128,3072]{1,0:T(8,128)S(1)}, f32[128,3072]{1,0:T(8,128)}, u32[]{:S(2)}) copy-start(f32[128,3072]{1,0:T(8,128)} %rest_0_.1) | copy-start | bytes 4718596
  23.0 19.8 %collective-permute-start.3 = (bf16[177,512]{1,0:T(8,128)(2,1)S(1)}, bf16[177,512]{1,0:T(8,128)(2,1)S(1)}, u32[]{:S(2)}, u32[]{:S(2)}) collective-permute-start(bf16[177,512]{1,0:T(8,128)(2,1)S(1)} %get-tuple-element.85), channel_id=1, source_target_pairs={{0,3},{1,0},{2,1},{3,2},{4,7},{5,4},{6,5},{7,6},{8,11},{9,8},{10,9... | collective-permute-start | bytes 543752 | tf_op jit(solution)/shard_map/ppermute | solution.py:42
  27.3 16.0 %collective-permute-start.4 = (bf16[177,512]{1,0:T(8,128)(2,1)S(1)}, bf16[177,512]{1,0:T(8,128)(2,1)S(1)}, u32[]{:S(2)}, u32[]{:S(2)}) collective-permute-start(bf16[177,512]{1,0:T(8,128)(2,1)S(1)} %get-tuple-element.86), channel_id=1, source_target_pairs={{0,2},{1,3},{2,0},{3,1},{4,6},{5,7},{6,4},{7,5},{8,10},{9,11},{10,... | collective-permute-start | bytes 543752 | tf_op jit(solution)/shard_map/ppermute | solution.py:42
  27.8 15.7 %collective-permute-start.5 = (bf16[177,512]{1,0:T(8,128)(2,1)S(1)}, bf16[177,512]{1,0:T(8,128)(2,1)S(1)}, u32[]{:S(2)}, u32[]{:S(2)}) collective-permute-start(bf16[177,512]{1,0:T(8,128)(2,1)S(1)} %get-tuple-element.87), channel_id=1, source_target_pairs={{0,1},{1,2},{2,3},{3,0},{4,5},{5,6},{6,7},{7,4},{8,9},{9,10},{10,1... | collective-permute-start | bytes 543752 | tf_op jit(solution)/shard_map/ppermute | solution.py:42
  28.7 15.2 %collective-permute-start.11 = (bf16[3,16,3072]{2,1,0:T(8,128)(2,1)S(1)}, bf16[3,16,3072]{2,1,0:T(8,128)(2,1)S(1)}, u32[]{:S(2)}, u32[]{:S(2)}) collective-permute-start(bf16[3,16,3072]{2,1,0:T(8,128)(2,1)S(1)} %collective-permute-done.7.rest_2_), channel_id=1, source_target_pairs={{0,16},{4,20},{8,24},{12,28},{16,0},{20,4},{24,8},{28,12},{1,17},{... | collective-permute-start | bytes 884744 | tf_op jit(solution)/shard_map/ppermute | solution.py:47
  42.8 8.2 %collective-permute-start.16 = (bf16[4,3,64,512]{3,2,1,0:T(8,128)(2,1)S(1)}, bf16[4,3,64,512]{3,2,1,0:T(8,128)(2,1)S(1)}, u32[]{:S(2)}, u32[]{:S(2)}) collective-permute-start(bf16[4,3,64,512]{3,2,1,0:T(8,128)(2,1)S(1)} %bitcast.23), channel_id=1, source_target_pairs={{0,4},{4,0},{8,12},{12,8},{16,20},{20,16},{24,28},{28,24},{1,5},{5... | collective-permute-start | bytes 2359304 | tf_op jit(solution)/shard_map/ppermute | solution.py:47
  42.9 2.7 %collective-permute-start.6 = (bf16[3,16,3072]{2,1,0:T(8,128)(2,1)S(1)}, bf16[3,16,3072]{2,1,0:T(8,128)(2,1)S(1)}, u32[]{:S(2)}, u32[]{:S(2)}) collective-permute-start(bf16[3,16,3072]{2,1,0:T(8,128)(2,1)S(1)} %stack_i.1.tie.rest_0_), channel_id=1, source_target_pairs={{0,4},{4,0},{8,12},{12,8},{16,20},{20,16},{24,28},{28,24},{1,5},{5... | collective-permute-start | bytes 884744 | tf_op jit(solution)/shard_map/ppermute | solution.py:47
  43.4 2.6 %collective-permute-start.10 = (bf16[3,16,3072]{2,1,0:T(8,128)(2,1)S(1)}, bf16[3,16,3072]{2,1,0:T(8,128)(2,1)S(1)}, u32[]{:S(2)}, u32[]{:S(2)}) collective-permute-start(bf16[3,16,3072]{2,1,0:T(8,128)(2,1)S(1)} %collective-permute-done.9.rest_4_.tie), channel_id=1, source_target_pairs={{0,4},{4,0},{8,12},{12,8},{16,20},{20,16},{24,28},{28,24},{1,5},{5... | collective-permute-start | bytes 884744 | tf_op jit(solution)/shard_map/ppermute | solution.py:47
  43.4 3.0 %collective-permute-start.8 = (bf16[3,16,3072]{2,1,0:T(8,128)(2,1)S(1)}, bf16[3,16,3072]{2,1,0:T(8,128)(2,1)S(1)}, u32[]{:S(2)}, u32[]{:S(2)}) collective-permute-start(bf16[3,16,3072]{2,1,0:T(8,128)(2,1)S(1)} %collective-permute-done.7.rest_2_), channel_id=1, source_target_pairs={{0,4},{4,0},{8,12},{12,8},{16,20},{20,16},{24,28},{28,24},{1,5},{5... | collective-permute-start | bytes 884744 | tf_op jit(solution)/shard_map/ppermute | solution.py:47
  43.9 2.9 %collective-permute-start.12 = (bf16[3,16,3072]{2,1,0:T(8,128)(2,1)S(1)}, bf16[3,16,3072]{2,1,0:T(8,128)(2,1)S(1)}, u32[]{:S(2)}, u32[]{:S(2)}) collective-permute-start(bf16[3,16,3072]{2,1,0:T(8,128)(2,1)S(1)} %collective-permute-done.11.rest_6_), channel_id=1, source_target_pairs={{0,4},{4,0},{8,12},{12,8},{16,20},{20,16},{24,28},{28,24},{1,5},{5... | collective-permute-start | bytes 884744 | tf_op jit(solution)/shard_map/ppermute | solution.py:47
  51.1 1.8 %copy-start.1 = (f32[384,512]{1,0:T(8,128)S(1)}, f32[384,512]{1,0:T(8,128)}, u32[]{:S(2)}) copy-start(f32[384,512]{1,0:T(8,128)} %rest_3_.1) | copy-start | bytes 2359300
  58.0 4.0 %collective-permute-start.17 = (bf16[4,448,512]{2,1,0:T(8,128)(2,1)S(1)}, bf16[4,448,512]{2,1,0:T(8,128)(2,1)S(1)}, u32[]{:S(2)}, u32[]{:S(2)}) collective-permute-start(bf16[4,448,512]{2,1,0:T(8,128)(2,1)S(1)} %get-tuple-element.109), channel_id=1, source_target_pairs={{0,4},{4,0},{8,12},{12,8},{16,20},{20,16},{24,28},{28,24},{1,5},{5... | collective-permute-start | bytes 5505032 | tf_op jit(solution)/shard_map/ppermute | solution.py:47
  61.6 11.4 %collective-permute-start.27 = (bf16[4,192,512]{2,1,0:T(8,128)(2,1)S(1)}, bf16[4,192,512]{2,1,0:T(8,128)(2,1)S(1)}, u32[]{:S(2)}, u32[]{:S(2)}) collective-permute-start(bf16[4,192,512]{2,1,0:T(8,128)(2,1)S(1)} %get-tuple-element.125), channel_id=1, source_target_pairs={{0,4},{4,0},{8,12},{12,8},{16,20},{20,16},{24,28},{28,24},{1,5},{5... | collective-permute-start | bytes 2359304 | tf_op jit(solution)/shard_map/ppermute | solution.py:47
  62.4 22.5 %collective-permute-start.22 = (bf16[448,512]{1,0:T(8,128)(2,1)S(1)}, bf16[448,512]{1,0:T(8,128)(2,1)S(1)}, u32[]{:S(2)}, u32[]{:S(2)}) collective-permute-start(bf16[448,512]{1,0:T(8,128)(2,1)S(1)} %get-tuple-element.119), channel_id=1, source_target_pairs={{0,16},{4,20},{8,24},{12,28},{16,0},{20,4},{24,8},{28,12},{1,17},{... | collective-permute-start | bytes 1376264 | tf_op jit(solution)/shard_map/ppermute | solution.py:47
  64.0 24.1 %collective-permute-start.23 = (bf16[448,512]{1,0:T(8,128)(2,1)S(1)}, bf16[448,512]{1,0:T(8,128)(2,1)S(1)}, u32[]{:S(2)}, u32[]{:S(2)}) collective-permute-start(bf16[448,512]{1,0:T(8,128)(2,1)S(1)} %get-tuple-element.110.rest_0_), channel_id=1, source_target_pairs={{0,24},{4,28},{8,16},{12,20},{16,8},{20,12},{24,0},{28,4},{1,25},{... | collective-permute-start | bytes 1376264 | tf_op jit(solution)/shard_map/ppermute | solution.py:47
  65.4 24.2 %collective-permute-start.21 = (bf16[448,512]{1,0:T(8,128)(2,1)S(1)}, bf16[448,512]{1,0:T(8,128)(2,1)S(1)}, u32[]{:S(2)}, u32[]{:S(2)}) collective-permute-start(bf16[448,512]{1,0:T(8,128)(2,1)S(1)} %get-tuple-element.118.tie), channel_id=1, source_target_pairs={{0,8},{4,12},{8,0},{12,4},{16,24},{20,28},{24,16},{28,20},{1,9},{5... | collective-permute-start | bytes 1376264 | tf_op jit(solution)/shard_map/ppermute | solution.py:47
  70.3 7.8 %collective-permute-start.18 = (bf16[177,512]{1,0:T(8,128)(2,1)S(1)}, bf16[177,512]{1,0:T(8,128)(2,1)S(1)}, u32[]{:S(2)}, u32[]{:S(2)}) collective-permute-start(bf16[177,512]{1,0:T(8,128)(2,1)S(1)} %get-tuple-element.112), channel_id=1, source_target_pairs={{0,1},{1,2},{2,3},{3,0},{4,5},{5,6},{6,7},{7,4},{8,9},{9,10},{10,1... | collective-permute-start | bytes 543752 | tf_op jit(solution)/shard_map/ppermute | solution.py:42
  72.9 1.2 collective-permute-start.28
  74.3 22.4 %collective-permute-start.29 = (bf16[208,512]{1,0:T(8,128)(2,1)S(1)}, bf16[208,512]{1,0:T(8,128)(2,1)S(1)}, u32[]{:S(2)}, u32[]{:S(2)}) collective-permute-start(bf16[208,512]{1,0:T(8,128)(2,1)S(1)} %get-tuple-element.129), channel_id=1, source_target_pairs={{0,8},{4,12},{8,0},{12,4},{16,24},{20,28},{24,16},{28,20},{1,9},{5... | collective-permute-start | bytes 638984 | tf_op jit(solution)/shard_map/ppermute | solution.py:47
  78.1 13.2 %collective-permute-start.19 = (bf16[177,512]{1,0:T(8,128)(2,1)S(1)}, bf16[177,512]{1,0:T(8,128)(2,1)S(1)}, u32[]{:S(2)}, u32[]{:S(2)}) collective-permute-start(bf16[177,512]{1,0:T(8,128)(2,1)S(1)} %get-tuple-element.113), channel_id=1, source_target_pairs={{0,2},{1,3},{2,0},{3,1},{4,6},{5,7},{6,4},{7,5},{8,10},{9,11},{10,... | collective-permute-start | bytes 543752 | tf_op jit(solution)/shard_map/ppermute | solution.py:42
  84.9 7.5 %collective-permute-start.20 = (bf16[177,512]{1,0:T(8,128)(2,1)S(1)}, bf16[177,512]{1,0:T(8,128)(2,1)S(1)}, u32[]{:S(2)}, u32[]{:S(2)}) collective-permute-start(bf16[177,512]{1,0:T(8,128)(2,1)S(1)} %get-tuple-element.114), channel_id=1, source_target_pairs={{0,3},{1,0},{2,1},{3,2},{4,7},{5,4},{6,5},{7,6},{8,11},{9,8},{10,9... | collective-permute-start | bytes 543752 | tf_op jit(solution)/shard_map/ppermute | solution.py:42
  88.1 10.8 %collective-permute-start.30 = (bf16[208,512]{1,0:T(8,128)(2,1)S(1)}, bf16[208,512]{1,0:T(8,128)(2,1)S(1)}, u32[]{:S(2)}, u32[]{:S(2)}) collective-permute-start(bf16[208,512]{1,0:T(8,128)(2,1)S(1)} %get-tuple-element.130), channel_id=1, source_target_pairs={{0,16},{4,20},{8,24},{12,28},{16,0},{20,4},{24,8},{28,12},{1,17},{... | collective-permute-start | bytes 638984 | tf_op jit(solution)/shard_map/ppermute | solution.py:47
  89.6 9.3 %collective-permute-start.31 = (bf16[208,512]{1,0:T(8,128)(2,1)S(1)}, bf16[208,512]{1,0:T(8,128)(2,1)S(1)}, u32[]{:S(2)}, u32[]{:S(2)}) collective-permute-start(bf16[208,512]{1,0:T(8,128)(2,1)S(1)} %get-tuple-element.131), channel_id=1, source_target_pairs={{0,24},{4,28},{8,16},{12,20},{16,8},{20,12},{24,0},{28,4},{1,25},{... | collective-permute-start | bytes 638984 | tf_op jit(solution)/shard_map/ppermute | solution.py:47
  91.3 11.7 %collective-permute-start.25 = (bf16[112,512]{1,0:T(8,128)(2,1)S(1)}, bf16[112,512]{1,0:T(8,128)(2,1)S(1)}, u32[]{:S(2)}, u32[]{:S(2)}) collective-permute-start(bf16[112,512]{1,0:T(8,128)(2,1)S(1)} %get-tuple-element.122), channel_id=1, source_target_pairs={{0,2},{1,3},{2,0},{3,1},{4,6},{5,7},{6,4},{7,5},{8,10},{9,11},{10,... | collective-permute-start | bytes 344072 | tf_op jit(solution)/shard_map/ppermute | solution.py:42
  92.4 10.6 %collective-permute-start.26 = (bf16[112,512]{1,0:T(8,128)(2,1)S(1)}, bf16[112,512]{1,0:T(8,128)(2,1)S(1)}, u32[]{:S(2)}, u32[]{:S(2)}) collective-permute-start(bf16[112,512]{1,0:T(8,128)(2,1)S(1)} %get-tuple-element.123), channel_id=1, source_target_pairs={{0,3},{1,0},{2,1},{3,2},{4,7},{5,4},{6,5},{7,6},{8,11},{9,8},{10,9... | collective-permute-start | bytes 344072 | tf_op jit(solution)/shard_map/ppermute | solution.py:42
  96.7 7.8 %collective-permute-start.24 = (bf16[112,512]{1,0:T(8,128)(2,1)S(1)}, bf16[112,512]{1,0:T(8,128)(2,1)S(1)}, u32[]{:S(2)}, u32[]{:S(2)}) collective-permute-start(bf16[112,512]{1,0:T(8,128)(2,1)S(1)} %get-tuple-element.121.tie), channel_id=1, source_target_pairs={{0,1},{1,2},{2,3},{3,0},{4,5},{5,6},{6,7},{7,4},{8,9},{9,10},{10,1... | collective-permute-start | bytes 344072 | tf_op jit(solution)/shard_map/ppermute | solution.py:42
  96.7 28.7 %copy-start.15 = (f32[8004]{0:T(1024)S(1)}, f32[8004]{0:T(1024)}, u32[]{:S(2)}) copy-start(f32[8004]{0:T(1024)} %param.31) | copy-start | bytes 96052
  96.7 28.7 %copy-start.16 = (f32[8004]{0:T(1024)S(1)}, f32[8004]{0:T(1024)}, u32[]{:S(2)}) copy-start(f32[8004]{0:T(1024)} %param.30) | copy-start | bytes 96052
  96.7 29.4 %copy-start.11 = (f32[81,324]{1,0:T(8,128)S(1)}, f32[81,324]{1,0:T(8,128)}, u32[]{:S(2)}) copy-start(f32[81,324]{1,0:T(8,128)} %rest_8_.1) | copy-start | bytes 314932
  98.5 17.6 %copy-start.7 = (f32[4,81,1,512]{3,2,1,0:T(1,128)S(1)}, f32[4,81,1,512]{3,2,1,0:T(1,128)}, u32[]{:S(2)}) copy-start(f32[4,81,1,512]{3,2,1,0:T(1,128)} %get-tuple-element.116.tie_home) | copy-start | bytes 1990660
  98.9 27.2 %copy-start.6 = (f32[384,512]{1,0:T(8,128)S(1)}, f32[384,512]{1,0:T(8,128)}, u32[]{:S(2)}) copy-start(f32[384,512]{1,0:T(8,128)} %rest_5_.1) | copy-start | bytes 2359300
  99.0 17.0 %collective-permute-start.32 = (bf16[64,512]{1,0:T(8,128)(2,1)S(1)}, bf16[64,512]{1,0:T(8,128)(2,1)S(1)}, u32[]{:S(2)}, u32[]{:S(2)}) collective-permute-start(bf16[64,512]{1,0:T(8,128)(2,1)S(1)} %get-tuple-element.134), channel_id=1, source_target_pairs={{0,1},{1,2},{2,3},{3,0},{4,5},{5,6},{6,7},{7,4},{8,9},{9,10},{10,1... | collective-permute-start | bytes 196616 | tf_op jit(solution)/shard_map/ppermute | solution.py:42
  99.1 16.9 %collective-permute-start.33 = (bf16[64,512]{1,0:T(8,128)(2,1)S(1)}, bf16[64,512]{1,0:T(8,128)(2,1)S(1)}, u32[]{:S(2)}, u32[]{:S(2)}) collective-permute-start(bf16[64,512]{1,0:T(8,128)(2,1)S(1)} %get-tuple-element.135), channel_id=1, source_target_pairs={{0,2},{1,3},{2,0},{3,1},{4,6},{5,7},{6,4},{7,5},{8,10},{9,11},{10,... | collective-permute-start | bytes 196616 | tf_op jit(solution)/shard_map/ppermute | solution.py:42
  103.0 13.0 %collective-permute-start.34 = (bf16[64,512]{1,0:T(8,128)(2,1)S(1)}, bf16[64,512]{1,0:T(8,128)(2,1)S(1)}, u32[]{:S(2)}, u32[]{:S(2)}) collective-permute-start(bf16[64,512]{1,0:T(8,128)(2,1)S(1)} %get-tuple-element.136), channel_id=1, source_target_pairs={{0,3},{1,0},{2,1},{3,2},{4,7},{5,4},{6,5},{7,6},{8,11},{9,8},{10,9... | collective-permute-start | bytes 196616 | tf_op jit(solution)/shard_map/ppermute | solution.py:42
  104.5 21.6 %copy-start.5 = (f32[384,512]{1,0:T(8,128)S(1)}, f32[384,512]{1,0:T(8,128)}, u32[]{:S(2)}) copy-start(f32[384,512]{1,0:T(8,128)} %rest_4_.1) | copy-start | bytes 2359300
  104.6 21.6 %copy-start.3 = (f32[128,3072]{1,0:T(8,128)S(1)}, f32[128,3072]{1,0:T(8,128)}, u32[]{:S(2)}) copy-start(f32[128,3072]{1,0:T(8,128)} %rest_1_.1) | copy-start | bytes 4718596
  104.6 21.6 %copy-start.4 = (f32[128,3072]{1,0:T(8,128)S(1)}, f32[128,3072]{1,0:T(8,128)}, u32[]{:S(2)}) copy-start(f32[128,3072]{1,0:T(8,128)} %rest_2_.1) | copy-start | bytes 4718596
  104.6 21.6 %copy-start.10 = (f32[81,324]{1,0:T(8,128)S(1)}, f32[81,324]{1,0:T(8,128)}, u32[]{:S(2)}) copy-start(f32[81,324]{1,0:T(8,128)} %rest_7_.1) | copy-start | bytes 314932
  (5 other events, 5.2 us)
